TPU v7x, 32 devices: a whole 2x2x4 slice. The times are simulated.
32 devices in a mesh: replica: 2 (over y), dp: 4 (over x, core), tp: 4 (over z).
Axes of the slice: x: 2, y: 2, z: 4, core: 2. Of those that a mesh axis runs over, the one named last changes fastest.
Arguments:
- query_nope: bfloat16 [2048, 64, 128], P(('replica', 'dp'), 'tp'), parts along dimension 0, may hold values from -6 to 6
- query_rope: bfloat16 [2048, 4096], P(('replica', 'dp'), 'tp'), parts along dimension 0, may hold values from -8 to 8
- new_latent: bfloat16 [2048, 512], P(('replica', 'dp')), parts along dimension 0, may hold values from -6 to 6
- new_rope: bfloat16 [2048, 64], P(('replica', 'dp')), parts along dimension 0, may hold values from -8 to 8
- cache_latent: bfloat16 [256, 64, 512], P(('replica', 'dp')), parts along dimension 0, may hold values from -6 to 6
- cache_rope: bfloat16 [256, 4096], P(('replica', 'dp')), parts along dimension 0, may hold values from -8 to 8
- absorb_key: bfloat16 [64, 128, 512], P('tp'), may hold values from -0.5 to 0.5
- absorb_value: bfloat16 [64, 512, 128], P('tp'), may hold values from -0.25 to 0.25
- output_weight: bfloat16 [8192, 7168], P('tp', 'dp'), may hold values from -0.5 to 0.5
- send_blocks: int32 [8, 4, 2], P(('replica', 'dp')), parts along dimension 0, may hold values from 0 to 31
- prefill_table: int32 [8, 16], P(('replica', 'dp')), parts along dimension 0, may hold values from 0 to 31, as said below
- prefill_offset: int32 [8], P(('replica', 'dp')), parts along dimension 0, may hold values from 0 to 1024, as said below
- decode_table: int32 [128, 4], P(('replica', 'dp')), parts along dimension 0, may hold values from 0 to 39
- decode_length: int32 [128], P(('replica', 'dp')), parts along dimension 0, may hold values from 1 to 256, as said below
Outputs:
- mixed: bfloat16 [2048, 7168], P(('replica', 'tp'), 'dp'), parts along dimension 0
There are 2 independent parts, one for each index of `replica`. A program takes and returns all parts, laid end to end along the dimension named above; an argument that names none is the same for every part. Nothing has to cross between parts.
Inputs may be any that keep to these rules, and one draw needn't show every extreme that they name: `prefill_table`: each row names 16 different blocks. Some group has prefill_offset 16 * 64. `decode_length`: some request has 256 cached tokens. `decode_table`: numbers below 32 name the group's own blocks; 32 + s * 2 + k names slot k of what group s sends it; numbers may repeat.
All inputs are finite; a program needn't handle non-finite values.
Results may differ from a plain program's by a relative error of at most 0.017.
Values may be sent and summed in bfloat16 or wider, within the bound.
No kernel may reach another device: no remote copies, remote signals or barrier semaphores. Data moves between devices by JAX's collectives and lax.ppermute only.
A program may use at most 192 MiB of HBM per device.

v0:
```python
import jax
import jax.numpy as jnp
from jax import lax
from jax.sharding import PartitionSpec as P


def normalized(scores, visible):
    masked = jnp.where(visible, scores, -jnp.inf)
    row_top = jnp.max(masked, axis=-1, keepdims=True)
    exp_terms = jnp.where(visible, jnp.exp(masked - row_top), 0.0)
    return (exp_terms / jnp.sum(exp_terms, axis=-1, keepdims=True)).astype(jnp.bfloat16)


def body(
    query_nope,
    query_rope,
    new_latent,
    new_rope,
    cache_latent,
    cache_rope,
    absorb_key,
    absorb_value,
    output_weight,
    send_blocks,
    prefill_table,
    prefill_offset,
    decode_table,
    decode_length,
):
    tok_group, heads_here, nope_dim = query_nope.shape
    pool_blocks, block_len, latent_dim = cache_latent.shape
    rope_dim = new_rope.shape[1]
    group_count = lax.axis_size("dp")
    capacity = send_blocks.shape[2]
    decodes = decode_length.shape[0]
    prefill_len = tok_group - decodes
    score_scale = (nope_dim + rope_dim) ** (-0.5)
    q_latent = jnp.einsum(
        "thd,hdl->thl", query_nope, absorb_key, preferred_element_type=jnp.float32
    ).astype(jnp.bfloat16)
    rope_query = query_rope.reshape(tok_group, heads_here, rope_dim)
    outgoing = send_blocks[0]
    send_latent = cache_latent[outgoing]
    send_rope = cache_rope[outgoing]
    recv_latent, recv_rope = (
        lax.all_to_all(send_latent, "dp", split_axis=0, concat_axis=0, tiled=True),
        lax.all_to_all(send_rope, "dp", split_axis=0, concat_axis=0, tiled=True),
    )
    ext_latent = jnp.concatenate(
        [cache_latent, recv_latent.reshape(group_count * capacity, block_len, latent_dim)], 0
    )
    ext_rope = jnp.concatenate(
        [cache_rope, recv_rope.reshape(group_count * capacity, block_len * rope_dim)], 0
    )
    prior_ids = prefill_table[0]
    prior_len = prior_ids.shape[0] * block_len
    key_latent = jnp.concatenate(
        [cache_latent[prior_ids].reshape(prior_len, latent_dim), new_latent[:prefill_len]], 0
    )
    key_rope = jnp.concatenate(
        [cache_rope[prior_ids].reshape(prior_len, rope_dim), new_rope[:prefill_len]], 0
    )
    scores = (
        jnp.einsum(
            "thl,kl->thk", q_latent[:prefill_len], key_latent, preferred_element_type=jnp.float32
        )
        + jnp.einsum(
            "the,ke->thk", rope_query[:prefill_len], key_rope, preferred_element_type=jnp.float32
        )
    ) * score_scale
    key_pos = jnp.arange(prior_len + prefill_len)
    token_pos = jnp.arange(prefill_len)
    visible = jnp.where(
        key_pos[None, :] < prior_len,
        key_pos[None, :] < prefill_offset[0],
        key_pos[None, :] - prior_len <= token_pos[:, None],
    )
    weights = normalized(scores, visible[:, None, :])
    prefill_out = jnp.einsum(
        "thk,kl->thl", weights, key_latent, preferred_element_type=jnp.float32
    ).astype(jnp.bfloat16)
    dec_span = decode_table.shape[1] * block_len
    decode_latent = jnp.concatenate(
        [
            ext_latent[decode_table].reshape(decodes, dec_span, latent_dim),
            new_latent[prefill_len:][:, None, :],
        ],
        1,
    )
    decode_rope = jnp.concatenate(
        [
            ext_rope[decode_table].reshape(decodes, dec_span, rope_dim),
            new_rope[prefill_len:][:, None, :],
        ],
        1,
    )
    dec_scores = (
        jnp.einsum(
            "rhl,rkl->rhk",
            q_latent[prefill_len:],
            decode_latent,
            preferred_element_type=jnp.float32,
        )
        + jnp.einsum(
            "rhe,rke->rhk",
            rope_query[prefill_len:],
            decode_rope,
            preferred_element_type=jnp.float32,
        )
    ) * score_scale
    slot_pos = jnp.arange(dec_span + 1)
    dec_visible = (slot_pos[None, :] < decode_length[:, None]) | (slot_pos[None, :] == dec_span)
    dec_weights = normalized(dec_scores, dec_visible[:, None, :])
    decode_out = jnp.einsum(
        "rhk,rkl->rhl", dec_weights, decode_latent, preferred_element_type=jnp.float32
    ).astype(jnp.bfloat16)
    attended = jnp.concatenate([prefill_out, decode_out], 0)
    head_out = jnp.einsum(
        "thl,hlv->thv", attended, absorb_value, preferred_element_type=jnp.float32
    ).astype(jnp.bfloat16)
    head_out = head_out.reshape(tok_group, heads_here * absorb_value.shape[2])
    partials = jnp.dot(
        lax.all_gather(head_out, "dp", axis=0, tiled=True),
        output_weight,
        preferred_element_type=jnp.float32,
    )
    return lax.psum_scatter(partials.astype(jnp.bfloat16), "tp", scatter_dimension=0, tiled=True)


def solution(mesh):
    return jax.shard_map(
        body,
        mesh=mesh,
        in_specs=(
            P(("replica", "dp"), "tp", None),
            P(("replica", "dp"), "tp"),
            P(("replica", "dp"), None),
            P(("replica", "dp"), None),
            P(("replica", "dp"), None, None),
            P(("replica", "dp"), None),
            P("tp", None, None),
            P("tp", None, None),
            P("tp", "dp"),
            P(("replica", "dp"), None, None),
            P(("replica", "dp"), None),
            P(("replica", "dp")),
            P(("replica", "dp"), None),
            P(("replica", "dp")),
        ),
        out_specs=P(("replica", "tp"), "dp"),
        check_vma=False,
    )
```

profile of v0, /device:TPU:0, one launch (start us, length us, event | category | flops | bytes accessed | tf_op | source)
XLA Modules:
  0.0 254.6 jit_solution(9594928798982666292)
XLA Ops:
  6.5 0.8 compare_select_fusion.1
  7.4 0.1 copy.29
  7.5 0.1 reshape.198
  7.6 1.6 gather_fusion.4
  9.2 0.7 reshape.213
  9.9 4.2 %all-to-all-start.1 = ((bf16[4,2,4096]{2,1,0:T(2,128)(2,1)}), bf16[4,2,4096]{2,1,0:T(2,128)(2,1)S(1)}, u32[]{:S(2)}, u32[]{:S(2)}) async-start(bf16[4,2,4096]{2,1,0:T(2,128)(2,1)} %reshape.213), calls=%async_computation.1 | async-start | bytes 131072 | tf_op jit(solution)/shard_map/all_to_all | solution.py:47
  14.1 0.6 iota_compare_fusion.4
  14.7 0.6 iota_add_fusion
  15.3 1.3 slice_bitcast_fusion
  16.6 1.0 slice.31
  18.2 0.7 fusion.38
  18.9 0.7 compare_select_fusion
  19.6 0.6 iota_compare_fusion.2
  20.1 0.1 copy.30
  20.2 0.7 reshape.206
  20.9 0.0 copy-done.12
  20.9 1.7 gather_fusion.1
  22.6 0.2 reshape.174
  22.9 0.1 copy.26
  23.0 0.0 slice-done.1
  23.0 0.2 copy.27
  23.2 3.3 %gather_fusion = bf16[16,64,512]{2,1,0:T(8,128)(2,1)} fusion(bf16[32,64,512]{2,1,0:T(8,128)(2,1)} %param.18, s32[1024]{0:T(1024)} %copy-done.12), kind=kCustom, calls=%fused_computation | custom fusion | bytes 2097216 | tf_op jit(solution)/shard_map/gather | solution.py:58
  26.6 2.5 convert_bitcast_fusion
  29.0 0.0 copy-start.7
  29.1 0.0 copy-start.5
  29.1 2.7 %slice.52 = bf16[240,16,512]{2,0,1:T(8,128)(2,1)} slice(bf16[256,16,512]{2,0,1:T(8,128)(2,1)S(1)} %convert_bitcast_fusion), slice={[0:240], [0:16], [0:512]} | slice | bytes 7864320 | tf_op jit(solution)/shard_map/slice | solution.py:65
  31.8 0.2 fusion.22
  32.0 0.0 copy-done.5
  32.0 0.0 copy-start.4
  32.0 8.2 %fusion.34 = f32[1264,240,16]{0,1,2:T(8,128)} fusion(bf16[240,16,64]{0,2,1:T(8,128)(2,1)S(1)} %bitcast.55, bf16[240,64]{0,1:T(8,128)(2,1)S(1)} %bitcast.60, bf16[1024,64]{0,1:T(8,128)(2,1)S(1)} %copy.26), kind=kOutput, calls=%fused_computation.50 | convolution fusion | flops 621604864 | bytes 20068352 | tf_op jit(solution)/shard_map/the,ke->thk/dot_general | solution.py:67
  40.2 36.1 %fusion.5 = (f32[240,16]{1,0:T(8,128)S(1)}, f32[240,16,1264]{2,1,0:T(8,128)}) fusion(pred[240,1264]{1,0:T(8,128)(4,1)S(1)} %fusion.22, f32[1264,240,16]{0,1,2:T(8,128)} %fusion.34, bf16[240,16,512]{2,0,1:T(8,128)(2,1)} %slice.52, bf16[240,512]{1,0:T(8,128)(2,1)S(1)} %slice.31, bf16[1024,512]{1,0:T(8,128)(2,1)S(1)} %bitcast.57), kind=kOutput, calls=%fused_computation.14 | convolution fusion | flops 5001962496 | bytes 44375296 | tf_op jit(solution)/shard_map/sub | solution.py:10
  76.2 9.5 %divide_convert_fusion = bf16[240,16,1264]{2,1,0:T(8,128)(2,1)S(1)} fusion(f32[240,16,1264]{2,1,0:T(8,128)} %get-tuple-element.8, f32[240,16]{1,0:T(8,128)S(1)} %get-tuple-element.7, pred[240,1264]{1,0:T(8,128)(4,1)S(1)} %fusion.22), kind=kLoop, calls=%fused_computation.12 | loop fusion | flops 14561280 | bytes 29441280 | tf_op jit(solution)/shard_map/convert_element_type | solution.py:11
  85.7 0.0 copy-start.14
  85.8 0.0 slice-start.2
  85.8 0.0 copy-start.3
  85.8 9.8 %fusion.15 = bf16[240,16,512]{2,0,1:T(8,128)(2,1)} fusion(bf16[240,16,1264]{2,1,0:T(8,128)(2,1)S(1)} %divide_convert_fusion, bf16[240,512]{1,0:T(8,128)(2,1)S(1)} %slice.31, bf16[1024,512]{1,0:T(8,128)(2,1)S(1)} %bitcast.58), kind=kOutput, calls=%fused_computation.28 | convolution fusion | flops 4974804992 | bytes 14934016 | tf_op jit(solution)/shard_map/thk,kl->thl/dot_general | solution.py:79
  95.6 0.1 fusion.37
  95.7 0.1 slice.37
  95.8 3.0 %gather_fusion.2 = bf16[8,64,512]{2,1,0:T(8,128)(2,1)} fusion(bf16[32,64,512]{2,1,0:T(8,128)(2,1)} %param.18, s32[1024]{0:T(1024)S(1)} %copy-done.9), kind=kCustom, calls=%fused_computation.2 | custom fusion | bytes 1048608 | tf_op jit(solution)/shard_map/gather | solution.py:43
  98.8 0.1 copy.40
  98.9 0.1 slice.39
  99.0 0.2 copy.35
  99.2 0.0 all-to-all-done.1
  99.2 3.5 %all-to-all-start = ((bf16[4,2,64,512]{3,2,1,0:T(8,128)(2,1)}), bf16[4,2,64,512]{3,2,1,0:T(8,128)(2,1)S(1)}, u32[]{:S(2)}, u32[]{:S(2)}) async-start(bf16[4,2,64,512]{3,2,1,0:T(8,128)(2,1)} %bitcast.10), calls=%async_computation | async-start | bytes 1048576 | tf_op jit(solution)/shard_map/all_to_all | solution.py:46
  102.7 0.0 all-gather.2.cloned.1.call-start
  102.8 0.9 gather_fusion.5
  103.7 1.1 reshape.178
  104.8 0.3 copy.34
  105.2 6.3 %all-to-all-done = bf16[4,2,64,512]{3,2,1,0:T(8,128)(2,1)S(1)} async-done(((bf16[4,2,64,512]{3,2,1,0:T(8,128)(2,1)}), bf16[4,2,64,512]{3,2,1,0:T(8,128)(2,1)S(1)}, u32[]{:S(2)}, u32[]{:S(2)}) %all-to-all-start) | async-done | bytes 524320 | tf_op jit(solution)/shard_map/all_to_all | solution.py:46
  111.5 3.4 %pad_maximum_fusion.3 = bf16[40,64,512]{2,1,0:T(8,128)(2,1)} fusion(bf16[8,64,512]{2,1,0:T(8,128)(2,1)S(1)} %bitcast.56, bf16[32,64,512]{2,1,0:T(8,128)(2,1)} %param.18), kind=kLoop, calls=%fused_computation.27 | loop fusion | flops 1310720 | bytes 5242880 | tf_op jit(solution)/shard_map/concatenate | solution.py:49
  114.9 4.5 %gather_fusion.3 = bf16[64,64,512]{2,1,0:T(8,128)(2,1)} fusion(bf16[40,64,512]{2,1,0:T(8,128)(2,1)} %pad_maximum_fusion.3, s32[1024]{0:T(1024)S(1)} %pad_clamp_fusion), kind=kCustom, calls=%fused_computation.3 | custom fusion | bytes 8388864 | tf_op jit(solution)/shard_map/gather | solution.py:85
  119.5 3.5 %fusion.14 = f32[16,16,257]{2,1,0:T(8,128)S(1)} fusion(bf16[16,1,512]{2,1,0:T(2,128)(2,1)S(1)} %copy.31, bf16[16,256,512]{2,1,0:T(8,128)(2,1)} %bitcast.53, bf16[16,16,512]{2,0,1:T(8,128)(2,1)S(1)} %slice-done), kind=kOutput, calls=%fused_computation.26 | convolution fusion | flops 75792384 | bytes 4736000 | tf_op jit(solution)/shard_map/rhl,rkl->rhk/dot_general | solution.py:98
  123.0 0.4 fusion.46
  123.4 0.0 copy-start.16
  123.4 3.3 %fusion.13 = bf16[16,16,512]{2,1,0:T(8,128)(2,1)S(1)} fusion(bf16[16,1,512]{2,1,0:T(2,128)(2,1)S(1)} %copy.31, bf16[16,256,512]{2,1,0:T(8,128)(2,1)} %bitcast.54, f32[16,16,257]{2,1,0:T(8,128)S(1)} %get-tuple-element.6, f32[16,16]{1,0:T(8,128)S(1)} %get-tuple-element.5), kind=kOutput, calls=%fused_computation.25 | convolution fusion | flops 75923968 | bytes 4737024 | tf_op jit(solution)/shard_map/rhk,rkl->rhl/dot_general | solution.py:114
  126.7 0.2 copy.53
  126.9 0.5 copy-done.17
  127.4 2.5 fusion.18
  130.0 0.0 all-gather.2.cloned.1.call-update
  130.0 0.0 reduce-scatter.2.cloned.1.call-start
  130.0 36.0 %all-gather.2.cloned.1.call-done = bf16[1024,2048]{0,1:T(8,128)(2,1)} async-done(((bf16[256,2048]{0,1:T(8,128)(2,1)}), bf16[1024,2048]{0,1:T(8,128)(2,1)}) %all-gather.2.cloned.1.call-update) | async-done | bytes 4194320 | tf_op jit(solution)/shard_map/all_gather | solution.py:123
  166.0 13.2 %convolution_convert_fusion = bf16[1024,1792]{1,0:T(8,128)(2,1)} fusion(bf16[1024,2048]{0,1:T(8,128)(2,1)} %all-gather.2.cloned.1.call-done, bf16[2048,1792]{1,0:T(8,128)(2,1)} %param.22), kind=kOutput, calls=%fused_computation.24 | convolution fusion | flops 7518027776 | bytes 15204352 | tf_op jit(solution)/shard_map/dot_general | solution.py:122
  179.2 0.0 reduce-scatter.2.cloned.1.call-update
  179.2 68.6 %reduce-scatter.2.cloned.1.call-done = bf16[256,1792]{1,0:T(8,128)(2,1)} async-done(((bf16[1024,1792]{1,0:T(8,128)(2,1)}), bf16[256,1792]{1,0:T(8,128)(2,1)}) %reduce-scatter.2.cloned.1.call-update) | async-done | bytes 917520 | tf_op jit(solution)/shard_map/reduce_scatter | solution.py:127
  (37 shorter events, 0.2 us)
Async XLA Ops:
  6.5 20.0 %copy-start = (bf16[16,128,512]{2,1,0:T(8,128)(2,1)S(1)}, bf16[16,128,512]{2,1,0:T(8,128)(2,1)}, u32[]{:S(2)}) copy-start(bf16[16,128,512]{2,1,0:T(8,128)(2,1)} %param.20) | copy-start | bytes 6291460
  6.5 16.5 %slice-start.1 = ((bf16[256,1024]{1,0:T(8,128)(2,1)}), bf16[240,1024]{1,0:T(8,128)(2,1)S(1)}, s32[]{:S(2)}) async-start(bf16[256,1024]{1,0:T(8,128)(2,1)} %param.15), calls=%async_computation.6 | async-start | bytes 983040 | tf_op jit(solution)/shard_map/slice | solution.py:68
  7.6 13.3 %copy-start.8 = (s32[1024]{0:T(1024)}, s32[1024]{0:T(1024)S(1)}, u32[]{:S(2)}) copy-start(s32[1024]{0:T(1024)S(1)} %pad_clamp_fusion.1) | copy-start | bytes 12292
  9.9 89.3 %all-to-all-start.1 = ((bf16[4,2,4096]{2,1,0:T(2,128)(2,1)}), bf16[4,2,4096]{2,1,0:T(2,128)(2,1)S(1)}, u32[]{:S(2)}, u32[]{:S(2)}) async-start(bf16[4,2,4096]{2,1,0:T(2,128)(2,1)} %reshape.213), calls=%async_computation.1 | async-start | bytes 131072 | tf_op jit(solution)/shard_map/all_to_all | solution.py:47
  19.5 1.3 copy-start.12
  29.0 11.1 %copy-start.2 = (bf16[256,16,512]{2,0,1:T(8,128)(2,1)}, bf16[256,16,512]{2,0,1:T(8,128)(2,1)S(1)}, u32[]{:S(2)}) copy-start(bf16[256,16,512]{2,0,1:T(8,128)(2,1)S(1)} %convert_bitcast_fusion) | copy-start | bytes 12582916
  29.0 2.7 %copy-start.7 = (s32[1264]{0:T(1024)S(1)}, s32[1264]{0:T(1024)}, u32[]{:S(2)}) copy-start(s32[1264]{0:T(1024)} %iota_add_fusion) | copy-start | bytes 15172
  29.1 2.7 %copy-start.10 = (pred[1264]{0:T(1024)(128)(4,1)S(1)}, pred[1264]{0:T(1024)(128)(4,1)}, u32[]{:S(2)}) copy-start(pred[1264]{0:T(1024)(128)(4,1)} %get-tuple-element.9) | copy-start | bytes 3796
  29.1 2.7 %copy-start.11 = (pred[1264]{0:T(1024)(128)(4,1)S(1)}, pred[1264]{0:T(1024)(128)(4,1)}, u32[]{:S(2)}) copy-start(pred[1264]{0:T(1024)(128)(4,1)} %get-tuple-element.10) | copy-start | bytes 3796
  29.1 2.9 %copy-start.5 = (bf16[256,64]{0,1:T(8,128)(2,1)S(1)}, bf16[256,64]{0,1:T(8,128)(2,1)}, u32[]{:S(2)}) copy-start(bf16[256,64]{0,1:T(8,128)(2,1)} %param.17) | copy-start | bytes 98308
  32.0 8.2 %copy-start.4 = (bf16[16,64,512]{2,1,0:T(8,128)(2,1)S(1)}, bf16[16,64,512]{2,1,0:T(8,128)(2,1)}, u32[]{:S(2)}) copy-start(bf16[16,64,512]{2,1,0:T(8,128)(2,1)} %gather_fusion) | copy-start | bytes 3145732
  85.7 9.9 %copy-start.14 = (s32[16]{0:T(128)S(1)}, s32[16]{0:T(128)}, u32[]{:S(2)}) copy-start(s32[16]{0:T(128)} %param.27) | copy-start | bytes 196
  85.7 9.9 %copy-start.15 = (pred[257]{0:T(512)(128)(4,1)S(1)}, pred[257]{0:T(512)(128)(4,1)}, u32[]{:S(2)}) copy-start(pred[257]{0:T(512)(128)(4,1)} %iota_compare_fusion.4) | copy-start | bytes 775
  85.7 9.9 %copy-start.13 = (s32[64]{0:T(128)S(1)}, s32[64]{0:T(128)}, u32[]{:S(2)}) copy-start(s32[64]{0:T(128)} %reshape.206) | copy-start | bytes 772
  85.8 10.0 %copy-start.9 = (s32[1024]{0:T(1024)S(1)}, s32[1024]{0:T(1024)}, u32[]{:S(2)}) copy-start(s32[1024]{0:T(1024)} %copy-done.8) | copy-start | bytes 12292
  85.8 13.0 %copy-start.6 = (bf16[16,1,512]{2,0,1:T(8,128)(2,1)S(1)}, bf16[16,1,512]{2,0,1:T(8,128)(2,1)}, u32[]{:S(2)}) copy-start(bf16[16,1,512]{2,0,1:T(8,128)(2,1)} %slice_bitcast_fusion) | copy-start | bytes 49156
  85.8 13.1 %slice-start.2 = ((bf16[256,1024]{1,0:T(8,128)(2,1)}), bf16[16,1024]{1,0:T(8,128)(2,1)S(1)}, s32[]{:S(2)}) async-start(bf16[256,1024]{1,0:T(8,128)(2,1)} %param.15), calls=%async_computation.7 | async-start | bytes 65536 | tf_op jit(solution)/shard_map/slice | solution.py:106
  85.8 17.0 %copy-start.3 = (bf16[32,4096]{1,0:T(8,128)(2,1)S(1)}, bf16[32,4096]{1,0:T(8,128)(2,1)}, u32[]{:S(2)}) copy-start(bf16[32,4096]{1,0:T(8,128)(2,1)} %param.19) | copy-start | bytes 786436
  99.2 12.3 %all-to-all-start = ((bf16[4,2,64,512]{3,2,1,0:T(8,128)(2,1)}), bf16[4,2,64,512]{3,2,1,0:T(8,128)(2,1)S(1)}, u32[]{:S(2)}, u32[]{:S(2)}) async-start(bf16[4,2,64,512]{3,2,1,0:T(8,128)(2,1)} %bitcast.10), calls=%async_computation | async-start | bytes 1048576 | tf_op jit(solution)/shard_map/all_to_all | solution.py:46
  102.7 63.3 %all-gather.2.cloned.1.call-start = ((), (), s32[]{:S(2)}) async-start(), calls=%async_computation.3 | async-start | bytes 5242880 | tf_op jit(solution)/shard_map/all_gather | solution.py:123
  114.9 4.5 %slice-start = ((bf16[256,16,512]{2,0,1:T(8,128)(2,1)}), bf16[16,16,512]{2,0,1:T(8,128)(2,1)S(1)}, s32[]{:S(2)}) async-start(bf16[256,16,512]{2,0,1:T(8,128)(2,1)} %copy-done.2), calls=%async_computation.5 | async-start | bytes 524288 | tf_op jit(solution)/shard_map/slice | solution.py:100
  123.4 3.5 %copy-start.16 = (bf16[16,512,128]{2,1,0:T(8,128)(2,1)S(1)}, bf16[16,512,128]{2,1,0:T(8,128)(2,1)}, u32[]{:S(2)}) copy-start(bf16[16,512,128]{2,1,0:T(8,128)(2,1)} %param.21) | copy-start | bytes 6291460
  123.4 4.0 %copy-start.17 = (bf16[240,16,512]{2,0,1:T(8,128)(2,1)S(1)}, bf16[240,16,512]{2,0,1:T(8,128)(2,1)}, u32[]{:S(2)}) copy-start(bf16[240,16,512]{2,0,1:T(8,128)(2,1)} %fusion.15) | copy-start | bytes 11796484
  130.0 117.8 %reduce-scatter.2.cloned.1.call-start = ((), (), s32[]{:S(2)}) async-start(), calls=%async_computation.4 | async-start | bytes 4587520 | tf_op jit(solution)/shard_map/reduce_scatter | solution.py:127
  166.0 81.8 %copy-start.1 = (bf16[16,128,512]{2,1,0:T(8,128)(2,1)S(1)}, bf16[16,128,512]{2,1,0:T(8,128)(2,1)}, u32[]{:S(2)}) copy-start(bf16[16,128,512]{2,1,0:T(8,128)(2,1)} %param.20) | copy-start | bytes 6291460
Sparse Core Ops, SparseCore 0:
  130.1 35.8 all-gather.1
  179.3 68.3 reduce-scatter.1
where the time goes:
time: 255 us
  waiting for transfers between devices  111 us (44%)
  matrix products  79.5 us (31%)
  local copies, waits for them, and re-layouts  25 us (10%)
  other arithmetic  17.1 us (7%)
  between operations  14.4 us (6%)
  starting transfers between devices  7.77 us (3%)
    reduce_scatter x1, waiting for transfers between devices, body(): lax.psum_scatter(partials.astype(jnp.bfloat16), 'tp', scatter_dimension=0...  68.6 us
    sub x2, matrix products, normalized(): exp_terms = jnp.where(visible, jnp.exp(masked - row_top), 0.0)  36.5 us
    all_gather x1, waiting for transfers between devices, body(): lax.all_gather(head_out, 'dp', axis=0, tiled=True)  36 us
    dot_general x1, matrix products, body(): jnp.dot(lax.all_gather(head_out, 'dp', axis=0, tiled=True), output_weight...  13.2 us
    dot_general x1, matrix products, body(): jnp.einsum('thk,kl->thl', weights, key_latent, preferred_element_type=jnp...  9.81 us
    convert_element_type x1, other arithmetic, normalized(): (exp_terms / jnp.sum(exp_terms, axis=-1, keepdims=True)).astype(jnp.bfloa...  9.47 us
    dot_general x1, matrix products, body(): jnp.einsum('the,ke->thk', rope_query[:prefill_len], key_rope, preferred_e...  8.18 us
    all_to_all x1, waiting for transfers between devices, body(): lax.all_to_all(send_latent, 'dp', split_axis=0, concat_axis=0, tiled=True)  6.34 us
  transfers between devices with their start and end apart: 4, of which 3 were waited for; matrix products, arithmetic and copies ran while one was open for 34% of the time, Pallas kernels for 0%

commit v1 on v0

v1 whole, which is shorter than its diff:
```python
import functools

import jax
import jax.numpy as jnp
from jax import lax
from jax.experimental import pallas as pl
from jax.experimental.pallas import tpu as pltpu
from jax.sharding import PartitionSpec as P

HIDDEN = -1e30
LANES = 128
VMEM_LIMIT = 48 * 1024 * 1024


def dot_nt(a, b):
    return lax.dot_general(a, b, (((1,), (1,)), ((), ())), preferred_element_type=jnp.float32)


def dot(a, b):
    return jnp.dot(a, b, preferred_element_type=jnp.float32)


def chunk_sizes(tok_group):
    if tok_group == 256:
        return (32, 64, 64, 96)
    return (tok_group,)


def attend_kernel(
    first,
    prefill_len,
    exp_scale,
    with_decode,
    table,
    offset,
    q_nope,
    q_rope,
    wk_hbm,
    wv_hbm,
    cache_latent,
    cache_rope,
    new_latent,
    new_rope,
    *rest,
):
    if with_decode:
        (recv_latent, recv_rope, decode_table, decode_length, out,
         wk, wv, keys, q, att, dkeys, sems, wsems, dsems) = rest
    else:
        out, wk, wv, keys, q, att, sems, wsems = rest
    heads, t, nope_dim = q_nope.shape
    block_len, latent = cache_latent.shape[1:]
    rope_dim = q_rope.shape[1] // heads
    blocks = table.shape[1]
    prior = blocks * block_len
    fresh = keys.shape[0] - prior

    wk_copy = pltpu.make_async_copy(wk_hbm, wk, wsems.at[0])
    wk_copy.start()
    copies = []
    for i in range(blocks):
        b = table[0, i]
        rows = pl.ds(i * block_len, block_len)
        copies.append(pltpu.make_async_copy(
            cache_latent.at[b], keys.at[rows, pl.ds(0, latent)], sems.at[2 * i]))
        copies.append(pltpu.make_async_copy(
            cache_rope.at[b], keys.at[rows, pl.ds(latent, LANES)], sems.at[2 * i + 1]))
    copies.append(pltpu.make_async_copy(
        new_latent.at[pl.ds(0, fresh)], keys.at[pl.ds(prior, fresh), pl.ds(0, latent)],
        sems.at[2 * blocks]))
    copies.append(pltpu.make_async_copy(
        new_rope.at[pl.ds(0, fresh)], keys.at[pl.ds(prior, fresh), pl.ds(latent, LANES)],
        sems.at[2 * blocks + 1]))
    for c in copies:
        c.start()
    wv_copy = pltpu.make_async_copy(wv_hbm, wv, wsems.at[1])
    wv_copy.start()
    dec_copies = []
    if with_decode:
        pool = cache_latent.shape[0]
        for i in range(pool):
            rows = pl.ds(i * block_len, block_len)
            dec_copies.append(pltpu.make_async_copy(
                cache_latent.at[i], dkeys.at[rows, pl.ds(0, latent)], dsems.at[2 * i]))
            dec_copies.append(pltpu.make_async_copy(
                cache_rope.at[i], dkeys.at[rows, pl.ds(latent, LANES)], dsems.at[2 * i + 1]))
        received = recv_latent.shape[0]
        tail = dkeys.shape[0] - pool * block_len - received
        start = new_latent.shape[0] - tail
        n = 2 * pool
        for src_l, src_r, at, size in (
            (recv_latent, recv_rope, pool * block_len, received),
            (new_latent.at[pl.ds(start, tail)], new_rope.at[pl.ds(start, tail)],
             pool * block_len + received, tail),
        ):
            dec_copies.append(pltpu.make_async_copy(
                src_l, dkeys.at[pl.ds(at, size), pl.ds(0, latent)], dsems.at[n]))
            dec_copies.append(pltpu.make_async_copy(
                src_r, dkeys.at[pl.ds(at, size), pl.ds(latent, LANES)], dsems.at[n + 1]))
            n += 2
        for c in dec_copies:
            c.start()

    lane = lax.broadcasted_iota(jnp.int32, (t, LANES), 1)
    one = jnp.where(lane == rope_dim, 1.0, 0.0)
    per_tile = LANES // rope_dim
    for h in range(heads):
        pair = q_rope[:, h // per_tile * LANES:(h // per_tile + 1) * LANES].astype(jnp.float32)
        turn = h % per_tile * rope_dim
        if turn:
            pair = pltpu.roll(pair, LANES - turn, 1)
        q[h * t:(h + 1) * t, latent:] = jnp.where(lane < rope_dim, pair, one).astype(jnp.bfloat16)
    wk_copy.wait()
    for h in range(heads):
        q[h * t:(h + 1) * t, :latent] = dot(q_nope[h], wk[h]).astype(jnp.bfloat16)

    for c in copies:
        c.wait()
    lane_k = lax.broadcasted_iota(jnp.int32, (prior, LANES), 1)
    pos_k = lax.broadcasted_iota(jnp.int32, (prior, LANES), 0)
    hide = jnp.where((lane_k == rope_dim) & (pos_k >= offset[0]), HIDDEN, 0.0)
    keys[:prior, latent:] = (keys[:prior, latent:].astype(jnp.float32) + hide).astype(jnp.bfloat16)

    together = 1
    while together * 2 <= heads and together * 2 * t <= 384:
        together *= 2
    tile = together * t
    token = first + lax.broadcasted_iota(jnp.int32, (t, fresh), 0)
    key_token = lax.broadcasted_iota(jnp.int32, (t, fresh), 1)
    causal = (key_token <= token)[None]

    def scores_of(i):
        rows = q[i * tile:(i + 1) * tile, :]
        return dot_nt(rows, keys[:prior, :]), dot_nt(rows, keys[prior:, :])

    steps = heads // together
    ahead = scores_of(0)
    for i in range(steps):
        s_old, s_new = ahead
        if i + 1 < steps:
            ahead = scores_of(i + 1)
        s_new = jnp.where(causal, s_new.reshape(together, t, fresh), HIDDEN).reshape(tile, fresh)
        top = jnp.maximum(jnp.max(s_old, axis=1, keepdims=True), jnp.max(s_new, axis=1, keepdims=True))
        p_old = jnp.exp2((s_old - top) * exp_scale)
        p_new = jnp.exp2((s_new - top) * exp_scale)
        total = jnp.sum(p_old, axis=1, keepdims=True) + jnp.sum(p_new, axis=1, keepdims=True)
        mixed = dot(p_old.astype(jnp.bfloat16), keys[:prior, :latent]) + dot(
            p_new.astype(jnp.bfloat16), keys[prior:, :latent])
        att[i * tile:(i + 1) * tile, :] = (mixed / total).astype(jnp.bfloat16)

    if with_decode:
        decodes = decode_table.shape[0]
        for c in dec_copies:
            c.wait()
        span = dkeys.shape[0]
        ext = span - tail
        key = lax.broadcasted_iota(jnp.int32, (decodes, span), 1)
        request = lax.broadcasted_iota(jnp.int32, (decodes, span), 0)
        block = key // block_len
        pos = key % block_len
        count = jnp.where(key - ext + start == request + prefill_len, 1.0, 0.0)
        for m in range(decode_table.shape[1]):
            hit = (block == decode_table[:, m:m + 1]) & (
                pos + m * block_len < decode_length[:, 0:1]) & (key < ext)
            count = count + jnp.where(hit, 1.0, 0.0)
        count = count[None]
        at = prefill_len - first
        half = heads // 2 if heads % 2 == 0 else heads
        for lo in range(0, heads, half):
            rows = jnp.concatenate(
                [q[h * t + at:h * t + at + decodes, :] for h in range(lo, lo + half)], axis=0)
            s = dot_nt(rows, dkeys[...]).reshape(half, decodes, span)
            s = jnp.where(count > 0.0, s, HIDDEN)
            top = jnp.max(s, axis=2, keepdims=True)
            p = count * jnp.exp2((s - top) * exp_scale)
            total = jnp.sum(p, axis=2, keepdims=True).reshape(half * decodes, 1)
            p = p.reshape(half * decodes, span).astype(jnp.bfloat16)
            mixed = (dot(p, dkeys[:, :latent]) / total).astype(jnp.bfloat16)
            for h in range(lo, lo + half):
                att[h * t + at:h * t + at + decodes, :] = mixed[(h - lo) * decodes:(h - lo + 1) * decodes]

    wv_copy.wait()
    dv = wv.shape[2]
    for h in range(heads):
        out[:, h * dv:(h + 1) * dv] = dot(att[h * t:(h + 1) * t, :], wv[h]).astype(jnp.bfloat16)


def attend(first, size, prefill_len, exp_scale, q_nope, q_rope, wk, wv, cache_latent, cache_rope,
           new_latent, new_rope, table, offset, decode=None):
    heads, _, latent = wk.shape
    tok_group = new_latent.shape[0]
    block_len = cache_latent.shape[1]
    blocks = table.shape[1]
    prior = blocks * block_len
    seen = min(first + size, prefill_len)
    fresh = min(-(-seen // LANES) * LANES, tok_group)
    width = latent + LANES
    dv = wv.shape[2]
    smem = pl.BlockSpec(memory_space=pltpu.SMEM)
    vmem = pl.BlockSpec(memory_space=pltpu.VMEM)
    hbm = pl.BlockSpec(memory_space=pl.ANY)
    args = [table, offset, q_nope, q_rope, wk, wv, cache_latent, cache_rope, new_latent, new_rope]
    in_specs = [smem, smem, vmem, vmem] + [hbm] * 6
    scratch = [
        pltpu.VMEM(wk.shape, jnp.bfloat16),
        pltpu.VMEM(wv.shape, jnp.bfloat16),
        pltpu.VMEM((prior + fresh, width), jnp.bfloat16),
        pltpu.VMEM((heads * size, width), jnp.bfloat16),
        pltpu.VMEM((heads * size, latent), jnp.bfloat16),
    ]
    flops = 2 * heads * size * ((prior + fresh) * (width + latent) + latent * 2 * LANES)
    if decode is not None:
        args += list(decode)
        in_specs += [hbm, hbm, vmem, vmem]
        received = decode[0].shape[0]
        pool = cache_latent.shape[0]
        span = pool * block_len + received + min(LANES, tok_group)
        scratch.append(pltpu.VMEM((span, width), jnp.bfloat16))
        flops += 2 * heads * decode[2].shape[0] * span * (width + latent)
    scratch += [pltpu.SemaphoreType.DMA((2 * blocks + 2,)), pltpu.SemaphoreType.DMA((2,))]
    if decode is not None:
        scratch.append(pltpu.SemaphoreType.DMA((2 * pool + 4,)))
    return pl.pallas_call(
        functools.partial(attend_kernel, first, prefill_len, exp_scale, decode is not None),
        out_shape=jax.ShapeDtypeStruct((size, heads * dv), jnp.bfloat16),
        in_specs=in_specs,
        out_specs=vmem,
        scratch_shapes=scratch,
        name="attend",
        compiler_params=pltpu.CompilerParams(vmem_limit_bytes=VMEM_LIMIT),
        cost_estimate=pl.CostEstimate(
            flops=2 * flops, bytes_accessed=6_000_000, transcendentals=heads * size * (prior + fresh)),
    )(*args)


def project_kernel(x, w, out):
    groups, t, depth = x.shape
    out[...] = dot(x[...].reshape(groups * t, depth), w[...]).astype(jnp.bfloat16).reshape(out.shape)


def project(x, w):
    groups, t, depth = x.shape
    columns = w.shape[1]
    step = 256 if columns % 256 == 0 else columns
    return pl.pallas_call(
        project_kernel,
        out_shape=jax.ShapeDtypeStruct((groups, t, columns), jnp.bfloat16),
        grid=(columns // step,),
        in_specs=[
            pl.BlockSpec((groups, t, depth), lambda j: (0, 0, 0)),
            pl.BlockSpec((depth, step), lambda j: (0, j)),
        ],
        out_specs=pl.BlockSpec((groups, t, step), lambda j: (0, 0, j)),
        name="project",
        compiler_params=pltpu.CompilerParams(vmem_limit_bytes=VMEM_LIMIT),
        cost_estimate=pl.CostEstimate(
            flops=2 * groups * t * depth * columns, bytes_accessed=2 * depth * columns, transcendentals=0),
    )(x, w)


def body(
    query_nope,
    query_rope,
    new_latent,
    new_rope,
    cache_latent,
    cache_rope,
    absorb_key,
    absorb_value,
    output_weight,
    send_blocks,
    prefill_table,
    prefill_offset,
    decode_table,
    decode_length,
):
    tok_group, heads, nope_dim = query_nope.shape
    pool_blocks, block_len, latent_dim = cache_latent.shape
    rope_dim = new_rope.shape[1]
    capacity = send_blocks.shape[2]
    group_count = lax.axis_size("dp")
    prefill_len = tok_group - decode_length.shape[0]
    exp_scale = float((nope_dim + rope_dim) ** (-0.5) * 1.4426950408889634)

    padded_rope = jnp.pad(
        cache_rope.reshape(pool_blocks, block_len, rope_dim), ((0, 0), (0, 0), (0, LANES - rope_dim)))
    padded_new = jnp.pad(new_rope, ((0, 0), (0, LANES - rope_dim)))

    outgoing = send_blocks[0]
    send = jnp.concatenate([cache_latent[outgoing], padded_rope[outgoing]], axis=3)
    me = lax.axis_index("dp")
    parts = [lax.dynamic_index_in_dim(send, me, 0, keepdims=False)]
    for shift in range(1, group_count):
        there = lax.rem(me + shift, group_count)
        parts.append(lax.ppermute(
            lax.dynamic_index_in_dim(send, there, 0, keepdims=False), "dp",
            [(i, (i + shift) % group_count) for i in range(group_count)]))
    received = jnp.stack(parts[::-1], axis=0)
    received = jnp.roll(received, me + 1, axis=0)
    received = received.reshape(group_count * capacity * block_len, latent_dim + LANES)

    first = 0
    outs = []
    sizes = chunk_sizes(tok_group)
    for n, size in enumerate(sizes):
        decode = None
        if n == len(sizes) - 1:
            decode = (received[:, :latent_dim], received[:, latent_dim:], decode_table,
                      decode_length[:, None])
        head_out = attend(
            first, size, prefill_len, exp_scale,
            query_nope[first:first + size].transpose(1, 0, 2), query_rope[first:first + size],
            absorb_key, absorb_value, cache_latent, padded_rope, new_latent, padded_new,
            prefill_table, prefill_offset, decode)
        gathered = lax.all_gather(head_out, "dp", axis=0, tiled=False)
        partials = project(gathered, output_weight)
        outs.append(lax.psum_scatter(partials, "tp", scatter_dimension=0, tiled=False))
        first += size
    return jnp.concatenate(outs, axis=0)


def solution(mesh):
    return jax.shard_map(
        body,
        mesh=mesh,
        in_specs=(
            P(("replica", "dp"), "tp", None),
            P(("replica", "dp"), "tp"),
            P(("replica", "dp"), None),
            P(("replica", "dp"), None),
            P(("replica", "dp"), None, None),
            P(("replica", "dp"), None),
            P("tp", None, None),
            P("tp", None, None),
            P("tp", "dp"),
            P(("replica", "dp"), None, None),
            P(("replica", "dp"), None),
            P(("replica", "dp")),
            P(("replica", "dp"), None),
            P(("replica", "dp")),
        ),
        out_specs=P(("replica", "tp"), "dp"),
        check_vma=False,
    )
```

time: 255 us -> 212 us (0.83)
  matrix products: 79.5 us -> 0 us
  Pallas kernels: 0 us -> 64 us
  waiting for transfers between devices: 111 us -> 80.7 us
  other arithmetic: 17.1 us -> 3.44 us
  blocking collectives: 0 us -> 10.6 us
  local copies, waits for them, and re-layouts: 25 us -> 31.6 us
  starting transfers between devices: 7.77 us -> 3.83 us
    pallas_call x0 -> x8, Pallas kernels: none -> 64 us  [the longest x4 33.5 us: attend(): pl.pallas_call(functools.partial(attend_kernel, first, prefill_len, exp_s...]
    dot_general x7 -> x0, matrix products: 43 us -> none  [the longest x1 13.2 us: body(): jnp.dot(lax.all_gather(head_out, 'dp', axis=0, tiled=True), output_weight...]
    sub x2 -> x0, matrix products: 36.5 us -> none  [normalized(): exp_terms = jnp.where(visible, jnp.exp(masked - row_top), 0.0)]
    all_gather x1 -> x3, waiting for transfers between devices: 36 us -> 0.06 us  [body(): gathered = lax.all_gather(head_out, 'dp', axis=0, tiled=False)]
    unnamed x37 -> x45, local copies, waits for them, and re-layouts: 0.69 us -> 17 us
    reduce_scatter x1 -> x4, waiting for transfers between devices: 68.6 us -> 79.8 us  [body(): lax.psum_scatter(partials, 'tp', scatter_dimension=0, tiled=False)]
    gather x7 -> x2, local copies, waits for them, and re-layouts: 15.7 us -> 4.58 us  [the longest x1 2.96 us: body(): cache_latent[outgoing]]
    all_gather x0 -> x1, blocking collectives: none -> 10.6 us  [body(): gathered = lax.all_gather(head_out, 'dp', axis=0, tiled=False)]
  transfers between devices with their start and end apart: 4 -> 10, of which waited for: 3 -> 4; matrix products, arithmetic and copies ran while one was open for 34% -> 10% of each run, Pallas kernels for 0% -> 27%
where the time goes in v1:
time: 212 us; the launch traced here: 210 us
  waiting for transfers between devices  80.7 us (38%)
  Pallas kernels  64 us (30%)
  local copies, waits for them, and re-layouts  31.6 us (15%)
  between operations  16 us (8%)
  blocking collectives  10.6 us (5%)
  starting transfers between devices  3.83 us (2%)
  other arithmetic  3.44 us (2%)
    reduce_scatter x4, waiting for transfers between devices, body(): lax.psum_scatter(partials, 'tp', scatter_dimension=0, tiled=False)  79.8 us
    pallas_call x4, Pallas kernels, attend(): pl.pallas_call(functools.partial(attend_kernel, first, prefill_len, exp_s...  33.5 us
    pallas_call x4, Pallas kernels, project(): pl.pallas_call(project_kernel, out_shape=jax.ShapeDtypeStruct((groups, t,...  30.5 us
    unnamed x45, local copies, waits for them, and re-layouts  17 us
    all_gather x1, blocking collectives, body(): gathered = lax.all_gather(head_out, 'dp', axis=0, tiled=False)  10.6 us
  transfers between devices with their start and end apart: 10, of which 4 were waited for; matrix products, arithmetic and copies ran while one was open for 10% of the time, Pallas kernels for 27%

profile of v1, /device:TPU:0, one launch (start us, length us, event | category | flops | bytes accessed | tf_op | source)
XLA Modules:
  0.0 210.2 jit_solution(10450722451242608201)
XLA Ops:
  7.4 1.5 reshape.34
  8.8 0.9 copy.24
  9.8 0.1 pad.9.cache_rope
  10.8 1.1 fusion.2
  11.8 0.1 copy.41
  12.0 1.6 copy-done.3
  13.6 7.2 %attend.5 = bf16[64,2048]{1,0:T(8,128)(2,1)} custom-call(s32[1,16]{1,0:T(1,128)S(1)} %copy-done.8, s32[1]{0:T(128)S(6)} %copy.50.offset, bf16[16,64,128]{2,1,0:T(8,128)(2,1)S(1)} %bitcast.47, bf16[64,1024]{1,0:T(8,128)(2,1)S(1)} %get-tuple-element.10.q_rope, bf16[16,128,512]{2,1,0:T(8,128)(2,1)S(1)} %copy-done.2, bf16[16,512,128]{2,1,0:T(8,128)(2,1)S(1)} %copy-done.3, ...), custom_call_target="tpu_custom_call" | custom-call | flops 5972688896 | bytes 6000000 | tf_op jit(solution)/shard_map/attend/pallas_call | solution.py:223
  20.8 0.0 all-gather.8.cloned.1.call-update
  20.9 0.0 all-gather.10.cloned.1.call-start
  20.9 0.1 copy.28
  21.0 0.1 reshape.38
  21.1 1.6 gather_fusion.1
  22.8 3.0 %gather_fusion = bf16[8,64,512]{2,1,0:T(8,128)(2,1)} fusion(bf16[32,64,512]{2,1,0:T(8,128)(2,1)} %cache_latent.7, s32[1024]{0:T(1024)S(1)} %pad_clamp_fusion), kind=kCustom, calls=%fused_computation | custom fusion | bytes 1048608 | tf_op jit(solution)/shard_map/gather | solution.py:290
  25.7 1.3 fusion.1
  27.0 0.9 dynamic-slice_bitcast_fusion
  27.9 2.4 %collective-permute-start = (bf16[2,64,640]{2,1,0:T(8,128)(2,1)}, bf16[2,64,640]{2,1,0:T(8,128)(2,1)}, u32[]{:S(2)}, u32[]{:S(2)}) collective-permute-start(bf16[2,64,640]{2,1,0:T(8,128)(2,1)} %get-tuple-element.9), channel_id=1, source_target_pairs={{0,12},{4,0},{8,4},{12,8},{1,13},{5,1},{9,5},{13,9},{2,14},{6,2},{... | collective-permute-start | bytes 491528 | tf_op jit(solution)/shard_map/ppermute | solution.py:295
  30.2 0.6 collective-permute-start.1
  30.8 0.2 collective-permute-start.2
  31.0 0.1 copy.40
  31.1 7.5 %attend.6 = bf16[64,2048]{1,0:T(8,128)(2,1)} custom-call(s32[1,16]{1,0:T(1,128)S(1)} %copy-done.8, s32[1]{0:T(128)S(6)} %copy.50.offset, bf16[16,64,128]{2,1,0:T(8,128)(2,1)S(1)} %bitcast.48, bf16[64,1024]{1,0:T(8,128)(2,1)S(1)} %get-tuple-element.11.q_rope, bf16[16,128,512]{2,1,0:T(8,128)(2,1)S(1)} %copy-done.2, bf16[16,512,128]{2,1,0:T(8,128)(2,1)S(1)} %copy-done.4, ...), custom_call_target="tpu_custom_call" | custom-call | flops 6576668672 | bytes 6000000 | tf_op jit(solution)/shard_map/attend/pallas_call | solution.py:223
  38.6 0.2 all-gather.12.cloned.1.call-start
  38.9 1.8 slice.36
  40.7 1.0 slice.37.q_rope
  41.6 1.1 copy.39
  42.7 0.1 copy.29.rest_2_
  42.8 0.7 copy.30.rest_3_
  43.6 0.9 bitcast_dynamic-update-slice_fusion.4
  44.5 0.6 collective-permute-done.1
  45.1 0.9 bitcast_dynamic-update-slice_fusion.2
  46.1 0.9 bitcast_dynamic-update-slice_fusion
  47.0 0.9 dynamic-slice_dynamic-update-slice_fusion
  48.0 0.9 bitcast_dynamic-update-slice_fusion.5
  48.9 0.9 bitcast_dynamic-update-slice_fusion.3
  49.8 0.9 bitcast_dynamic-update-slice_fusion.1
  50.8 0.9 dynamic-slice_dynamic-update-slice_fusion.1
  51.7 0.1 constant_dynamic-slice_fusion
  51.9 0.5 copy-done.9
  52.4 14.2 %attend.7 = bf16[96,2048]{1,0:T(8,128)(2,1)} custom-call(s32[1,16]{1,0:T(1,128)S(1)} %copy-done.9, s32[1]{0:T(128)S(6)} %copy.50.offset, bf16[16,96,128]{2,1,0:T(8,128)(2,1)S(1)} %bitcast.46, bf16[96,1024]{1,0:T(8,128)(2,1)S(1)} %slice.37.q_rope, bf16[16,128,512]{2,1,0:T(8,128)(2,1)S(1)} %copy-done.2, bf16[16,512,128]{2,1,0:T(8,128)(2,1)} %wv_hbm.7, ...), custom_call_target="tpu_custom_call" | custom-call | flops 13035896832 | bytes 6000000 | tf_op jit(solution)/shard_map/attend/pallas_call | solution.py:223
  66.6 0.3 reduce-scatter.5.cloned.1.call-start
  66.8 0.9 slice.30
  67.8 0.8 slice.31.q_rope
  68.7 1.6 copy-done.5
  70.3 0.7 copy-done.10
  70.9 4.6 %attend.4 = bf16[32,2048]{1,0:T(8,128)(2,1)S(1)} custom-call(s32[1,16]{1,0:T(1,128)S(1)} %copy-done.10, s32[1]{0:T(128)S(6)} %copy.50.offset, bf16[16,32,128]{2,1,0:T(8,128)(2,1)S(1)} %bitcast.49, bf16[32,1024]{1,0:T(8,128)(2,1)S(1)} %slice.31.q_rope, bf16[16,128,512]{2,1,0:T(8,128)(2,1)S(1)} %copy-done.2, bf16[16,512,128]{2,1,0:T(8,128)(2,1)S(1)} %copy-done.5, ...), custom_call_target="tpu_custom_call" | custom-call | flops 2986344448 | bytes 6000000 | tf_op jit(solution)/shard_map/attend/pallas_call | solution.py:223
  75.5 10.6 %all-gather = bf16[128,2048]{1,0:T(8,128)(2,1)S(1)} all-gather(bf16[32,2048]{1,0:T(8,128)(2,1)S(1)} %attend.4), channel_id=2, replica_groups=mesh['replica'=2,'dp'=4,'tp'=4] {'dp'}, dimensions={0}, use_global_device_ids=true | all-gather | bytes 655360 | tf_op jit(solution)/shard_map/all_gather | solution.py:315
  86.1 7.1 %project.4 = bf16[4,32,1792]{2,1,0:T(8,128)(2,1)} custom-call(bf16[4,32,2048]{2,1,0:T(8,128)(2,1)S(1)} %bitcast.43, bf16[2048,1792]{1,0:T(8,128)(2,1)} %w.7), custom_call_target="tpu_custom_call" | custom-call | flops 939524096 | bytes 7340032 | tf_op jit(solution)/shard_map/project/pallas_call | solution.py:245
  93.2 0.0 reduce-scatter.7.cloned.1.call-start
  93.3 0.0 all-gather.8.cloned.1.call-done
  93.3 1.2 copy-done
  94.5 7.6 %project.5 = bf16[4,64,1792]{2,1,0:T(8,128)(2,1)} custom-call(bf16[4,64,2048]{2,1,0:T(8,128)(2,1)S(1)} %bitcast.44, bf16[2048,1792]{1,0:T(8,128)(2,1)} %w.7), custom_call_target="tpu_custom_call" | custom-call | flops 1879048192 | bytes 7340032 | tf_op jit(solution)/shard_map/project/pallas_call | solution.py:245
  102.2 0.0 reduce-scatter.9.cloned.1.call-start
  102.2 0.0 all-gather.10.cloned.1.call-done
  102.3 1.2 copy-done.1
  103.5 7.6 %project.6 = bf16[4,64,1792]{2,1,0:T(8,128)(2,1)} custom-call(bf16[4,64,2048]{2,1,0:T(8,128)(2,1)S(1)} %bitcast.45, bf16[2048,1792]{1,0:T(8,128)(2,1)} %w.7), custom_call_target="tpu_custom_call" | custom-call | flops 1879048192 | bytes 7340032 | tf_op jit(solution)/shard_map/project/pallas_call | solution.py:245
  111.1 0.0 reduce-scatter.9.cloned.1.call-update
  111.1 0.0 reduce-scatter.11.cloned.1.call-start
  111.2 0.0 all-gather.12.cloned.1.call-done
  111.2 1.4 copy-done.6
  112.6 8.2 %project.7 = bf16[4,96,1792]{2,1,0:T(8,128)(2,1)} custom-call(bf16[4,96,2048]{2,1,0:T(8,128)(2,1)S(1)} %bitcast.50, bf16[2048,1792]{1,0:T(8,128)(2,1)} %w.7), custom_call_target="tpu_custom_call" | custom-call | flops 2818572288 | bytes 7340032 | tf_op jit(solution)/shard_map/project/pallas_call | solution.py:245
  120.8 0.0 reduce-scatter.5.cloned.1.call-done
  120.9 20.0 %reduce-scatter.7.cloned.1.call-done = bf16[1,64,1792]{2,1,0:T(8,128)(2,1)} async-done(((bf16[4,64,1792]{2,1,0:T(8,128)(2,1)}), bf16[1,64,1792]{2,1,0:T(8,128)(2,1)}) %reduce-scatter.7.cloned.1.call-update) | async-done | bytes 229392 | tf_op jit(solution)/shard_map/reduce_scatter | solution.py:317
  140.9 26.2 %reduce-scatter.9.cloned.1.call-done = bf16[1,64,1792]{2,1,0:T(8,128)(2,1)} async-done(((bf16[4,64,1792]{2,1,0:T(8,128)(2,1)}), bf16[1,64,1792]{2,1,0:T(8,128)(2,1)}) %reduce-scatter.9.cloned.1.call-update) | async-done | bytes 229392 | tf_op jit(solution)/shard_map/reduce_scatter | solution.py:317
  167.1 33.5 %reduce-scatter.11.cloned.1.call-done = bf16[1,96,1792]{2,1,0:T(8,128)(2,1)} async-done(((bf16[4,96,1792]{2,1,0:T(8,128)(2,1)}), bf16[1,96,1792]{2,1,0:T(8,128)(2,1)}) %reduce-scatter.11.cloned.1.call-update) | async-done | bytes 344080 | tf_op jit(solution)/shard_map/reduce_scatter | solution.py:317
  200.7 2.2 %pad_maximum_fusion = bf16[256,1792]{1,0:T(8,128)(2,1)} fusion(bf16[96,1792]{1,0:T(8,128)(2,1)} %bitcast.55, bf16[64,1792]{1,0:T(8,128)(2,1)} %bitcast.57, bf16[64,1792]{1,0:T(8,128)(2,1)} %bitcast.56, bf16[32,1792]{1,0:T(8,128)(2,1)} %bitcast.58), kind=kLoop, calls=%fused_computation.4 | loop fusion | flops 3670016 | bytes 1835008 | tf_op jit(solution)/shard_map/concatenate | solution.py:319
  (40 shorter events, 0.3 us)
Async XLA Ops:
  7.4 85.9 %all-gather.8.cloned.1.call-start = ((), (), s32[]{:S(2)}) async-start(), calls=%async_computation.8 | async-start | bytes 1310720 | tf_op jit(solution)/shard_map/all_gather | solution.py:315
  8.8 0.9 copy-start.12
  9.8 2.2 %copy-start.13 = (bf16[256,1024]{1,0:T(8,128)(2,1)S(1)}, bf16[256,1024]{1,0:T(8,128)(2,1)}, u32[]{:S(2)}) copy-start(bf16[256,1024]{1,0:T(8,128)(2,1)} %param.15) | copy-start | bytes 1572868
  9.8 2.2 %copy-start.7 = (bf16[256,512]{1,0:T(8,128)(2,1)S(1)}, bf16[256,512]{1,0:T(8,128)(2,1)}, u32[]{:S(2)}) copy-start(bf16[256,512]{1,0:T(8,128)(2,1)} %new_latent.7) | copy-start | bytes 786436
  9.9 2.0 copy-start.2
  9.9 2.0 copy-start.8
  12.0 1.6 copy-start.3
  13.6 7.3 %copy-start.15 = (s32[1,4,2]{1,2,0:T(2,128)S(1)}, s32[1,4,2]{1,2,0:T(2,128)}, u32[]{:S(2)}) copy-start(s32[1,4,2]{1,2,0:T(2,128)} %param.23) | copy-start | bytes 100
  20.9 81.4 %all-gather.10.cloned.1.call-start = ((), (), s32[]{:S(2)}) async-start(), calls=%async_computation.9 | async-start | bytes 1310720 | tf_op jit(solution)/shard_map/all_gather | solution.py:315
  25.7 5.4 %copy-start.4 = (bf16[16,512,128]{2,1,0:T(8,128)(2,1)S(1)}, bf16[16,512,128]{2,1,0:T(8,128)(2,1)}, u32[]{:S(2)}) copy-start(bf16[16,512,128]{2,1,0:T(8,128)(2,1)} %wv_hbm.7) | copy-start | bytes 6291460
  27.0 4.0 %copy-start.11 = (bf16[4,2,64,640]{3,2,1,0:T(8,128)(2,1)}, bf16[4,2,64,640]{3,2,1,0:T(8,128)(2,1)S(1)}, u32[]{:S(2)}) copy-start(bf16[4,2,64,640]{3,2,1,0:T(8,128)(2,1)S(1)} %fusion.1) | copy-start | bytes 1966084
  27.9 15.7 %collective-permute-start = (bf16[2,64,640]{2,1,0:T(8,128)(2,1)}, bf16[2,64,640]{2,1,0:T(8,128)(2,1)}, u32[]{:S(2)}, u32[]{:S(2)}) collective-permute-start(bf16[2,64,640]{2,1,0:T(8,128)(2,1)} %get-tuple-element.9), channel_id=1, source_target_pairs={{0,12},{4,0},{8,4},{12,8},{1,13},{5,1},{9,5},{13,9},{2,14},{6,2},{... | collective-permute-start | bytes 491528 | tf_op jit(solution)/shard_map/ppermute | solution.py:295
  30.2 14.9 %collective-permute-start.1 = (bf16[2,64,640]{2,1,0:T(8,128)(2,1)}, bf16[2,64,640]{2,1,0:T(8,128)(2,1)}, u32[]{:S(2)}, u32[]{:S(2)}) collective-permute-start(bf16[2,64,640]{2,1,0:T(8,128)(2,1)} %get-tuple-element.8), channel_id=1, source_target_pairs={{0,8},{4,12},{8,0},{12,4},{1,9},{5,13},{9,1},{13,5},{2,10},{6,14},... | collective-permute-start | bytes 491528 | tf_op jit(solution)/shard_map/ppermute | solution.py:295
  30.8 15.3 %collective-permute-start.2 = (bf16[2,64,640]{2,1,0:T(8,128)(2,1)}, bf16[2,64,640]{2,1,0:T(8,128)(2,1)}, u32[]{:S(2)}, u32[]{:S(2)}) collective-permute-start(bf16[2,64,640]{2,1,0:T(8,128)(2,1)} %get-tuple-element.7), channel_id=1, source_target_pairs={{0,4},{4,8},{8,12},{12,0},{1,5},{5,9},{9,13},{13,1},{2,6},{6,10},{... | collective-permute-start | bytes 491528 | tf_op jit(solution)/shard_map/ppermute | solution.py:295
  38.6 4.1 %copy-start.14 = (s32[16,4]{0,1:T(4,128)S(1)}, s32[16,4]{0,1:T(4,128)}, u32[]{:S(2)}) copy-start(s32[16,4]{0,1:T(4,128)} %param.26) | copy-start | bytes 772
  38.6 72.5 %all-gather.12.cloned.1.call-start = ((), (), s32[]{:S(2)}) async-start(), calls=%async_computation.10 | async-start | bytes 1966080 | tf_op jit(solution)/shard_map/all_gather | solution.py:315
  51.7 0.7 copy-start.9
  66.6 54.3 %reduce-scatter.5.cloned.1.call-start = ((), (), s32[]{:S(2)}) async-start(), calls=%async_computation.4 | async-start | bytes 573440 | tf_op jit(solution)/shard_map/reduce_scatter | solution.py:317
  68.7 1.6 copy-start.5
  70.2 0.7 copy-start.10
  93.2 47.7 %reduce-scatter.7.cloned.1.call-start = ((), (), s32[]{:S(2)}) async-start(), calls=%async_computation.5 | async-start | bytes 1146880 | tf_op jit(solution)/shard_map/reduce_scatter | solution.py:317
  93.3 1.2 copy-start
  102.2 65.0 %reduce-scatter.9.cloned.1.call-start = ((), (), s32[]{:S(2)}) async-start(), calls=%async_computation.6 | async-start | bytes 1146880 | tf_op jit(solution)/shard_map/reduce_scatter | solution.py:317
  102.2 1.2 copy-start.1
  111.1 89.5 %reduce-scatter.11.cloned.1.call-start = ((), (), s32[]{:S(2)}) async-start(), calls=%async_computation.7 | async-start | bytes 1720320 | tf_op jit(solution)/shard_map/reduce_scatter | solution.py:317
  111.2 1.4 copy-start.6
Sparse Core Ops, SparseCore 0:
  21.0 24.9 all-gather.7
  47.6 16.7 all-gather.9
  66.7 23.4 all-gather.11
Sparse Core Ops, SparseCore 1:
  93.3 21.8 reduce-scatter.4
  117.4 23.4 reduce-scatter.6
  143.2 23.9 reduce-scatter.8
  169.6 31.0 reduce-scatter.10

commit v2 on v1

--- a/solution.py
+++ b/solution.py
@@ -2,6 +2,7 @@
 
 import jax
 import jax.numpy as jnp
+import numpy as np
 from jax import lax
 from jax.experimental import pallas as pl
 from jax.experimental.pallas import tpu as pltpu
@@ -9,7 +10,7 @@
 
 HIDDEN = -1e30
 LANES = 128
-VMEM_LIMIT = 48 * 1024 * 1024
+VMEM_LIMIT = 32 * 1024 * 1024
 
 
 def dot_nt(a, b):
@@ -35,8 +36,8 @@
     offset,
     q_nope,
     q_rope,
-    wk_hbm,
-    wv_hbm,
+    wk,
+    wv,
     cache_latent,
     cache_rope,
     new_latent,
@@ -45,9 +46,9 @@
 ):
     if with_decode:
         (recv_latent, recv_rope, decode_table, decode_length, out,
-         wk, wv, keys, q, att, dkeys, sems, wsems, dsems) = rest
+         keys, q, att, dkeys, sems, dsems) = rest
     else:
-        out, wk, wv, keys, q, att, sems, wsems = rest
+        out, keys, q, att, sems = rest
     heads, t, nope_dim = q_nope.shape
     block_len, latent = cache_latent.shape[1:]
     rope_dim = q_rope.shape[1] // heads
@@ -55,8 +56,6 @@
     prior = blocks * block_len
     fresh = keys.shape[0] - prior
 
-    wk_copy = pltpu.make_async_copy(wk_hbm, wk, wsems.at[0])
-    wk_copy.start()
     copies = []
     for i in range(blocks):
         b = table[0, i]
@@ -73,8 +72,6 @@
         sems.at[2 * blocks + 1]))
     for c in copies:
         c.start()
-    wv_copy = pltpu.make_async_copy(wv_hbm, wv, wsems.at[1])
-    wv_copy.start()
     dec_copies = []
     if with_decode:
         pool = cache_latent.shape[0]
@@ -110,7 +107,6 @@
         if turn:
             pair = pltpu.roll(pair, LANES - turn, 1)
         q[h * t:(h + 1) * t, latent:] = jnp.where(lane < rope_dim, pair, one).astype(jnp.bfloat16)
-    wk_copy.wait()
     for h in range(heads):
         q[h * t:(h + 1) * t, :latent] = dot(q_nope[h], wk[h]).astype(jnp.bfloat16)
 
@@ -179,7 +175,6 @@
             for h in range(lo, lo + half):
                 att[h * t + at:h * t + at + decodes, :] = mixed[(h - lo) * decodes:(h - lo + 1) * decodes]
 
-    wv_copy.wait()
     dv = wv.shape[2]
     for h in range(heads):
         out[:, h * dv:(h + 1) * dv] = dot(att[h * t:(h + 1) * t, :], wv[h]).astype(jnp.bfloat16)
@@ -200,10 +195,8 @@
     vmem = pl.BlockSpec(memory_space=pltpu.VMEM)
     hbm = pl.BlockSpec(memory_space=pl.ANY)
     args = [table, offset, q_nope, q_rope, wk, wv, cache_latent, cache_rope, new_latent, new_rope]
-    in_specs = [smem, smem, vmem, vmem] + [hbm] * 6
+    in_specs = [smem, smem, vmem, vmem, vmem, vmem] + [hbm] * 4
     scratch = [
-        pltpu.VMEM(wk.shape, jnp.bfloat16),
-        pltpu.VMEM(wv.shape, jnp.bfloat16),
         pltpu.VMEM((prior + fresh, width), jnp.bfloat16),
         pltpu.VMEM((heads * size, width), jnp.bfloat16),
         pltpu.VMEM((heads * size, latent), jnp.bfloat16),
@@ -217,7 +210,7 @@
         span = pool * block_len + received + min(LANES, tok_group)
         scratch.append(pltpu.VMEM((span, width), jnp.bfloat16))
         flops += 2 * heads * decode[2].shape[0] * span * (width + latent)
-    scratch += [pltpu.SemaphoreType.DMA((2 * blocks + 2,)), pltpu.SemaphoreType.DMA((2,))]
+    scratch.append(pltpu.SemaphoreType.DMA((2 * blocks + 2,)))
     if decode is not None:
         scratch.append(pltpu.SemaphoreType.DMA((2 * pool + 4,)))
     return pl.pallas_call(
@@ -233,29 +226,74 @@
     )(*args)
 
 
-def project_kernel(x, w, out):
-    groups, t, depth = x.shape
-    out[...] = dot(x[...].reshape(groups * t, depth), w[...]).astype(jnp.bfloat16).reshape(out.shape)
-
-
-def project(x, w):
-    groups, t, depth = x.shape
+def project_kernel(place, w, *rest):
+    groups = (len(rest) - 1) // 2
+    parts, outs, x = rest[:groups], rest[groups:2 * groups], rest[-1]
+    t = parts[0].shape[0]
+    for i in range(groups):
+        x[pl.ds(pl.multiple_of(place[i] * t, t), t), :] = parts[i][...]
     columns = w.shape[1]
     step = 256 if columns % 256 == 0 else columns
+    for at in range(0, columns, step):
+        y = dot(x[...], w[:, at:at + step]).astype(jnp.bfloat16)
+        for i in range(groups):
+            outs[i][:, at:at + step] = y[i * t:(i + 1) * t]
+
+
+def project(place, parts, w):
+    groups = len(parts)
+    t, depth = parts[0].shape
+    columns = w.shape[1]
+    vmem = pl.BlockSpec(memory_space=pltpu.VMEM)
     return pl.pallas_call(
         project_kernel,
-        out_shape=jax.ShapeDtypeStruct((groups, t, columns), jnp.bfloat16),
-        grid=(columns // step,),
-        in_specs=[
-            pl.BlockSpec((groups, t, depth), lambda j: (0, 0, 0)),
-            pl.BlockSpec((depth, step), lambda j: (0, j)),
-        ],
-        out_specs=pl.BlockSpec((groups, t, step), lambda j: (0, 0, j)),
+        out_shape=[jax.ShapeDtypeStruct((t, columns), jnp.bfloat16)] * groups,
+        in_specs=[pl.BlockSpec(memory_space=pltpu.SMEM)] + [vmem] * (groups + 1),
+        out_specs=[vmem] * groups,
+        scratch_shapes=[pltpu.VMEM((groups * t, depth), jnp.bfloat16)],
         name="project",
         compiler_params=pltpu.CompilerParams(vmem_limit_bytes=VMEM_LIMIT),
         cost_estimate=pl.CostEstimate(
-            flops=2 * groups * t * depth * columns, bytes_accessed=2 * depth * columns, transcendentals=0),
-    )(x, w)
+            flops=2 * groups * t * depth * columns, bytes_accessed=4 * groups * t * columns,
+            transcendentals=0),
+    )(place, w, *parts)
+
+
+def gather_groups(x):
+    groups = lax.axis_size("dp")
+    if groups % 2:
+        return [x] + [lax.ppermute(x, "dp", [(i, (i + s) % groups) for i in range(groups)])
+                      for s in range(1, groups)]
+    mine = [x] + [lax.ppermute(x, "dp", [(i, (i + 2 * s) % groups) for i in range(groups)])
+                  for s in range(1, groups // 2)]
+    swap = [(i, i ^ 1) for i in range(groups)]
+    return mine + [lax.ppermute(y, "dp", swap) for y in mine]
+
+
+def gathered_ids(groups, me):
+    if groups % 2:
+        return [(me - s) % groups for s in range(groups)]
+    return [(who - 2 * s) % groups for who in (me, me ^ 1) for s in range(groups // 2)]
+
+
+LINE_ORDER = ((0, 3, 2, 1), (1, 3, 2, 0), (2, 0, 1, 3), (3, 0, 1, 2))
+
+
+def add(*terms):
+    return sum(x.astype(jnp.float32) for x in terms).astype(jnp.bfloat16)
+
+
+def reduce_line(own, far, mid, near):
+    inward = [(0, 1), (3, 2)]
+    across = [(1, 2), (2, 1)]
+    outward = [(1, 0), (2, 3)]
+    far_in = lax.ppermute(far, "tp", inward)
+    mid_in = lax.ppermute(mid, "tp", inward)
+    near_in = lax.ppermute(near, "tp", inward)
+    far_on = lax.ppermute(add(far, far_in), "tp", across)
+    mid_on = lax.ppermute(add(mid, mid_in), "tp", across)
+    last = lax.ppermute(add(near, far_on), "tp", outward)
+    return add(own, near_in, mid_on, last)
 
 
 def body(
@@ -299,6 +337,16 @@
     received = jnp.roll(received, me + 1, axis=0)
     received = received.reshape(group_count * capacity * block_len, latent_dim + LANES)
 
+    on_line = lax.axis_size("tp") == 4 and group_count == 4
+    ids = np.array([gathered_ids(group_count, g) for g in range(group_count)], np.int32)
+    if on_line:
+        places = np.argsort(np.array(LINE_ORDER), axis=1)[None, :, :]
+        places = np.take_along_axis(
+            np.broadcast_to(places, (4, 4, 4)), np.broadcast_to(ids[:, None, :], (4, 4, 4)), axis=2)
+        place = jnp.asarray(places.astype(np.int32))[me, lax.axis_index("tp")]
+    else:
+        place = jnp.asarray(ids)[me]
+
     first = 0
     outs = []
     sizes = chunk_sizes(tok_group)
@@ -312,9 +360,11 @@
             query_nope[first:first + size].transpose(1, 0, 2), query_rope[first:first + size],
             absorb_key, absorb_value, cache_latent, padded_rope, new_latent, padded_new,
             prefill_table, prefill_offset, decode)
-        gathered = lax.all_gather(head_out, "dp", axis=0, tiled=False)
-        partials = project(gathered, output_weight)
-        outs.append(lax.psum_scatter(partials, "tp", scatter_dimension=0, tiled=False))
+        partials = project(place, gather_groups(head_out), output_weight)
+        if on_line:
+            outs.append(reduce_line(*partials))
+        else:
+            outs.append(lax.psum_scatter(jnp.stack(partials), "tp", scatter_dimension=0, tiled=False))
         first += size
     return jnp.concatenate(outs, axis=0)
 

time: 212 us -> 195 us (0.920)
  starting transfers between devices: 3.83 us -> 71 us
  waiting for transfers between devices: 80.7 us -> 55.7 us
  Pallas kernels: 64 us -> 39.6 us
  between operations: 16 us -> 1.61 us
  blocking collectives: 10.6 us -> 0 us
  local copies, waits for them, and re-layouts: 31.6 us -> 23.8 us
    reduce_scatter x4 -> x0, waiting for transfers between devices: 79.8 us -> none  [body(): lax.psum_scatter(partials, 'tp', scatter_dimension=0, tiled=False)]
    ppermute x0 -> x36, starting transfers between devices: none -> 69 us  [the longest x4 24.2 us: reduce_line(): mid_in = lax.ppermute(mid, 'tp', inward)]
    ppermute x0 -> x36, waiting for transfers between devices: none -> 44.6 us  [the longest x4 19 us: reduce_line(): last = lax.ppermute(add(near, far_on), 'tp', outward)]
    pallas_call x4, Pallas kernels: 30.5 us -> 11.1 us  [project(): pl.pallas_call(project_kernel, out_shape=[jax.ShapeDtypeStruct((t, column...]
    all_gather x1 -> x0, blocking collectives: 10.6 us -> none  [body(): gathered = lax.all_gather(head_out, 'dp', axis=0, tiled=False)]
    ppermute x3, waiting for transfers between devices: 0.64 us -> 11.1 us  [body(): lax.ppermute(lax.dynamic_index_in_dim(send, there, 0, keepdims=False), 'd...]
    pallas_call x4, Pallas kernels: 33.5 us -> 28.5 us  [attend(): pl.pallas_call(functools.partial(attend_kernel, first, prefill_len, exp_s...]
    unnamed x45 -> x65, local copies, waits for them, and re-layouts: 17 us -> 12.7 us
  transfers between devices with their start and end apart: 10 -> 39, of which waited for: 4 -> 12; matrix products, arithmetic and copies ran while one was open for 10% -> 5% of each run, Pallas kernels for 27% -> 18%
where the time goes in v2:
time: 195 us; the launch traced here: 194 us
  starting transfers between devices  71 us (36%)
  waiting for transfers between devices  55.7 us (29%)
  Pallas kernels  39.6 us (20%)
  local copies, waits for them, and re-layouts  23.8 us (12%)
  other arithmetic  2.24 us (1%)
    pallas_call x4, Pallas kernels, attend(): pl.pallas_call(functools.partial(attend_kernel, first, prefill_len, exp_s...  28.5 us
    ppermute x4, starting transfers between devices, reduce_line(): mid_in = lax.ppermute(mid, 'tp', inward)  24.2 us
    ppermute x4, waiting for transfers between devices, reduce_line(): last = lax.ppermute(add(near, far_on), 'tp', outward)  19 us
    ppermute x4, waiting for transfers between devices, reduce_line(): far_in = lax.ppermute(far, 'tp', inward)  16.9 us
    ppermute x4, starting transfers between devices, reduce_line(): far_in = lax.ppermute(far, 'tp', inward)  14.1 us
    ppermute x4, starting transfers between devices, reduce_line(): near_in = lax.ppermute(near, 'tp', inward)  12.7 us
    unnamed x65, local copies, waits for them, and re-layouts  12.7 us
    ppermute x3, waiting for transfers between devices, body(): lax.ppermute(lax.dynamic_index_in_dim(send, there, 0, keepdims=False), 'd...  11.1 us
  transfers between devices with their start and end apart: 39, of which 12 were waited for; matrix products, arithmetic and copies ran while one was open for 5% of the time, Pallas kernels for 18%

profile of v2, /device:TPU:0, one launch (start us, length us, event | category | flops | bytes accessed | tf_op | source)
XLA Modules:
  0.0 194.0 jit_solution(18439928368874032058)
XLA Ops:
  0.0 1.6 reshape.34
  1.6 1.5 copy.25
  3.3 0.9 pad.10.new_rope
  4.9 0.8 slice.31.q_rope
  5.7 1.6 copy-done.7
  7.3 1.6 copy-done.10
  8.9 3.8 %attend.4.rest_0_ = bf16[32,2048]{1,0:T(8,128)(2,1)S(1)} custom-call(s32[1,16]{1,0:T(1,128)S(1)} %copy-done.16, s32[1]{0:T(128)S(6)} %copy.51.offset, bf16[16,32,128]{2,1,0:T(8,128)(2,1)S(1)} %bitcast.42, bf16[32,1024]{1,0:T(8,128)(2,1)S(1)} %slice.31.q_rope, bf16[16,128,512]{2,1,0:T(8,128)(2,1)S(1)} %copy-done.7, bf16[16,512,128]{2,1,0:T(8,128)(2,1)S(1)} %copy-done.10, ...), custom_call_target="tpu_custom_call" | custom-call | flops 2986344448 | bytes 6000000 | tf_op jit(solution)/shard_map/attend/pallas_call | solution.py:216
  12.7 3.0 %collective-permute-start = (bf16[32,2048]{1,0:T(8,128)(2,1)S(1)}, bf16[32,2048]{1,0:T(8,128)(2,1)S(1)}, u32[]{:S(2)}, u32[]{:S(2)}) collective-permute-start(bf16[32,2048]{1,0:T(8,128)(2,1)S(1)} %attend.4.rest_0_), channel_id=1, source_target_pairs={{0,8},{4,12},{8,0},{12,4},{1,9},{5,13},{9,1},{13,5},{2,10},{6,14},... | collective-permute-start | bytes 393224 | tf_op jit(solution)/shard_map/ppermute | solution.py:267
  15.9 5.7 %attend.5.rest_0_ = bf16[64,2048]{1,0:T(8,128)(2,1)S(1)} custom-call(s32[1,16]{1,0:T(1,128)S(1)} %copy-done.16, s32[1]{0:T(128)S(6)} %copy.51.offset, bf16[16,64,128]{2,1,0:T(8,128)(2,1)S(1)} %bitcast.41, bf16[64,1024]{1,0:T(8,128)(2,1)S(1)} %get-tuple-element.42.q_rope, bf16[16,128,512]{2,1,0:T(8,128)(2,1)S(1)} %copy-done.7, ...), custom_call_target="tpu_custom_call" | custom-call | flops 5972688896 | bytes 6000000 | tf_op jit(solution)/shard_map/attend/pallas_call | solution.py:216
  21.6 1.4 collective-permute-start.9
  23.2 1.6 gather_fusion.1
  24.8 2.2 %gather_fusion = bf16[8,64,512]{2,1,0:T(8,128)(2,1)S(1)} fusion(bf16[32,64,512]{2,1,0:T(8,128)(2,1)} %cache_latent.7, s32[1024]{0:T(1024)S(1)} %pad_clamp_fusion), kind=kCustom, calls=%fused_computation | custom fusion | bytes 1048608 | tf_op jit(solution)/shard_map/gather | solution.py:328
  27.2 0.8 dynamic-slice_bitcast_fusion
  28.0 0.8 collective-permute-start.27
  29.1 1.6 copy-done.8
  30.6 1.6 copy-done.11
  32.2 5.8 %attend.6.rest_0_ = bf16[64,2048]{1,0:T(8,128)(2,1)S(1)} custom-call(s32[1,16]{1,0:T(1,128)S(1)} %copy-done.16, s32[1]{0:T(128)S(6)} %copy.51.offset, bf16[16,64,128]{2,1,0:T(8,128)(2,1)S(1)} %bitcast.40, bf16[64,1024]{1,0:T(8,128)(2,1)S(1)} %get-tuple-element.43.q_rope, bf16[16,128,512]{2,1,0:T(8,128)(2,1)S(1)} %copy-done.8, ...), custom_call_target="tpu_custom_call" | custom-call | flops 6576668672 | bytes 6000000 | tf_op jit(solution)/shard_map/attend/pallas_call | solution.py:216
  38.1 1.0 slice.37.q_rope
  39.4 0.7 fusion.2.place
  40.1 1.2 collective-permute-start.28
  41.3 5.6 %collective-permute-done.28 = bf16[2,64,640]{2,1,0:T(8,128)(2,1)S(1)} collective-permute-done((bf16[2,64,640]{2,1,0:T(8,128)(2,1)}, bf16[2,64,640]{2,1,0:T(8,128)(2,1)S(1)}, u32[]{:S(2)}, u32[]{:S(2)}) %collective-permute-start.28) | collective-permute-done | bytes 163872 | tf_op jit(solution)/shard_map/ppermute | solution.py:333
  47.0 0.8 collective-permute-start.18
  47.7 5.5 %collective-permute-done.29 = bf16[2,64,640]{2,1,0:T(8,128)(2,1)S(1)} collective-permute-done((bf16[2,64,640]{2,1,0:T(8,128)(2,1)}, bf16[2,64,640]{2,1,0:T(8,128)(2,1)S(1)}, u32[]{:S(2)}, u32[]{:S(2)}) %collective-permute-start.29) | collective-permute-done | bytes 163872 | tf_op jit(solution)/shard_map/ppermute | solution.py:333
  53.3 0.9 dynamic-slice_dynamic-update-slice_fusion
  54.3 0.9 dynamic-slice_dynamic-update-slice_fusion.1
  56.0 3.1 %copy-done = bf16[2048,1792]{1,0:T(8,128)(2,1)S(1)} copy-done((bf16[2048,1792]{1,0:T(8,128)(2,1)S(1)}, bf16[2048,1792]{1,0:T(8,128)(2,1)}, u32[]{:S(2)}) %copy-start) | copy-done | bytes 7340056
  59.1 1.8 project.4
  60.8 3.8 %collective-permute-start.6 = (bf16[32,1792]{1,0:T(8,128)(2,1)S(1)}, bf16[32,1792]{1,0:T(8,128)(2,1)S(1)}, u32[]{:S(2)}, u32[]{:S(2)}) collective-permute-start(bf16[32,1792]{1,0:T(8,128)(2,1)S(1)} %get-tuple-element.24), channel_id=1, source_target_pairs={{0,1},{3,2},{4,5},{7,6},{8,9},{11,10},{12,13},{15,14},{16,17},{19,... | collective-permute-start | bytes 344072 | tf_op jit(solution)/shard_map/ppermute | solution.py:290
  64.7 13.2 %attend.7.rest_0_ = bf16[96,2048]{1,0:T(8,128)(2,1)S(1)} custom-call(s32[1,16]{1,0:T(1,128)S(1)} %copy-done.16, s32[1]{0:T(128)S(6)} %copy.51.offset, bf16[16,96,128]{2,1,0:T(8,128)(2,1)S(1)} %bitcast.39, bf16[96,1024]{1,0:T(8,128)(2,1)S(1)} %slice.37.q_rope, bf16[16,128,512]{2,1,0:T(8,128)(2,1)S(1)} %copy-done.9, bf16[16,512,128]{2,1,0:T(8,128)(2,1)S(1)} %copy-done.12, ...), custom_call_target="tpu_custom_call" | custom-call | flops 13035896832 | bytes 6000000 | tf_op jit(solution)/shard_map/attend/pallas_call | solution.py:216
  78.0 1.3 collective-permute-start.4
  79.3 2.5 %collective-permute-done.4 = bf16[32,1792]{1,0:T(8,128)(2,1)S(1)} collective-permute-done((bf16[32,1792]{1,0:T(8,128)(2,1)S(1)}, bf16[32,1792]{1,0:T(8,128)(2,1)S(1)}, u32[]{:S(2)}, u32[]{:S(2)}) %collective-permute-start.4) | collective-permute-done | bytes 114720 | tf_op jit(solution)/shard_map/ppermute | solution.py:291
  82.6 0.8 collective-permute-start.30
  84.0 0.8 collective-permute-done.11.rest_3_
  84.9 8.7 %collective-permute-start.3 = (bf16[32,1792]{1,0:T(8,128)(2,1)S(1)}, bf16[32,1792]{1,0:T(8,128)(2,1)S(1)}, u32[]{:S(2)}, u32[]{:S(2)}) collective-permute-start(bf16[32,1792]{1,0:T(8,128)(2,1)S(1)} %get-tuple-element.22), channel_id=1, source_target_pairs={{0,1},{3,2},{4,5},{7,6},{8,9},{11,10},{12,13},{15,14},{16,17},{19,... | collective-permute-start | bytes 344072 | tf_op jit(solution)/shard_map/ppermute | solution.py:292
  93.6 2.8 %project.5 = (bf16[64,1792]{1,0:T(8,128)(2,1)S(1)}, bf16[64,1792]{1,0:T(8,128)(2,1)S(1)}, bf16[64,1792]{1,0:T(8,128)(2,1)S(1)}, bf16[64,1792]{1,0:T(8,128)(2,1)S(1)}) custom-call(s32[4]{0:T(128)S(1)} %fusion.2.place, bf16[2048,1792]{1,0:T(8,128)(2,1)S(1)} %bitcast.38, bf16[64,2048]{1,0:T(8,128)(2,1)S(1)} %attend.5.rest_0_, ...), custom_call_target="tpu_custom_call" | custom-call | flops 1879048192 | bytes 1835008 | tf_op jit(solution)/shard_map/project/pallas_call | solution.py:248
  96.4 0.7 collective-permute-start.5
  97.1 1.6 collective-permute-start.8
  98.6 2.8 %project.6 = (bf16[64,1792]{1,0:T(8,128)(2,1)S(1)}, bf16[64,1792]{1,0:T(8,128)(2,1)S(1)}, bf16[64,1792]{1,0:T(8,128)(2,1)S(1)}, bf16[64,1792]{1,0:T(8,128)(2,1)S(1)}) custom-call(s32[4]{0:T(128)S(1)} %fusion.2.place, bf16[2048,1792]{1,0:T(8,128)(2,1)S(1)} %bitcast.38, bf16[64,2048]{1,0:T(8,128)(2,1)S(1)} %attend.6.rest_0_, ...), custom_call_target="tpu_custom_call" | custom-call | flops 1879048192 | bytes 1835008 | tf_op jit(solution)/shard_map/project/pallas_call | solution.py:248
  101.4 4.6 %collective-permute-start.15 = (bf16[64,1792]{1,0:T(8,128)(2,1)S(1)}, bf16[64,1792]{1,0:T(8,128)(2,1)S(1)}, u32[]{:S(2)}, u32[]{:S(2)}) collective-permute-start(bf16[64,1792]{1,0:T(8,128)(2,1)S(1)} %get-tuple-element.28), channel_id=1, source_target_pairs={{0,1},{3,2},{4,5},{7,6},{8,9},{11,10},{12,13},{15,14},{16,17},{19,... | collective-permute-start | bytes 688136 | tf_op jit(solution)/shard_map/ppermute | solution.py:290
  106.0 1.3 collective-permute-start.13
  107.3 1.3 collective-permute-start.12
  108.7 3.3 %collective-permute-done.15 = bf16[64,1792]{1,0:T(8,128)(2,1)S(1)} collective-permute-done((bf16[64,1792]{1,0:T(8,128)(2,1)S(1)}, bf16[64,1792]{1,0:T(8,128)(2,1)S(1)}, u32[]{:S(2)}, u32[]{:S(2)}) %collective-permute-start.15) | collective-permute-done | bytes 229408 | tf_op jit(solution)/shard_map/ppermute | solution.py:290
  112.0 4.4 %collective-permute-start.24 = (bf16[64,1792]{1,0:T(8,128)(2,1)S(1)}, bf16[64,1792]{1,0:T(8,128)(2,1)S(1)}, u32[]{:S(2)}, u32[]{:S(2)}) collective-permute-start(bf16[64,1792]{1,0:T(8,128)(2,1)S(1)} %get-tuple-element.32), channel_id=1, source_target_pairs={{0,1},{3,2},{4,5},{7,6},{8,9},{11,10},{12,13},{15,14},{16,17},{19,... | collective-permute-start | bytes 688136 | tf_op jit(solution)/shard_map/ppermute | solution.py:290
  117.0 4.4 %collective-permute-start.22 = (bf16[64,1792]{1,0:T(8,128)(2,1)S(1)}, bf16[64,1792]{1,0:T(8,128)(2,1)S(1)}, u32[]{:S(2)}, u32[]{:S(2)}) collective-permute-start(bf16[64,1792]{1,0:T(8,128)(2,1)S(1)} %get-tuple-element.31), channel_id=1, source_target_pairs={{0,1},{3,2},{4,5},{7,6},{8,9},{11,10},{12,13},{15,14},{16,17},{19,... | collective-permute-start | bytes 688136 | tf_op jit(solution)/shard_map/ppermute | solution.py:291
  121.4 1.3 collective-permute-start.21
  122.7 4.0 %collective-permute-done.24 = bf16[64,1792]{1,0:T(8,128)(2,1)S(1)} collective-permute-done((bf16[64,1792]{1,0:T(8,128)(2,1)S(1)}, bf16[64,1792]{1,0:T(8,128)(2,1)S(1)}, u32[]{:S(2)}, u32[]{:S(2)}) %collective-permute-start.24) | collective-permute-done | bytes 229408 | tf_op jit(solution)/shard_map/ppermute | solution.py:290
  126.8 4.9 %collective-permute-done.22 = bf16[64,1792]{1,0:T(8,128)(2,1)S(1)} collective-permute-done((bf16[64,1792]{1,0:T(8,128)(2,1)S(1)}, bf16[64,1792]{1,0:T(8,128)(2,1)S(1)}, u32[]{:S(2)}, u32[]{:S(2)}) %collective-permute-start.22) | collective-permute-done | bytes 229408 | tf_op jit(solution)/shard_map/ppermute | solution.py:291
  131.7 0.7 collective-permute-start.16
  132.4 0.7 collective-permute-start.14
  133.1 0.7 collective-permute-start.25
  133.8 3.8 %project.7 = (bf16[96,1792]{1,0:T(8,128)(2,1)S(1)}, bf16[96,1792]{1,0:T(8,128)(2,1)S(1)}, bf16[96,1792]{1,0:T(8,128)(2,1)S(1)}, bf16[96,1792]{1,0:T(8,128)(2,1)S(1)}) custom-call(s32[4]{0:T(128)S(1)} %fusion.2.place, bf16[2048,1792]{1,0:T(8,128)(2,1)S(1)} %bitcast.38, bf16[96,2048]{1,0:T(8,128)(2,1)S(1)} %attend.7.rest_0_, ...), custom_call_target="tpu_custom_call" | custom-call | flops 2818572288 | bytes 2752512 | tf_op jit(solution)/shard_map/project/pallas_call | solution.py:248
  137.6 0.7 collective-permute-start.23
  138.4 1.3 collective-permute-start.17
  139.7 17.2 %collective-permute-start.34 = (bf16[96,1792]{1,0:T(8,128)(2,1)S(1)}, bf16[96,1792]{1,0:T(8,128)(2,1)S(1)}, u32[]{:S(2)}, u32[]{:S(2)}) collective-permute-start(bf16[96,1792]{1,0:T(8,128)(2,1)S(1)} %get-tuple-element.35), channel_id=1, source_target_pairs={{0,1},{3,2},{4,5},{7,6},{8,9},{11,10},{12,13},{15,14},{16,17},{19,... | collective-permute-start | bytes 1032200 | tf_op jit(solution)/shard_map/ppermute | solution.py:291
  157.0 1.3 collective-permute-start.36
  158.9 1.5 collective-permute-start.33
  160.5 9.5 %collective-permute-done.36 = bf16[96,1792]{1,0:T(8,128)(2,1)S(1)} collective-permute-done((bf16[96,1792]{1,0:T(8,128)(2,1)S(1)}, bf16[96,1792]{1,0:T(8,128)(2,1)S(1)}, u32[]{:S(2)}, u32[]{:S(2)}) %collective-permute-start.36) | collective-permute-done | bytes 344096 | tf_op jit(solution)/shard_map/ppermute | solution.py:290
  170.0 1.3 collective-permute-start.26
  171.4 0.7 collective-permute-start.37
  172.2 0.7 collective-permute-start.35
  173.0 1.3 collective-permute-start.38
  174.3 5.3 %collective-permute-done.26 = bf16[64,1792]{1,0:T(8,128)(2,1)S(1)} collective-permute-done((bf16[64,1792]{1,0:T(8,128)(2,1)S(1)}, bf16[64,1792]{1,0:T(8,128)(2,1)S(1)}, u32[]{:S(2)}, u32[]{:S(2)}) %collective-permute-start.26) | collective-permute-done | bytes 229408 | tf_op jit(solution)/shard_map/ppermute | solution.py:295
  179.8 13.0 %collective-permute-done.38 = bf16[96,1792]{1,0:T(8,128)(2,1)S(1)} collective-permute-done((bf16[96,1792]{1,0:T(8,128)(2,1)S(1)}, bf16[96,1792]{1,0:T(8,128)(2,1)S(1)}, u32[]{:S(2)}, u32[]{:S(2)}) %collective-permute-start.38) | collective-permute-done | bytes 344096 | tf_op jit(solution)/shard_map/ppermute | solution.py:295
  193.0 1.0 pad_maximum_fusion
  (130 shorter events, 5.7 us)
Async XLA Ops:
  0.0 4.8 %slice-start.2 = ((bf16[256,16,128]{2,1,0:T(8,128)(2,1)}), bf16[32,16,128]{2,1,0:T(8,128)(2,1)S(1)}, s32[]{:S(2)}) async-start(bf16[256,16,128]{2,1,0:T(8,128)(2,1)} %param.15), calls=%async_computation.2 | async-start | bytes 262144 | tf_op jit(solution)/shard_map/slice | solution.py:360
  0.0 5.7 %copy-start.13 = (bf16[256,512]{1,0:T(8,128)(2,1)S(1)}, bf16[256,512]{1,0:T(8,128)(2,1)}, u32[]{:S(2)}) copy-start(bf16[256,512]{1,0:T(8,128)(2,1)} %new_latent.7) | copy-start | bytes 786436
  0.0 5.7 %copy-start.1 = (bf16[32,64,512]{2,1,0:T(8,128)(2,1)S(1)}, bf16[32,64,512]{2,1,0:T(8,128)(2,1)}, u32[]{:S(2)}) copy-start(bf16[32,64,512]{2,1,0:T(8,128)(2,1)} %cache_latent.7) | copy-start | bytes 6291460
  0.0 5.7 %copy-start.16 = (s32[1,16]{1,0:T(1,128)S(1)}, s32[1,16]{1,0:T(1,128)}, u32[]{:S(2)}) copy-start(s32[1,16]{1,0:T(1,128)} %table.7) | copy-start | bytes 196
  1.6 1.5 copy-start.18
  4.2 11.7 %copy-start.5 = (bf16[256,128]{1,0:T(8,128)(2,1)}, bf16[256,128]{1,0:T(8,128)(2,1)S(1)}, u32[]{:S(2)}) copy-start(bf16[256,128]{1,0:T(8,128)(2,1)S(1)} %pad.10.new_rope) | copy-start | bytes 196612
  5.7 1.6 copy-start.7
  7.3 1.6 copy-start.10
  8.9 6.8 %copy-start.19 = (bf16[256,16,128]{2,1,0:T(8,128)(2,1)S(1)}, bf16[256,16,128]{2,1,0:T(8,128)(2,1)}, u32[]{:S(2)}) copy-start(bf16[256,16,128]{2,1,0:T(8,128)(2,1)} %param.15) | copy-start | bytes 3145732
  8.9 6.9 %copy-start.20 = (bf16[256,1024]{1,0:T(8,128)(2,1)S(1)}, bf16[256,1024]{1,0:T(8,128)(2,1)}, u32[]{:S(2)}) copy-start(bf16[256,1024]{1,0:T(8,128)(2,1)} %param.16) | copy-start | bytes 1572868
  8.9 7.0 %copy-start.14 = (bf16[256,512]{1,0:T(8,128)(2,1)S(1)}, bf16[256,512]{1,0:T(8,128)(2,1)}, u32[]{:S(2)}) copy-start(bf16[256,512]{1,0:T(8,128)(2,1)} %new_latent.7) | copy-start | bytes 786436
  12.7 3.2 %copy-start.2 = (bf16[32,64,512]{2,1,0:T(8,128)(2,1)S(1)}, bf16[32,64,512]{2,1,0:T(8,128)(2,1)}, u32[]{:S(2)}) copy-start(bf16[32,64,512]{2,1,0:T(8,128)(2,1)} %cache_latent.7) | copy-start | bytes 6291460
  12.7 34.2 %collective-permute-start = (bf16[32,2048]{1,0:T(8,128)(2,1)S(1)}, bf16[32,2048]{1,0:T(8,128)(2,1)S(1)}, u32[]{:S(2)}, u32[]{:S(2)}) collective-permute-start(bf16[32,2048]{1,0:T(8,128)(2,1)S(1)} %attend.4.rest_0_), channel_id=1, source_target_pairs={{0,8},{4,12},{8,0},{12,4},{1,9},{5,13},{9,1},{13,5},{2,10},{6,14},... | collective-permute-start | bytes 393224 | tf_op jit(solution)/shard_map/ppermute | solution.py:267
  15.7 39.7 %collective-permute-start.1 = (bf16[32,2048]{1,0:T(8,128)(2,1)S(1)}, bf16[32,2048]{1,0:T(8,128)(2,1)S(1)}, u32[]{:S(2)}, u32[]{:S(2)}) collective-permute-start(bf16[32,2048]{1,0:T(8,128)(2,1)S(1)} %attend.4.rest_0_), channel_id=1, source_target_pairs={{0,4},{4,0},{8,12},{12,8},{1,5},{5,1},{9,13},{13,9},{2,6},{6,2},{1... | collective-permute-start | bytes 393224 | tf_op jit(solution)/shard_map/ppermute | solution.py:270
  15.9 7.1 %copy-start.22 = (s32[1,4,2]{1,2,0:T(2,128)S(1)}, s32[1,4,2]{1,2,0:T(2,128)}, u32[]{:S(2)}) copy-start(s32[1,4,2]{1,2,0:T(2,128)} %param.24) | copy-start | bytes 100
  21.6 60.9 %collective-permute-start.9 = (bf16[64,2048]{1,0:T(8,128)(2,1)S(1)}, bf16[64,2048]{1,0:T(8,128)(2,1)S(1)}, u32[]{:S(2)}, u32[]{:S(2)}) collective-permute-start(bf16[64,2048]{1,0:T(8,128)(2,1)S(1)} %attend.5.rest_0_), channel_id=1, source_target_pairs={{0,8},{4,12},{8,0},{12,4},{1,9},{5,13},{9,1},{13,5},{2,10},{6,14},... | collective-permute-start | bytes 786440 | tf_op jit(solution)/shard_map/ppermute | solution.py:267
  23.0 60.9 %collective-permute-start.10 = (bf16[64,2048]{1,0:T(8,128)(2,1)S(1)}, bf16[64,2048]{1,0:T(8,128)(2,1)S(1)}, u32[]{:S(2)}, u32[]{:S(2)}) collective-permute-start(bf16[64,2048]{1,0:T(8,128)(2,1)S(1)} %attend.5.rest_0_), channel_id=1, source_target_pairs={{0,4},{4,0},{8,12},{12,8},{1,5},{5,1},{9,13},{13,9},{2,6},{6,2},{1... | collective-permute-start | bytes 786440 | tf_op jit(solution)/shard_map/ppermute | solution.py:270
  27.0 2.0 %copy-start.3 = (bf16[32,64,512]{2,1,0:T(8,128)(2,1)S(1)}, bf16[32,64,512]{2,1,0:T(8,128)(2,1)}, u32[]{:S(2)}) copy-start(bf16[32,64,512]{2,1,0:T(8,128)(2,1)} %cache_latent.7) | copy-start | bytes 6291460
  27.0 2.0 %copy-start.6 = (bf16[256,128]{1,0:T(8,128)(2,1)S(1)}, bf16[256,128]{1,0:T(8,128)(2,1)}, u32[]{:S(2)}) copy-start(bf16[256,128]{1,0:T(8,128)(2,1)} %copy-done.5) | copy-start | bytes 196612
  27.1 2.0 %copy-start.15 = (bf16[256,512]{1,0:T(8,128)(2,1)S(1)}, bf16[256,512]{1,0:T(8,128)(2,1)}, u32[]{:S(2)}) copy-start(bf16[256,512]{1,0:T(8,128)(2,1)} %new_latent.7) | copy-start | bytes 786436
  27.2 1.7 copy-start.17
  28.0 12.1 %collective-permute-start.27 = (bf16[2,64,640]{2,1,0:T(8,128)(2,1)}, bf16[2,64,640]{2,1,0:T(8,128)(2,1)S(1)}, u32[]{:S(2)}, u32[]{:S(2)}) collective-permute-start(bf16[2,64,640]{2,1,0:T(8,128)(2,1)} %get-tuple-element.41), channel_id=1, source_target_pairs={{0,12},{4,0},{8,4},{12,8},{1,13},{5,1},{9,5},{13,9},{2,14},{6,2},{... | collective-permute-start | bytes 491528 | tf_op jit(solution)/shard_map/ppermute | solution.py:333
  29.1 1.6 copy-start.8
  30.6 1.6 copy-start.11
  40.1 6.8 %collective-permute-start.28 = (bf16[2,64,640]{2,1,0:T(8,128)(2,1)}, bf16[2,64,640]{2,1,0:T(8,128)(2,1)S(1)}, u32[]{:S(2)}, u32[]{:S(2)}) collective-permute-start(bf16[2,64,640]{2,1,0:T(8,128)(2,1)} %get-tuple-element.40), channel_id=1, source_target_pairs={{0,8},{4,12},{8,0},{12,4},{1,9},{5,13},{9,1},{13,5},{2,10},{6,14},... | collective-permute-start | bytes 491528 | tf_op jit(solution)/shard_map/ppermute | solution.py:333
  46.9 6.3 %collective-permute-start.29 = (bf16[2,64,640]{2,1,0:T(8,128)(2,1)}, bf16[2,64,640]{2,1,0:T(8,128)(2,1)S(1)}, u32[]{:S(2)}, u32[]{:S(2)}) collective-permute-start(bf16[2,64,640]{2,1,0:T(8,128)(2,1)} %get-tuple-element.39), channel_id=1, source_target_pairs={{0,4},{4,8},{8,12},{12,0},{1,5},{5,9},{9,13},{13,1},{2,6},{6,10},{... | collective-permute-start | bytes 491528 | tf_op jit(solution)/shard_map/ppermute | solution.py:333
  47.0 36.4 %collective-permute-start.18 = (bf16[64,2048]{1,0:T(8,128)(2,1)S(1)}, bf16[64,2048]{1,0:T(8,128)(2,1)S(1)}, u32[]{:S(2)}, u32[]{:S(2)}) collective-permute-start(bf16[64,2048]{1,0:T(8,128)(2,1)S(1)} %attend.6.rest_0_), channel_id=1, source_target_pairs={{0,8},{4,12},{8,0},{12,4},{1,9},{5,13},{9,1},{13,5},{2,10},{6,14},... | collective-permute-start | bytes 786440 | tf_op jit(solution)/shard_map/ppermute | solution.py:267
  53.2 2.7 %collective-permute-start.2 = (bf16[32,2048]{1,0:T(8,128)(2,1)S(1)}, bf16[32,2048]{1,0:T(8,128)(2,1)S(1)}, u32[]{:S(2)}, u32[]{:S(2)}) collective-permute-start(bf16[32,2048]{1,0:T(8,128)(2,1)S(1)} %collective-permute-done.rest_1_), channel_id=1, source_target_pairs={{0,4},{4,0},{8,12},{12,8},{1,5},{5,1},{9,13},{13,9},{2,6},{6,2},{1... | collective-permute-start | bytes 393224 | tf_op jit(solution)/shard_map/ppermute | solution.py:270
  55.4 41.0 %collective-permute-start.19 = (bf16[64,2048]{1,0:T(8,128)(2,1)S(1)}, bf16[64,2048]{1,0:T(8,128)(2,1)S(1)}, u32[]{:S(2)}, u32[]{:S(2)}) collective-permute-start(bf16[64,2048]{1,0:T(8,128)(2,1)S(1)} %attend.6.rest_0_), channel_id=1, source_target_pairs={{0,4},{4,0},{8,12},{12,8},{1,5},{5,1},{9,13},{13,9},{2,6},{6,2},{1... | collective-permute-start | bytes 786440 | tf_op jit(solution)/shard_map/ppermute | solution.py:270
  56.0 3.1 %copy-start = (bf16[2048,1792]{1,0:T(8,128)(2,1)S(1)}, bf16[2048,1792]{1,0:T(8,128)(2,1)}, u32[]{:S(2)}) copy-start(bf16[2048,1792]{1,0:T(8,128)(2,1)} %w.7) | copy-start | bytes 22020100
  59.1 5.6 %copy-start.4 = (bf16[32,64,512]{2,1,0:T(8,128)(2,1)S(1)}, bf16[32,64,512]{2,1,0:T(8,128)(2,1)}, u32[]{:S(2)}) copy-start(bf16[32,64,512]{2,1,0:T(8,128)(2,1)} %cache_latent.7) | copy-start | bytes 6291460
  59.1 5.6 %copy-start.9 = (bf16[16,128,512]{2,1,0:T(8,128)(2,1)S(1)}, bf16[16,128,512]{2,1,0:T(8,128)(2,1)}, u32[]{:S(2)}) copy-start(bf16[16,128,512]{2,1,0:T(8,128)(2,1)} %wk.7) | copy-start | bytes 6291460
  59.1 5.7 %copy-start.12 = (bf16[16,512,128]{2,1,0:T(8,128)(2,1)S(1)}, bf16[16,512,128]{2,1,0:T(8,128)(2,1)}, u32[]{:S(2)}) copy-start(bf16[16,512,128]{2,1,0:T(8,128)(2,1)} %wv.7) | copy-start | bytes 6291460
  60.8 17.2 %collective-permute-start.6 = (bf16[32,1792]{1,0:T(8,128)(2,1)S(1)}, bf16[32,1792]{1,0:T(8,128)(2,1)S(1)}, u32[]{:S(2)}, u32[]{:S(2)}) collective-permute-start(bf16[32,1792]{1,0:T(8,128)(2,1)S(1)} %get-tuple-element.24), channel_id=1, source_target_pairs={{0,1},{3,2},{4,5},{7,6},{8,9},{11,10},{12,13},{15,14},{16,17},{19,... | collective-permute-start | bytes 344072 | tf_op jit(solution)/shard_map/ppermute | solution.py:290
  64.7 28.9 %slice-start = ((s8[7340032]{0:T(1024)(128)(4,1)}), s8[4194304]{0:T(1024)(128)(4,1)S(1)}, s32[]{:S(2)}) async-start(s8[7340032]{0:T(1024)(128)(4,1)} %bitcast.37), calls=%async_computation | async-start | bytes 8388608
  64.7 28.8 %slice-start.1 = ((s8[7340032]{0:T(1024)(128)(4,1)}), s8[3145728]{0:T(1024)(128)(4,1)S(1)}, s32[]{:S(2)}) async-start(s8[7340032]{0:T(1024)(128)(4,1)} %bitcast.37), calls=%async_computation.1 | async-start | bytes 6291456
  78.0 3.9 %collective-permute-start.4 = (bf16[32,1792]{1,0:T(8,128)(2,1)S(1)}, bf16[32,1792]{1,0:T(8,128)(2,1)S(1)}, u32[]{:S(2)}, u32[]{:S(2)}) collective-permute-start(bf16[32,1792]{1,0:T(8,128)(2,1)S(1)} %get-tuple-element.23), channel_id=1, source_target_pairs={{0,1},{3,2},{4,5},{7,6},{8,9},{11,10},{12,13},{15,14},{16,17},{19,... | collective-permute-start | bytes 344072 | tf_op jit(solution)/shard_map/ppermute | solution.py:291
  81.9 1.5 collective-permute-start.7
  82.6 38.8 %collective-permute-start.30 = (bf16[96,2048]{1,0:T(8,128)(2,1)S(1)}, bf16[96,2048]{1,0:T(8,128)(2,1)S(1)}, u32[]{:S(2)}, u32[]{:S(2)}) collective-permute-start(bf16[96,2048]{1,0:T(8,128)(2,1)S(1)} %attend.7.rest_0_), channel_id=1, source_target_pairs={{0,8},{4,12},{8,0},{12,4},{1,9},{5,13},{9,1},{13,5},{2,10},{6,14},... | collective-permute-start | bytes 1179656 | tf_op jit(solution)/shard_map/ppermute | solution.py:267
  83.4 1.5 collective-permute-start.11
  83.4 13.7 %collective-permute-start.20 = (bf16[64,2048]{1,0:T(8,128)(2,1)S(1)}, bf16[64,2048]{1,0:T(8,128)(2,1)S(1)}, u32[]{:S(2)}, u32[]{:S(2)}) collective-permute-start(bf16[64,2048]{1,0:T(8,128)(2,1)S(1)} %collective-permute-done.18.rest_1_), channel_id=1, source_target_pairs={{0,4},{4,0},{8,12},{12,8},{1,5},{5,1},{9,13},{13,9},{2,6},{6,2},{1... | collective-permute-start | bytes 786440 | tf_op jit(solution)/shard_map/ppermute | solution.py:270
  83.9 48.5 %collective-permute-start.31 = (bf16[96,2048]{1,0:T(8,128)(2,1)S(1)}, bf16[96,2048]{1,0:T(8,128)(2,1)S(1)}, u32[]{:S(2)}, u32[]{:S(2)}) collective-permute-start(bf16[96,2048]{1,0:T(8,128)(2,1)S(1)} %attend.7.rest_0_), channel_id=1, source_target_pairs={{0,4},{4,0},{8,12},{12,8},{1,5},{5,1},{9,13},{13,9},{2,6},{6,2},{1... | collective-permute-start | bytes 1179656 | tf_op jit(solution)/shard_map/ppermute | solution.py:270
  84.9 16.5 %collective-permute-start.3 = (bf16[32,1792]{1,0:T(8,128)(2,1)S(1)}, bf16[32,1792]{1,0:T(8,128)(2,1)S(1)}, u32[]{:S(2)}, u32[]{:S(2)}) collective-permute-start(bf16[32,1792]{1,0:T(8,128)(2,1)S(1)} %get-tuple-element.22), channel_id=1, source_target_pairs={{0,1},{3,2},{4,5},{7,6},{8,9},{11,10},{12,13},{15,14},{16,17},{19,... | collective-permute-start | bytes 344072 | tf_op jit(solution)/shard_map/ppermute | solution.py:292
  96.4 9.6 %collective-permute-start.5 = (bf16[32,1792]{1,0:T(8,128)(2,1)S(1)}, bf16[32,1792]{1,0:T(8,128)(2,1)S(1)}, u32[]{:S(2)}, u32[]{:S(2)}) collective-permute-start(bf16[32,1792]{1,0:T(8,128)(2,1)S(1)} %add_convert_fusion.15), channel_id=1, source_target_pairs={{1,2},{2,1},{5,6},{6,5},{9,10},{10,9},{13,14},{14,13},{17,18},{18,... | collective-permute-start | bytes 344072 | tf_op jit(solution)/shard_map/ppermute | solution.py:294
  97.1 10.3 %collective-permute-start.8 = (bf16[32,1792]{1,0:T(8,128)(2,1)S(1)}, bf16[32,1792]{1,0:T(8,128)(2,1)S(1)}, u32[]{:S(2)}, u32[]{:S(2)}) collective-permute-start(bf16[32,1792]{1,0:T(8,128)(2,1)S(1)} %add_convert_fusion.13), channel_id=1, source_target_pairs={{1,0},{2,3},{5,4},{6,7},{9,8},{10,11},{13,12},{14,15},{17,16},{18,... | collective-permute-start | bytes 344072 | tf_op jit(solution)/shard_map/ppermute | solution.py:295
  101.4 10.6 %collective-permute-start.15 = (bf16[64,1792]{1,0:T(8,128)(2,1)S(1)}, bf16[64,1792]{1,0:T(8,128)(2,1)S(1)}, u32[]{:S(2)}, u32[]{:S(2)}) collective-permute-start(bf16[64,1792]{1,0:T(8,128)(2,1)S(1)} %get-tuple-element.28), channel_id=1, source_target_pairs={{0,1},{3,2},{4,5},{7,6},{8,9},{11,10},{12,13},{15,14},{16,17},{19,... | collective-permute-start | bytes 688136 | tf_op jit(solution)/shard_map/ppermute | solution.py:290
  106.0 10.9 %collective-permute-start.13 = (bf16[64,1792]{1,0:T(8,128)(2,1)S(1)}, bf16[64,1792]{1,0:T(8,128)(2,1)S(1)}, u32[]{:S(2)}, u32[]{:S(2)}) collective-permute-start(bf16[64,1792]{1,0:T(8,128)(2,1)S(1)} %get-tuple-element.27), channel_id=1, source_target_pairs={{0,1},{3,2},{4,5},{7,6},{8,9},{11,10},{12,13},{15,14},{16,17},{19,... | collective-permute-start | bytes 688136 | tf_op jit(solution)/shard_map/ppermute | solution.py:291
  107.3 32.4 %collective-permute-start.12 = (bf16[64,1792]{1,0:T(8,128)(2,1)S(1)}, bf16[64,1792]{1,0:T(8,128)(2,1)S(1)}, u32[]{:S(2)}, u32[]{:S(2)}) collective-permute-start(bf16[64,1792]{1,0:T(8,128)(2,1)S(1)} %get-tuple-element.26), channel_id=1, source_target_pairs={{0,1},{3,2},{4,5},{7,6},{8,9},{11,10},{12,13},{15,14},{16,17},{19,... | collective-permute-start | bytes 688136 | tf_op jit(solution)/shard_map/ppermute | solution.py:292
  112.0 14.7 %collective-permute-start.24 = (bf16[64,1792]{1,0:T(8,128)(2,1)S(1)}, bf16[64,1792]{1,0:T(8,128)(2,1)S(1)}, u32[]{:S(2)}, u32[]{:S(2)}) collective-permute-start(bf16[64,1792]{1,0:T(8,128)(2,1)S(1)} %get-tuple-element.32), channel_id=1, source_target_pairs={{0,1},{3,2},{4,5},{7,6},{8,9},{11,10},{12,13},{15,14},{16,17},{19,... | collective-permute-start | bytes 688136 | tf_op jit(solution)/shard_map/ppermute | solution.py:290
  117.0 14.7 %collective-permute-start.22 = (bf16[64,1792]{1,0:T(8,128)(2,1)S(1)}, bf16[64,1792]{1,0:T(8,128)(2,1)S(1)}, u32[]{:S(2)}, u32[]{:S(2)}) collective-permute-start(bf16[64,1792]{1,0:T(8,128)(2,1)S(1)} %get-tuple-element.31), channel_id=1, source_target_pairs={{0,1},{3,2},{4,5},{7,6},{8,9},{11,10},{12,13},{15,14},{16,17},{19,... | collective-permute-start | bytes 688136 | tf_op jit(solution)/shard_map/ppermute | solution.py:291
  121.4 51.6 %collective-permute-start.21 = (bf16[64,1792]{1,0:T(8,128)(2,1)S(1)}, bf16[64,1792]{1,0:T(8,128)(2,1)S(1)}, u32[]{:S(2)}, u32[]{:S(2)}) collective-permute-start(bf16[64,1792]{1,0:T(8,128)(2,1)S(1)} %get-tuple-element.30), channel_id=1, source_target_pairs={{0,1},{3,2},{4,5},{7,6},{8,9},{11,10},{12,13},{15,14},{16,17},{19,... | collective-permute-start | bytes 688136 | tf_op jit(solution)/shard_map/ppermute | solution.py:292
  126.8 6.3 %collective-permute-start.32 = (bf16[96,2048]{1,0:T(8,128)(2,1)S(1)}, bf16[96,2048]{1,0:T(8,128)(2,1)S(1)}, u32[]{:S(2)}, u32[]{:S(2)}) collective-permute-start(bf16[96,2048]{1,0:T(8,128)(2,1)S(1)} %collective-permute-done.30.rest_1_), channel_id=1, source_target_pairs={{0,4},{4,0},{8,12},{12,8},{1,5},{5,1},{9,13},{13,9},{2,6},{6,2},{1... | collective-permute-start | bytes 1179656 | tf_op jit(solution)/shard_map/ppermute | solution.py:270
  131.7 5.9 %collective-permute-start.16 = (bf16[64,1792]{1,0:T(8,128)(2,1)S(1)}, bf16[64,1792]{1,0:T(8,128)(2,1)S(1)}, u32[]{:S(2)}, u32[]{:S(2)}) collective-permute-start(bf16[64,1792]{1,0:T(8,128)(2,1)S(1)} %add_convert_fusion.10), channel_id=1, source_target_pairs={{1,2},{2,1},{5,6},{6,5},{9,10},{10,9},{13,14},{14,13},{17,18},{18,... | collective-permute-start | bytes 688136 | tf_op jit(solution)/shard_map/ppermute | solution.py:293
  132.4 24.5 %collective-permute-start.14 = (bf16[64,1792]{1,0:T(8,128)(2,1)S(1)}, bf16[64,1792]{1,0:T(8,128)(2,1)S(1)}, u32[]{:S(2)}, u32[]{:S(2)}) collective-permute-start(bf16[64,1792]{1,0:T(8,128)(2,1)S(1)} %add_convert_fusion.11), channel_id=1, source_target_pairs={{1,2},{2,1},{5,6},{6,5},{9,10},{10,9},{13,14},{14,13},{17,18},{18,... | collective-permute-start | bytes 688136 | tf_op jit(solution)/shard_map/ppermute | solution.py:294
  133.1 5.2 %collective-permute-start.25 = (bf16[64,1792]{1,0:T(8,128)(2,1)S(1)}, bf16[64,1792]{1,0:T(8,128)(2,1)S(1)}, u32[]{:S(2)}, u32[]{:S(2)}) collective-permute-start(bf16[64,1792]{1,0:T(8,128)(2,1)S(1)} %add_convert_fusion.6), channel_id=1, source_target_pairs={{1,2},{2,1},{5,6},{6,5},{9,10},{10,9},{13,14},{14,13},{17,18},{18,... | collective-permute-start | bytes 688136 | tf_op jit(solution)/shard_map/ppermute | solution.py:293
  137.6 36.7 %collective-permute-start.23 = (bf16[64,1792]{1,0:T(8,128)(2,1)S(1)}, bf16[64,1792]{1,0:T(8,128)(2,1)S(1)}, u32[]{:S(2)}, u32[]{:S(2)}) collective-permute-start(bf16[64,1792]{1,0:T(8,128)(2,1)S(1)} %add_convert_fusion.7), channel_id=1, source_target_pairs={{1,2},{2,1},{5,6},{6,5},{9,10},{10,9},{13,14},{14,13},{17,18},{18,... | collective-permute-start | bytes 688136 | tf_op jit(solution)/shard_map/ppermute | solution.py:294
  138.4 20.6 %collective-permute-start.17 = (bf16[64,1792]{1,0:T(8,128)(2,1)S(1)}, bf16[64,1792]{1,0:T(8,128)(2,1)S(1)}, u32[]{:S(2)}, u32[]{:S(2)}) collective-permute-start(bf16[64,1792]{1,0:T(8,128)(2,1)S(1)} %add_convert_fusion.9), channel_id=1, source_target_pairs={{1,0},{2,3},{5,4},{6,7},{9,8},{10,11},{13,12},{14,15},{17,16},{18,... | collective-permute-start | bytes 688136 | tf_op jit(solution)/shard_map/ppermute | solution.py:295
  139.7 31.7 %collective-permute-start.34 = (bf16[96,1792]{1,0:T(8,128)(2,1)S(1)}, bf16[96,1792]{1,0:T(8,128)(2,1)S(1)}, u32[]{:S(2)}, u32[]{:S(2)}) collective-permute-start(bf16[96,1792]{1,0:T(8,128)(2,1)S(1)} %get-tuple-element.35), channel_id=1, source_target_pairs={{0,1},{3,2},{4,5},{7,6},{8,9},{11,10},{12,13},{15,14},{16,17},{19,... | collective-permute-start | bytes 1032200 | tf_op jit(solution)/shard_map/ppermute | solution.py:291
  157.0 13.0 %collective-permute-start.36 = (bf16[96,1792]{1,0:T(8,128)(2,1)S(1)}, bf16[96,1792]{1,0:T(8,128)(2,1)S(1)}, u32[]{:S(2)}, u32[]{:S(2)}) collective-permute-start(bf16[96,1792]{1,0:T(8,128)(2,1)S(1)} %get-tuple-element.36), channel_id=1, source_target_pairs={{0,1},{3,2},{4,5},{7,6},{8,9},{11,10},{12,13},{15,14},{16,17},{19,... | collective-permute-start | bytes 1032200 | tf_op jit(solution)/shard_map/ppermute | solution.py:290
  158.9 20.8 %collective-permute-start.33 = (bf16[96,1792]{1,0:T(8,128)(2,1)S(1)}, bf16[96,1792]{1,0:T(8,128)(2,1)S(1)}, u32[]{:S(2)}, u32[]{:S(2)}) collective-permute-start(bf16[96,1792]{1,0:T(8,128)(2,1)S(1)} %get-tuple-element.34), channel_id=1, source_target_pairs={{0,1},{3,2},{4,5},{7,6},{8,9},{11,10},{12,13},{15,14},{16,17},{19,... | collective-permute-start | bytes 1032200 | tf_op jit(solution)/shard_map/ppermute | solution.py:292
  170.0 9.6 %collective-permute-start.26 = (bf16[64,1792]{1,0:T(8,128)(2,1)S(1)}, bf16[64,1792]{1,0:T(8,128)(2,1)S(1)}, u32[]{:S(2)}, u32[]{:S(2)}) collective-permute-start(bf16[64,1792]{1,0:T(8,128)(2,1)S(1)} %add_convert_fusion.5), channel_id=1, source_target_pairs={{1,0},{2,3},{5,4},{6,7},{9,8},{10,11},{13,12},{14,15},{17,16},{18,... | collective-permute-start | bytes 688136 | tf_op jit(solution)/shard_map/ppermute | solution.py:295
  171.4 0.8 collective-permute-start.37
  172.2 7.5 %collective-permute-start.35 = (bf16[96,1792]{1,0:T(8,128)(2,1)S(1)}, bf16[96,1792]{1,0:T(8,128)(2,1)S(1)}, u32[]{:S(2)}, u32[]{:S(2)}) collective-permute-start(bf16[96,1792]{1,0:T(8,128)(2,1)S(1)} %add_convert_fusion.3), channel_id=1, source_target_pairs={{1,2},{2,1},{5,6},{6,5},{9,10},{10,9},{13,14},{14,13},{17,18},{18,... | collective-permute-start | bytes 1032200 | tf_op jit(solution)/shard_map/ppermute | solution.py:294
  173.0 19.8 %collective-permute-start.38 = (bf16[96,1792]{1,0:T(8,128)(2,1)S(1)}, bf16[96,1792]{1,0:T(8,128)(2,1)S(1)}, u32[]{:S(2)}, u32[]{:S(2)}) collective-permute-start(bf16[96,1792]{1,0:T(8,128)(2,1)S(1)} %add_convert_fusion.1), channel_id=1, source_target_pairs={{1,0},{2,3},{5,4},{6,7},{9,8},{10,11},{13,12},{14,15},{17,16},{18,... | collective-permute-start | bytes 1032200 | tf_op jit(solution)/shard_map/ppermute | solution.py:295
  (3 other events, 3.6 us)

commit v3 on v0

v3 whole, which is shorter than its diff:
```python
import functools

import jax
import jax.numpy as jnp
import numpy as np
from jax import lax
from jax.experimental import pallas as pl
from jax.experimental.pallas import tpu as pltpu
from jax.sharding import PartitionSpec as P

HIDDEN = -1e30
LANES = 128
MIB = 1024 * 1024

SMEM = pl.BlockSpec(memory_space=pltpu.SMEM)
VMEM = pl.BlockSpec(memory_space=pltpu.VMEM)
HBM = pl.BlockSpec(memory_space=pltpu.HBM)
ANY = pl.BlockSpec(memory_space=pl.ANY)


def params(mib):
    return pltpu.CompilerParams(vmem_limit_bytes=mib * MIB)


def dot_nt(a, b):
    return lax.dot_general(a, b, (((1,), (1,)), ((), ())), preferred_element_type=jnp.float32)


def dot(a, b):
    return jnp.dot(a, b, preferred_element_type=jnp.float32)


def chunk_sizes(tok_group):
    if tok_group == 256:
        return (48, 64, 64, 80)
    return (tok_group,)


def rope_rows(rope_t):
    rows = jnp.transpose(rope_t.astype(jnp.float32), (1, 0))
    return jnp.concatenate(
        [rows, jnp.zeros((rows.shape[0], LANES - rows.shape[1]), jnp.float32)], axis=1
    ).astype(jnp.bfloat16)


def build_queries(q, q_nope, q_rope, wk, ready=None):
    heads, t, _ = q_nope.shape
    latent = wk.shape[2]
    rope_dim = q_rope.shape[1] // heads
    lane = lax.broadcasted_iota(jnp.int32, (t, LANES), 1)
    one = jnp.where(lane == rope_dim, 1.0, 0.0)
    per_tile = LANES // rope_dim
    for h in range(heads):
        pair = q_rope[:, h // per_tile * LANES:(h // per_tile + 1) * LANES].astype(jnp.float32)
        turn = h % per_tile * rope_dim
        if turn:
            pair = pltpu.roll(pair, LANES - turn, 1)
        q[h * t:(h + 1) * t, latent:] = jnp.where(lane < rope_dim, pair, one).astype(jnp.bfloat16)
    for h in range(heads):
        if ready is not None:
            ready(h)
        q[h * t:(h + 1) * t, :latent] = dot(q_nope[h], wk[h]).astype(jnp.bfloat16)


def prefill(q, keys, att, heads, t, first, prior, fresh, exp_scale):
    latent = att.shape[1]
    together = 1
    while together * 2 <= heads and together * 2 * t <= 384:
        together *= 2
    tile = together * t
    token = first + lax.broadcasted_iota(jnp.int32, (t, fresh), 0)
    key_token = lax.broadcasted_iota(jnp.int32, (t, fresh), 1)
    causal = (key_token <= token)[None]
    end = prior + fresh

    def scores_of(i):
        rows = q[i * tile:(i + 1) * tile, :]
        return dot_nt(rows, keys[:prior, :]), dot_nt(rows, keys[prior:end, :])

    steps = heads // together
    ahead = scores_of(0)
    for i in range(steps):
        s_old, s_new = ahead
        if i + 1 < steps:
            ahead = scores_of(i + 1)
        s_new = jnp.where(causal, s_new.reshape(together, t, fresh), HIDDEN).reshape(tile, fresh)
        top = jnp.maximum(jnp.max(s_old, axis=1, keepdims=True), jnp.max(s_new, axis=1, keepdims=True))
        p_old = jnp.exp2((s_old - top) * exp_scale)
        p_new = jnp.exp2((s_new - top) * exp_scale)
        total = jnp.sum(p_old, axis=1, keepdims=True) + jnp.sum(p_new, axis=1, keepdims=True)
        mixed = dot(p_old.astype(jnp.bfloat16), keys[:prior, :latent]) + dot(
            p_new.astype(jnp.bfloat16), keys[prior:end, :latent])
        att[i * tile:(i + 1) * tile, :] = (mixed / total).astype(jnp.bfloat16)


def head_outputs(out, att, wv, t):
    heads, _, dv = wv.shape
    for h in range(heads):
        out[:, h * dv:(h + 1) * dv] = dot(att[h * t:(h + 1) * t, :], wv[h]).astype(jnp.bfloat16)


def first_kernel(fresh, exp_scale, table, offset, q_nope, q_rope_hbm, wk_hbm, wv_hbm, cache_latent,
                 cache_rope, new_latent, new_rope_t, out, keys, wk, wv, q_rope, q, att, sems, wsems):
    heads, t, _ = q_nope.shape
    block_len, latent = cache_latent.shape[1:]
    rope_dim = new_rope_t.shape[0]
    blocks = table.shape[1]
    prior = blocks * block_len
    tok_group = new_latent.shape[0]

    rope_copy = pltpu.make_async_copy(q_rope_hbm.at[pl.ds(0, t)], q_rope, wsems.at[0])
    rope_copy.start()
    wk_copies = [pltpu.make_async_copy(wk_hbm.at[h], wk.at[h], wsems.at[1 + h]) for h in range(heads)]
    for c in wk_copies:
        c.start()
    copies = []
    for i in range(blocks):
        b = table[0, i]
        rows = pl.ds(i * block_len, block_len)
        copies.append(pltpu.make_async_copy(
            cache_latent.at[b], keys.at[rows, pl.ds(0, latent)], sems.at[2 * i]))
        copies.append(pltpu.make_async_copy(
            cache_rope.at[b], keys.at[rows, pl.ds(latent, LANES)], sems.at[2 * i + 1]))
    copies.append(pltpu.make_async_copy(
        new_latent, keys.at[pl.ds(prior, tok_group), pl.ds(0, latent)], sems.at[2 * blocks]))
    for c in copies:
        c.start()
    wv_copy = pltpu.make_async_copy(wv_hbm, wv, sems.at[2 * blocks + 1])
    wv_copy.start()

    keys[prior:, latent:] = rope_rows(new_rope_t[...])
    rope_copy.wait()
    build_queries(q, q_nope, q_rope, wk, lambda h: wk_copies[h].wait())

    for c in copies:
        c.wait()
    lane = lax.broadcasted_iota(jnp.int32, (prior, LANES), 1)
    pos = lax.broadcasted_iota(jnp.int32, (prior, LANES), 0)
    hide = jnp.where((lane == rope_dim) & (pos >= offset[0]), HIDDEN, 0.0)
    keys[:prior, latent:] = (keys[:prior, latent:].astype(jnp.float32) + hide).astype(jnp.bfloat16)
    prefill(q, keys, att, heads, t, 0, prior, fresh, exp_scale)
    wv_copy.wait()
    head_outputs(out, att, wv, t)


def later_kernel(first, fresh, prior, exp_scale, n_after, q_nope, q_rope, wk, wv, keys, *rest):
    out, q, att = rest[n_after:]
    heads, t, _ = q_nope.shape
    build_queries(q, q_nope, q_rope, wk)
    prefill(q, keys, att, heads, t, first, prior, fresh, exp_scale)
    head_outputs(out, att, wv, t)


def last_kernel(first, fresh, prior, prefill_len, exp_scale, n_after, q_nope, q_rope, wk, wv, keys,
                cache_latent, cache_rope, received, decode_table, decode_length, *rest):
    out, q, att, dkeys, sems = rest[n_after:]
    heads, t, _ = q_nope.shape
    pool, block_len, latent = cache_latent.shape
    got = received.shape[0]
    ext = pool * block_len + got
    tail = dkeys.shape[0] - ext
    start = keys.shape[0] - tail
    copies = []
    for i in range(pool):
        rows = pl.ds(i * block_len, block_len)
        copies.append(pltpu.make_async_copy(
            cache_latent.at[i], dkeys.at[rows, pl.ds(0, latent)], sems.at[2 * i]))
        copies.append(pltpu.make_async_copy(
            cache_rope.at[i], dkeys.at[rows, pl.ds(latent, LANES)], sems.at[2 * i + 1]))
    copies.append(pltpu.make_async_copy(
        received, dkeys.at[pl.ds(pool * block_len, got)], sems.at[2 * pool]))
    for c in copies:
        c.start()
    dkeys[ext:, :] = keys[start:, :]

    build_queries(q, q_nope, q_rope, wk)
    prefill(q, keys, att, heads, t, first, prior, fresh, exp_scale)

    decodes = decode_table.shape[0]
    for c in copies:
        c.wait()
    span = dkeys.shape[0]
    key = lax.broadcasted_iota(jnp.int32, (decodes, span), 1)
    request = lax.broadcasted_iota(jnp.int32, (decodes, span), 0)
    block = key // block_len
    pos = key % block_len
    own_key = key - ext + (start - prior) == request + prefill_len
    count = jnp.where(own_key, 1.0, 0.0)
    for m in range(decode_table.shape[1]):
        hit = (block == decode_table[:, m:m + 1]) & (
            pos + m * block_len < decode_length[:, 0:1]) & (key < ext)
        count = count + jnp.where(hit, 1.0, 0.0)
    count = count[None]
    at = prefill_len - first
    half = heads // 2 if heads % 2 == 0 else heads
    for lo in range(0, heads, half):
        rows = jnp.concatenate(
            [q[h * t + at:h * t + at + decodes, :] for h in range(lo, lo + half)], axis=0)
        s = dot_nt(rows, dkeys[...]).reshape(half, decodes, span)
        s = jnp.where(count > 0.0, s, HIDDEN)
        top = jnp.max(s, axis=2, keepdims=True)
        p = count * jnp.exp2((s - top) * exp_scale)
        total = jnp.sum(p, axis=2, keepdims=True).reshape(half * decodes, 1)
        p = p.reshape(half * decodes, span).astype(jnp.bfloat16)
        mixed = (dot(p, dkeys[:, :latent]) / total).astype(jnp.bfloat16)
        for h in range(lo, lo + half):
            att[h * t + at:h * t + at + decodes, :] = mixed[(h - lo) * decodes:(h - lo + 1) * decodes]
    head_outputs(out, att, wv, t)


COST = pl.CostEstimate(flops=1000, bytes_accessed=1000, transcendentals=0)
LONG = pl.CostEstimate(flops=40_000_000_000, bytes_accessed=1000, transcendentals=0)


def in_hbm(x):
    return pltpu.with_memory_space_constraint(x, pltpu.HBM)


def pack_kernel(ids, cache_latent, cache_rope, out, sems):
    latent = cache_latent.shape[2]
    _, groups, capacity = ids.shape
    copies = []
    for g in range(groups):
        for k in range(capacity):
            n = g * capacity + k
            b = ids[0, g, k]
            copies.append(pltpu.make_async_copy(
                cache_latent.at[b], out.at[n, :, pl.ds(0, latent)], sems.at[2 * n]))
            copies.append(pltpu.make_async_copy(
                cache_rope.at[b], out.at[n, :, pl.ds(latent, LANES)], sems.at[2 * n + 1]))
    for c in copies:
        c.start()
    for c in copies:
        c.wait()


def project_kernel(n_after, place, w, *rest):
    parts, (own, others, x) = rest[:-3 - n_after], rest[-3:]
    t = own.shape[0]
    i = 0
    for part in parts:
        for at in range(0, part.shape[0], t):
            x[pl.ds(pl.multiple_of(place[i] * t, t), t), :] = part[at:at + t, :]
            i += 1
    columns = w.shape[1]
    step = 256 if columns % 256 == 0 else columns
    for at in range(0, columns, step):
        y = dot(x[...], w[:, at:at + step]).astype(jnp.bfloat16)
        own[:, at:at + step] = y[:t]
        others[:, at:at + step] = y[t:]


def project(place, parts, w, t, after=()):
    depth, columns = w.shape
    rows = sum(p.shape[0] for p in parts)
    return pl.pallas_call(
        functools.partial(project_kernel, len(after)),
        out_shape=[jax.ShapeDtypeStruct((t, columns), jnp.bfloat16),
                   jax.ShapeDtypeStruct((rows - t, columns), jnp.bfloat16)],
        in_specs=[SMEM, VMEM] + [VMEM] * len(parts) + [ANY] * len(after),
        out_specs=[VMEM, VMEM],
        scratch_shapes=[pltpu.VMEM((rows, depth), jnp.bfloat16)],
        name="project",
        compiler_params=params(12),
        cost_estimate=COST,
    )(place, w, *parts, *after)


def add_kernel(spans, n_after, *refs):
    out = refs[-1]
    n = out.shape[0]
    total = None
    for ref, at in zip(refs, spans):
        x = ref[at:at + n, :].astype(jnp.float32)
        total = x if total is None else total + x
    out[...] = total.astype(jnp.bfloat16)


def add(rows, terms, after=()):
    return pl.pallas_call(
        functools.partial(add_kernel, [at for _, at in terms], len(after)),
        out_shape=jax.ShapeDtypeStruct((rows, terms[0][0].shape[1]), jnp.bfloat16),
        in_specs=[VMEM] * len(terms) + [ANY] * len(after),
        out_specs=VMEM,
        name="add",
        compiler_params=params(8),
        cost_estimate=COST,
    )(*[x for x, _ in terms], *after)


def gathered_ids(groups, me):
    if groups % 2:
        return [(me - s) % groups for s in range(groups)]
    return [(who - 2 * s) % groups for who in (me, me ^ 1) for s in range(groups // 2)]


def shift_groups(x):
    groups = lax.axis_size("dp")
    step = 1 if groups % 2 else 2
    return [x] + [lax.ppermute(x, "dp", [(i, (i + s) % groups) for i in range(groups)])
                  for s in range(step, groups, step)]


def stack_kernel(count, *refs):
    out, at = refs[-1], 0
    for ref in refs[:count]:
        out[at:at + ref.shape[0], :] = ref[...]
        at += ref.shape[0]


def stack(parts, after=()):
    rows = sum(p.shape[0] for p in parts)
    return pl.pallas_call(
        functools.partial(stack_kernel, len(parts)),
        out_shape=jax.ShapeDtypeStruct((rows, parts[0].shape[1]), parts[0].dtype),
        in_specs=[VMEM] * len(parts) + [ANY] * len(after),
        out_specs=VMEM,
        name="stack",
        compiler_params=params(4),
        cost_estimate=COST,
    )(*parts, *after)


def swap_cores(x):
    return lax.ppermute(x, "dp", [(i, i ^ 1) for i in range(lax.axis_size("dp"))])


LINE_ORDER = ((0, 3, 2, 1), (1, 3, 2, 0), (2, 0, 1, 3), (3, 0, 1, 2))
INWARD = [(0, 1), (3, 2)]
ACROSS = [(1, 2), (2, 1)]
OUTWARD = [(1, 0), (2, 3)]


def body(
    query_nope,
    query_rope,
    new_latent,
    new_rope,
    cache_latent,
    cache_rope,
    absorb_key,
    absorb_value,
    output_weight,
    send_blocks,
    prefill_table,
    prefill_offset,
    decode_table,
    decode_length,
):
    tok_group, heads, nope_dim = query_nope.shape
    pool, block_len, latent = cache_latent.shape
    rope_dim = new_rope.shape[1]
    capacity = send_blocks.shape[2]
    groups = lax.axis_size("dp")
    decodes = decode_length.shape[0]
    prefill_len = tok_group - decodes
    dv = absorb_value.shape[2]
    columns = output_weight.shape[1]
    exp_scale = float((nope_dim + rope_dim) ** (-0.5) * 1.4426950408889634)
    blocks = prefill_table.shape[1]
    prior = blocks * block_len
    width = latent + LANES
    on_line = lax.axis_size("tp") == 4 and groups == 4
    bf16 = jnp.bfloat16

    me = lax.axis_index("dp")
    ids = np.array([gathered_ids(groups, g) for g in range(groups)], np.int32)
    if on_line:
        places = np.argsort(np.array(LINE_ORDER), axis=1)[None, :, :]
        places = np.take_along_axis(
            np.broadcast_to(places, (4, 4, 4)), np.broadcast_to(ids[:, None, :], (4, 4, 4)), axis=2)
        place = jnp.asarray(places.astype(np.int32))[me, lax.axis_index("tp")]
    else:
        place = jnp.asarray(ids)[me]

    padded_rope = jnp.pad(
        cache_rope.reshape(pool, block_len, rope_dim), ((0, 0), (0, 0), (0, LANES - rope_dim)))
    sizes = chunk_sizes(tok_group)
    starts = [sum(sizes[:i]) for i in range(len(sizes))]

    def fresh_of(n):
        seen = min(starts[n] + sizes[n], prefill_len)
        return min(-(-seen // LANES) * LANES, tok_group)

    def scratch(t):
        return [pltpu.VMEM((heads * t, width), bf16), pltpu.VMEM((heads * t, latent), bf16)]

    def nope_of(n):
        return query_nope[starts[n]:starts[n] + sizes[n]].transpose(1, 0, 2)

    def first_chunk():
        t = sizes[0]
        return pl.pallas_call(
            functools.partial(first_kernel, fresh_of(0), exp_scale),
            out_shape=[jax.ShapeDtypeStruct((t, heads * dv), bf16),
                       jax.ShapeDtypeStruct((prior + tok_group, width), bf16)],
            in_specs=[SMEM, SMEM, VMEM, HBM, HBM, HBM, HBM, ANY, HBM, VMEM],
            out_specs=[VMEM, VMEM],
            scratch_shapes=[
                pltpu.VMEM(absorb_key.shape, bf16),
                pltpu.VMEM(absorb_value.shape, bf16),
                pltpu.VMEM((t, query_rope.shape[1]), bf16),
                *scratch(t),
                pltpu.SemaphoreType.DMA((2 * blocks + 2,)),
                pltpu.SemaphoreType.DMA((heads + 1,)),
            ],
            name="attend_first",
            compiler_params=params(20),
            cost_estimate=LONG,
        )(prefill_table, prefill_offset, nope_of(0), in_hbm(query_rope), in_hbm(absorb_key),
          in_hbm(absorb_value), in_hbm(cache_latent), padded_rope, in_hbm(new_latent), new_rope.T)

    def later_chunk(n, keys, after, decode=None):
        t = sizes[n]
        args = [nope_of(n), query_rope[starts[n]:starts[n] + t], absorb_key, absorb_value, keys]
        specs = [VMEM] * 5
        scratches = scratch(t)
        if decode is None:
            kernel = functools.partial(
                later_kernel, starts[n], fresh_of(n), prior, exp_scale, len(after))
            limit = 20
        else:
            kernel = functools.partial(
                last_kernel, starts[n], fresh_of(n), prior, prefill_len, exp_scale, len(after))
            args += [in_hbm(cache_latent), padded_rope, *decode]
            specs += [HBM, ANY, ANY, VMEM, VMEM]
            span = pool * block_len + decode[0].shape[0] + min(LANES, tok_group)
            scratches += [pltpu.VMEM((span, width), bf16), pltpu.SemaphoreType.DMA((2 * pool + 1,))]
            limit = 26
        return pl.pallas_call(
            kernel,
            out_shape=jax.ShapeDtypeStruct((t, heads * dv), bf16),
            in_specs=specs + [ANY] * len(after),
            out_specs=VMEM,
            scratch_shapes=scratches,
            name="attend",
            compiler_params=params(limit),
            cost_estimate=LONG,
        )(*args, *after)

    def pack():
        return pl.pallas_call(
            pack_kernel,
            out_shape=jax.ShapeDtypeStruct((groups * capacity, block_len, width), bf16),
            in_specs=[SMEM, HBM, ANY],
            out_specs=VMEM,
            scratch_shapes=[pltpu.SemaphoreType.DMA((2 * groups * capacity,))],
            name="pack",
            compiler_params=params(8),
            cost_estimate=COST,
        )(send_blocks, in_hbm(cache_latent), padded_rope)

    def migrate(packed):
        got = lax.all_to_all(packed, "dp", split_axis=0, concat_axis=0, tiled=True)
        return (got.reshape(groups * capacity * block_len, width), decode_table,
                decode_length[:, None])

    if len(sizes) != 4 or not on_line:
        outs = []
        keys = None
        for n, t in enumerate(sizes):
            if n == 0:
                x, keys = first_chunk()
            else:
                x = later_chunk(n, keys, (), migrate(pack()) if n == len(sizes) - 1 else None)
            mine = shift_groups(x)
            if groups % 2 == 0:
                mine += [swap_cores(y) for y in mine]
            own, others = project(place, mine, output_weight, t)
            partials = jnp.concatenate([own, others], axis=0).reshape(groups, t, columns)
            outs.append(lax.psum_scatter(partials, "tp", scatter_dimension=0, tiled=False))
        return jnp.concatenate(outs, axis=0)

    def inward(x):
        return lax.ppermute(x, "tp", INWARD)

    def across(x):
        return lax.ppermute(x, "tp", ACROSS)

    def outward(x):
        return lax.ppermute(x, "tp", OUTWARD)

    def gather(x, after):
        came = shift_groups(x)[1]
        return [x, came, swap_cores(x), swap_cores(stack([came], after))]

    t0, t1, t2, t3 = sizes
    x0, keys = first_chunk()
    decode = migrate(pack())
    x1 = later_chunk(1, keys, (decode[0],))
    own0, rest0 = project(place, gather(x0, (x1,)), output_weight, t0, (x1,))
    in0 = inward(rest0)
    x2 = later_chunk(2, keys, (own0,))
    own1, rest1 = project(place, gather(x1, (x2,)), output_weight, t1, (x2,))
    in1 = inward(rest1)
    to_across0 = add(2 * t0, [(rest0, 0), (in0, 0)], (own1,))
    on0 = across(to_across0)
    x3 = later_chunk(3, keys, (to_across0,), decode)
    own2, rest2 = project(place, gather(x2, (x3,)), output_weight, t2, (x3,))
    in2 = inward(rest2)
    to_across1 = add(2 * t1, [(rest1, 0), (in1, 0)], (own2,))
    on1 = across(to_across1)
    to_out0 = add(t0, [(rest0, 2 * t0), (on0, 0)], (own2,))
    out0 = outward(to_out0)
    own3, rest3 = project(place, gather(x3, (own2,)), output_weight, t3, (to_across1, to_out0))
    far3, mid3, near3 = (rest3[i * t3:(i + 1) * t3] for i in range(3))
    in3 = [inward(far3), inward(mid3), inward(near3)]
    to_across2 = add(2 * t2, [(rest2, 0), (in2, 0)], (own3,))
    on2 = across(to_across2)
    to_out1 = add(t1, [(rest1, 2 * t1), (on1, 0)], (to_across2,))
    out1 = outward(to_out1)
    to_far = add(t3, [(far3, 0), (in3[0], 0)], (to_out1,))
    far_on = across(to_far)
    to_out2 = add(t2, [(rest2, 2 * t2), (on2, 0)], (to_far,))
    out2 = outward(to_out2)
    to_mid = add(t3, [(mid3, 0), (in3[1], 0)], (to_out2,))
    mid_on = across(to_mid)
    out3 = outward(add(t3, [(near3, 0), (far_on, 0)], (to_mid,)))
    done = [
        add(t, [(own, 0), (came, 2 * t), (on, t), (out, 0)])
        for t, own, came, on, out in (
            (t0, own0, in0, on0, out0), (t1, own1, in1, on1, out1), (t2, own2, in2, on2, out2))
    ]
    done.append(add(t3, [(own3, 0), (in3[2], 0), (mid_on, 0), (out3, 0)]))
    return jnp.concatenate(done, axis=0)


def solution(mesh):
    return jax.shard_map(
        body,
        mesh=mesh,
        in_specs=(
            P(("replica", "dp"), "tp", None),
            P(("replica", "dp"), "tp"),
            P(("replica", "dp"), None),
            P(("replica", "dp"), None),
            P(("replica", "dp"), None, None),
            P(("replica", "dp"), None),
            P("tp", None, None),
            P("tp", None, None),
            P("tp", "dp"),
            P(("replica", "dp"), None, None),
            P(("replica", "dp"), None),
            P(("replica", "dp")),
            P(("replica", "dp"), None),
            P(("replica", "dp")),
        ),
        out_specs=P(("replica", "tp"), "dp"),
        check_vma=False,
    )
```

time: 255 us -> 138 us (0.54)
  waiting for transfers between devices: 111 us -> 29.9 us
  matrix products: 79.5 us -> 0 us
  Pallas kernels: 0 us -> 43.1 us
  starting transfers between devices: 7.77 us -> 44.8 us
  other arithmetic: 17.1 us -> 0.99 us
  between operations: 14.4 us -> 1.34 us
  local copies, waits for them, and re-layouts: 25 us -> 17.3 us
    reduce_scatter x1 -> x0, waiting for transfers between devices: 68.6 us -> none  [body(): lax.psum_scatter(partials.astype(jnp.bfloat16), 'tp', scatter_dimension=0...]
    pallas_call x0 -> x26, Pallas kernels: none -> 43.1 us  [the longest x3 19.7 us: later_chunk(): pl.pallas_call(kernel, out_shape=jax.ShapeDtypeStruct((t, heads * dv), bf...]
    dot_general x7 -> x0, matrix products: 43 us -> none  [the longest x1 13.2 us: body(): jnp.dot(lax.all_gather(head_out, 'dp', axis=0, tiled=True), output_weight...]
    ppermute x0 -> x27, starting transfers between devices: none -> 40.5 us  [the longest x6 25.8 us: inward(): return lax.ppermute(x, 'tp', INWARD)]
    sub x2 -> x0, matrix products: 36.5 us -> none  [normalized(): exp_terms = jnp.where(visible, jnp.exp(masked - row_top), 0.0)]
    all_gather x1 -> x0, waiting for transfers between devices: 36 us -> none  [body(): lax.all_gather(head_out, 'dp', axis=0, tiled=True)]
    ppermute x0 -> x27, waiting for transfers between devices: none -> 29.9 us  [the longest x4 19.3 us: outward(): return lax.ppermute(x, 'tp', OUTWARD)]
    gather x7 -> x0, local copies, waits for them, and re-layouts: 15.7 us -> none  [the longest x1 4.53 us: body(): ext_latent[decode_table].reshape(decodes, dec_span, latent_dim)]
  transfers between devices with their start and end apart: 4 -> 28, of which waited for: 3 -> 7; matrix products, arithmetic and copies ran while one was open for 34% -> 2% of each run, Pallas kernels for 0% -> 29%
where the time goes in v3:
time: 138 us; the launch traced here: 137 us
  starting transfers between devices  44.8 us (32%)
  Pallas kernels  43.1 us (31%)
  waiting for transfers between devices  29.9 us (22%)
  local copies, waits for them, and re-layouts  17.3 us (13%)
    ppermute x6, starting transfers between devices, inward(): return lax.ppermute(x, 'tp', INWARD)  25.8 us
    pallas_call x3, Pallas kernels, later_chunk(): pl.pallas_call(kernel, out_shape=jax.ShapeDtypeStruct((t, heads * dv), bf...  19.7 us
    ppermute x4, waiting for transfers between devices, outward(): return lax.ppermute(x, 'tp', OUTWARD)  19.3 us
    unnamed x52, local copies, waits for them, and re-layouts  13.2 us
    pallas_call x4, Pallas kernels, project(): pl.pallas_call(functools.partial(project_kernel, len(after)), out_shape=[...  11.3 us
    pallas_call x1, Pallas kernels, first_chunk(): pl.pallas_call(functools.partial(first_kernel, fresh_of(0), exp_scale), o...  7.58 us
    ppermute x6, waiting for transfers between devices, inward(): return lax.ppermute(x, 'tp', INWARD)  5.31 us
    ppermute x4, starting transfers between devices, outward(): return lax.ppermute(x, 'tp', OUTWARD)  5.17 us
  transfers between devices with their start and end apart: 28, of which 7 were waited for; matrix products, arithmetic and copies ran while one was open for 2% of the time, Pallas kernels for 29%

profile of v3, /device:TPU:0, one launch (start us, length us, event | category | flops | bytes accessed | tf_op | source)
XLA Modules:
  0.0 137.4 jit_solution(7388117867433109917)
XLA Ops:
  0.0 1.5 %reshape.6 = bf16[32,64,64]{2,1,0:T(8,128)(2,1)S(1)} reshape(bf16[32,4096]{1,0:T(8,128)(2,1)} %param.20) | data formatting | bytes 524288 | tf_op jit(solution)/shard_map/reshape | solution.py:377
  1.5 0.8 copy.18.ids
  2.2 0.1 pad.4.cache_rope
  2.4 2.6 %pack.1 = bf16[8,64,640]{2,1,0:T(8,128)(2,1)} custom-call(s32[1,4,2]{2,1,0:T(4,128)S(1)} %copy.18.ids, bf16[32,64,512]{2,1,0:T(8,128)(2,1)} %cache_latent.5, bf16[32,64,128]{2,1,0:T(8,128)(2,1)S(1)} %pad.4.cache_rope), custom_call_target="tpu_custom_call" | custom-call | flops 1000 | bytes 1000 | tf_op jit(solution)/shard_map/pack/pallas_call | solution.py:442
  5.0 4.2 %all-to-all-start = ((bf16[8,64,640]{2,1,0:T(8,128)(2,1)}), bf16[8,64,640]{2,1,0:T(8,128)(2,1)S(1)}, u32[]{:S(2)}, u32[]{:S(2)}) async-start(bf16[8,64,640]{2,1,0:T(8,128)(2,1)} %pack.1), calls=%async_computation | async-start | bytes 1310720 | tf_op jit(solution)/shard_map/all_to_all | solution.py:454
  10.0 7.6 %attend_first.1 = (bf16[48,2048]{1,0:T(8,128)(2,1)S(1)}, bf16[1280,640]{1,0:T(8,128)(2,1)S(1)}) custom-call(s32[1,16]{1,0:T(1,128)S(1)} %copy-done.12, s32[1]{0:T(128)S(6)} %copy.35.offset, bf16[16,48,128]{2,1,0:T(8,128)(2,1)S(1)} %bitcast.24, bf16[256,1024]{1,0:T(8,128)(2,1)} %q_rope_hbm.1, bf16[16,128,512]{2,1,0:T(8,128)(2,1)} %wk.5, ...), custom_call_target="tpu_custom_call" | custom-call | flops 40000000000 | bytes 1000 | tf_op jit(solution)/shard_map/attend_first/pallas_call | solution.py:393
  17.6 1.2 copy-done.13
  18.8 2.2 %collective-permute-start = (bf16[48,2048]{1,0:T(8,128)(2,1)S(1)}, bf16[48,2048]{1,0:T(8,128)(2,1)S(1)}, u32[]{:S(2)}, u32[]{:S(2)}) collective-permute-start(bf16[48,2048]{1,0:T(8,128)(2,1)S(1)} %get-tuple-element.15.rest_0_), channel_id=1, source_target_pairs={{0,8},{4,12},{8,0},{12,4},{1,9},{5,13},{9,1},{13,5},{2,10},{6,14},... | collective-permute-start | bytes 589832 | tf_op jit(solution)/shard_map/ppermute | solution.py:300
  21.2 0.7 fusion.2
  21.8 1.6 %copy-done.5 = bf16[16,128,512]{2,1,0:T(8,128)(2,1)S(1)} copy-done((bf16[16,128,512]{2,1,0:T(8,128)(2,1)S(1)}, bf16[16,128,512]{2,1,0:T(8,128)(2,1)}, u32[]{:S(2)}) %copy-start.5) | copy-done | bytes 2097176
  23.4 1.6 %copy-done.8 = bf16[16,512,128]{2,1,0:T(8,128)(2,1)S(1)} copy-done((bf16[16,512,128]{2,1,0:T(8,128)(2,1)S(1)}, bf16[16,512,128]{2,1,0:T(8,128)(2,1)}, u32[]{:S(2)}) %copy-start.8) | copy-done | bytes 2097176
  25.0 1.4 %copy-done.14 = bf16[1280,640]{1,0:T(8,128)(2,1)S(1)} copy-done((bf16[1280,640]{1,0:T(8,128)(2,1)S(1)}, bf16[1280,640]{1,0:T(8,128)(2,1)}, u32[]{:S(2)}) %copy-start.14) | copy-done | bytes 1638424
  26.5 4.3 %attend.3.refs_1_.rest_4_.rest_0_ = bf16[64,2048]{1,0:T(8,128)(2,1)S(1)} custom-call(bf16[16,64,128]{2,1,0:T(8,128)(2,1)S(1)} %bitcast.23, bf16[64,1024]{1,0:T(8,128)(2,1)S(1)} %get-tuple-element.31.q_rope, bf16[16,128,512]{2,1,0:T(8,128)(2,1)S(1)} %copy-done.5, bf16[16,512,128]{2,1,0:T(8,128)(2,1)S(1)} %copy-done.8, bf16[1280,640]{1,0:T(8,128)(2,1)S(1)} %copy-done.14, ...), custom_call_target="tpu_custom_call" | custom-call | flops 40000000000 | bytes 1000 | tf_op jit(solution)/shard_map/attend/pallas_call | solution.py:430
  30.8 0.6 collective-permute-start.2
  31.5 0.7 dynamic-slice_bitcast_fusion.place
  32.2 0.3 collective-permute-done.2.rest_3_
  32.5 3.1 %copy-done = bf16[2048,1792]{1,0:T(8,128)(2,1)S(1)} copy-done((bf16[2048,1792]{1,0:T(8,128)(2,1)S(1)}, bf16[2048,1792]{1,0:T(8,128)(2,1)}, u32[]{:S(2)}) %copy-start) | copy-done | bytes 7340056
  35.6 2.2 %project.4 = (bf16[48,1792]{1,0:T(8,128)(2,1)S(1)}, bf16[144,1792]{1,0:T(8,128)(2,1)S(1)}) custom-call(s32[4]{0:T(128)S(1)} %dynamic-slice_bitcast_fusion.place, bf16[2048,1792]{1,0:T(8,128)(2,1)S(1)} %copy-done, bf16[48,2048]{1,0:T(8,128)(2,1)S(1)} %get-tuple-element.15.rest_0_, bf16[48,2048]{1,0:T(8,128)(2,1)S(1)} %collective-permute-done.refs_0_.rest_1_, ...), custom_call_target="tpu_custom_call" | custom-call | flops 1000 | bytes 1000 | tf_op jit(solution)/shard_map/project/pallas_call | solution.py:256
  37.8 4.2 %collective-permute-start.3 = (bf16[144,1792]{1,0:T(8,128)(2,1)S(1)}, bf16[144,1792]{1,0:T(8,128)(2,1)S(1)}, u32[]{:S(2)}, u32[]{:S(2)}) collective-permute-start(bf16[144,1792]{1,0:T(8,128)(2,1)S(1)} %get-tuple-element.18.refs_0_), channel_id=1, source_target_pairs={{0,1},{3,2},{4,5},{7,6},{8,9},{11,10},{12,13},{15,14},{16,17},{19,... | collective-permute-start | bytes 1548296 | tf_op jit(solution)/shard_map/ppermute | solution.py:475
  42.0 4.8 %attend.4.refs_1_.rest_4_.rest_0_ = bf16[64,2048]{1,0:T(8,128)(2,1)S(1)} custom-call(bf16[16,64,128]{2,1,0:T(8,128)(2,1)S(1)} %bitcast.22, bf16[64,1024]{1,0:T(8,128)(2,1)S(1)} %copy-done.4, bf16[16,128,512]{2,1,0:T(8,128)(2,1)S(1)} %copy-done.6, bf16[16,512,128]{2,1,0:T(8,128)(2,1)S(1)} %copy-done.9, bf16[1280,640]{1,0:T(8,128)(2,1)S(1)} %copy-done.15, ...), custom_call_target="tpu_custom_call" | custom-call | flops 40000000000 | bytes 1000 | tf_op jit(solution)/shard_map/attend/pallas_call | solution.py:430
  46.9 0.7 stack.5
  47.6 0.1 collective-permute-start.6
  47.7 0.9 slice.36.q_rope
  48.6 0.1 copy.31
  48.7 0.1 copy.21.decode_table
  48.8 0.1 copy.22.decode_length
  48.9 1.9 %collective-permute-start.8 = (bf16[64,2048]{1,0:T(8,128)(2,1)S(1)}, bf16[64,2048]{1,0:T(8,128)(2,1)S(1)}, u32[]{:S(2)}, u32[]{:S(2)}) collective-permute-start(bf16[64,2048]{1,0:T(8,128)(2,1)S(1)} %attend.4.refs_1_.rest_4_.rest_0_), channel_id=1, source_target_pairs={{0,8},{4,12},{8,0},{12,4},{1,9},{5,13},{9,1},{13,5},{2,10},{6,14},... | collective-permute-start | bytes 786440 | tf_op jit(solution)/shard_map/ppermute | solution.py:300
  50.8 3.1 %copy-done.1 = bf16[2048,1792]{1,0:T(8,128)(2,1)S(1)} copy-done((bf16[2048,1792]{1,0:T(8,128)(2,1)S(1)}, bf16[2048,1792]{1,0:T(8,128)(2,1)}, u32[]{:S(2)}) %copy-start.1) | copy-done | bytes 7340056
  53.8 3.3 %project.5 = (bf16[64,1792]{1,0:T(8,128)(2,1)S(1)}, bf16[192,1792]{1,0:T(8,128)(2,1)S(1)}) custom-call(s32[4]{0:T(128)S(1)} %dynamic-slice_bitcast_fusion.place, bf16[2048,1792]{1,0:T(8,128)(2,1)S(1)} %copy-done.1, bf16[64,2048]{1,0:T(8,128)(2,1)S(1)} %attend.3.refs_1_.rest_4_.rest_0_, bf16[64,2048]{1,0:T(8,128)(2,1)S(1)} %collective-permute-done.4.refs_0_.rest_1_, ...), custom_call_target="tpu_custom_call" | custom-call | flops 1000 | bytes 1000 | tf_op jit(solution)/shard_map/project/pallas_call | solution.py:256
  57.2 1.8 %collective-permute-start.12 = (bf16[192,1792]{1,0:T(8,128)(2,1)S(1)}, bf16[192,1792]{1,0:T(8,128)(2,1)S(1)}, u32[]{:S(2)}, u32[]{:S(2)}) collective-permute-start(bf16[192,1792]{1,0:T(8,128)(2,1)S(1)} %get-tuple-element.21.refs_0_), channel_id=1, source_target_pairs={{0,1},{3,2},{4,5},{7,6},{8,9},{11,10},{12,13},{15,14},{16,17},{19,... | collective-permute-start | bytes 2064392 | tf_op jit(solution)/shard_map/ppermute | solution.py:475
  59.0 0.1 add.23.rest_0_
  59.1 10.6 %attend.5.refs_1_.rest_4_.rest_0_ = bf16[80,2048]{1,0:T(8,128)(2,1)S(1)} custom-call(bf16[16,80,128]{2,1,0:T(8,128)(2,1)S(1)} %bitcast.21, bf16[80,1024]{1,0:T(8,128)(2,1)S(1)} %slice.36.q_rope, bf16[16,128,512]{2,1,0:T(8,128)(2,1)S(1)} %copy-done.7, bf16[16,512,128]{2,1,0:T(8,128)(2,1)S(1)} %copy-done.10, bf16[1280,640]{1,0:T(8,128)(2,1)S(1)} %copy-done.16, ...), custom_call_target="tpu_custom_call" | custom-call | flops 40000000000 | bytes 1000 | tf_op jit(solution)/shard_map/attend/pallas_call | solution.py:430
  69.7 0.4 collective-permute-start.15
  70.1 0.6 collective-permute-start.10
  70.7 0.7 collective-permute-start.7
  71.3 0.3 collective-permute-done.9.rest_2_
  71.6 0.1 collective-permute-start.16
  71.7 0.2 collective-permute-done.10.rest_3_
  72.0 2.7 %project.6 = (bf16[64,1792]{1,0:T(8,128)(2,1)S(1)}, bf16[192,1792]{1,0:T(8,128)(2,1)S(1)}) custom-call(s32[4]{0:T(128)S(1)} %dynamic-slice_bitcast_fusion.place, bf16[2048,1792]{1,0:T(8,128)(2,1)S(1)} %bitcast.18, bf16[64,2048]{1,0:T(8,128)(2,1)S(1)} %attend.4.refs_1_.rest_4_.rest_0_, bf16[64,2048]{1,0:T(8,128)(2,1)S(1)} %collective-permute-done.8.refs_0_.rest_1_, ...), custom_call_target="tpu_custom_call" | custom-call | flops 1000 | bytes 1000 | tf_op jit(solution)/shard_map/project/pallas_call | solution.py:256
  74.6 4.5 %collective-permute-done.15.refs_0_.rest_1_ = bf16[80,2048]{1,0:T(8,128)(2,1)S(1)} collective-permute-done((bf16[80,2048]{1,0:T(8,128)(2,1)S(1)}, bf16[80,2048]{1,0:T(8,128)(2,1)S(1)}, u32[]{:S(2)}, u32[]{:S(2)}) %collective-permute-start.15) | collective-permute-done | bytes 327712 | tf_op jit(solution)/shard_map/ppermute | solution.py:300
  79.2 0.1 collective-permute-start.17
  79.2 1.3 collective-permute-start.14
  80.6 0.1 add.26.rest_4_
  80.8 1.0 collective-permute-start.13
  81.7 3.1 %project.7 = (bf16[80,1792]{1,0:T(8,128)(2,1)S(1)}, bf16[240,1792]{1,0:T(8,128)(2,1)S(1)}) custom-call(s32[4]{0:T(128)S(1)} %dynamic-slice_bitcast_fusion.place, bf16[2048,1792]{1,0:T(8,128)(2,1)S(1)} %bitcast.18, bf16[80,2048]{1,0:T(8,128)(2,1)S(1)} %attend.5.refs_1_.rest_4_.rest_0_, bf16[80,2048]{1,0:T(8,128)(2,1)S(1)} %collective-permute-done.15.refs_0_.rest_1_, ...), custom_call_target="tpu_custom_call" | custom-call | flops 1000 | bytes 1000 | tf_op jit(solution)/shard_map/project/pallas_call | solution.py:256
  85.0 6.1 %collective-permute-start.20 = (bf16[80,1792]{1,0:T(8,128)(2,1)S(1)}, bf16[80,1792]{1,0:T(8,128)(2,1)S(1)}, u32[]{:S(2)}, u32[]{:S(2)}) collective-permute-start(bf16[80,1792]{1,0:T(8,128)(2,1)S(1)} %get-tuple-element.27.refs_0_), channel_id=1, source_target_pairs={{0,1},{3,2},{4,5},{7,6},{8,9},{11,10},{12,13},{15,14},{16,17},{19,... | collective-permute-start | bytes 860168 | tf_op jit(solution)/shard_map/ppermute | solution.py:475
  91.0 5.3 %collective-permute-done.14.refs_1_ = bf16[192,1792]{1,0:T(8,128)(2,1)S(1)} collective-permute-done((bf16[192,1792]{1,0:T(8,128)(2,1)S(1)}, bf16[192,1792]{1,0:T(8,128)(2,1)S(1)}, u32[]{:S(2)}, u32[]{:S(2)}) %collective-permute-start.14) | collective-permute-done | bytes 688160 | tf_op jit(solution)/shard_map/ppermute | solution.py:475
  96.3 0.1 add.27.refs_2_
  96.4 0.7 collective-permute-start.19
  97.1 7.2 %collective-permute-start.23 = (bf16[80,1792]{1,0:T(8,128)(2,1)S(1)}, bf16[80,1792]{1,0:T(8,128)(2,1)S(1)}, u32[]{:S(2)}, u32[]{:S(2)}) collective-permute-start(bf16[80,1792]{1,0:T(8,128)(2,1)S(1)} %get-tuple-element.28.refs_0_), channel_id=1, source_target_pairs={{0,1},{3,2},{4,5},{7,6},{8,9},{11,10},{12,13},{15,14},{16,17},{19,... | collective-permute-start | bytes 860168 | tf_op jit(solution)/shard_map/ppermute | solution.py:475
  104.5 0.7 collective-permute-start.25
  105.2 1.3 collective-permute-start.11
  106.5 5.2 %collective-permute-start.22 = (bf16[80,1792]{1,0:T(8,128)(2,1)S(1)}, bf16[80,1792]{1,0:T(8,128)(2,1)S(1)}, u32[]{:S(2)}, u32[]{:S(2)}) collective-permute-start(bf16[80,1792]{1,0:T(8,128)(2,1)S(1)} %get-tuple-element.29.refs_0_), channel_id=1, source_target_pairs={{0,1},{3,2},{4,5},{7,6},{8,9},{11,10},{12,13},{15,14},{16,17},{19,... | collective-permute-start | bytes 860168 | tf_op jit(solution)/shard_map/ppermute | solution.py:475
  112.0 1.3 collective-permute-start.26
  113.3 0.7 collective-permute-start.24
  113.9 1.3 collective-permute-start.18
  115.3 1.3 collective-permute-start.21
  116.6 0.1 add.25
  116.7 16.1 %collective-permute-done.18.refs_3_ = bf16[64,1792]{1,0:T(8,128)(2,1)S(1)} collective-permute-done((bf16[64,1792]{1,0:T(8,128)(2,1)S(1)}, bf16[64,1792]{1,0:T(8,128)(2,1)S(1)}, u32[]{:S(2)}, u32[]{:S(2)}) %collective-permute-start.18) | collective-permute-done | bytes 229408 | tf_op jit(solution)/shard_map/ppermute | solution.py:481
  132.7 0.1 add.29
  132.8 3.2 %collective-permute-done.21.refs_3_ = bf16[64,1792]{1,0:T(8,128)(2,1)S(1)} collective-permute-done((bf16[64,1792]{1,0:T(8,128)(2,1)S(1)}, bf16[64,1792]{1,0:T(8,128)(2,1)S(1)}, u32[]{:S(2)}, u32[]{:S(2)}) %collective-permute-start.21) | collective-permute-done | bytes 229408 | tf_op jit(solution)/shard_map/ppermute | solution.py:481
  136.1 0.1 add.32
  136.2 0.1 add.35
  136.4 1.0 pad_maximum_fusion
  (84 shorter events, 0.9 us)
Async XLA Ops:
  2.4 6.9 %slice-start.2 = ((bf16[256,16,128]{2,1,0:T(8,128)(2,1)}), bf16[48,16,128]{2,1,0:T(8,128)(2,1)S(1)}, s32[]{:S(2)}) async-start(bf16[256,16,128]{2,1,0:T(8,128)(2,1)} %param.15), calls=%async_computation.3 | async-start | bytes 393216 | tf_op jit(solution)/shard_map/slice | solution.py:389
  5.0 5.0 %copy-start.11 = (bf16[256,64]{0,1:T(8,128)(2,1)S(1)}, bf16[256,64]{0,1:T(8,128)(2,1)}, u32[]{:S(2)}) copy-start(bf16[256,64]{0,1:T(8,128)(2,1)} %param.18) | copy-start | bytes 98308
  5.0 5.0 %copy-start.12 = (s32[1,16]{1,0:T(1,128)S(1)}, s32[1,16]{1,0:T(1,128)}, u32[]{:S(2)}) copy-start(s32[1,16]{1,0:T(1,128)} %table.1) | copy-start | bytes 196
  5.0 16.8 %all-to-all-start = ((bf16[8,64,640]{2,1,0:T(8,128)(2,1)}), bf16[8,64,640]{2,1,0:T(8,128)(2,1)S(1)}, u32[]{:S(2)}, u32[]{:S(2)}) async-start(bf16[8,64,640]{2,1,0:T(8,128)(2,1)} %pack.1), calls=%async_computation | async-start | bytes 1310720 | tf_op jit(solution)/shard_map/all_to_all | solution.py:454
  10.0 11.0 %copy-start.17 = (bf16[256,16,128]{2,1,0:T(8,128)(2,1)S(1)}, bf16[256,16,128]{2,1,0:T(8,128)(2,1)}, u32[]{:S(2)}) copy-start(bf16[256,16,128]{2,1,0:T(8,128)(2,1)} %param.15) | copy-start | bytes 3145732
  10.0 11.2 %copy-start.18 = (bf16[256,1024]{1,0:T(8,128)(2,1)S(1)}, bf16[256,1024]{1,0:T(8,128)(2,1)}, u32[]{:S(2)}) copy-start(bf16[256,1024]{1,0:T(8,128)(2,1)} %q_rope_hbm.1) | copy-start | bytes 1572868
  17.6 1.2 copy-start.13
  18.8 12.0 %collective-permute-start = (bf16[48,2048]{1,0:T(8,128)(2,1)S(1)}, bf16[48,2048]{1,0:T(8,128)(2,1)S(1)}, u32[]{:S(2)}, u32[]{:S(2)}) collective-permute-start(bf16[48,2048]{1,0:T(8,128)(2,1)S(1)} %get-tuple-element.15.rest_0_), channel_id=1, source_target_pairs={{0,8},{4,12},{8,0},{12,4},{1,9},{5,13},{9,1},{13,5},{2,10},{6,14},... | collective-permute-start | bytes 589832 | tf_op jit(solution)/shard_map/ppermute | solution.py:300
  21.0 11.2 %collective-permute-start.1 = (bf16[48,2048]{1,0:T(8,128)(2,1)S(1)}, bf16[48,2048]{1,0:T(8,128)(2,1)S(1)}, u32[]{:S(2)}, u32[]{:S(2)}) collective-permute-start(bf16[48,2048]{1,0:T(8,128)(2,1)S(1)} %get-tuple-element.15.rest_0_), channel_id=1, source_target_pairs={{0,4},{4,0},{8,12},{12,8},{1,5},{5,1},{9,13},{13,9},{2,6},{6,2},{1... | collective-permute-start | bytes 589832 | tf_op jit(solution)/shard_map/ppermute | solution.py:325
  21.8 1.6 %copy-start.5 = (bf16[16,128,512]{2,1,0:T(8,128)(2,1)S(1)}, bf16[16,128,512]{2,1,0:T(8,128)(2,1)}, u32[]{:S(2)}) copy-start(bf16[16,128,512]{2,1,0:T(8,128)(2,1)} %wk.5) | copy-start | bytes 6291460
  23.4 1.6 %copy-start.8 = (bf16[16,512,128]{2,1,0:T(8,128)(2,1)S(1)}, bf16[16,512,128]{2,1,0:T(8,128)(2,1)}, u32[]{:S(2)}) copy-start(bf16[16,512,128]{2,1,0:T(8,128)(2,1)} %wv.5) | copy-start | bytes 6291460
  25.0 1.4 %copy-start.14 = (bf16[1280,640]{1,0:T(8,128)(2,1)S(1)}, bf16[1280,640]{1,0:T(8,128)(2,1)}, u32[]{:S(2)}) copy-start(bf16[1280,640]{1,0:T(8,128)(2,1)} %copy-done.13) | copy-start | bytes 4915204
  30.8 1.7 %collective-permute-start.2 = (bf16[48,2048]{1,0:T(8,128)(2,1)S(1)}, bf16[48,2048]{1,0:T(8,128)(2,1)S(1)}, u32[]{:S(2)}, u32[]{:S(2)}) collective-permute-start(bf16[48,2048]{1,0:T(8,128)(2,1)S(1)} %stack.4), channel_id=1, source_target_pairs={{0,4},{4,0},{8,12},{12,8},{1,5},{5,1},{9,13},{13,9},{2,6},{6,2},{1... | collective-permute-start | bytes 589832 | tf_op jit(solution)/shard_map/ppermute | solution.py:325
  32.2 14.7 %collective-permute-start.4 = (bf16[64,2048]{1,0:T(8,128)(2,1)S(1)}, bf16[64,2048]{1,0:T(8,128)(2,1)S(1)}, u32[]{:S(2)}, u32[]{:S(2)}) collective-permute-start(bf16[64,2048]{1,0:T(8,128)(2,1)S(1)} %attend.3.refs_1_.rest_4_.rest_0_), channel_id=1, source_target_pairs={{0,8},{4,12},{8,0},{12,4},{1,9},{5,13},{9,1},{13,5},{2,10},{6,14},... | collective-permute-start | bytes 786440 | tf_op jit(solution)/shard_map/ppermute | solution.py:300
  32.2 18.6 %collective-permute-start.5 = (bf16[64,2048]{1,0:T(8,128)(2,1)S(1)}, bf16[64,2048]{1,0:T(8,128)(2,1)}, u32[]{:S(2)}, u32[]{:S(2)}) collective-permute-start(bf16[64,2048]{1,0:T(8,128)(2,1)S(1)} %attend.3.refs_1_.rest_4_.rest_0_), channel_id=1, source_target_pairs={{0,4},{4,0},{8,12},{12,8},{1,5},{5,1},{9,13},{13,9},{2,6},{6,2},{1... | collective-permute-start | bytes 786440 | tf_op jit(solution)/shard_map/ppermute | solution.py:325
  32.5 3.1 %copy-start = (bf16[2048,1792]{1,0:T(8,128)(2,1)S(1)}, bf16[2048,1792]{1,0:T(8,128)(2,1)}, u32[]{:S(2)}) copy-start(bf16[2048,1792]{1,0:T(8,128)(2,1)} %w.7) | copy-start | bytes 22020100
  35.6 6.4 %copy-start.4 = (bf16[64,1024]{1,0:T(8,128)(2,1)S(1)}, bf16[64,1024]{1,0:T(8,128)(2,1)}, u32[]{:S(2)}) copy-start(bf16[64,1024]{1,0:T(8,128)(2,1)} %get-tuple-element.30.q_rope) | copy-start | bytes 393220
  35.6 6.4 %copy-start.6 = (bf16[16,128,512]{2,1,0:T(8,128)(2,1)S(1)}, bf16[16,128,512]{2,1,0:T(8,128)(2,1)}, u32[]{:S(2)}) copy-start(bf16[16,128,512]{2,1,0:T(8,128)(2,1)} %wk.5) | copy-start | bytes 6291460
  35.6 6.4 %copy-start.9 = (bf16[16,512,128]{2,1,0:T(8,128)(2,1)S(1)}, bf16[16,512,128]{2,1,0:T(8,128)(2,1)}, u32[]{:S(2)}) copy-start(bf16[16,512,128]{2,1,0:T(8,128)(2,1)} %wv.5) | copy-start | bytes 6291460
  35.6 6.4 %copy-start.15 = (bf16[1280,640]{1,0:T(8,128)(2,1)S(1)}, bf16[1280,640]{1,0:T(8,128)(2,1)}, u32[]{:S(2)}) copy-start(bf16[1280,640]{1,0:T(8,128)(2,1)} %copy-done.13) | copy-start | bytes 4915204
  37.8 9.0 %copy-start.2 = (bf16[48,1792]{1,0:T(8,128)(2,1)}, bf16[48,1792]{1,0:T(8,128)(2,1)S(1)}, u32[]{:S(2)}) copy-start(bf16[48,1792]{1,0:T(8,128)(2,1)S(1)} %get-tuple-element.17.rest_0_.refs_0_) | copy-start | bytes 516100
  37.8 21.2 %collective-permute-start.3 = (bf16[144,1792]{1,0:T(8,128)(2,1)S(1)}, bf16[144,1792]{1,0:T(8,128)(2,1)S(1)}, u32[]{:S(2)}, u32[]{:S(2)}) collective-permute-start(bf16[144,1792]{1,0:T(8,128)(2,1)S(1)} %get-tuple-element.18.refs_0_), channel_id=1, source_target_pairs={{0,1},{3,2},{4,5},{7,6},{8,9},{11,10},{12,13},{15,14},{16,17},{19,... | collective-permute-start | bytes 1548296 | tf_op jit(solution)/shard_map/ppermute | solution.py:475
  46.8 1.8 %slice-start.3 = ((bf16[256,16,128]{2,1,0:T(8,128)(2,1)}), bf16[80,16,128]{2,1,0:T(8,128)(2,1)S(1)}, s32[]{:S(2)}) async-start(bf16[256,16,128]{2,1,0:T(8,128)(2,1)} %param.15), calls=%async_computation.4 | async-start | bytes 655360 | tf_op jit(solution)/shard_map/slice | solution.py:389
  46.8 1.9 %copy-start.19 = (s32[16,4]{0,1:T(4,128)S(1)}, s32[16,4]{0,1:T(4,128)}, u32[]{:S(2)}) copy-start(s32[16,4]{0,1:T(4,128)} %param.27) | copy-start | bytes 772
  46.8 2.0 %copy-start.20 = (s32[16]{0:T(128)S(1)}, s32[16]{0:T(128)}, u32[]{:S(2)}) copy-start(s32[16]{0:T(128)} %param.28) | copy-start | bytes 196
  47.6 3.2 %collective-permute-start.6 = (bf16[64,2048]{1,0:T(8,128)(2,1)}, bf16[64,2048]{1,0:T(8,128)(2,1)}, u32[]{:S(2)}, u32[]{:S(2)}) collective-permute-start(bf16[64,2048]{1,0:T(8,128)(2,1)} %stack.5), channel_id=1, source_target_pairs={{0,4},{4,0},{8,12},{12,8},{1,5},{5,1},{9,13},{13,9},{2,6},{6,2},{1... | collective-permute-start | bytes 786440 | tf_op jit(solution)/shard_map/ppermute | solution.py:325
  48.9 21.2 %collective-permute-start.8 = (bf16[64,2048]{1,0:T(8,128)(2,1)S(1)}, bf16[64,2048]{1,0:T(8,128)(2,1)S(1)}, u32[]{:S(2)}, u32[]{:S(2)}) collective-permute-start(bf16[64,2048]{1,0:T(8,128)(2,1)S(1)} %attend.4.refs_1_.rest_4_.rest_0_), channel_id=1, source_target_pairs={{0,8},{4,12},{8,0},{12,4},{1,9},{5,13},{9,1},{13,5},{2,10},{6,14},... | collective-permute-start | bytes 786440 | tf_op jit(solution)/shard_map/ppermute | solution.py:300
  50.7 3.1 %copy-start.1 = (bf16[2048,1792]{1,0:T(8,128)(2,1)S(1)}, bf16[2048,1792]{1,0:T(8,128)(2,1)}, u32[]{:S(2)}) copy-start(bf16[2048,1792]{1,0:T(8,128)(2,1)} %w.7) | copy-start | bytes 22020100
  53.8 5.3 %copy-start.7 = (bf16[16,128,512]{2,1,0:T(8,128)(2,1)S(1)}, bf16[16,128,512]{2,1,0:T(8,128)(2,1)}, u32[]{:S(2)}) copy-start(bf16[16,128,512]{2,1,0:T(8,128)(2,1)} %wk.5) | copy-start | bytes 6291460
  53.8 5.3 %copy-start.10 = (bf16[16,512,128]{2,1,0:T(8,128)(2,1)S(1)}, bf16[16,512,128]{2,1,0:T(8,128)(2,1)}, u32[]{:S(2)}) copy-start(bf16[16,512,128]{2,1,0:T(8,128)(2,1)} %wv.5) | copy-start | bytes 6291460
  53.8 5.3 %copy-start.16 = (bf16[1280,640]{1,0:T(8,128)(2,1)S(1)}, bf16[1280,640]{1,0:T(8,128)(2,1)}, u32[]{:S(2)}) copy-start(bf16[1280,640]{1,0:T(8,128)(2,1)} %copy-done.13) | copy-start | bytes 4915204
  57.2 23.5 %collective-permute-start.12 = (bf16[192,1792]{1,0:T(8,128)(2,1)S(1)}, bf16[192,1792]{1,0:T(8,128)(2,1)S(1)}, u32[]{:S(2)}, u32[]{:S(2)}) collective-permute-start(bf16[192,1792]{1,0:T(8,128)(2,1)S(1)} %get-tuple-element.21.refs_0_), channel_id=1, source_target_pairs={{0,1},{3,2},{4,5},{7,6},{8,9},{11,10},{12,13},{15,14},{16,17},{19,... | collective-permute-start | bytes 2064392 | tf_op jit(solution)/shard_map/ppermute | solution.py:475
  59.1 12.9 %slice-start = ((s8[7340032]{0:T(1024)(128)(4,1)}), s8[4194304]{0:T(1024)(128)(4,1)S(1)}, s32[]{:S(2)}) async-start(s8[7340032]{0:T(1024)(128)(4,1)} %bitcast.17), calls=%async_computation.1 | async-start | bytes 8388608
  59.1 12.9 %slice-start.1 = ((s8[7340032]{0:T(1024)(128)(4,1)}), s8[3145728]{0:T(1024)(128)(4,1)S(1)}, s32[]{:S(2)}) async-start(s8[7340032]{0:T(1024)(128)(4,1)} %bitcast.17), calls=%async_computation.2 | async-start | bytes 6291456
  69.7 9.4 %collective-permute-start.15 = (bf16[80,2048]{1,0:T(8,128)(2,1)S(1)}, bf16[80,2048]{1,0:T(8,128)(2,1)S(1)}, u32[]{:S(2)}, u32[]{:S(2)}) collective-permute-start(bf16[80,2048]{1,0:T(8,128)(2,1)S(1)} %attend.5.refs_1_.rest_4_.rest_0_), channel_id=1, source_target_pairs={{0,8},{4,12},{8,0},{12,4},{1,9},{5,13},{9,1},{13,5},{2,10},{6,14},... | collective-permute-start | bytes 983048 | tf_op jit(solution)/shard_map/ppermute | solution.py:300
  70.1 1.5 %collective-permute-start.9 = (bf16[64,2048]{1,0:T(8,128)(2,1)S(1)}, bf16[64,2048]{1,0:T(8,128)(2,1)S(1)}, u32[]{:S(2)}, u32[]{:S(2)}) collective-permute-start(bf16[64,2048]{1,0:T(8,128)(2,1)S(1)} %attend.4.refs_1_.rest_4_.rest_0_), channel_id=1, source_target_pairs={{0,4},{4,0},{8,12},{12,8},{1,5},{5,1},{9,13},{13,9},{2,6},{6,2},{1... | collective-permute-start | bytes 786440 | tf_op jit(solution)/shard_map/ppermute | solution.py:325
  70.1 1.9 %collective-permute-start.10 = (bf16[64,2048]{1,0:T(8,128)(2,1)S(1)}, bf16[64,2048]{1,0:T(8,128)(2,1)S(1)}, u32[]{:S(2)}, u32[]{:S(2)}) collective-permute-start(bf16[64,2048]{1,0:T(8,128)(2,1)S(1)} %stack.6), channel_id=1, source_target_pairs={{0,4},{4,0},{8,12},{12,8},{1,5},{5,1},{9,13},{13,9},{2,6},{6,2},{1... | collective-permute-start | bytes 786440 | tf_op jit(solution)/shard_map/ppermute | solution.py:325
  70.7 9.9 %collective-permute-start.7 = (bf16[96,1792]{1,0:T(8,128)(2,1)S(1)}, bf16[96,1792]{1,0:T(8,128)(2,1)S(1)}, u32[]{:S(2)}, u32[]{:S(2)}) collective-permute-start(bf16[96,1792]{1,0:T(8,128)(2,1)S(1)} %add.23.rest_0_), channel_id=1, source_target_pairs={{1,2},{2,1},{5,6},{6,5},{9,10},{10,9},{13,14},{14,13},{17,18},{18,... | collective-permute-start | bytes 1032200 | tf_op jit(solution)/shard_map/ppermute | solution.py:478
  71.6 10.1 %collective-permute-start.16 = (bf16[80,2048]{1,0:T(8,128)(2,1)S(1)}, bf16[80,2048]{1,0:T(8,128)(2,1)S(1)}, u32[]{:S(2)}, u32[]{:S(2)}) collective-permute-start(bf16[80,2048]{1,0:T(8,128)(2,1)S(1)} %attend.5.refs_1_.rest_4_.rest_0_), channel_id=1, source_target_pairs={{0,4},{4,0},{8,12},{12,8},{1,5},{5,1},{9,13},{13,9},{2,6},{6,2},{1... | collective-permute-start | bytes 983048 | tf_op jit(solution)/shard_map/ppermute | solution.py:325
  79.2 2.6 %collective-permute-start.17 = (bf16[80,2048]{1,0:T(8,128)(2,1)S(1)}, bf16[80,2048]{1,0:T(8,128)(2,1)S(1)}, u32[]{:S(2)}, u32[]{:S(2)}) collective-permute-start(bf16[80,2048]{1,0:T(8,128)(2,1)S(1)} %stack.7), channel_id=1, source_target_pairs={{0,4},{4,0},{8,12},{12,8},{1,5},{5,1},{9,13},{13,9},{2,6},{6,2},{1... | collective-permute-start | bytes 983048 | tf_op jit(solution)/shard_map/ppermute | solution.py:325
  79.2 17.1 %collective-permute-start.14 = (bf16[192,1792]{1,0:T(8,128)(2,1)S(1)}, bf16[192,1792]{1,0:T(8,128)(2,1)S(1)}, u32[]{:S(2)}, u32[]{:S(2)}) collective-permute-start(bf16[192,1792]{1,0:T(8,128)(2,1)S(1)} %get-tuple-element.22.refs_0_), channel_id=1, source_target_pairs={{0,1},{3,2},{4,5},{7,6},{8,9},{11,10},{12,13},{15,14},{16,17},{19,... | collective-permute-start | bytes 2064392 | tf_op jit(solution)/shard_map/ppermute | solution.py:475
  80.8 23.6 %collective-permute-start.13 = (bf16[128,1792]{1,0:T(8,128)(2,1)S(1)}, bf16[128,1792]{1,0:T(8,128)(2,1)S(1)}, u32[]{:S(2)}, u32[]{:S(2)}) collective-permute-start(bf16[128,1792]{1,0:T(8,128)(2,1)S(1)} %add.26.rest_4_), channel_id=1, source_target_pairs={{1,2},{2,1},{5,6},{6,5},{9,10},{10,9},{13,14},{14,13},{17,18},{18,... | collective-permute-start | bytes 1376264 | tf_op jit(solution)/shard_map/ppermute | solution.py:478
  85.0 19.5 %collective-permute-start.20 = (bf16[80,1792]{1,0:T(8,128)(2,1)S(1)}, bf16[80,1792]{1,0:T(8,128)(2,1)S(1)}, u32[]{:S(2)}, u32[]{:S(2)}) collective-permute-start(bf16[80,1792]{1,0:T(8,128)(2,1)S(1)} %get-tuple-element.27.refs_0_), channel_id=1, source_target_pairs={{0,1},{3,2},{4,5},{7,6},{8,9},{11,10},{12,13},{15,14},{16,17},{19,... | collective-permute-start | bytes 860168 | tf_op jit(solution)/shard_map/ppermute | solution.py:475
  96.4 15.3 %collective-permute-start.19 = (bf16[128,1792]{1,0:T(8,128)(2,1)S(1)}, bf16[128,1792]{1,0:T(8,128)(2,1)S(1)}, u32[]{:S(2)}, u32[]{:S(2)}) collective-permute-start(bf16[128,1792]{1,0:T(8,128)(2,1)S(1)} %add.27.refs_2_), channel_id=1, source_target_pairs={{1,2},{2,1},{5,6},{6,5},{9,10},{10,9},{13,14},{14,13},{17,18},{18,... | collective-permute-start | bytes 1376264 | tf_op jit(solution)/shard_map/ppermute | solution.py:478
  97.1 14.6 %collective-permute-start.23 = (bf16[80,1792]{1,0:T(8,128)(2,1)S(1)}, bf16[80,1792]{1,0:T(8,128)(2,1)S(1)}, u32[]{:S(2)}, u32[]{:S(2)}) collective-permute-start(bf16[80,1792]{1,0:T(8,128)(2,1)S(1)} %get-tuple-element.28.refs_0_), channel_id=1, source_target_pairs={{0,1},{3,2},{4,5},{7,6},{8,9},{11,10},{12,13},{15,14},{16,17},{19,... | collective-permute-start | bytes 860168 | tf_op jit(solution)/shard_map/ppermute | solution.py:475
  104.5 7.4 %collective-permute-start.25 = (bf16[80,1792]{1,0:T(8,128)(2,1)S(1)}, bf16[80,1792]{1,0:T(8,128)(2,1)S(1)}, u32[]{:S(2)}, u32[]{:S(2)}) collective-permute-start(bf16[80,1792]{1,0:T(8,128)(2,1)S(1)} %add.30.refs_2_), channel_id=1, source_target_pairs={{1,2},{2,1},{5,6},{6,5},{9,10},{10,9},{13,14},{14,13},{17,18},{18,... | collective-permute-start | bytes 860168 | tf_op jit(solution)/shard_map/ppermute | solution.py:478
  105.2 10.0 %collective-permute-start.11 = (bf16[48,1792]{1,0:T(8,128)(2,1)S(1)}, bf16[48,1792]{1,0:T(8,128)(2,1)S(1)}, u32[]{:S(2)}, u32[]{:S(2)}) collective-permute-start(bf16[48,1792]{1,0:T(8,128)(2,1)S(1)} %add.24.rest_5_), channel_id=1, source_target_pairs={{1,0},{2,3},{5,4},{6,7},{9,8},{10,11},{13,12},{14,15},{17,16},{18,... | collective-permute-start | bytes 516104 | tf_op jit(solution)/shard_map/ppermute | solution.py:481
  106.5 10.1 %copy-start.3 = (bf16[48,1792]{1,0:T(8,128)(2,1)S(1)}, bf16[48,1792]{1,0:T(8,128)(2,1)}, u32[]{:S(2)}) copy-start(bf16[48,1792]{1,0:T(8,128)(2,1)} %copy-done.2) | copy-start | bytes 516100
  106.5 29.7 %collective-permute-start.22 = (bf16[80,1792]{1,0:T(8,128)(2,1)S(1)}, bf16[80,1792]{1,0:T(8,128)(2,1)S(1)}, u32[]{:S(2)}, u32[]{:S(2)}) collective-permute-start(bf16[80,1792]{1,0:T(8,128)(2,1)S(1)} %get-tuple-element.29.refs_0_), channel_id=1, source_target_pairs={{0,1},{3,2},{4,5},{7,6},{8,9},{11,10},{12,13},{15,14},{16,17},{19,... | collective-permute-start | bytes 860168 | tf_op jit(solution)/shard_map/ppermute | solution.py:475
  112.0 24.3 %collective-permute-start.26 = (bf16[80,1792]{1,0:T(8,128)(2,1)S(1)}, bf16[80,1792]{1,0:T(8,128)(2,1)S(1)}, u32[]{:S(2)}, u32[]{:S(2)}) collective-permute-start(bf16[80,1792]{1,0:T(8,128)(2,1)S(1)} %add.34), channel_id=1, source_target_pairs={{1,0},{2,3},{5,4},{6,7},{9,8},{10,11},{13,12},{14,15},{17,16},{18,... | collective-permute-start | bytes 860168 | tf_op jit(solution)/shard_map/ppermute | solution.py:481
  113.3 23.0 %collective-permute-start.24 = (bf16[80,1792]{1,0:T(8,128)(2,1)S(1)}, bf16[80,1792]{1,0:T(8,128)(2,1)S(1)}, u32[]{:S(2)}, u32[]{:S(2)}) collective-permute-start(bf16[80,1792]{1,0:T(8,128)(2,1)S(1)} %add.33.refs_2_), channel_id=1, source_target_pairs={{1,2},{2,1},{5,6},{6,5},{9,10},{10,9},{13,14},{14,13},{17,18},{18,... | collective-permute-start | bytes 860168 | tf_op jit(solution)/shard_map/ppermute | solution.py:478
  113.9 18.8 %collective-permute-start.18 = (bf16[64,1792]{1,0:T(8,128)(2,1)S(1)}, bf16[64,1792]{1,0:T(8,128)(2,1)S(1)}, u32[]{:S(2)}, u32[]{:S(2)}) collective-permute-start(bf16[64,1792]{1,0:T(8,128)(2,1)S(1)} %add.28.refs_2_), channel_id=1, source_target_pairs={{1,0},{2,3},{5,4},{6,7},{9,8},{10,11},{13,12},{14,15},{17,16},{18,... | collective-permute-start | bytes 688136 | tf_op jit(solution)/shard_map/ppermute | solution.py:481
  115.3 20.8 %collective-permute-start.21 = (bf16[64,1792]{1,0:T(8,128)(2,1)S(1)}, bf16[64,1792]{1,0:T(8,128)(2,1)S(1)}, u32[]{:S(2)}, u32[]{:S(2)}) collective-permute-start(bf16[64,1792]{1,0:T(8,128)(2,1)S(1)} %add.31.refs_2_), channel_id=1, source_target_pairs={{1,0},{2,3},{5,4},{6,7},{9,8},{10,11},{13,12},{14,15},{17,16},{18,... | collective-permute-start | bytes 688136 | tf_op jit(solution)/shard_map/ppermute | solution.py:481

commit v4 on v3

--- a/solution.py
+++ b/solution.py
@@ -32,7 +32,7 @@
 
 def chunk_sizes(tok_group):
     if tok_group == 256:
-        return (48, 64, 64, 80)
+        return (48, 64, 80, 64)
     return (tok_group,)
 
 
@@ -43,7 +43,7 @@
     ).astype(jnp.bfloat16)
 
 
-def build_queries(q, q_nope, q_rope, wk, ready=None):
+def build_queries(q, q_nope, q_rope, first, wk, ready=None):
     heads, t, _ = q_nope.shape
     latent = wk.shape[2]
     rope_dim = q_rope.shape[1] // heads
@@ -51,7 +51,7 @@
     one = jnp.where(lane == rope_dim, 1.0, 0.0)
     per_tile = LANES // rope_dim
     for h in range(heads):
-        pair = q_rope[:, h // per_tile * LANES:(h // per_tile + 1) * LANES].astype(jnp.float32)
+        pair = q_rope[first:first + t, h // per_tile * LANES:(h // per_tile + 1) * LANES].astype(jnp.float32)
         turn = h % per_tile * rope_dim
         if turn:
             pair = pltpu.roll(pair, LANES - turn, 1)
@@ -99,8 +99,9 @@
         out[:, h * dv:(h + 1) * dv] = dot(att[h * t:(h + 1) * t, :], wv[h]).astype(jnp.bfloat16)
 
 
-def first_kernel(fresh, exp_scale, table, offset, q_nope, q_rope_hbm, wk_hbm, wv_hbm, cache_latent,
-                 cache_rope, new_latent, new_rope_t, out, keys, wk, wv, q_rope, q, att, sems, wsems):
+def first_kernel(fresh, exp_scale, table, offset, q_nope, q_nope_hbm, q_rope_hbm, wk_hbm, wv_hbm,
+                 cache_latent, cache_rope, new_latent, new_rope_t, out, keys, wk, wv, q_nope_out,
+                 q_rope, q, att, sems, wsems):
     heads, t, _ = q_nope.shape
     block_len, latent = cache_latent.shape[1:]
     rope_dim = new_rope_t.shape[0]
@@ -108,7 +109,8 @@
     prior = blocks * block_len
     tok_group = new_latent.shape[0]
 
-    rope_copy = pltpu.make_async_copy(q_rope_hbm.at[pl.ds(0, t)], q_rope, wsems.at[0])
+    rope_copy = pltpu.make_async_copy(
+        q_rope_hbm.at[pl.ds(0, t)], q_rope.at[pl.ds(0, t)], wsems.at[0])
     rope_copy.start()
     wk_copies = [pltpu.make_async_copy(wk_hbm.at[h], wk.at[h], wsems.at[1 + h]) for h in range(heads)]
     for c in wk_copies:
@@ -127,10 +129,17 @@
         c.start()
     wv_copy = pltpu.make_async_copy(wv_hbm, wv, sems.at[2 * blocks + 1])
     wv_copy.start()
+    others = [pltpu.make_async_copy(q_nope_hbm, q_nope_out, wsems.at[heads + 1])]
+    if t < tok_group:
+        others.append(pltpu.make_async_copy(
+            q_rope_hbm.at[pl.ds(t, tok_group - t)], q_rope.at[pl.ds(t, tok_group - t)],
+            wsems.at[heads + 2]))
+    for c in others:
+        c.start()
 
     keys[prior:, latent:] = rope_rows(new_rope_t[...])
     rope_copy.wait()
-    build_queries(q, q_nope, q_rope, wk, lambda h: wk_copies[h].wait())
+    build_queries(q, q_nope, q_rope, 0, wk, lambda h: wk_copies[h].wait())
 
     for c in copies:
         c.wait()
@@ -141,23 +150,56 @@
     prefill(q, keys, att, heads, t, 0, prior, fresh, exp_scale)
     wv_copy.wait()
     head_outputs(out, att, wv, t)
+    for c in others:
+        c.wait()
+
+
+def second_kernel(first, fresh, prior, exp_scale, n_after, me, ids, q_nope, q_rope, wk, wv, keys, w_hbm,
+                  cache_latent, cache_rope, *rest):
+    rest = rest[n_after:]
+    groups = ids.shape[1]
+    out, w, packed = rest[0], rest[1], rest[2:2 + groups]
+    q, att, sems = rest[2 + groups:]
+    heads, t, _ = q_nope.shape
+    block_len, latent = cache_latent.shape[1:]
+    capacity = ids.shape[2]
+    copies = []
+    for s in range(groups):
+        to = lax.rem(me[0] + s, groups)
+        for k in range(capacity):
+            b = ids[0, to, k]
+            rows = pl.ds(k * block_len, block_len)
+            copies.append(pltpu.make_async_copy(
+                cache_latent.at[b], packed[s].at[rows, pl.ds(0, latent)], sems.at[len(copies)]))
+            copies.append(pltpu.make_async_copy(
+                cache_rope.at[b], packed[s].at[rows, pl.ds(latent, LANES)], sems.at[len(copies)]))
+    copies.append(pltpu.make_async_copy(w_hbm, w, sems.at[len(copies)]))
+    for c in copies:
+        c.start()
+    build_queries(q, q_nope, q_rope, first, wk)
+    prefill(q, keys, att, heads, t, first, prior, fresh, exp_scale)
+    head_outputs(out, att, wv, t)
+    for c in copies:
+        c.wait()
 
 
 def later_kernel(first, fresh, prior, exp_scale, n_after, q_nope, q_rope, wk, wv, keys, *rest):
     out, q, att = rest[n_after:]
     heads, t, _ = q_nope.shape
-    build_queries(q, q_nope, q_rope, wk)
+    build_queries(q, q_nope, q_rope, first, wk)
     prefill(q, keys, att, heads, t, first, prior, fresh, exp_scale)
     head_outputs(out, att, wv, t)
 
 
-def last_kernel(first, fresh, prior, prefill_len, exp_scale, n_after, q_nope, q_rope, wk, wv, keys,
-                cache_latent, cache_rope, received, decode_table, decode_length, *rest):
-    out, q, att, dkeys, sems = rest[n_after:]
+def last_kernel(first, fresh, prior, prefill_len, exp_scale, n_after, me, q_nope, q_rope, wk, wv, keys,
+                cache_latent, cache_rope, decode_table, decode_length, *rest):
+    received = rest[:-5 - n_after]
+    out, q, att, dkeys, sems = rest[-5:]
+    groups = len(received)
     heads, t, _ = q_nope.shape
     pool, block_len, latent = cache_latent.shape
-    got = received.shape[0]
-    ext = pool * block_len + got
+    got = received[0].shape[0]
+    ext = pool * block_len + groups * got
     tail = dkeys.shape[0] - ext
     start = keys.shape[0] - tail
     copies = []
@@ -167,13 +209,15 @@
             cache_latent.at[i], dkeys.at[rows, pl.ds(0, latent)], sems.at[2 * i]))
         copies.append(pltpu.make_async_copy(
             cache_rope.at[i], dkeys.at[rows, pl.ds(latent, LANES)], sems.at[2 * i + 1]))
-    copies.append(pltpu.make_async_copy(
-        received, dkeys.at[pl.ds(pool * block_len, got)], sems.at[2 * pool]))
     for c in copies:
         c.start()
+    for s in range(groups):
+        source = lax.rem(me[0] + groups - s, groups)
+        at = pl.multiple_of(pool * block_len + source * got, block_len)
+        dkeys[pl.ds(at, got), :] = received[s][...]
     dkeys[ext:, :] = keys[start:, :]
 
-    build_queries(q, q_nope, q_rope, wk)
+    build_queries(q, q_nope, q_rope, first, wk)
     prefill(q, keys, att, heads, t, first, prior, fresh, exp_scale)
 
     decodes = decode_table.shape[0]
@@ -216,27 +260,13 @@
     return pltpu.with_memory_space_constraint(x, pltpu.HBM)
 
 
-def pack_kernel(ids, cache_latent, cache_rope, out, sems):
-    latent = cache_latent.shape[2]
-    _, groups, capacity = ids.shape
-    copies = []
-    for g in range(groups):
-        for k in range(capacity):
-            n = g * capacity + k
-            b = ids[0, g, k]
-            copies.append(pltpu.make_async_copy(
-                cache_latent.at[b], out.at[n, :, pl.ds(0, latent)], sems.at[2 * n]))
-            copies.append(pltpu.make_async_copy(
-                cache_rope.at[b], out.at[n, :, pl.ds(latent, LANES)], sems.at[2 * n + 1]))
-    for c in copies:
-        c.start()
-    for c in copies:
-        c.wait()
-
-
-def project_kernel(n_after, place, w, *rest):
-    parts, (own, others, x) = rest[:-3 - n_after], rest[-3:]
+def project_kernel(n_parts, tails, place, w, *rest):
+    parts, rest, x = rest[:n_parts], rest[n_parts:], rest[-1]
+    own, outs = rest[-2 - len(tails)], rest[-1 - len(tails):-1]
     t = own.shape[0]
+    lead = outs[-1].shape[0] - tails[-1] * t
+    if lead:
+        outs[-1][:lead, :] = rest[0][...]
     i = 0
     for part in parts:
         for at in range(0, part.shape[0], t):
@@ -247,23 +277,29 @@
     for at in range(0, columns, step):
         y = dot(x[...], w[:, at:at + step]).astype(jnp.bfloat16)
         own[:, at:at + step] = y[:t]
-        others[:, at:at + step] = y[t:]
-
-
-def project(place, parts, w, t, after=()):
+        row = t
+        for i, n in enumerate(tails):
+            skip = lead if i == len(tails) - 1 else 0
+            outs[i][skip:skip + n * t, at:at + step] = y[row:row + n * t]
+            row += n * t
+
+
+def project(place, parts, w, tails, earlier=(), after=()):
     depth, columns = w.shape
     rows = sum(p.shape[0] for p in parts)
+    t = rows // (1 + sum(tails))
+    sizes = [t] + [n * t for n in tails]
+    sizes[-1] += sum(e.shape[0] for e in earlier)
     return pl.pallas_call(
-        functools.partial(project_kernel, len(after)),
-        out_shape=[jax.ShapeDtypeStruct((t, columns), jnp.bfloat16),
-                   jax.ShapeDtypeStruct((rows - t, columns), jnp.bfloat16)],
-        in_specs=[SMEM, VMEM] + [VMEM] * len(parts) + [ANY] * len(after),
-        out_specs=[VMEM, VMEM],
+        functools.partial(project_kernel, len(parts), tails),
+        out_shape=[jax.ShapeDtypeStruct((n, columns), jnp.bfloat16) for n in sizes],
+        in_specs=[SMEM, VMEM] + [VMEM] * (len(parts) + len(earlier)) + [ANY] * len(after),
+        out_specs=[VMEM] * len(sizes),
         scratch_shapes=[pltpu.VMEM((rows, depth), jnp.bfloat16)],
         name="project",
         compiler_params=params(12),
         cost_estimate=COST,
-    )(place, w, *parts, *after)
+    )(place, w, *parts, *earlier, *after)
 
 
 def add_kernel(spans, n_after, *refs):
@@ -286,6 +322,28 @@
         compiler_params=params(8),
         cost_estimate=COST,
     )(*[x for x, _ in terms], *after)
+
+
+def finish_kernel(n_ready, spans, *refs):
+    out = refs[-1]
+    row = 0
+    for ref in refs[:n_ready]:
+        out[row:row + ref.shape[0], :] = ref[...]
+        row += ref.shape[0]
+    add_kernel(spans, 0, *refs[n_ready:-1], out.at[row:, :])
+
+
+def finish(ready, terms):
+    rows = sum(r.shape[0] for r in ready) + terms[0][0].shape[0]
+    return pl.pallas_call(
+        functools.partial(finish_kernel, len(ready), [at for _, at in terms]),
+        out_shape=jax.ShapeDtypeStruct((rows, terms[0][0].shape[1]), jnp.bfloat16),
+        in_specs=[VMEM] * (len(ready) + len(terms)),
+        out_specs=VMEM,
+        name="finish",
+        compiler_params=params(8),
+        cost_estimate=COST,
+    )(*ready, *[x for x, _ in terms])
 
 
 def gathered_ids(groups, me):
@@ -385,88 +443,91 @@
     def scratch(t):
         return [pltpu.VMEM((heads * t, width), bf16), pltpu.VMEM((heads * t, latent), bf16)]
 
-    def nope_of(n):
-        return query_nope[starts[n]:starts[n] + sizes[n]].transpose(1, 0, 2)
-
     def first_chunk():
         t = sizes[0]
+        q_nope = query_nope[:t].transpose(1, 0, 2)
         return pl.pallas_call(
             functools.partial(first_kernel, fresh_of(0), exp_scale),
             out_shape=[jax.ShapeDtypeStruct((t, heads * dv), bf16),
-                       jax.ShapeDtypeStruct((prior + tok_group, width), bf16)],
-            in_specs=[SMEM, SMEM, VMEM, HBM, HBM, HBM, HBM, ANY, HBM, VMEM],
-            out_specs=[VMEM, VMEM],
+                       jax.ShapeDtypeStruct((prior + tok_group, width), bf16),
+                       jax.ShapeDtypeStruct(absorb_key.shape, bf16),
+                       jax.ShapeDtypeStruct(absorb_value.shape, bf16),
+                       jax.ShapeDtypeStruct(query_nope.shape, bf16),
+                       jax.ShapeDtypeStruct(query_rope.shape, bf16)],
+            in_specs=[SMEM, SMEM, VMEM, HBM, HBM, HBM, HBM, HBM, ANY, HBM, VMEM],
+            out_specs=[VMEM] * 6,
             scratch_shapes=[
-                pltpu.VMEM(absorb_key.shape, bf16),
-                pltpu.VMEM(absorb_value.shape, bf16),
-                pltpu.VMEM((t, query_rope.shape[1]), bf16),
                 *scratch(t),
                 pltpu.SemaphoreType.DMA((2 * blocks + 2,)),
-                pltpu.SemaphoreType.DMA((heads + 1,)),
+                pltpu.SemaphoreType.DMA((heads + 3,)),
             ],
             name="attend_first",
             compiler_params=params(20),
             cost_estimate=LONG,
-        )(prefill_table, prefill_offset, nope_of(0), in_hbm(query_rope), in_hbm(absorb_key),
-          in_hbm(absorb_value), in_hbm(cache_latent), padded_rope, in_hbm(new_latent), new_rope.T)
-
-    def later_chunk(n, keys, after, decode=None):
+        )(prefill_table, prefill_offset, q_nope, in_hbm(query_nope), in_hbm(query_rope),
+          in_hbm(absorb_key), in_hbm(absorb_value), in_hbm(cache_latent), padded_rope,
+          in_hbm(new_latent), new_rope.T)
+
+    def attend(n, held, after, brought=None):
+        keys, wk, wv, q_nope, q_rope = held
         t = sizes[n]
-        args = [nope_of(n), query_rope[starts[n]:starts[n] + t], absorb_key, absorb_value, keys]
+        q_nope = q_nope[starts[n]:starts[n] + t].transpose(1, 0, 2)
+        args = [q_nope, q_rope, wk, wv, keys]
         specs = [VMEM] * 5
+        outs = [jax.ShapeDtypeStruct((t, heads * dv), bf16)]
         scratches = scratch(t)
-        if decode is None:
-            kernel = functools.partial(
-                later_kernel, starts[n], fresh_of(n), prior, exp_scale, len(after))
-            limit = 20
+        limit = 20
+        static = (starts[n], fresh_of(n), prior)
+        if n == 1:
+            kernel = functools.partial(second_kernel, *static, exp_scale, len(after))
+            args = [me[None], send_blocks] + args + [
+                in_hbm(output_weight), in_hbm(cache_latent), padded_rope]
+            specs = [SMEM, SMEM] + specs + [HBM, HBM, ANY]
+            outs.append(jax.ShapeDtypeStruct(output_weight.shape, bf16))
+            outs += [jax.ShapeDtypeStruct((capacity * block_len, width), bf16)] * groups
+            scratches.append(pltpu.SemaphoreType.DMA((2 * groups * capacity + 1,)))
+        elif n == len(sizes) - 1:
+            kernel = functools.partial(last_kernel, *static, prefill_len, exp_scale, len(after))
+            args = [me[None]] + args + [
+                in_hbm(cache_latent), padded_rope, decode_table, decode_length[:, None], *brought]
+            specs = [SMEM] + specs + [HBM, ANY, VMEM, VMEM] + [VMEM] * len(brought)
+            span = pool * block_len + groups * capacity * block_len + min(LANES, tok_group)
+            scratches += [pltpu.VMEM((span, width), bf16), pltpu.SemaphoreType.DMA((2 * pool,))]
+            limit = 26
         else:
-            kernel = functools.partial(
-                last_kernel, starts[n], fresh_of(n), prior, prefill_len, exp_scale, len(after))
-            args += [in_hbm(cache_latent), padded_rope, *decode]
-            specs += [HBM, ANY, ANY, VMEM, VMEM]
-            span = pool * block_len + decode[0].shape[0] + min(LANES, tok_group)
-            scratches += [pltpu.VMEM((span, width), bf16), pltpu.SemaphoreType.DMA((2 * pool + 1,))]
-            limit = 26
+            kernel = functools.partial(later_kernel, *static, exp_scale, len(after))
         return pl.pallas_call(
             kernel,
-            out_shape=jax.ShapeDtypeStruct((t, heads * dv), bf16),
+            out_shape=outs,
             in_specs=specs + [ANY] * len(after),
-            out_specs=VMEM,
+            out_specs=[VMEM] * len(outs),
             scratch_shapes=scratches,
             name="attend",
             compiler_params=params(limit),
             cost_estimate=LONG,
         )(*args, *after)
 
-    def pack():
-        return pl.pallas_call(
-            pack_kernel,
-            out_shape=jax.ShapeDtypeStruct((groups * capacity, block_len, width), bf16),
-            in_specs=[SMEM, HBM, ANY],
-            out_specs=VMEM,
-            scratch_shapes=[pltpu.SemaphoreType.DMA((2 * groups * capacity,))],
-            name="pack",
-            compiler_params=params(8),
-            cost_estimate=COST,
-        )(send_blocks, in_hbm(cache_latent), padded_rope)
-
     def migrate(packed):
-        got = lax.all_to_all(packed, "dp", split_axis=0, concat_axis=0, tiled=True)
-        return (got.reshape(groups * capacity * block_len, width), decode_table,
-                decode_length[:, None])
-
-    if len(sizes) != 4 or not on_line:
+        return [packed[0]] + [
+            lax.ppermute(packed[s], "dp", [(i, (i + s) % groups) for i in range(groups)])
+            for s in range(1, groups)]
+
+    x0, *held = first_chunk()
+    if not on_line:
         outs = []
-        keys = None
+        w = brought = None
         for n, t in enumerate(sizes):
             if n == 0:
-                x, keys = first_chunk()
+                x = x0
+            elif n == 1:
+                x, w, *packed = attend(n, held, ())
+                brought = migrate(packed)
             else:
-                x = later_chunk(n, keys, (), migrate(pack()) if n == len(sizes) - 1 else None)
+                x, = attend(n, held, (), brought)
             mine = shift_groups(x)
             if groups % 2 == 0:
                 mine += [swap_cores(y) for y in mine]
-            own, others = project(place, mine, output_weight, t)
+            own, others = project(place, mine, output_weight, (groups - 1,))
             partials = jnp.concatenate([own, others], axis=0).reshape(groups, t, columns)
             outs.append(lax.psum_scatter(partials, "tp", scatter_dimension=0, tiled=False))
         return jnp.concatenate(outs, axis=0)
@@ -485,44 +546,42 @@
         return [x, came, swap_cores(x), swap_cores(stack([came], after))]
 
     t0, t1, t2, t3 = sizes
-    x0, keys = first_chunk()
-    decode = migrate(pack())
-    x1 = later_chunk(1, keys, (decode[0],))
-    own0, rest0 = project(place, gather(x0, (x1,)), output_weight, t0, (x1,))
+    x1, w, *packed = attend(1, held, (x0,))
+    own0, rest0 = project(place, gather(x0, (x1,)), w, (3,), (), (x1,))
     in0 = inward(rest0)
-    x2 = later_chunk(2, keys, (own0,))
-    own1, rest1 = project(place, gather(x1, (x2,)), output_weight, t1, (x2,))
+    brought = migrate(packed)
+    x2, = attend(2, held, (own0,))
+    own1, rest1 = project(place, gather(x1, (x2,)), w, (3,), (), (x2,))
     in1 = inward(rest1)
     to_across0 = add(2 * t0, [(rest0, 0), (in0, 0)], (own1,))
     on0 = across(to_across0)
-    x3 = later_chunk(3, keys, (to_across0,), decode)
-    own2, rest2 = project(place, gather(x2, (x3,)), output_weight, t2, (x3,))
+    x3, = attend(3, held, (to_across0,), brought)
+    own2, rest2, near2 = project(place, gather(x2, (x3,)), w, (2, 1), (), (x3,))
     in2 = inward(rest2)
     to_across1 = add(2 * t1, [(rest1, 0), (in1, 0)], (own2,))
     on1 = across(to_across1)
     to_out0 = add(t0, [(rest0, 2 * t0), (on0, 0)], (own2,))
     out0 = outward(to_out0)
-    own3, rest3 = project(place, gather(x3, (own2,)), output_weight, t3, (to_across1, to_out0))
-    far3, mid3, near3 = (rest3[i * t3:(i + 1) * t3] for i in range(3))
-    in3 = [inward(far3), inward(mid3), inward(near3)]
+    done0 = add(t0, [(own0, 0), (in0, 2 * t0), (on0, t0), (out0, 0)], (to_across1,))
+    own3, rest3, near = project(
+        place, gather(x3, (to_across1, to_out0)), w, (2, 1), (near2,), (done0,))
+    in3 = inward(rest3)
     to_across2 = add(2 * t2, [(rest2, 0), (in2, 0)], (own3,))
     on2 = across(to_across2)
+    near_in = inward(near)
     to_out1 = add(t1, [(rest1, 2 * t1), (on1, 0)], (to_across2,))
     out1 = outward(to_out1)
-    to_far = add(t3, [(far3, 0), (in3[0], 0)], (to_out1,))
+    to_far = add(t3, [(rest3, 0), (in3, 0)], (to_out1,))
     far_on = across(to_far)
-    to_out2 = add(t2, [(rest2, 2 * t2), (on2, 0)], (to_far,))
+    done1 = add(t1, [(own1, 0), (in1, 2 * t1), (on1, t1), (out1, 0)], (to_far,))
+    to_mid = add(t3, [(rest3, t3), (in3, t3)], (done1,))
+    mid_on = across(to_mid)
+    to_out2 = add(t2, [(near2, 0), (on2, 0)], (to_mid,))
     out2 = outward(to_out2)
-    to_mid = add(t3, [(mid3, 0), (in3[1], 0)], (to_out2,))
-    mid_on = across(to_mid)
-    out3 = outward(add(t3, [(near3, 0), (far_on, 0)], (to_mid,)))
-    done = [
-        add(t, [(own, 0), (came, 2 * t), (on, t), (out, 0)])
-        for t, own, came, on, out in (
-            (t0, own0, in0, on0, out0), (t1, own1, in1, on1, out1), (t2, own2, in2, on2, out2))
-    ]
-    done.append(add(t3, [(own3, 0), (in3[2], 0), (mid_on, 0), (out3, 0)]))
-    return jnp.concatenate(done, axis=0)
+    to_out3 = add(t3, [(near, t2), (far_on, 0)], (to_out2,))
+    out3 = outward(to_out3)
+    done2 = add(t2, [(own2, 0), (near_in, 0), (on2, t2), (out2, 0)], (to_out3,))
+    return finish([done0, done1, done2], [(own3, 0), (near_in, t2), (mid_on, 0), (out3, 0)])
 
 
 def solution(mesh):

time: 138 us -> 127 us (0.920)
  waiting for transfers between devices: 29.9 us -> 21.4 us
  starting transfers between devices: 44.8 us -> 38.2 us
  local copies, waits for them, and re-layouts: 17.3 us -> 22.8 us
    ppermute x6 -> x5, starting transfers between devices: 25.8 us -> 19.1 us  [inward(): return lax.ppermute(x, 'tp', INWARD)]
    unnamed x52 -> x63, local copies, waits for them, and re-layouts: 13.2 us -> 18.2 us
    ppermute x4, waiting for transfers between devices: 4.49 us -> 0.01 us  [shift_groups(): lax.ppermute(x, 'dp', [(i, (i + s) % groups) for i in range(groups)])]
    all_to_all x1 -> x0, starting transfers between devices: 4.22 us -> none  [migrate(): got = lax.all_to_all(packed, 'dp', split_axis=0, concat_axis=0, tiled=True)]
    ppermute x4, waiting for transfers between devices: 19.3 us -> 16.3 us  [outward(): return lax.ppermute(x, 'tp', OUTWARD)]
    ppermute x0 -> x3, starting transfers between devices: none -> 2.53 us  [migrate(): lax.ppermute(packed[s], 'dp', [(i, (i + s) % groups) for i in range(group...]
    ppermute x4, starting transfers between devices: 4.45 us -> 6.04 us  [shift_groups(): lax.ppermute(x, 'dp', [(i, (i + s) % groups) for i in range(groups)])]
    ppermute x6 -> x5, waiting for transfers between devices: 5.31 us -> 5 us  [inward(): return lax.ppermute(x, 'tp', INWARD)]
  transfers between devices with their start and end apart: 28 -> 29, of which waited for: 7 -> 7; matrix products, arithmetic and copies ran while one was open for 2% -> 2% of each run, Pallas kernels for 29% -> 27%
where the time goes in v4:
time: 127 us
  Pallas kernels  42.7 us (34%)
  starting transfers between devices  38.2 us (30%)
  local copies, waits for them, and re-layouts  22.8 us (18%)
  waiting for transfers between devices  21.4 us (17%)
  between operations  1.35 us (1%)
    pallas_call x3, Pallas kernels, attend(): pl.pallas_call(kernel, out_shape=outs, in_specs=specs + [ANY] * len(after...  22.2 us
    ppermute x5, starting transfers between devices, inward(): return lax.ppermute(x, 'tp', INWARD)  19.1 us
    unnamed x63, local copies, waits for them, and re-layouts  18.2 us
    ppermute x4, waiting for transfers between devices, outward(): return lax.ppermute(x, 'tp', OUTWARD)  16.3 us
    pallas_call x4, Pallas kernels, project(): pl.pallas_call(functools.partial(project_kernel, len(parts), tails), out_...  10.7 us
    pallas_call x1, Pallas kernels, first_chunk(): pl.pallas_call(functools.partial(first_kernel, fresh_of(0), exp_scale), o...  7.61 us
    ppermute x4, starting transfers between devices, shift_groups(): lax.ppermute(x, 'dp', [(i, (i + s) % groups) for i in range(groups)])  6.04 us
    ppermute x4, starting transfers between devices, outward(): return lax.ppermute(x, 'tp', OUTWARD)  5.16 us
  transfers between devices with their start and end apart: 29, of which 7 were waited for; matrix products, arithmetic and copies ran while one was open for 2% of the time, Pallas kernels for 27%

profile of v4, /device:TPU:0, one launch (start us, length us, event | category | flops | bytes accessed | tf_op | source)
XLA Modules:
  0.0 126.5 jit_solution(510628865413391807)
XLA Ops:
  0.0 1.5 %reshape.3 = bf16[32,64,64]{2,1,0:T(8,128)(2,1)S(1)} reshape(bf16[32,4096]{1,0:T(8,128)(2,1)} %param.20) | data formatting | bytes 524288 | tf_op jit(solution)/shard_map/reshape | solution.py:435
  1.5 0.9 slice.12
  3.1 0.1 pad.4.cache_rope
  3.3 7.6 %attend_first.1 = (bf16[48,2048]{1,0:T(8,128)(2,1)S(1)}, bf16[1280,640]{1,0:T(8,128)(2,1)S(1)}, bf16[16,128,512]{2,1,0:T(8,128)(2,1)S(1)}, bf16[16,512,128]{2,1,...) custom-call(s32[1,16]{1,0:T(1,128)S(1)} %copy-done.6, s32[1]{0:T(128)S(6)} %copy.26.offset, ...), custom_call_target="tpu_custom_call" | custom-call | flops 40000000000 | bytes 1000 | tf_op jit(solution)/shard_map/attend_first/pallas_call | solution.py:449
  10.9 1.3 %copy-done.11 = bf16[16,512,128]{2,1,0:T(8,128)(2,1)} copy-done((bf16[16,512,128]{2,1,0:T(8,128)(2,1)}, bf16[16,512,128]{2,1,0:T(8,128)(2,1)S(1)}, u32[]{:S(2)}) %copy-start.11) | copy-done | bytes 2097176
  12.3 1.2 copy-done.15
  13.5 2.9 %collective-permute-start = (bf16[48,2048]{1,0:T(8,128)(2,1)S(1)}, bf16[48,2048]{1,0:T(8,128)(2,1)S(1)}, u32[]{:S(2)}, u32[]{:S(2)}) collective-permute-start(bf16[48,2048]{1,0:T(8,128)(2,1)S(1)} %get-tuple-element.32.rest_0_), channel_id=1, source_target_pairs={{0,8},{4,12},{8,0},{12,4},{1,9},{5,13},{9,1},{13,5},{2,10},{6,14},... | collective-permute-start | bytes 589832 | tf_op jit(solution)/shard_map/ppermute | solution.py:358
  16.4 0.3 copy.17
  16.7 1.0 copy-done.24
  17.8 0.1 copy.18.ids
  17.9 1.6 %copy-done.8 = bf16[16,128,512]{2,1,0:T(8,128)(2,1)S(1)} copy-done((bf16[16,128,512]{2,1,0:T(8,128)(2,1)S(1)}, bf16[16,128,512]{2,1,0:T(8,128)(2,1)}, u32[]{:S(2)}) %copy-start.8) | copy-done | bytes 2097176
  19.5 1.6 %copy-done.12 = bf16[16,512,128]{2,1,0:T(8,128)(2,1)S(1)} copy-done((bf16[16,512,128]{2,1,0:T(8,128)(2,1)S(1)}, bf16[16,512,128]{2,1,0:T(8,128)(2,1)}, u32[]{:S(2)}) %copy-start.12) | copy-done | bytes 2097176
  21.1 1.4 %copy-done.16 = bf16[1280,640]{1,0:T(8,128)(2,1)S(1)} copy-done((bf16[1280,640]{1,0:T(8,128)(2,1)S(1)}, bf16[1280,640]{1,0:T(8,128)(2,1)}, u32[]{:S(2)}) %copy-start.16) | copy-done | bytes 1638424
  22.5 6.0 %attend.3 = (bf16[64,2048]{1,0:T(8,128)(2,1)S(1)}, bf16[2048,1792]{1,0:T(8,128)(2,1)S(1)}, bf16[128,640]{1,0:T(8,128)(2,1)S(1)}, bf16[128,640]{1,0:T(8,128)(2,1)...) custom-call(s32[1]{0:T(128)} %bitcast.1.me, s32[1,4,2]{2,1,0:T(4,128)S(1)} %copy.18.ids, ...), custom_call_target="tpu_custom_call" | custom-call | flops 40000000000 | bytes 1000 | tf_op jit(solution)/shard_map/attend/pallas_call | solution.py:499
  28.5 2.9 %copy-done = bf16[2048,1792]{1,0:T(8,128)(2,1)} copy-done((bf16[2048,1792]{1,0:T(8,128)(2,1)}, bf16[2048,1792]{1,0:T(8,128)(2,1)S(1)}, u32[]{:S(2)}) %copy-start) | copy-done | bytes 7340056
  31.4 0.7 copy-done.22
  32.0 1.0 collective-permute-start.4
  33.1 0.7 dynamic-slice_bitcast_fusion.place
  33.8 0.6 collective-permute-start.2
  34.3 1.0 slice_bitcast_fusion.q_nope
  35.4 3.1 %copy-done.1 = bf16[2048,1792]{1,0:T(8,128)(2,1)S(1)} copy-done((bf16[2048,1792]{1,0:T(8,128)(2,1)S(1)}, bf16[2048,1792]{1,0:T(8,128)(2,1)}, u32[]{:S(2)}) %copy-start.1) | copy-done | bytes 7340056
  38.5 2.2 %project.4 = (bf16[48,1792]{1,0:T(8,128)(2,1)S(1)}, bf16[144,1792]{1,0:T(8,128)(2,1)S(1)}) custom-call(s32[4]{0:T(128)S(1)} %dynamic-slice_bitcast_fusion.place, bf16[2048,1792]{1,0:T(8,128)(2,1)S(1)} %copy-done.1, bf16[48,2048]{1,0:T(8,128)(2,1)S(1)} %get-tuple-element.32.rest_0_, bf16[48,2048]{1,0:T(8,128)(2,1)S(1)} %collective-permute-done.refs_0_.rest_1_, ...), custom_call_target="tpu_custom_call" | custom-call | flops 1000 | bytes 1000 | tf_op jit(solution)/shard_map/project/pallas_call | solution.py:293
  40.7 3.7 %collective-permute-start.3 = (bf16[144,1792]{1,0:T(8,128)(2,1)S(1)}, bf16[144,1792]{1,0:T(8,128)(2,1)S(1)}, u32[]{:S(2)}, u32[]{:S(2)}) collective-permute-start(bf16[144,1792]{1,0:T(8,128)(2,1)S(1)} %get-tuple-element.36.refs_0_), channel_id=1, source_target_pairs={{0,1},{3,2},{4,5},{7,6},{8,9},{11,10},{12,13},{15,14},{16,17},{19,... | collective-permute-start | bytes 1548296 | tf_op jit(solution)/shard_map/ppermute | solution.py:536
  44.5 5.8 %attend.4.refs_1_.rest_4_.rest_0_ = bf16[80,2048]{1,0:T(8,128)(2,1)S(1)} custom-call(bf16[16,80,128]{2,1,0:T(8,128)(2,1)S(1)} %slice_bitcast_fusion.q_nope, bf16[256,1024]{1,0:T(8,128)(2,1)S(1)} %copy-done.20, bf16[16,128,512]{2,1,0:T(8,128)(2,1)S(1)} %copy-done.9, bf16[16,512,128]{2,1,0:T(8,128)(2,1)S(1)} %copy-done.13, bf16[1280,640]{1,0:T(8,128)(2,1)S(1)} %copy-done.17, ...), custom_call_target="tpu_custom_call" | custom-call | flops 40000000000 | bytes 1000 | tf_op jit(solution)/shard_map/attend/pallas_call | solution.py:499
  50.3 0.1 collective-permute-start.6
  50.5 0.4 collective-permute-start.10
  50.9 1.1 collective-permute-start.11
  52.0 1.0 collective-permute-start.12
  53.0 0.1 copy.21.decode_table
  53.2 1.0 collective-permute-start.8
  54.1 3.1 %copy-done.2 = bf16[2048,1792]{1,0:T(8,128)(2,1)S(1)} copy-done((bf16[2048,1792]{1,0:T(8,128)(2,1)S(1)}, bf16[2048,1792]{1,0:T(8,128)(2,1)}, u32[]{:S(2)}) %copy-start.2) | copy-done | bytes 7340056
  57.2 2.7 %project.5 = (bf16[64,1792]{1,0:T(8,128)(2,1)S(1)}, bf16[192,1792]{1,0:T(8,128)(2,1)S(1)}) custom-call(s32[4]{0:T(128)S(1)} %dynamic-slice_bitcast_fusion.place, bf16[2048,1792]{1,0:T(8,128)(2,1)S(1)} %copy-done.2, bf16[64,2048]{1,0:T(8,128)(2,1)S(1)} %get-tuple-element.34.refs_1_.rest_4_.rest_0_, ...), custom_call_target="tpu_custom_call" | custom-call | flops 1000 | bytes 1000 | tf_op jit(solution)/shard_map/project/pallas_call | solution.py:293
  60.0 0.1 add.22.rest_4_
  60.1 1.8 %collective-permute-start.15 = (bf16[192,1792]{1,0:T(8,128)(2,1)S(1)}, bf16[192,1792]{1,0:T(8,128)(2,1)S(1)}, u32[]{:S(2)}, u32[]{:S(2)}) collective-permute-start(bf16[192,1792]{1,0:T(8,128)(2,1)S(1)} %get-tuple-element.43.refs_0_), channel_id=1, source_target_pairs={{0,1},{3,2},{4,5},{7,6},{8,9},{11,10},{12,13},{15,14},{16,17},{19,... | collective-permute-start | bytes 2064392 | tf_op jit(solution)/shard_map/ppermute | solution.py:536
  62.0 10.5 %attend.5.refs_1_.rest_4_.rest_0_ = bf16[64,2048]{1,0:T(8,128)(2,1)S(1)} custom-call(s32[1]{0:T(128)} %bitcast.1.me, bf16[16,64,128]{2,1,0:T(8,128)(2,1)S(1)} %get-tuple-element.49.q_nope, bf16[256,1024]{1,0:T(8,128)(2,1)S(1)} %copy-done.21, bf16[16,128,512]{2,1,0:T(8,128)(2,1)S(1)} %copy-done.10, bf16[16,512,128]{2,1,0:T(8,128)(2,1)S(1)} %copy-done.14, ...), custom_call_target="tpu_custom_call" | custom-call | flops 40000000000 | bytes 1000 | tf_op jit(solution)/shard_map/attend/pallas_call | solution.py:499
  72.6 0.3 collective-permute-start.13
  72.9 0.7 collective-permute-start.7
  73.6 1.1 collective-permute-start.18
  74.7 3.1 %project.6 = (bf16[80,1792]{1,0:T(8,128)(2,1)S(1)}, bf16[160,1792]{1,0:T(8,128)(2,1)S(1)}, bf16[80,1792]{1,0:T(8,128)(2,1)S(1)}) custom-call(s32[4]{0:T(128)S(1)} %dynamic-slice_bitcast_fusion.place, bf16[2048,1792]{1,0:T(8,128)(2,1)S(1)} %bitcast.15, bf16[80,2048]{1,0:T(8,128)(2,1)S(1)} %attend.4.refs_1_.rest_4_.rest_0_, ...), custom_call_target="tpu_custom_call" | custom-call | flops 1000 | bytes 1000 | tf_op jit(solution)/shard_map/project/pallas_call | solution.py:293
  77.9 4.3 %collective-permute-start.17 = (bf16[160,1792]{1,0:T(8,128)(2,1)S(1)}, bf16[160,1792]{1,0:T(8,128)(2,1)S(1)}, u32[]{:S(2)}, u32[]{:S(2)}) collective-permute-start(bf16[160,1792]{1,0:T(8,128)(2,1)S(1)} %get-tuple-element.44.refs_0_), channel_id=1, source_target_pairs={{0,1},{3,2},{4,5},{7,6},{8,9},{11,10},{12,13},{15,14},{16,17},{19,... | collective-permute-start | bytes 1720328 | tf_op jit(solution)/shard_map/ppermute | solution.py:536
  82.3 0.1 add.24.refs_4_.refs_1_
  82.5 0.5 collective-permute-start.20
  83.0 1.3 %collective-permute-start.14 = (bf16[48,1792]{1,0:T(8,128)(2,1)S(1)}, bf16[48,1792]{1,0:T(8,128)(2,1)S(1)}, u32[]{:S(2)}, u32[]{:S(2)}) collective-permute-start(bf16[48,1792]{1,0:T(8,128)(2,1)S(1)} %add.23.refs_2_), channel_id=1, source_target_pairs={{1,0},{2,3},{5,4},{6,7},{9,8},{10,11},{13,12},{14,15},{17,16},{18,... | collective-permute-start | bytes 516104 | tf_op jit(solution)/shard_map/ppermute | solution.py:542
  84.3 1.0 collective-permute-start.16
  85.3 5.9 %collective-permute-done.14.refs_3_ = bf16[48,1792]{1,0:T(8,128)(2,1)S(1)} collective-permute-done((bf16[48,1792]{1,0:T(8,128)(2,1)S(1)}, bf16[48,1792]{1,0:T(8,128)(2,1)S(1)}, u32[]{:S(2)}, u32[]{:S(2)}) %collective-permute-start.14) | collective-permute-done | bytes 172064 | tf_op jit(solution)/shard_map/ppermute | solution.py:542
  91.2 0.1 add.25.rest_5_.refs_0_
  91.3 2.7 %project.7 = (bf16[64,1792]{1,0:T(8,128)(2,1)S(1)}, bf16[128,1792]{1,0:T(8,128)(2,1)S(1)}, bf16[144,1792]{1,0:T(8,128)(2,1)S(1)}) custom-call(s32[4]{0:T(128)S(1)} %dynamic-slice_bitcast_fusion.place, bf16[2048,1792]{1,0:T(8,128)(2,1)S(1)} %bitcast.15, bf16[64,2048]{1,0:T(8,128)(2,1)S(1)} %attend.5.refs_1_.rest_4_.rest_0_, ...), custom_call_target="tpu_custom_call" | custom-call | flops 1000 | bytes 1000 | tf_op jit(solution)/shard_map/project/pallas_call | solution.py:293
  94.0 1.5 %collective-permute-start.22 = (bf16[128,1792]{1,0:T(8,128)(2,1)S(1)}, bf16[128,1792]{1,0:T(8,128)(2,1)S(1)}, u32[]{:S(2)}, u32[]{:S(2)}) collective-permute-start(bf16[128,1792]{1,0:T(8,128)(2,1)S(1)} %get-tuple-element.47.refs_0_), channel_id=1, source_target_pairs={{0,1},{3,2},{4,5},{7,6},{8,9},{11,10},{12,13},{15,14},{16,17},{19,... | collective-permute-start | bytes 1376264 | tf_op jit(solution)/shard_map/ppermute | solution.py:536
  95.5 0.1 add.26.refs_2_
  95.7 0.7 collective-permute-start.24
  96.4 1.3 %collective-permute-start.21 = (bf16[64,1792]{1,0:T(8,128)(2,1)S(1)}, bf16[64,1792]{1,0:T(8,128)(2,1)S(1)}, u32[]{:S(2)}, u32[]{:S(2)}) collective-permute-start(bf16[64,1792]{1,0:T(8,128)(2,1)S(1)} %add.27.refs_2_), channel_id=1, source_target_pairs={{1,0},{2,3},{5,4},{6,7},{9,8},{10,11},{13,12},{14,15},{17,16},{18,... | collective-permute-start | bytes 688136 | tf_op jit(solution)/shard_map/ppermute | solution.py:542
  97.7 7.8 %collective-permute-start.23 = (bf16[144,1792]{1,0:T(8,128)(2,1)S(1)}, bf16[144,1792]{1,0:T(8,128)(2,1)S(1)}, u32[]{:S(2)}, u32[]{:S(2)}) collective-permute-start(bf16[144,1792]{1,0:T(8,128)(2,1)S(1)} %get-tuple-element.48.refs_0_), channel_id=1, source_target_pairs={{0,1},{3,2},{4,5},{7,6},{8,9},{11,10},{12,13},{15,14},{16,17},{19,... | collective-permute-start | bytes 1548296 | tf_op jit(solution)/shard_map/ppermute | solution.py:536
  105.6 0.5 collective-permute-done.22.refs_1_
  106.1 0.7 collective-permute-start.26
  106.8 0.8 collective-permute-done.21.refs_3_
  107.6 0.1 add.29.refs_2_.refs_1_
  107.9 1.3 %collective-permute-start.25 = (bf16[80,1792]{1,0:T(8,128)(2,1)S(1)}, bf16[80,1792]{1,0:T(8,128)(2,1)S(1)}, u32[]{:S(2)}, u32[]{:S(2)}) collective-permute-start(bf16[80,1792]{1,0:T(8,128)(2,1)S(1)} %add.31.refs_2_), channel_id=1, source_target_pairs={{1,0},{2,3},{5,4},{6,7},{9,8},{10,11},{13,12},{14,15},{17,16},{18,... | collective-permute-start | bytes 860168 | tf_op jit(solution)/shard_map/ppermute | solution.py:542
  109.2 0.7 collective-permute-start.27
  109.9 1.3 %collective-permute-start.28 = (bf16[64,1792]{1,0:T(8,128)(2,1)S(1)}, bf16[64,1792]{1,0:T(8,128)(2,1)S(1)}, u32[]{:S(2)}, u32[]{:S(2)}) collective-permute-start(bf16[64,1792]{1,0:T(8,128)(2,1)S(1)} %add.32.refs_4_), channel_id=1, source_target_pairs={{1,0},{2,3},{5,4},{6,7},{9,8},{10,11},{13,12},{14,15},{17,16},{18,... | collective-permute-start | bytes 688136 | tf_op jit(solution)/shard_map/ppermute | solution.py:542
  111.2 4.5 %collective-permute-done.23.refs_1_.refs_4_ = bf16[144,1792]{1,0:T(8,128)(2,1)S(1)} collective-permute-done((bf16[144,1792]{1,0:T(8,128)(2,1)S(1)}, bf16[144,1792]{1,0:T(8,128)(2,1)S(1)}, u32[]{:S(2)}, u32[]{:S(2)}) %collective-permute-start.23) | collective-permute-done | bytes 516128 | tf_op jit(solution)/shard_map/ppermute | solution.py:536
  115.8 5.9 %collective-permute-done.25.refs_3_ = bf16[80,1792]{1,0:T(8,128)(2,1)S(1)} collective-permute-done((bf16[80,1792]{1,0:T(8,128)(2,1)S(1)}, bf16[80,1792]{1,0:T(8,128)(2,1)S(1)}, u32[]{:S(2)}, u32[]{:S(2)}) %collective-permute-start.25) | collective-permute-done | bytes 286752 | tf_op jit(solution)/shard_map/ppermute | solution.py:542
  121.7 0.1 add.33.refs_2_
  121.8 3.6 %collective-permute-done.28.refs_6_ = bf16[64,1792]{1,0:T(8,128)(2,1)S(1)} collective-permute-done((bf16[64,1792]{1,0:T(8,128)(2,1)S(1)}, bf16[64,1792]{1,0:T(8,128)(2,1)S(1)}, u32[]{:S(2)}, u32[]{:S(2)}) %collective-permute-start.28) | collective-permute-done | bytes 229408 | tf_op jit(solution)/shard_map/ppermute | solution.py:542
  125.4 1.1 finish.1
  (91 shorter events, 1.0 us)
Async XLA Ops:
  0.0 3.3 %copy-start.5 = (bf16[256,64]{0,1:T(8,128)(2,1)S(1)}, bf16[256,64]{0,1:T(8,128)(2,1)}, u32[]{:S(2)}) copy-start(bf16[256,64]{0,1:T(8,128)(2,1)} %param.18) | copy-start | bytes 98308
  0.0 3.3 %copy-start.6 = (s32[1,16]{1,0:T(1,128)S(1)}, s32[1,16]{1,0:T(1,128)}, u32[]{:S(2)}) copy-start(s32[1,16]{1,0:T(1,128)} %table.1) | copy-start | bytes 196
  10.9 1.4 %copy-start.11 = (bf16[16,512,128]{2,1,0:T(8,128)(2,1)}, bf16[16,512,128]{2,1,0:T(8,128)(2,1)S(1)}, u32[]{:S(2)}) copy-start(bf16[16,512,128]{2,1,0:T(8,128)(2,1)S(1)} %get-tuple-element.30.wv) | copy-start | bytes 6291460
  12.3 1.2 copy-start.15
  13.5 3.2 %copy-start.7 = (bf16[16,128,512]{2,1,0:T(8,128)(2,1)}, bf16[16,128,512]{2,1,0:T(8,128)(2,1)S(1)}, u32[]{:S(2)}) copy-start(bf16[16,128,512]{2,1,0:T(8,128)(2,1)S(1)} %get-tuple-element.29.wk) | copy-start | bytes 6291460
  13.5 15.0 %copy-start.19 = (bf16[256,1024]{1,0:T(8,128)(2,1)}, bf16[256,1024]{1,0:T(8,128)(2,1)S(1)}, u32[]{:S(2)}) copy-start(bf16[256,1024]{1,0:T(8,128)(2,1)S(1)} %get-tuple-element.28.q_rope) | copy-start | bytes 1572868
  13.5 4.3 %copy-start.26 = (s32[1,4,2]{1,2,0:T(2,128)S(1)}, s32[1,4,2]{1,2,0:T(2,128)}, u32[]{:S(2)}) copy-start(s32[1,4,2]{1,2,0:T(2,128)} %param.24) | copy-start | bytes 100
  13.5 20.3 %collective-permute-start = (bf16[48,2048]{1,0:T(8,128)(2,1)S(1)}, bf16[48,2048]{1,0:T(8,128)(2,1)S(1)}, u32[]{:S(2)}, u32[]{:S(2)}) collective-permute-start(bf16[48,2048]{1,0:T(8,128)(2,1)S(1)} %get-tuple-element.32.rest_0_), channel_id=1, source_target_pairs={{0,8},{4,12},{8,0},{12,4},{1,9},{5,13},{9,1},{13,5},{2,10},{6,14},... | collective-permute-start | bytes 589832 | tf_op jit(solution)/shard_map/ppermute | solution.py:358
  16.4 18.9 %collective-permute-start.1 = (bf16[48,2048]{1,0:T(8,128)(2,1)S(1)}, bf16[48,2048]{1,0:T(8,128)(2,1)S(1)}, u32[]{:S(2)}, u32[]{:S(2)}) collective-permute-start(bf16[48,2048]{1,0:T(8,128)(2,1)S(1)} %get-tuple-element.32.rest_0_), channel_id=1, source_target_pairs={{0,4},{4,0},{8,12},{12,8},{1,5},{5,1},{9,13},{13,9},{2,6},{6,2},{1... | collective-permute-start | bytes 589832 | tf_op jit(solution)/shard_map/ppermute | solution.py:383
  16.7 1.0 copy-start.24
  17.9 1.6 %copy-start.8 = (bf16[16,128,512]{2,1,0:T(8,128)(2,1)S(1)}, bf16[16,128,512]{2,1,0:T(8,128)(2,1)}, u32[]{:S(2)}) copy-start(bf16[16,128,512]{2,1,0:T(8,128)(2,1)} %copy-done.7) | copy-start | bytes 6291460
  19.5 1.6 %copy-start.12 = (bf16[16,512,128]{2,1,0:T(8,128)(2,1)S(1)}, bf16[16,512,128]{2,1,0:T(8,128)(2,1)}, u32[]{:S(2)}) copy-start(bf16[16,512,128]{2,1,0:T(8,128)(2,1)} %copy-done.11) | copy-start | bytes 6291460
  21.1 1.4 %copy-start.16 = (bf16[1280,640]{1,0:T(8,128)(2,1)S(1)}, bf16[1280,640]{1,0:T(8,128)(2,1)}, u32[]{:S(2)}) copy-start(bf16[1280,640]{1,0:T(8,128)(2,1)} %copy-done.15) | copy-start | bytes 4915204
  28.5 2.9 %copy-start = (bf16[2048,1792]{1,0:T(8,128)(2,1)}, bf16[2048,1792]{1,0:T(8,128)(2,1)S(1)}, u32[]{:S(2)}) copy-start(bf16[2048,1792]{1,0:T(8,128)(2,1)S(1)} %get-tuple-element.33.w) | copy-start | bytes 22020100
  31.4 0.7 copy-start.22
  32.0 18.2 %collective-permute-start.4 = (bf16[64,2048]{1,0:T(8,128)(2,1)S(1)}, bf16[64,2048]{1,0:T(8,128)(2,1)S(1)}, u32[]{:S(2)}, u32[]{:S(2)}) collective-permute-start(bf16[64,2048]{1,0:T(8,128)(2,1)S(1)} %get-tuple-element.34.refs_1_.rest_4_.rest_0_), channel_id=1, source_target_pairs={{0,8},{4,12},{8,0},{12,4},{1,9},{5,13},{9,1},{13,5},{2,10},{6,14},... | collective-permute-start | bytes 786440 | tf_op jit(solution)/shard_map/ppermute | solution.py:358
  33.1 18.9 %collective-permute-start.5 = (bf16[64,2048]{1,0:T(8,128)(2,1)S(1)}, bf16[64,2048]{1,0:T(8,128)(2,1)S(1)}, u32[]{:S(2)}, u32[]{:S(2)}) collective-permute-start(bf16[64,2048]{1,0:T(8,128)(2,1)S(1)} %get-tuple-element.34.refs_1_.rest_4_.rest_0_), channel_id=1, source_target_pairs={{0,4},{4,0},{8,12},{12,8},{1,5},{5,1},{9,13},{13,9},{2,6},{6,2},{1... | collective-permute-start | bytes 786440 | tf_op jit(solution)/shard_map/ppermute | solution.py:383
  33.8 1.6 %collective-permute-start.2 = (bf16[48,2048]{1,0:T(8,128)(2,1)S(1)}, bf16[48,2048]{1,0:T(8,128)(2,1)S(1)}, u32[]{:S(2)}, u32[]{:S(2)}) collective-permute-start(bf16[48,2048]{1,0:T(8,128)(2,1)S(1)} %stack.4), channel_id=1, source_target_pairs={{0,4},{4,0},{8,12},{12,8},{1,5},{5,1},{9,13},{13,9},{2,6},{6,2},{1... | collective-permute-start | bytes 589832 | tf_op jit(solution)/shard_map/ppermute | solution.py:383
  35.4 3.1 %copy-start.1 = (bf16[2048,1792]{1,0:T(8,128)(2,1)S(1)}, bf16[2048,1792]{1,0:T(8,128)(2,1)}, u32[]{:S(2)}) copy-start(bf16[2048,1792]{1,0:T(8,128)(2,1)} %copy-done) | copy-start | bytes 22020100
  38.5 6.0 %copy-start.9 = (bf16[16,128,512]{2,1,0:T(8,128)(2,1)S(1)}, bf16[16,128,512]{2,1,0:T(8,128)(2,1)}, u32[]{:S(2)}) copy-start(bf16[16,128,512]{2,1,0:T(8,128)(2,1)} %copy-done.7) | copy-start | bytes 6291460
  38.5 6.0 %copy-start.13 = (bf16[16,512,128]{2,1,0:T(8,128)(2,1)S(1)}, bf16[16,512,128]{2,1,0:T(8,128)(2,1)}, u32[]{:S(2)}) copy-start(bf16[16,512,128]{2,1,0:T(8,128)(2,1)} %copy-done.11) | copy-start | bytes 6291460
  38.5 6.0 %copy-start.17 = (bf16[1280,640]{1,0:T(8,128)(2,1)S(1)}, bf16[1280,640]{1,0:T(8,128)(2,1)}, u32[]{:S(2)}) copy-start(bf16[1280,640]{1,0:T(8,128)(2,1)} %copy-done.15) | copy-start | bytes 4915204
  38.5 6.0 %copy-start.20 = (bf16[256,1024]{1,0:T(8,128)(2,1)S(1)}, bf16[256,1024]{1,0:T(8,128)(2,1)}, u32[]{:S(2)}) copy-start(bf16[256,1024]{1,0:T(8,128)(2,1)} %copy-done.19) | copy-start | bytes 1572868
  40.7 9.5 %copy-start.3 = (bf16[48,1792]{1,0:T(8,128)(2,1)}, bf16[48,1792]{1,0:T(8,128)(2,1)S(1)}, u32[]{:S(2)}) copy-start(bf16[48,1792]{1,0:T(8,128)(2,1)S(1)} %get-tuple-element.35.rest_0_.refs_0_) | copy-start | bytes 516100
  40.7 19.2 %collective-permute-start.3 = (bf16[144,1792]{1,0:T(8,128)(2,1)S(1)}, bf16[144,1792]{1,0:T(8,128)(2,1)S(1)}, u32[]{:S(2)}, u32[]{:S(2)}) collective-permute-start(bf16[144,1792]{1,0:T(8,128)(2,1)S(1)} %get-tuple-element.36.refs_0_), channel_id=1, source_target_pairs={{0,1},{3,2},{4,5},{7,6},{8,9},{11,10},{12,13},{15,14},{16,17},{19,... | collective-permute-start | bytes 1548296 | tf_op jit(solution)/shard_map/ppermute | solution.py:536
  44.5 8.5 %copy-start.25 = (s32[16,4]{0,1:T(4,128)S(1)}, s32[16,4]{0,1:T(4,128)}, u32[]{:S(2)}) copy-start(s32[16,4]{0,1:T(4,128)} %param.27) | copy-start | bytes 772
  44.5 8.6 %copy-start.27 = (s32[16]{0:T(128)S(1)}, s32[16]{0:T(128)}, u32[]{:S(2)}) copy-start(s32[16]{0:T(128)} %param.28) | copy-start | bytes 196
  50.3 2.9 %collective-permute-start.6 = (bf16[64,2048]{1,0:T(8,128)(2,1)S(1)}, bf16[64,2048]{1,0:T(8,128)(2,1)S(1)}, u32[]{:S(2)}, u32[]{:S(2)}) collective-permute-start(bf16[64,2048]{1,0:T(8,128)(2,1)S(1)} %stack.5), channel_id=1, source_target_pairs={{0,4},{4,0},{8,12},{12,8},{1,5},{5,1},{9,13},{13,9},{2,6},{6,2},{1... | collective-permute-start | bytes 786440 | tf_op jit(solution)/shard_map/ppermute | solution.py:383
  50.5 9.6 %collective-permute-start.10 = (bf16[128,640]{1,0:T(8,128)(2,1)}, bf16[128,640]{1,0:T(8,128)(2,1)}, u32[]{:S(2)}, u32[]{:S(2)}) collective-permute-start(bf16[128,640]{1,0:T(8,128)(2,1)} %get-tuple-element.39), channel_id=1, source_target_pairs={{0,4},{4,8},{8,12},{12,0},{1,5},{5,9},{9,13},{13,1},{2,6},{6,10},{... | collective-permute-start | bytes 491528 | tf_op jit(solution)/shard_map/ppermute | solution.py:512
  50.9 11.0 %collective-permute-start.11 = (bf16[128,640]{1,0:T(8,128)(2,1)}, bf16[128,640]{1,0:T(8,128)(2,1)}, u32[]{:S(2)}, u32[]{:S(2)}) collective-permute-start(bf16[128,640]{1,0:T(8,128)(2,1)} %get-tuple-element.40), channel_id=1, source_target_pairs={{0,8},{4,12},{8,0},{12,4},{1,9},{5,13},{9,1},{13,5},{2,10},{6,14},... | collective-permute-start | bytes 491528 | tf_op jit(solution)/shard_map/ppermute | solution.py:512
  52.0 9.9 %collective-permute-start.12 = (bf16[128,640]{1,0:T(8,128)(2,1)}, bf16[128,640]{1,0:T(8,128)(2,1)}, u32[]{:S(2)}, u32[]{:S(2)}) collective-permute-start(bf16[128,640]{1,0:T(8,128)(2,1)} %get-tuple-element.41), channel_id=1, source_target_pairs={{0,12},{4,0},{8,4},{12,8},{1,13},{5,1},{9,5},{13,9},{2,14},{6,2},{... | collective-permute-start | bytes 491528 | tf_op jit(solution)/shard_map/ppermute | solution.py:512
  53.2 19.4 %collective-permute-start.8 = (bf16[80,2048]{1,0:T(8,128)(2,1)S(1)}, bf16[80,2048]{1,0:T(8,128)(2,1)S(1)}, u32[]{:S(2)}, u32[]{:S(2)}) collective-permute-start(bf16[80,2048]{1,0:T(8,128)(2,1)S(1)} %attend.4.refs_1_.rest_4_.rest_0_), channel_id=1, source_target_pairs={{0,8},{4,12},{8,0},{12,4},{1,9},{5,13},{9,1},{13,5},{2,10},{6,14},... | collective-permute-start | bytes 983048 | tf_op jit(solution)/shard_map/ppermute | solution.py:358
  54.1 3.1 %copy-start.2 = (bf16[2048,1792]{1,0:T(8,128)(2,1)S(1)}, bf16[2048,1792]{1,0:T(8,128)(2,1)}, u32[]{:S(2)}) copy-start(bf16[2048,1792]{1,0:T(8,128)(2,1)} %copy-done) | copy-start | bytes 22020100
  57.2 4.7 %copy-start.10 = (bf16[16,128,512]{2,1,0:T(8,128)(2,1)S(1)}, bf16[16,128,512]{2,1,0:T(8,128)(2,1)}, u32[]{:S(2)}) copy-start(bf16[16,128,512]{2,1,0:T(8,128)(2,1)} %copy-done.7) | copy-start | bytes 6291460
  57.2 4.7 %copy-start.14 = (bf16[16,512,128]{2,1,0:T(8,128)(2,1)S(1)}, bf16[16,512,128]{2,1,0:T(8,128)(2,1)}, u32[]{:S(2)}) copy-start(bf16[16,512,128]{2,1,0:T(8,128)(2,1)} %copy-done.11) | copy-start | bytes 6291460
  57.2 4.7 %copy-start.18 = (bf16[1280,640]{1,0:T(8,128)(2,1)S(1)}, bf16[1280,640]{1,0:T(8,128)(2,1)}, u32[]{:S(2)}) copy-start(bf16[1280,640]{1,0:T(8,128)(2,1)} %copy-done.15) | copy-start | bytes 4915204
  57.2 4.7 %copy-start.21 = (bf16[256,1024]{1,0:T(8,128)(2,1)S(1)}, bf16[256,1024]{1,0:T(8,128)(2,1)}, u32[]{:S(2)}) copy-start(bf16[256,1024]{1,0:T(8,128)(2,1)} %copy-done.19) | copy-start | bytes 1572868
  57.2 4.7 %copy-start.23 = (bf16[128,640]{1,0:T(8,128)(2,1)S(1)}, bf16[128,640]{1,0:T(8,128)(2,1)}, u32[]{:S(2)}) copy-start(bf16[128,640]{1,0:T(8,128)(2,1)} %copy-done.22) | copy-start | bytes 491524
  59.9 14.8 %collective-permute-start.9 = (bf16[80,2048]{1,0:T(8,128)(2,1)S(1)}, bf16[80,2048]{1,0:T(8,128)(2,1)S(1)}, u32[]{:S(2)}, u32[]{:S(2)}) collective-permute-start(bf16[80,2048]{1,0:T(8,128)(2,1)S(1)} %attend.4.refs_1_.rest_4_.rest_0_), channel_id=1, source_target_pairs={{0,4},{4,0},{8,12},{12,8},{1,5},{5,1},{9,13},{13,9},{2,6},{6,2},{1... | collective-permute-start | bytes 983048 | tf_op jit(solution)/shard_map/ppermute | solution.py:383
  60.1 22.2 %collective-permute-start.15 = (bf16[192,1792]{1,0:T(8,128)(2,1)S(1)}, bf16[192,1792]{1,0:T(8,128)(2,1)S(1)}, u32[]{:S(2)}, u32[]{:S(2)}) collective-permute-start(bf16[192,1792]{1,0:T(8,128)(2,1)S(1)} %get-tuple-element.43.refs_0_), channel_id=1, source_target_pairs={{0,1},{3,2},{4,5},{7,6},{8,9},{11,10},{12,13},{15,14},{16,17},{19,... | collective-permute-start | bytes 2064392 | tf_op jit(solution)/shard_map/ppermute | solution.py:536
  61.9 12.8 %slice-start = ((s8[7340032]{0:T(1024)(128)(4,1)}), s8[4194304]{0:T(1024)(128)(4,1)S(1)}, s32[]{:S(2)}) async-start(s8[7340032]{0:T(1024)(128)(4,1)} %bitcast.14), calls=%async_computation | async-start | bytes 8388608
  62.0 12.7 %slice-start.1 = ((s8[7340032]{0:T(1024)(128)(4,1)}), s8[3145728]{0:T(1024)(128)(4,1)S(1)}, s32[]{:S(2)}) async-start(s8[7340032]{0:T(1024)(128)(4,1)} %bitcast.14), calls=%async_computation.1 | async-start | bytes 6291456
  72.6 2.1 %collective-permute-start.13 = (bf16[80,2048]{1,0:T(8,128)(2,1)S(1)}, bf16[80,2048]{1,0:T(8,128)(2,1)S(1)}, u32[]{:S(2)}, u32[]{:S(2)}) collective-permute-start(bf16[80,2048]{1,0:T(8,128)(2,1)S(1)} %stack.6), channel_id=1, source_target_pairs={{0,4},{4,0},{8,12},{12,8},{1,5},{5,1},{9,13},{13,9},{2,6},{6,2},{1... | collective-permute-start | bytes 983048 | tf_op jit(solution)/shard_map/ppermute | solution.py:383
  72.9 9.4 %collective-permute-start.7 = (bf16[96,1792]{1,0:T(8,128)(2,1)S(1)}, bf16[96,1792]{1,0:T(8,128)(2,1)S(1)}, u32[]{:S(2)}, u32[]{:S(2)}) collective-permute-start(bf16[96,1792]{1,0:T(8,128)(2,1)S(1)} %add.22.rest_4_), channel_id=1, source_target_pairs={{1,2},{2,1},{5,6},{6,5},{9,10},{10,9},{13,14},{14,13},{17,18},{18,... | collective-permute-start | bytes 1032200 | tf_op jit(solution)/shard_map/ppermute | solution.py:539
  73.6 8.9 %collective-permute-start.18 = (bf16[64,2048]{1,0:T(8,128)(2,1)S(1)}, bf16[64,2048]{1,0:T(8,128)(2,1)S(1)}, u32[]{:S(2)}, u32[]{:S(2)}) collective-permute-start(bf16[64,2048]{1,0:T(8,128)(2,1)S(1)} %attend.5.refs_1_.rest_4_.rest_0_), channel_id=1, source_target_pairs={{0,8},{4,12},{8,0},{12,4},{1,9},{5,13},{9,1},{13,5},{2,10},{6,14},... | collective-permute-start | bytes 786440 | tf_op jit(solution)/shard_map/ppermute | solution.py:358
  77.9 17.6 %collective-permute-start.17 = (bf16[160,1792]{1,0:T(8,128)(2,1)S(1)}, bf16[160,1792]{1,0:T(8,128)(2,1)S(1)}, u32[]{:S(2)}, u32[]{:S(2)}) collective-permute-start(bf16[160,1792]{1,0:T(8,128)(2,1)S(1)} %get-tuple-element.44.refs_0_), channel_id=1, source_target_pairs={{0,1},{3,2},{4,5},{7,6},{8,9},{11,10},{12,13},{15,14},{16,17},{19,... | collective-permute-start | bytes 1720328 | tf_op jit(solution)/shard_map/ppermute | solution.py:536
  82.2 9.1 %collective-permute-start.19 = (bf16[64,2048]{1,0:T(8,128)(2,1)S(1)}, bf16[64,2048]{1,0:T(8,128)(2,1)S(1)}, u32[]{:S(2)}, u32[]{:S(2)}) collective-permute-start(bf16[64,2048]{1,0:T(8,128)(2,1)S(1)} %attend.5.refs_1_.rest_4_.rest_0_), channel_id=1, source_target_pairs={{0,4},{4,0},{8,12},{12,8},{1,5},{5,1},{9,13},{13,9},{2,6},{6,2},{1... | collective-permute-start | bytes 786440 | tf_op jit(solution)/shard_map/ppermute | solution.py:383
  82.3 9.0 %copy-start.4 = (bf16[48,1792]{1,0:T(8,128)(2,1)S(1)}, bf16[48,1792]{1,0:T(8,128)(2,1)}, u32[]{:S(2)}) copy-start(bf16[48,1792]{1,0:T(8,128)(2,1)} %copy-done.3) | copy-start | bytes 516100
  82.5 8.8 %collective-permute-start.20 = (bf16[64,2048]{1,0:T(8,128)(2,1)S(1)}, bf16[64,2048]{1,0:T(8,128)(2,1)S(1)}, u32[]{:S(2)}, u32[]{:S(2)}) collective-permute-start(bf16[64,2048]{1,0:T(8,128)(2,1)S(1)} %stack.7), channel_id=1, source_target_pairs={{0,4},{4,0},{8,12},{12,8},{1,5},{5,1},{9,13},{13,9},{2,6},{6,2},{1... | collective-permute-start | bytes 786440 | tf_op jit(solution)/shard_map/ppermute | solution.py:383
  83.0 8.2 %collective-permute-start.14 = (bf16[48,1792]{1,0:T(8,128)(2,1)S(1)}, bf16[48,1792]{1,0:T(8,128)(2,1)S(1)}, u32[]{:S(2)}, u32[]{:S(2)}) collective-permute-start(bf16[48,1792]{1,0:T(8,128)(2,1)S(1)} %add.23.refs_2_), channel_id=1, source_target_pairs={{1,0},{2,3},{5,4},{6,7},{9,8},{10,11},{13,12},{14,15},{17,16},{18,... | collective-permute-start | bytes 516104 | tf_op jit(solution)/shard_map/ppermute | solution.py:542
  84.3 12.1 %collective-permute-start.16 = (bf16[128,1792]{1,0:T(8,128)(2,1)S(1)}, bf16[128,1792]{1,0:T(8,128)(2,1)S(1)}, u32[]{:S(2)}, u32[]{:S(2)}) collective-permute-start(bf16[128,1792]{1,0:T(8,128)(2,1)S(1)} %add.24.refs_4_.refs_1_), channel_id=1, source_target_pairs={{1,2},{2,1},{5,6},{6,5},{9,10},{10,9},{13,14},{14,13},{17,18},{18,... | collective-permute-start | bytes 1376264 | tf_op jit(solution)/shard_map/ppermute | solution.py:539
  94.0 12.0 %collective-permute-start.22 = (bf16[128,1792]{1,0:T(8,128)(2,1)S(1)}, bf16[128,1792]{1,0:T(8,128)(2,1)S(1)}, u32[]{:S(2)}, u32[]{:S(2)}) collective-permute-start(bf16[128,1792]{1,0:T(8,128)(2,1)S(1)} %get-tuple-element.47.refs_0_), channel_id=1, source_target_pairs={{0,1},{3,2},{4,5},{7,6},{8,9},{11,10},{12,13},{15,14},{16,17},{19,... | collective-permute-start | bytes 1376264 | tf_op jit(solution)/shard_map/ppermute | solution.py:536
  95.7 12.1 %collective-permute-start.24 = (bf16[160,1792]{1,0:T(8,128)(2,1)S(1)}, bf16[160,1792]{1,0:T(8,128)(2,1)S(1)}, u32[]{:S(2)}, u32[]{:S(2)}) collective-permute-start(bf16[160,1792]{1,0:T(8,128)(2,1)S(1)} %add.26.refs_2_), channel_id=1, source_target_pairs={{1,2},{2,1},{5,6},{6,5},{9,10},{10,9},{13,14},{14,13},{17,18},{18,... | collective-permute-start | bytes 1720328 | tf_op jit(solution)/shard_map/ppermute | solution.py:539
  96.4 11.2 %collective-permute-start.21 = (bf16[64,1792]{1,0:T(8,128)(2,1)S(1)}, bf16[64,1792]{1,0:T(8,128)(2,1)S(1)}, u32[]{:S(2)}, u32[]{:S(2)}) collective-permute-start(bf16[64,1792]{1,0:T(8,128)(2,1)S(1)} %add.27.refs_2_), channel_id=1, source_target_pairs={{1,0},{2,3},{5,4},{6,7},{9,8},{10,11},{13,12},{14,15},{17,16},{18,... | collective-permute-start | bytes 688136 | tf_op jit(solution)/shard_map/ppermute | solution.py:542
  97.7 18.0 %collective-permute-start.23 = (bf16[144,1792]{1,0:T(8,128)(2,1)S(1)}, bf16[144,1792]{1,0:T(8,128)(2,1)S(1)}, u32[]{:S(2)}, u32[]{:S(2)}) collective-permute-start(bf16[144,1792]{1,0:T(8,128)(2,1)S(1)} %get-tuple-element.48.refs_0_), channel_id=1, source_target_pairs={{0,1},{3,2},{4,5},{7,6},{8,9},{11,10},{12,13},{15,14},{16,17},{19,... | collective-permute-start | bytes 1548296 | tf_op jit(solution)/shard_map/ppermute | solution.py:536
  106.1 3.7 %collective-permute-start.26 = (bf16[64,1792]{1,0:T(8,128)(2,1)S(1)}, bf16[64,1792]{1,0:T(8,128)(2,1)S(1)}, u32[]{:S(2)}, u32[]{:S(2)}) collective-permute-start(bf16[64,1792]{1,0:T(8,128)(2,1)S(1)} %add.28.refs_4_), channel_id=1, source_target_pairs={{1,2},{2,1},{5,6},{6,5},{9,10},{10,9},{13,14},{14,13},{17,18},{18,... | collective-permute-start | bytes 688136 | tf_op jit(solution)/shard_map/ppermute | solution.py:539
  107.9 13.8 %collective-permute-start.25 = (bf16[80,1792]{1,0:T(8,128)(2,1)S(1)}, bf16[80,1792]{1,0:T(8,128)(2,1)S(1)}, u32[]{:S(2)}, u32[]{:S(2)}) collective-permute-start(bf16[80,1792]{1,0:T(8,128)(2,1)S(1)} %add.31.refs_2_), channel_id=1, source_target_pairs={{1,0},{2,3},{5,4},{6,7},{9,8},{10,11},{13,12},{14,15},{17,16},{18,... | collective-permute-start | bytes 860168 | tf_op jit(solution)/shard_map/ppermute | solution.py:542
  109.2 12.6 %collective-permute-start.27 = (bf16[64,1792]{1,0:T(8,128)(2,1)S(1)}, bf16[64,1792]{1,0:T(8,128)(2,1)S(1)}, u32[]{:S(2)}, u32[]{:S(2)}) collective-permute-start(bf16[64,1792]{1,0:T(8,128)(2,1)S(1)} %add.30.refs_2_), channel_id=1, source_target_pairs={{1,2},{2,1},{5,6},{6,5},{9,10},{10,9},{13,14},{14,13},{17,18},{18,... | collective-permute-start | bytes 688136 | tf_op jit(solution)/shard_map/ppermute | solution.py:539
  109.9 15.5 %collective-permute-start.28 = (bf16[64,1792]{1,0:T(8,128)(2,1)S(1)}, bf16[64,1792]{1,0:T(8,128)(2,1)S(1)}, u32[]{:S(2)}, u32[]{:S(2)}) collective-permute-start(bf16[64,1792]{1,0:T(8,128)(2,1)S(1)} %add.32.refs_4_), channel_id=1, source_target_pairs={{1,0},{2,3},{5,4},{6,7},{9,8},{10,11},{13,12},{14,15},{17,16},{18,... | collective-permute-start | bytes 688136 | tf_op jit(solution)/shard_map/ppermute | solution.py:542

commit v5 on v4

--- a/solution.py
+++ b/solution.py
@@ -11,6 +11,7 @@
 HIDDEN = -1e30
 LANES = 128
 MIB = 1024 * 1024
+WEIGHT_PIECES = 16
 
 SMEM = pl.BlockSpec(memory_space=pltpu.SMEM)
 VMEM = pl.BlockSpec(memory_space=pltpu.VMEM)
@@ -44,7 +45,8 @@
 
 
 def build_queries(q, q_nope, q_rope, first, wk, ready=None):
-    heads, t, _ = q_nope.shape
+    heads = q_nope.shape[0]
+    t = q.shape[0] // heads
     latent = wk.shape[2]
     rope_dim = q_rope.shape[1] // heads
     lane = lax.broadcasted_iota(jnp.int32, (t, LANES), 1)
@@ -59,7 +61,7 @@
     for h in range(heads):
         if ready is not None:
             ready(h)
-        q[h * t:(h + 1) * t, :latent] = dot(q_nope[h], wk[h]).astype(jnp.bfloat16)
+        q[h * t:(h + 1) * t, :latent] = dot(q_nope[h, first:first + t, :], wk[h]).astype(jnp.bfloat16)
 
 
 def prefill(q, keys, att, heads, t, first, prior, fresh, exp_scale):
@@ -99,10 +101,10 @@
         out[:, h * dv:(h + 1) * dv] = dot(att[h * t:(h + 1) * t, :], wv[h]).astype(jnp.bfloat16)
 
 
-def first_kernel(fresh, exp_scale, table, offset, q_nope, q_nope_hbm, q_rope_hbm, wk_hbm, wv_hbm,
-                 cache_latent, cache_rope, new_latent, new_rope_t, out, keys, wk, wv, q_nope_out,
-                 q_rope, q, att, sems, wsems):
-    heads, t, _ = q_nope.shape
+def first_kernel(fresh, exp_scale, table, offset, q_nope, q_rope_hbm, wk_hbm, wv_hbm, cache_latent,
+                 cache_rope, new_latent, new_rope_t, out, keys, wk, wv, q_rope, q, att, sems, wsems):
+    heads = q_nope.shape[0]
+    t = out.shape[0]
     block_len, latent = cache_latent.shape[1:]
     rope_dim = new_rope_t.shape[0]
     blocks = table.shape[1]
@@ -127,15 +129,15 @@
         new_latent, keys.at[pl.ds(prior, tok_group), pl.ds(0, latent)], sems.at[2 * blocks]))
     for c in copies:
         c.start()
-    wv_copy = pltpu.make_async_copy(wv_hbm, wv, sems.at[2 * blocks + 1])
-    wv_copy.start()
-    others = [pltpu.make_async_copy(q_nope_hbm, q_nope_out, wsems.at[heads + 1])]
+    wv_copies = [
+        pltpu.make_async_copy(wv_hbm.at[h], wv.at[h], wsems.at[1 + heads + h]) for h in range(heads)]
+    for c in wv_copies:
+        c.start()
     if t < tok_group:
-        others.append(pltpu.make_async_copy(
+        others = pltpu.make_async_copy(
             q_rope_hbm.at[pl.ds(t, tok_group - t)], q_rope.at[pl.ds(t, tok_group - t)],
-            wsems.at[heads + 2]))
-    for c in others:
-        c.start()
+            sems.at[2 * blocks + 1])
+        others.start()
 
     keys[prior:, latent:] = rope_rows(new_rope_t[...])
     rope_copy.wait()
@@ -148,32 +150,37 @@
     hide = jnp.where((lane == rope_dim) & (pos >= offset[0]), HIDDEN, 0.0)
     keys[:prior, latent:] = (keys[:prior, latent:].astype(jnp.float32) + hide).astype(jnp.bfloat16)
     prefill(q, keys, att, heads, t, 0, prior, fresh, exp_scale)
-    wv_copy.wait()
+    for c in wv_copies:
+        c.wait()
     head_outputs(out, att, wv, t)
-    for c in others:
-        c.wait()
+    if t < tok_group:
+        others.wait()
 
 
 def second_kernel(first, fresh, prior, exp_scale, n_after, me, ids, q_nope, q_rope, wk, wv, keys, w_hbm,
                   cache_latent, cache_rope, *rest):
     rest = rest[n_after:]
-    groups = ids.shape[1]
+    groups = ids.shape[2]
     out, w, packed = rest[0], rest[1], rest[2:2 + groups]
     q, att, sems = rest[2 + groups:]
-    heads, t, _ = q_nope.shape
+    heads = q_nope.shape[0]
+    t = out.shape[0]
     block_len, latent = cache_latent.shape[1:]
-    capacity = ids.shape[2]
+    capacity = ids.shape[1]
     copies = []
     for s in range(groups):
         to = lax.rem(me[0] + s, groups)
         for k in range(capacity):
-            b = ids[0, to, k]
+            b = ids[0, k, to]
             rows = pl.ds(k * block_len, block_len)
             copies.append(pltpu.make_async_copy(
                 cache_latent.at[b], packed[s].at[rows, pl.ds(0, latent)], sems.at[len(copies)]))
             copies.append(pltpu.make_async_copy(
                 cache_rope.at[b], packed[s].at[rows, pl.ds(latent, LANES)], sems.at[len(copies)]))
-    copies.append(pltpu.make_async_copy(w_hbm, w, sems.at[len(copies)]))
+    depth = w.shape[0] // WEIGHT_PIECES
+    for i in range(WEIGHT_PIECES):
+        rows = pl.ds(i * depth, depth)
+        copies.append(pltpu.make_async_copy(w_hbm.at[rows], w.at[rows], sems.at[len(copies)]))
     for c in copies:
         c.start()
     build_queries(q, q_nope, q_rope, first, wk)
@@ -185,7 +192,8 @@
 
 def later_kernel(first, fresh, prior, exp_scale, n_after, q_nope, q_rope, wk, wv, keys, *rest):
     out, q, att = rest[n_after:]
-    heads, t, _ = q_nope.shape
+    heads = q_nope.shape[0]
+    t = out.shape[0]
     build_queries(q, q_nope, q_rope, first, wk)
     prefill(q, keys, att, heads, t, first, prior, fresh, exp_scale)
     head_outputs(out, att, wv, t)
@@ -196,7 +204,8 @@
     received = rest[:-5 - n_after]
     out, q, att, dkeys, sems = rest[-5:]
     groups = len(received)
-    heads, t, _ = q_nope.shape
+    heads = q_nope.shape[0]
+    t = out.shape[0]
     pool, block_len, latent = cache_latent.shape
     got = received[0].shape[0]
     ext = pool * block_len + groups * got
@@ -220,7 +229,7 @@
     build_queries(q, q_nope, q_rope, first, wk)
     prefill(q, keys, att, heads, t, first, prior, fresh, exp_scale)
 
-    decodes = decode_table.shape[0]
+    slots, decodes = decode_table.shape
     for c in copies:
         c.wait()
     span = dkeys.shape[0]
@@ -230,9 +239,18 @@
     pos = key % block_len
     own_key = key - ext + (start - prior) == request + prefill_len
     count = jnp.where(own_key, 1.0, 0.0)
-    for m in range(decode_table.shape[1]):
-        hit = (block == decode_table[:, m:m + 1]) & (
-            pos + m * block_len < decode_length[:, 0:1]) & (key < ext)
+    row = lax.broadcasted_iota(jnp.int32, (decodes, LANES), 0)
+
+    def column(read):
+        value = jnp.zeros((decodes, LANES), jnp.int32)
+        for r in range(decodes):
+            value = jnp.where(row == r, read(r), value)
+        return value[:, :1]
+
+    length = column(lambda r: decode_length[r])
+    for m in range(slots):
+        hit = (block == column(lambda r: decode_table[m, r])) & (pos + m * block_len < length) & (
+            key < ext)
         count = count + jnp.where(hit, 1.0, 0.0)
     count = count[None]
     at = prefill_len - first
@@ -260,18 +278,19 @@
     return pltpu.with_memory_space_constraint(x, pltpu.HBM)
 
 
-def project_kernel(n_parts, tails, place, w, *rest):
+def project_kernel(n_parts, tails, places, me, z, w, *rest):
     parts, rest, x = rest[:n_parts], rest[n_parts:], rest[-1]
     own, outs = rest[-2 - len(tails)], rest[-1 - len(tails):-1]
     t = own.shape[0]
     lead = outs[-1].shape[0] - tails[-1] * t
     if lead:
         outs[-1][:lead, :] = rest[0][...]
-    i = 0
-    for part in parts:
-        for at in range(0, part.shape[0], t):
-            x[pl.ds(pl.multiple_of(place[i] * t, t), t), :] = part[at:at + t, :]
-            i += 1
+    for i, part in enumerate(parts):
+        place = 0
+        for g, row in enumerate(places):
+            for p, column in enumerate(row):
+                place = jnp.where((me[0] == g) & (z[0] == p), column[i], place)
+        x[pl.ds(pl.multiple_of(place * t, t), t), :] = part[...]
     columns = w.shape[1]
     step = 256 if columns % 256 == 0 else columns
     for at in range(0, columns, step):
@@ -284,22 +303,23 @@
             row += n * t
 
 
-def project(place, parts, w, tails, earlier=(), after=()):
+def project(where, parts, w, tails, earlier=(), after=()):
     depth, columns = w.shape
     rows = sum(p.shape[0] for p in parts)
     t = rows // (1 + sum(tails))
     sizes = [t] + [n * t for n in tails]
     sizes[-1] += sum(e.shape[0] for e in earlier)
+    places, me, z = where
     return pl.pallas_call(
-        functools.partial(project_kernel, len(parts), tails),
+        functools.partial(project_kernel, len(parts), tails, places),
         out_shape=[jax.ShapeDtypeStruct((n, columns), jnp.bfloat16) for n in sizes],
-        in_specs=[SMEM, VMEM] + [VMEM] * (len(parts) + len(earlier)) + [ANY] * len(after),
+        in_specs=[SMEM, SMEM, VMEM] + [VMEM] * (len(parts) + len(earlier)) + [ANY] * len(after),
         out_specs=[VMEM] * len(sizes),
         scratch_shapes=[pltpu.VMEM((rows, depth), jnp.bfloat16)],
         name="project",
         compiler_params=params(12),
         cost_estimate=COST,
-    )(place, w, *parts, *earlier, *after)
+    )(me[None], z[None], w, *parts, *earlier, *after)
 
 
 def add_kernel(spans, n_after, *refs):
@@ -422,17 +442,19 @@
     bf16 = jnp.bfloat16
 
     me = lax.axis_index("dp")
-    ids = np.array([gathered_ids(groups, g) for g in range(groups)], np.int32)
-    if on_line:
-        places = np.argsort(np.array(LINE_ORDER), axis=1)[None, :, :]
-        places = np.take_along_axis(
-            np.broadcast_to(places, (4, 4, 4)), np.broadcast_to(ids[:, None, :], (4, 4, 4)), axis=2)
-        place = jnp.asarray(places.astype(np.int32))[me, lax.axis_index("tp")]
-    else:
-        place = jnp.asarray(ids)[me]
+    z = lax.axis_index("tp")
+    places = []
+    for g in range(groups):
+        came = gathered_ids(groups, g)
+        if on_line:
+            places.append([[order.index(k) for k in came] for order in LINE_ORDER])
+        else:
+            places.append([came])
+    where = (places, me, z if on_line else z * 0)
 
     padded_rope = jnp.pad(
         cache_rope.reshape(pool, block_len, rope_dim), ((0, 0), (0, 0), (0, LANES - rope_dim)))
+    q_nope = query_nope.transpose(1, 0, 2)
     sizes = chunk_sizes(tok_group)
     starts = [sum(sizes[:i]) for i in range(len(sizes))]
 
@@ -445,33 +467,30 @@
 
     def first_chunk():
         t = sizes[0]
-        q_nope = query_nope[:t].transpose(1, 0, 2)
         return pl.pallas_call(
             functools.partial(first_kernel, fresh_of(0), exp_scale),
             out_shape=[jax.ShapeDtypeStruct((t, heads * dv), bf16),
                        jax.ShapeDtypeStruct((prior + tok_group, width), bf16),
                        jax.ShapeDtypeStruct(absorb_key.shape, bf16),
                        jax.ShapeDtypeStruct(absorb_value.shape, bf16),
-                       jax.ShapeDtypeStruct(query_nope.shape, bf16),
                        jax.ShapeDtypeStruct(query_rope.shape, bf16)],
-            in_specs=[SMEM, SMEM, VMEM, HBM, HBM, HBM, HBM, HBM, ANY, HBM, VMEM],
-            out_specs=[VMEM] * 6,
+            in_specs=[SMEM, SMEM, VMEM, HBM, HBM, HBM, HBM, ANY, HBM, VMEM],
+            out_specs=[VMEM] * 5,
             scratch_shapes=[
                 *scratch(t),
                 pltpu.SemaphoreType.DMA((2 * blocks + 2,)),
-                pltpu.SemaphoreType.DMA((heads + 3,)),
+                pltpu.SemaphoreType.DMA((2 * heads + 1,)),
             ],
             name="attend_first",
             compiler_params=params(20),
             cost_estimate=LONG,
-        )(prefill_table, prefill_offset, q_nope, in_hbm(query_nope), in_hbm(query_rope),
-          in_hbm(absorb_key), in_hbm(absorb_value), in_hbm(cache_latent), padded_rope,
+        )(prefill_table, prefill_offset, q_nope, in_hbm(query_rope), in_hbm(absorb_key),
+          in_hbm(absorb_value), in_hbm(cache_latent), padded_rope,
           in_hbm(new_latent), new_rope.T)
 
     def attend(n, held, after, brought=None):
-        keys, wk, wv, q_nope, q_rope = held
+        keys, wk, wv, q_rope = held
         t = sizes[n]
-        q_nope = q_nope[starts[n]:starts[n] + t].transpose(1, 0, 2)
         args = [q_nope, q_rope, wk, wv, keys]
         specs = [VMEM] * 5
         outs = [jax.ShapeDtypeStruct((t, heads * dv), bf16)]
@@ -480,17 +499,17 @@
         static = (starts[n], fresh_of(n), prior)
         if n == 1:
             kernel = functools.partial(second_kernel, *static, exp_scale, len(after))
-            args = [me[None], send_blocks] + args + [
+            args = [me[None], send_blocks.transpose(0, 2, 1)] + args + [
                 in_hbm(output_weight), in_hbm(cache_latent), padded_rope]
             specs = [SMEM, SMEM] + specs + [HBM, HBM, ANY]
             outs.append(jax.ShapeDtypeStruct(output_weight.shape, bf16))
             outs += [jax.ShapeDtypeStruct((capacity * block_len, width), bf16)] * groups
-            scratches.append(pltpu.SemaphoreType.DMA((2 * groups * capacity + 1,)))
+            scratches.append(pltpu.SemaphoreType.DMA((2 * groups * capacity + WEIGHT_PIECES,)))
         elif n == len(sizes) - 1:
             kernel = functools.partial(last_kernel, *static, prefill_len, exp_scale, len(after))
             args = [me[None]] + args + [
-                in_hbm(cache_latent), padded_rope, decode_table, decode_length[:, None], *brought]
-            specs = [SMEM] + specs + [HBM, ANY, VMEM, VMEM] + [VMEM] * len(brought)
+                in_hbm(cache_latent), padded_rope, decode_table.T, decode_length, *brought]
+            specs = [SMEM] + specs + [HBM, ANY, SMEM, SMEM] + [VMEM] * len(brought)
             span = pool * block_len + groups * capacity * block_len + min(LANES, tok_group)
             scratches += [pltpu.VMEM((span, width), bf16), pltpu.SemaphoreType.DMA((2 * pool,))]
             limit = 26
@@ -527,7 +546,7 @@
             mine = shift_groups(x)
             if groups % 2 == 0:
                 mine += [swap_cores(y) for y in mine]
-            own, others = project(place, mine, output_weight, (groups - 1,))
+            own, others = project(where, mine, output_weight, (groups - 1,))
             partials = jnp.concatenate([own, others], axis=0).reshape(groups, t, columns)
             outs.append(lax.psum_scatter(partials, "tp", scatter_dimension=0, tiled=False))
         return jnp.concatenate(outs, axis=0)
@@ -547,16 +566,16 @@
 
     t0, t1, t2, t3 = sizes
     x1, w, *packed = attend(1, held, (x0,))
-    own0, rest0 = project(place, gather(x0, (x1,)), w, (3,), (), (x1,))
+    own0, rest0 = project(where, gather(x0, (x1,)), w, (3,), (), (x1,))
     in0 = inward(rest0)
     brought = migrate(packed)
     x2, = attend(2, held, (own0,))
-    own1, rest1 = project(place, gather(x1, (x2,)), w, (3,), (), (x2,))
+    own1, rest1 = project(where, gather(x1, (x2,)), w, (3,), (), (x2,))
     in1 = inward(rest1)
     to_across0 = add(2 * t0, [(rest0, 0), (in0, 0)], (own1,))
     on0 = across(to_across0)
     x3, = attend(3, held, (to_across0,), brought)
-    own2, rest2, near2 = project(place, gather(x2, (x3,)), w, (2, 1), (), (x3,))
+    own2, rest2, near2 = project(where, gather(x2, (x3,)), w, (2, 1), (), (x3,))
     in2 = inward(rest2)
     to_across1 = add(2 * t1, [(rest1, 0), (in1, 0)], (own2,))
     on1 = across(to_across1)
@@ -564,7 +583,7 @@
     out0 = outward(to_out0)
     done0 = add(t0, [(own0, 0), (in0, 2 * t0), (on0, t0), (out0, 0)], (to_across1,))
     own3, rest3, near = project(
-        place, gather(x3, (to_across1, to_out0)), w, (2, 1), (near2,), (done0,))
+        where, gather(x3, (to_across1, to_out0)), w, (2, 1), (near2,), (done0,))
     in3 = inward(rest3)
     to_across2 = add(2 * t2, [(rest2, 0), (in2, 0)], (own3,))
     on2 = across(to_across2)

time: 127 us -> 125 us (0.984)
  local copies, waits for them, and re-layouts: 22.8 us -> 19.9 us
  starting transfers between devices: 38.2 us -> 40.4 us
  Pallas kernels: 42.7 us -> 40.6 us
    ppermute x5, starting transfers between devices: 19.1 us -> 22.1 us  [inward(): return lax.ppermute(x, 'tp', INWARD)]
    pallas_call x4, Pallas kernels: 10.7 us -> 9.08 us  [project(): pl.pallas_call(functools.partial(project_kernel, len(parts), tails, place...]
    unnamed x63 -> x57, local copies, waits for them, and re-layouts: 18.2 us -> 19.2 us
  transfers between devices with their start and end apart: 29 -> 29, of which waited for: 7 -> 6; matrix products, arithmetic and copies ran while one was open for 2% -> 0% of each run, Pallas kernels for 27% -> 25%
where the time goes in v5:
time: 125 us; the launch traced here: 124 us
  Pallas kernels  40.6 us (32%)
  starting transfers between devices  40.4 us (32%)
  waiting for transfers between devices  22.3 us (18%)
  local copies, waits for them, and re-layouts  19.9 us (16%)
  between operations  1.25 us (1%)
    ppermute x5, starting transfers between devices, inward(): return lax.ppermute(x, 'tp', INWARD)  22.1 us
    pallas_call x3, Pallas kernels, attend(): pl.pallas_call(kernel, out_shape=outs, in_specs=specs + [ANY] * len(after...  21.5 us
    unnamed x57, local copies, waits for them, and re-layouts  19.2 us
    ppermute x4, waiting for transfers between devices, outward(): return lax.ppermute(x, 'tp', OUTWARD)  17 us
    pallas_call x4, Pallas kernels, project(): pl.pallas_call(functools.partial(project_kernel, len(parts), tails, place...  9.08 us
    pallas_call x1, Pallas kernels, first_chunk(): pl.pallas_call(functools.partial(first_kernel, fresh_of(0), exp_scale), o...  7.79 us
    ppermute x4, starting transfers between devices, outward(): return lax.ppermute(x, 'tp', OUTWARD)  5.16 us
    ppermute x4, starting transfers between devices, shift_groups(): lax.ppermute(x, 'dp', [(i, (i + s) % groups) for i in range(groups)])  4.86 us
  transfers between devices with their start and end apart: 29, of which 6 were waited for; matrix products, arithmetic and copies ran while one was open for 0% of the time, Pallas kernels for 25%

profile of v5, /device:TPU:0, one launch (start us, length us, event | category | flops | bytes accessed | tf_op | source)
XLA Modules:
  0.0 124.4 jit_solution(7348160064093716788)
XLA Ops:
  0.0 1.5 %copy.17 = bf16[256,16,128]{2,0,1:T(8,128)(2,1)S(1)} copy(bf16[256,16,128]{2,1,0:T(8,128)(2,1)} %param.14) | data formatting | bytes 2097152 | tf_op args[0]
  1.6 0.5 reshape.3
  2.8 0.1 pad.4.cache_rope
  2.9 7.8 %attend_first.1 = (bf16[48,2048]{1,0:T(8,128)(2,1)S(1)}, bf16[1280,640]{1,0:T(8,128)(2,1)S(1)}, bf16[16,128,512]{2,1,0:T(8,128)(2,1)S(1)}, bf16[16,512,128]{2,1,0:T(8,128)(2,1)S(1)}, bf16[256,1024]{1,0:T(8,128)(2,1)S(1)}) custom-call(s32[1,16]{1,0:T(1,128)S(1)} %copy-done.9, s32[1]{0:T(128)S(6)} %copy.18.offset, bf16[16,256,128]{2,1,0:T(8,128)(2,1)S(1)} %bitcast.10, ...), custom_call_target="tpu_custom_call" | custom-call | flops 40000000000 | bytes 1000 | tf_op jit(solution)/shard_map/attend_first/pallas_call | solution.py:470
  10.7 1.4 %copy-done.11 = bf16[16,128,512]{2,1,0:T(8,128)(2,1)} copy-done((bf16[16,128,512]{2,1,0:T(8,128)(2,1)}, bf16[16,128,512]{2,1,0:T(8,128)(2,1)S(1)}, u32[]{:S(2)}) %copy-start.11) | copy-done | bytes 2097176
  12.1 1.3 %copy-done.14 = bf16[16,512,128]{2,1,0:T(8,128)(2,1)} copy-done((bf16[16,512,128]{2,1,0:T(8,128)(2,1)}, bf16[16,512,128]{2,1,0:T(8,128)(2,1)S(1)}, u32[]{:S(2)}) %copy-start.14) | copy-done | bytes 2097176
  13.4 1.2 copy-done.17
  14.6 0.8 copy-done.20
  15.4 2.9 %collective-permute-start = (bf16[48,2048]{1,0:T(8,128)(2,1)S(1)}, bf16[48,2048]{1,0:T(8,128)(2,1)S(1)}, u32[]{:S(2)}, u32[]{:S(2)}) collective-permute-start(bf16[48,2048]{1,0:T(8,128)(2,1)S(1)} %get-tuple-element.30.rest_0_), channel_id=1, source_target_pairs={{0,8},{4,12},{8,0},{12,4},{1,9},{5,13},{9,1},{13,5},{2,10},{6,14},... | collective-permute-start | bytes 589832 | tf_op jit(solution)/shard_map/ppermute | solution.py:378
  18.4 1.6 %copy-done.12 = bf16[16,128,512]{2,1,0:T(8,128)(2,1)S(1)} copy-done((bf16[16,128,512]{2,1,0:T(8,128)(2,1)S(1)}, bf16[16,128,512]{2,1,0:T(8,128)(2,1)}, u32[]{:S(2)}) %copy-start.12) | copy-done | bytes 2097176
  20.0 1.6 %copy-done.15 = bf16[16,512,128]{2,1,0:T(8,128)(2,1)S(1)} copy-done((bf16[16,512,128]{2,1,0:T(8,128)(2,1)S(1)}, bf16[16,512,128]{2,1,0:T(8,128)(2,1)}, u32[]{:S(2)}) %copy-start.15) | copy-done | bytes 2097176
  21.6 1.4 %copy-done.18 = bf16[1280,640]{1,0:T(8,128)(2,1)S(1)} copy-done((bf16[1280,640]{1,0:T(8,128)(2,1)S(1)}, bf16[1280,640]{1,0:T(8,128)(2,1)}, u32[]{:S(2)}) %copy-start.18) | copy-done | bytes 1638424
  23.0 1.0 copy-done.21
  24.0 6.1 %attend.3 = (bf16[64,2048]{1,0:T(8,128)(2,1)S(1)}, bf16[2048,1792]{1,0:T(8,128)(2,1)S(1)}, bf16[128,640]{1,0:T(8,128)(2,1)S(1)}, bf16[128,640]{1,0:T(8,128)(2,1)...) custom-call(s32[1]{0:T(128)} %bitcast.me, s32[1,2,4]{2,1,0:T(2,128)S(1)} %bitcast.16, ...), custom_call_target="tpu_custom_call" | custom-call | flops 40000000000 | bytes 1000 | tf_op jit(solution)/shard_map/attend/pallas_call | solution.py:518
  30.2 2.9 %copy-done = bf16[2048,1792]{1,0:T(8,128)(2,1)} copy-done((bf16[2048,1792]{1,0:T(8,128)(2,1)}, bf16[2048,1792]{1,0:T(8,128)(2,1)S(1)}, u32[]{:S(2)}) %copy-start) | copy-done | bytes 7340056
  33.1 0.7 copy-done.2
  33.8 0.6 copy-done.23
  34.4 0.5 collective-permute-start.2
  35.0 1.0 collective-permute-done.2.rest_3_
  36.0 3.1 %copy-done.1 = bf16[2048,1792]{1,0:T(8,128)(2,1)S(1)} copy-done((bf16[2048,1792]{1,0:T(8,128)(2,1)S(1)}, bf16[2048,1792]{1,0:T(8,128)(2,1)}, u32[]{:S(2)}) %copy-start.1) | copy-done | bytes 7340056
  39.1 1.7 %project.4 = (bf16[48,1792]{1,0:T(8,128)(2,1)S(1)}, bf16[144,1792]{1,0:T(8,128)(2,1)S(1)}) custom-call(s32[1]{0:T(128)} %bitcast.me, s32[1]{0:T(128)} %bitcast.1.z, bf16[2048,1792]{1,0:T(8,128)(2,1)S(1)} %copy-done.1, bf16[48,2048]{1,0:T(8,128)(2,1)S(1)} %get-tuple-element.30.rest_0_, bf16[48,2048]{1,0:T(8,128)(2,1)S(1)} %collective-permute-done.refs_0_.rest_1_, ...), custom_call_target="tpu_custom_call" | custom-call | flops 1000 | bytes 1000 | tf_op jit(solution)/shard_map/project/pallas_call | solution.py:313
  40.9 3.8 %collective-permute-start.3 = (bf16[144,1792]{1,0:T(8,128)(2,1)S(1)}, bf16[144,1792]{1,0:T(8,128)(2,1)S(1)}, u32[]{:S(2)}, u32[]{:S(2)}) collective-permute-start(bf16[144,1792]{1,0:T(8,128)(2,1)S(1)} %get-tuple-element.34.refs_0_), channel_id=1, source_target_pairs={{0,1},{3,2},{4,5},{7,6},{8,9},{11,10},{12,13},{15,14},{16,17},{19,... | collective-permute-start | bytes 1548296 | tf_op jit(solution)/shard_map/ppermute | solution.py:555
  44.8 5.5 %attend.4.refs_1_.rest_4_.rest_0_ = bf16[80,2048]{1,0:T(8,128)(2,1)S(1)} custom-call(bf16[16,256,128]{2,1,0:T(8,128)(2,1)S(1)} %bitcast.12, bf16[256,1024]{1,0:T(8,128)(2,1)S(1)} %copy-done.22, bf16[16,128,512]{2,1,0:T(8,128)(2,1)S(1)} %copy-done.13, bf16[16,512,128]{2,1,0:T(8,128)(2,1)S(1)} %copy-done.16, bf16[1280,640]{1,0:T(8,128)(2,1)S(1)} %copy-done.19, ...), custom_call_target="tpu_custom_call" | custom-call | flops 40000000000 | bytes 1000 | tf_op jit(solution)/shard_map/attend/pallas_call | solution.py:518
  50.3 0.1 collective-permute-start.6
  50.4 0.4 collective-permute-start.10
  50.9 1.0 collective-permute-start.11
  51.8 1.2 collective-permute-start.12
  53.1 0.9 collective-permute-start.8
  54.0 2.3 %project.5 = (bf16[64,1792]{1,0:T(8,128)(2,1)S(1)}, bf16[192,1792]{1,0:T(8,128)(2,1)S(1)}) custom-call(s32[1]{0:T(128)} %bitcast.me, s32[1]{0:T(128)} %bitcast.1.z, bf16[2048,1792]{1,0:T(8,128)(2,1)S(1)} %bitcast.9, bf16[64,2048]{1,0:T(8,128)(2,1)S(1)} %get-tuple-element.32.refs_1_.rest_4_.rest_0_, ...), custom_call_target="tpu_custom_call" | custom-call | flops 1000 | bytes 1000 | tf_op jit(solution)/shard_map/project/pallas_call | solution.py:313
  56.3 0.1 collective-permute-start.9
  56.4 0.1 add.14.rest_4_
  56.5 4.3 %collective-permute-start.15 = (bf16[192,1792]{1,0:T(8,128)(2,1)S(1)}, bf16[192,1792]{1,0:T(8,128)(2,1)S(1)}, u32[]{:S(2)}, u32[]{:S(2)}) collective-permute-start(bf16[192,1792]{1,0:T(8,128)(2,1)S(1)} %get-tuple-element.41.refs_0_), channel_id=1, source_target_pairs={{0,1},{3,2},{4,5},{7,6},{8,9},{11,10},{12,13},{15,14},{16,17},{19,... | collective-permute-start | bytes 2064392 | tf_op jit(solution)/shard_map/ppermute | solution.py:555
  60.8 9.8 %attend.5.refs_1_.rest_4_.rest_0_ = bf16[64,2048]{1,0:T(8,128)(2,1)S(1)} custom-call(s32[1]{0:T(128)} %bitcast.me, bf16[16,256,128]{2,1,0:T(8,128)(2,1)S(1)} %bitcast.13, bf16[256,1024]{1,0:T(8,128)(2,1)S(1)} %copy-done.22, bf16[16,128,512]{2,1,0:T(8,128)(2,1)S(1)} %copy-done.13, bf16[16,512,128]{2,1,0:T(8,128)(2,1)S(1)} %copy-done.16, ...), custom_call_target="tpu_custom_call" | custom-call | flops 40000000000 | bytes 1000 | tf_op jit(solution)/shard_map/attend/pallas_call | solution.py:518
  70.7 0.6 collective-permute-start.13
  71.3 0.7 collective-permute-start.7
  71.9 1.0 collective-permute-start.18
  72.9 2.8 %project.6 = (bf16[80,1792]{1,0:T(8,128)(2,1)S(1)}, bf16[160,1792]{1,0:T(8,128)(2,1)S(1)}, bf16[80,1792]{1,0:T(8,128)(2,1)S(1)}) custom-call(s32[1]{0:T(128)} %bitcast.me, s32[1]{0:T(128)} %bitcast.1.z, bf16[2048,1792]{1,0:T(8,128)(2,1)S(1)} %bitcast.9, bf16[80,2048]{1,0:T(8,128)(2,1)S(1)} %attend.4.refs_1_.rest_4_.rest_0_, ...), custom_call_target="tpu_custom_call" | custom-call | flops 1000 | bytes 1000 | tf_op jit(solution)/shard_map/project/pallas_call | solution.py:313
  75.7 4.3 %collective-permute-start.17 = (bf16[160,1792]{1,0:T(8,128)(2,1)S(1)}, bf16[160,1792]{1,0:T(8,128)(2,1)S(1)}, u32[]{:S(2)}, u32[]{:S(2)}) collective-permute-start(bf16[160,1792]{1,0:T(8,128)(2,1)S(1)} %get-tuple-element.42.refs_0_), channel_id=1, source_target_pairs={{0,1},{3,2},{4,5},{7,6},{8,9},{11,10},{12,13},{15,14},{16,17},{19,... | collective-permute-start | bytes 1720328 | tf_op jit(solution)/shard_map/ppermute | solution.py:555
  80.0 0.1 collective-permute-start.19
  80.2 0.1 add.16.refs_4_.refs_1_
  80.3 0.6 collective-permute-start.20
  80.9 1.3 %collective-permute-start.14 = (bf16[48,1792]{1,0:T(8,128)(2,1)S(1)}, bf16[48,1792]{1,0:T(8,128)(2,1)S(1)}, u32[]{:S(2)}, u32[]{:S(2)}) collective-permute-start(bf16[48,1792]{1,0:T(8,128)(2,1)S(1)} %add.15.refs_2_), channel_id=1, source_target_pairs={{1,0},{2,3},{5,4},{6,7},{9,8},{10,11},{13,12},{14,15},{17,16},{18,... | collective-permute-start | bytes 516104 | tf_op jit(solution)/shard_map/ppermute | solution.py:561
  82.2 1.0 collective-permute-start.16
  83.1 5.9 %collective-permute-done.14.refs_3_ = bf16[48,1792]{1,0:T(8,128)(2,1)S(1)} collective-permute-done((bf16[48,1792]{1,0:T(8,128)(2,1)S(1)}, bf16[48,1792]{1,0:T(8,128)(2,1)S(1)}, u32[]{:S(2)}, u32[]{:S(2)}) %collective-permute-start.14) | collective-permute-done | bytes 172064 | tf_op jit(solution)/shard_map/ppermute | solution.py:561
  89.1 0.1 add.17.rest_5_.refs_0_
  89.2 2.3 %project.7 = (bf16[64,1792]{1,0:T(8,128)(2,1)S(1)}, bf16[128,1792]{1,0:T(8,128)(2,1)S(1)}, bf16[144,1792]{1,0:T(8,128)(2,1)S(1)}) custom-call(s32[1]{0:T(128)} %bitcast.me, s32[1]{0:T(128)} %bitcast.1.z, bf16[2048,1792]{1,0:T(8,128)(2,1)S(1)} %bitcast.9, bf16[64,2048]{1,0:T(8,128)(2,1)S(1)} %attend.5.refs_1_.rest_4_.rest_0_, ...), custom_call_target="tpu_custom_call" | custom-call | flops 1000 | bytes 1000 | tf_op jit(solution)/shard_map/project/pallas_call | solution.py:313
  91.5 1.5 %collective-permute-start.22 = (bf16[128,1792]{1,0:T(8,128)(2,1)S(1)}, bf16[128,1792]{1,0:T(8,128)(2,1)S(1)}, u32[]{:S(2)}, u32[]{:S(2)}) collective-permute-start(bf16[128,1792]{1,0:T(8,128)(2,1)S(1)} %get-tuple-element.45.refs_0_), channel_id=1, source_target_pairs={{0,1},{3,2},{4,5},{7,6},{8,9},{11,10},{12,13},{15,14},{16,17},{19,... | collective-permute-start | bytes 1376264 | tf_op jit(solution)/shard_map/ppermute | solution.py:555
  93.0 0.1 add.18.refs_2_
  93.1 0.7 collective-permute-start.24
  93.9 1.3 %collective-permute-start.21 = (bf16[64,1792]{1,0:T(8,128)(2,1)S(1)}, bf16[64,1792]{1,0:T(8,128)(2,1)S(1)}, u32[]{:S(2)}, u32[]{:S(2)}) collective-permute-start(bf16[64,1792]{1,0:T(8,128)(2,1)S(1)} %add.19.refs_2_), channel_id=1, source_target_pairs={{1,0},{2,3},{5,4},{6,7},{9,8},{10,11},{13,12},{14,15},{17,16},{18,... | collective-permute-start | bytes 688136 | tf_op jit(solution)/shard_map/ppermute | solution.py:561
  95.2 8.2 %collective-permute-start.23 = (bf16[144,1792]{1,0:T(8,128)(2,1)S(1)}, bf16[144,1792]{1,0:T(8,128)(2,1)S(1)}, u32[]{:S(2)}, u32[]{:S(2)}) collective-permute-start(bf16[144,1792]{1,0:T(8,128)(2,1)S(1)} %get-tuple-element.46.refs_0_), channel_id=1, source_target_pairs={{0,1},{3,2},{4,5},{7,6},{8,9},{11,10},{12,13},{15,14},{16,17},{19,... | collective-permute-start | bytes 1548296 | tf_op jit(solution)/shard_map/ppermute | solution.py:555
  103.5 0.7 collective-permute-start.26
  104.2 1.3 %collective-permute-done.21.refs_3_ = bf16[64,1792]{1,0:T(8,128)(2,1)S(1)} collective-permute-done((bf16[64,1792]{1,0:T(8,128)(2,1)S(1)}, bf16[64,1792]{1,0:T(8,128)(2,1)S(1)}, u32[]{:S(2)}, u32[]{:S(2)}) %collective-permute-start.21) | collective-permute-done | bytes 229408 | tf_op jit(solution)/shard_map/ppermute | solution.py:561
  105.5 0.1 add.21.refs_2_.refs_1_
  105.7 0.1 add.23.refs_2_
  105.8 1.3 %collective-permute-start.25 = (bf16[80,1792]{1,0:T(8,128)(2,1)S(1)}, bf16[80,1792]{1,0:T(8,128)(2,1)S(1)}, u32[]{:S(2)}, u32[]{:S(2)}) collective-permute-start(bf16[80,1792]{1,0:T(8,128)(2,1)S(1)} %add.23.refs_2_), channel_id=1, source_target_pairs={{1,0},{2,3},{5,4},{6,7},{9,8},{10,11},{13,12},{14,15},{17,16},{18,... | collective-permute-start | bytes 860168 | tf_op jit(solution)/shard_map/ppermute | solution.py:561
  107.1 0.7 collective-permute-start.27
  107.7 0.1 add.24.refs_4_
  107.8 1.3 %collective-permute-start.28 = (bf16[64,1792]{1,0:T(8,128)(2,1)S(1)}, bf16[64,1792]{1,0:T(8,128)(2,1)S(1)}, u32[]{:S(2)}, u32[]{:S(2)}) collective-permute-start(bf16[64,1792]{1,0:T(8,128)(2,1)S(1)} %add.24.refs_4_), channel_id=1, source_target_pairs={{1,0},{2,3},{5,4},{6,7},{9,8},{10,11},{13,12},{14,15},{17,16},{18,... | collective-permute-start | bytes 688136 | tf_op jit(solution)/shard_map/ppermute | solution.py:561
  109.1 4.2 %collective-permute-done.23.refs_1_.refs_4_ = bf16[144,1792]{1,0:T(8,128)(2,1)S(1)} collective-permute-done((bf16[144,1792]{1,0:T(8,128)(2,1)S(1)}, bf16[144,1792]{1,0:T(8,128)(2,1)S(1)}, u32[]{:S(2)}, u32[]{:S(2)}) %collective-permute-start.23) | collective-permute-done | bytes 516128 | tf_op jit(solution)/shard_map/ppermute | solution.py:555
  113.4 5.9 %collective-permute-done.25.refs_3_ = bf16[80,1792]{1,0:T(8,128)(2,1)S(1)} collective-permute-done((bf16[80,1792]{1,0:T(8,128)(2,1)S(1)}, bf16[80,1792]{1,0:T(8,128)(2,1)S(1)}, u32[]{:S(2)}, u32[]{:S(2)}) %collective-permute-start.25) | collective-permute-done | bytes 286752 | tf_op jit(solution)/shard_map/ppermute | solution.py:561
  119.2 0.2 add.25.refs_2_
  119.4 3.9 %collective-permute-done.28.refs_6_ = bf16[64,1792]{1,0:T(8,128)(2,1)S(1)} collective-permute-done((bf16[64,1792]{1,0:T(8,128)(2,1)S(1)}, bf16[64,1792]{1,0:T(8,128)(2,1)S(1)}, u32[]{:S(2)}, u32[]{:S(2)}) %collective-permute-start.28) | collective-permute-done | bytes 229408 | tf_op jit(solution)/shard_map/ppermute | solution.py:561
  123.3 1.1 finish.1
  (79 shorter events, 0.5 us)
Async XLA Ops:
  0.0 1.5 %copy-start.25 = (bf16[32,4096]{1,0:T(8,128)(2,1)S(1)}, bf16[32,4096]{1,0:T(8,128)(2,1)}, u32[]{:S(2)}) copy-start(bf16[32,4096]{1,0:T(8,128)(2,1)} %param.19) | copy-start | bytes 786436
  0.0 2.9 %copy-start.6 = (bf16[256,64]{0,1:T(8,128)(2,1)S(1)}, bf16[256,64]{0,1:T(8,128)(2,1)}, u32[]{:S(2)}) copy-start(bf16[256,64]{0,1:T(8,128)(2,1)} %param.17) | copy-start | bytes 98308
  0.0 2.9 %copy-start.9 = (s32[1,16]{1,0:T(1,128)S(1)}, s32[1,16]{1,0:T(1,128)}, u32[]{:S(2)}) copy-start(s32[1,16]{1,0:T(1,128)} %table.1) | copy-start | bytes 196
  2.9 15.5 %copy-start.8 = (s32[1,4,2]{1,2,0:T(2,128)S(1)}, s32[1,4,2]{1,2,0:T(2,128)}, u32[]{:S(2)}) copy-start(s32[1,4,2]{1,2,0:T(2,128)} %param.23) | copy-start | bytes 100
  10.7 1.4 %copy-start.11 = (bf16[16,128,512]{2,1,0:T(8,128)(2,1)}, bf16[16,128,512]{2,1,0:T(8,128)(2,1)S(1)}, u32[]{:S(2)}) copy-start(bf16[16,128,512]{2,1,0:T(8,128)(2,1)S(1)} %get-tuple-element.27.wk) | copy-start | bytes 6291460
  12.1 1.3 %copy-start.14 = (bf16[16,512,128]{2,1,0:T(8,128)(2,1)}, bf16[16,512,128]{2,1,0:T(8,128)(2,1)S(1)}, u32[]{:S(2)}) copy-start(bf16[16,512,128]{2,1,0:T(8,128)(2,1)S(1)} %get-tuple-element.28.wv) | copy-start | bytes 6291460
  13.4 1.2 copy-start.17
  14.6 0.8 copy-start.20
  15.4 18.3 %collective-permute-start = (bf16[48,2048]{1,0:T(8,128)(2,1)S(1)}, bf16[48,2048]{1,0:T(8,128)(2,1)S(1)}, u32[]{:S(2)}, u32[]{:S(2)}) collective-permute-start(bf16[48,2048]{1,0:T(8,128)(2,1)S(1)} %get-tuple-element.30.rest_0_), channel_id=1, source_target_pairs={{0,8},{4,12},{8,0},{12,4},{1,9},{5,13},{9,1},{13,5},{2,10},{6,14},... | collective-permute-start | bytes 589832 | tf_op jit(solution)/shard_map/ppermute | solution.py:378
  18.4 16.6 %collective-permute-start.1 = (bf16[48,2048]{1,0:T(8,128)(2,1)S(1)}, bf16[48,2048]{1,0:T(8,128)(2,1)S(1)}, u32[]{:S(2)}, u32[]{:S(2)}) collective-permute-start(bf16[48,2048]{1,0:T(8,128)(2,1)S(1)} %get-tuple-element.30.rest_0_), channel_id=1, source_target_pairs={{0,4},{4,0},{8,12},{12,8},{1,5},{5,1},{9,13},{13,9},{2,6},{6,2},{1... | collective-permute-start | bytes 589832 | tf_op jit(solution)/shard_map/ppermute | solution.py:403
  18.4 1.6 %copy-start.12 = (bf16[16,128,512]{2,1,0:T(8,128)(2,1)S(1)}, bf16[16,128,512]{2,1,0:T(8,128)(2,1)}, u32[]{:S(2)}) copy-start(bf16[16,128,512]{2,1,0:T(8,128)(2,1)} %copy-done.11) | copy-start | bytes 6291460
  20.0 1.6 %copy-start.15 = (bf16[16,512,128]{2,1,0:T(8,128)(2,1)S(1)}, bf16[16,512,128]{2,1,0:T(8,128)(2,1)}, u32[]{:S(2)}) copy-start(bf16[16,512,128]{2,1,0:T(8,128)(2,1)} %copy-done.14) | copy-start | bytes 6291460
  21.6 1.4 %copy-start.18 = (bf16[1280,640]{1,0:T(8,128)(2,1)S(1)}, bf16[1280,640]{1,0:T(8,128)(2,1)}, u32[]{:S(2)}) copy-start(bf16[1280,640]{1,0:T(8,128)(2,1)} %copy-done.17) | copy-start | bytes 4915204
  23.0 1.0 copy-start.21
  30.2 2.9 %copy-start = (bf16[2048,1792]{1,0:T(8,128)(2,1)}, bf16[2048,1792]{1,0:T(8,128)(2,1)S(1)}, u32[]{:S(2)}) copy-start(bf16[2048,1792]{1,0:T(8,128)(2,1)S(1)} %get-tuple-element.31.w) | copy-start | bytes 22020100
  33.1 0.7 copy-start.2
  33.8 0.7 copy-start.23
  33.8 1.2 copy-start.4
  34.4 1.6 %collective-permute-start.2 = (bf16[48,2048]{1,0:T(8,128)(2,1)S(1)}, bf16[48,2048]{1,0:T(8,128)(2,1)S(1)}, u32[]{:S(2)}, u32[]{:S(2)}) collective-permute-start(bf16[48,2048]{1,0:T(8,128)(2,1)S(1)} %stack.4), channel_id=1, source_target_pairs={{0,4},{4,0},{8,12},{12,8},{1,5},{5,1},{9,13},{13,9},{2,6},{6,2},{1... | collective-permute-start | bytes 589832 | tf_op jit(solution)/shard_map/ppermute | solution.py:403
  34.9 15.3 %collective-permute-start.4 = (bf16[64,2048]{1,0:T(8,128)(2,1)S(1)}, bf16[64,2048]{1,0:T(8,128)(2,1)S(1)}, u32[]{:S(2)}, u32[]{:S(2)}) collective-permute-start(bf16[64,2048]{1,0:T(8,128)(2,1)S(1)} %get-tuple-element.32.refs_1_.rest_4_.rest_0_), channel_id=1, source_target_pairs={{0,8},{4,12},{8,0},{12,4},{1,9},{5,13},{9,1},{13,5},{2,10},{6,14},... | collective-permute-start | bytes 786440 | tf_op jit(solution)/shard_map/ppermute | solution.py:378
  35.0 16.9 %collective-permute-start.5 = (bf16[64,2048]{1,0:T(8,128)(2,1)S(1)}, bf16[64,2048]{1,0:T(8,128)(2,1)S(1)}, u32[]{:S(2)}, u32[]{:S(2)}) collective-permute-start(bf16[64,2048]{1,0:T(8,128)(2,1)S(1)} %get-tuple-element.32.refs_1_.rest_4_.rest_0_), channel_id=1, source_target_pairs={{0,4},{4,0},{8,12},{12,8},{1,5},{5,1},{9,13},{13,9},{2,6},{6,2},{1... | collective-permute-start | bytes 786440 | tf_op jit(solution)/shard_map/ppermute | solution.py:403
  36.0 3.1 %copy-start.1 = (bf16[2048,1792]{1,0:T(8,128)(2,1)S(1)}, bf16[2048,1792]{1,0:T(8,128)(2,1)}, u32[]{:S(2)}) copy-start(bf16[2048,1792]{1,0:T(8,128)(2,1)} %copy-done) | copy-start | bytes 22020100
  39.1 5.6 %copy-start.13 = (bf16[16,128,512]{2,1,0:T(8,128)(2,1)S(1)}, bf16[16,128,512]{2,1,0:T(8,128)(2,1)}, u32[]{:S(2)}) copy-start(bf16[16,128,512]{2,1,0:T(8,128)(2,1)} %copy-done.11) | copy-start | bytes 6291460
  39.1 5.6 %copy-start.16 = (bf16[16,512,128]{2,1,0:T(8,128)(2,1)S(1)}, bf16[16,512,128]{2,1,0:T(8,128)(2,1)}, u32[]{:S(2)}) copy-start(bf16[16,512,128]{2,1,0:T(8,128)(2,1)} %copy-done.14) | copy-start | bytes 6291460
  39.1 5.6 %copy-start.19 = (bf16[1280,640]{1,0:T(8,128)(2,1)S(1)}, bf16[1280,640]{1,0:T(8,128)(2,1)}, u32[]{:S(2)}) copy-start(bf16[1280,640]{1,0:T(8,128)(2,1)} %copy-done.17) | copy-start | bytes 4915204
  39.1 5.6 %copy-start.22 = (bf16[256,1024]{1,0:T(8,128)(2,1)S(1)}, bf16[256,1024]{1,0:T(8,128)(2,1)}, u32[]{:S(2)}) copy-start(bf16[256,1024]{1,0:T(8,128)(2,1)} %copy-done.20) | copy-start | bytes 1572868
  40.9 15.4 %collective-permute-start.3 = (bf16[144,1792]{1,0:T(8,128)(2,1)S(1)}, bf16[144,1792]{1,0:T(8,128)(2,1)S(1)}, u32[]{:S(2)}, u32[]{:S(2)}) collective-permute-start(bf16[144,1792]{1,0:T(8,128)(2,1)S(1)} %get-tuple-element.34.refs_0_), channel_id=1, source_target_pairs={{0,1},{3,2},{4,5},{7,6},{8,9},{11,10},{12,13},{15,14},{16,17},{19,... | collective-permute-start | bytes 1548296 | tf_op jit(solution)/shard_map/ppermute | solution.py:555
  44.7 9.3 %slice-start = ((s8[7340032]{0:T(1024)(128)(4,1)}), s8[4194304]{0:T(1024)(128)(4,1)S(1)}, s32[]{:S(2)}) async-start(s8[7340032]{0:T(1024)(128)(4,1)} %bitcast.8), calls=%async_computation | async-start | bytes 8388608
  44.8 5.7 %copy-start.5 = (bf16[128,640]{1,0:T(8,128)(2,1)S(1)}, bf16[128,640]{1,0:T(8,128)(2,1)}, u32[]{:S(2)}) copy-start(bf16[128,640]{1,0:T(8,128)(2,1)} %copy-done.4) | copy-start | bytes 491524
  44.8 6.1 %copy-start.3 = (bf16[128,640]{1,0:T(8,128)(2,1)S(1)}, bf16[128,640]{1,0:T(8,128)(2,1)}, u32[]{:S(2)}) copy-start(bf16[128,640]{1,0:T(8,128)(2,1)} %copy-done.2) | copy-start | bytes 491524
  44.8 9.2 %slice-start.1 = ((s8[7340032]{0:T(1024)(128)(4,1)}), s8[3145728]{0:T(1024)(128)(4,1)S(1)}, s32[]{:S(2)}) async-start(s8[7340032]{0:T(1024)(128)(4,1)} %bitcast.8), calls=%async_computation.1 | async-start | bytes 6291456
  50.3 2.8 %collective-permute-start.6 = (bf16[64,2048]{1,0:T(8,128)(2,1)S(1)}, bf16[64,2048]{1,0:T(8,128)(2,1)S(1)}, u32[]{:S(2)}, u32[]{:S(2)}) collective-permute-start(bf16[64,2048]{1,0:T(8,128)(2,1)S(1)} %stack.5), channel_id=1, source_target_pairs={{0,4},{4,0},{8,12},{12,8},{1,5},{5,1},{9,13},{13,9},{2,6},{6,2},{1... | collective-permute-start | bytes 786440 | tf_op jit(solution)/shard_map/ppermute | solution.py:403
  50.4 6.0 %collective-permute-start.10 = (bf16[128,640]{1,0:T(8,128)(2,1)S(1)}, bf16[128,640]{1,0:T(8,128)(2,1)S(1)}, u32[]{:S(2)}, u32[]{:S(2)}) collective-permute-start(bf16[128,640]{1,0:T(8,128)(2,1)S(1)} %copy-done.5), channel_id=1, source_target_pairs={{0,4},{4,8},{8,12},{12,0},{1,5},{5,9},{9,13},{13,1},{2,6},{6,10},{... | collective-permute-start | bytes 491528 | tf_op jit(solution)/shard_map/ppermute | solution.py:531
  50.9 9.9 %collective-permute-start.11 = (bf16[128,640]{1,0:T(8,128)(2,1)S(1)}, bf16[128,640]{1,0:T(8,128)(2,1)S(1)}, u32[]{:S(2)}, u32[]{:S(2)}) collective-permute-start(bf16[128,640]{1,0:T(8,128)(2,1)S(1)} %copy-done.3), channel_id=1, source_target_pairs={{0,8},{4,12},{8,0},{12,4},{1,9},{5,13},{9,1},{13,5},{2,10},{6,14},... | collective-permute-start | bytes 491528 | tf_op jit(solution)/shard_map/ppermute | solution.py:531
  51.8 8.9 %copy-start.7 = (s32[16,4]{0,1:T(4,128)S(1)}, s32[16,4]{0,1:T(4,128)}, u32[]{:S(2)}) copy-start(s32[16,4]{0,1:T(4,128)} %param.26) | copy-start | bytes 772
  51.8 9.0 %copy-start.10 = (s32[16]{0:T(128)S(1)}, s32[16]{0:T(128)}, u32[]{:S(2)}) copy-start(s32[16]{0:T(128)} %decode_length.1) | copy-start | bytes 196
  51.8 9.0 %copy-start.24 = (bf16[128,640]{1,0:T(8,128)(2,1)S(1)}, bf16[128,640]{1,0:T(8,128)(2,1)}, u32[]{:S(2)}) copy-start(bf16[128,640]{1,0:T(8,128)(2,1)} %copy-done.23) | copy-start | bytes 491524
  51.8 8.9 %collective-permute-start.12 = (bf16[128,640]{1,0:T(8,128)(2,1)S(1)}, bf16[128,640]{1,0:T(8,128)(2,1)S(1)}, u32[]{:S(2)}, u32[]{:S(2)}) collective-permute-start(bf16[128,640]{1,0:T(8,128)(2,1)S(1)} %get-tuple-element.39), channel_id=1, source_target_pairs={{0,12},{4,0},{8,4},{12,8},{1,13},{5,1},{9,5},{13,9},{2,14},{6,2},{... | collective-permute-start | bytes 491528 | tf_op jit(solution)/shard_map/ppermute | solution.py:531
  53.1 17.6 %collective-permute-start.8 = (bf16[80,2048]{1,0:T(8,128)(2,1)S(1)}, bf16[80,2048]{1,0:T(8,128)(2,1)S(1)}, u32[]{:S(2)}, u32[]{:S(2)}) collective-permute-start(bf16[80,2048]{1,0:T(8,128)(2,1)S(1)} %attend.4.refs_1_.rest_4_.rest_0_), channel_id=1, source_target_pairs={{0,8},{4,12},{8,0},{12,4},{1,9},{5,13},{9,1},{13,5},{2,10},{6,14},... | collective-permute-start | bytes 983048 | tf_op jit(solution)/shard_map/ppermute | solution.py:378
  56.3 16.6 %collective-permute-start.9 = (bf16[80,2048]{1,0:T(8,128)(2,1)S(1)}, bf16[80,2048]{1,0:T(8,128)(2,1)S(1)}, u32[]{:S(2)}, u32[]{:S(2)}) collective-permute-start(bf16[80,2048]{1,0:T(8,128)(2,1)S(1)} %attend.4.refs_1_.rest_4_.rest_0_), channel_id=1, source_target_pairs={{0,4},{4,0},{8,12},{12,8},{1,5},{5,1},{9,13},{13,9},{2,6},{6,2},{1... | collective-permute-start | bytes 983048 | tf_op jit(solution)/shard_map/ppermute | solution.py:403
  56.5 23.7 %collective-permute-start.15 = (bf16[192,1792]{1,0:T(8,128)(2,1)S(1)}, bf16[192,1792]{1,0:T(8,128)(2,1)S(1)}, u32[]{:S(2)}, u32[]{:S(2)}) collective-permute-start(bf16[192,1792]{1,0:T(8,128)(2,1)S(1)} %get-tuple-element.41.refs_0_), channel_id=1, source_target_pairs={{0,1},{3,2},{4,5},{7,6},{8,9},{11,10},{12,13},{15,14},{16,17},{19,... | collective-permute-start | bytes 2064392 | tf_op jit(solution)/shard_map/ppermute | solution.py:555
  70.7 2.2 %collective-permute-start.13 = (bf16[80,2048]{1,0:T(8,128)(2,1)S(1)}, bf16[80,2048]{1,0:T(8,128)(2,1)S(1)}, u32[]{:S(2)}, u32[]{:S(2)}) collective-permute-start(bf16[80,2048]{1,0:T(8,128)(2,1)S(1)} %stack.6), channel_id=1, source_target_pairs={{0,4},{4,0},{8,12},{12,8},{1,5},{5,1},{9,13},{13,9},{2,6},{6,2},{1... | collective-permute-start | bytes 983048 | tf_op jit(solution)/shard_map/ppermute | solution.py:403
  71.3 8.9 %collective-permute-start.7 = (bf16[96,1792]{1,0:T(8,128)(2,1)S(1)}, bf16[96,1792]{1,0:T(8,128)(2,1)S(1)}, u32[]{:S(2)}, u32[]{:S(2)}) collective-permute-start(bf16[96,1792]{1,0:T(8,128)(2,1)S(1)} %add.14.rest_4_), channel_id=1, source_target_pairs={{1,2},{2,1},{5,6},{6,5},{9,10},{10,9},{13,14},{14,13},{17,18},{18,... | collective-permute-start | bytes 1032200 | tf_op jit(solution)/shard_map/ppermute | solution.py:558
  71.9 8.4 %collective-permute-start.18 = (bf16[64,2048]{1,0:T(8,128)(2,1)S(1)}, bf16[64,2048]{1,0:T(8,128)(2,1)S(1)}, u32[]{:S(2)}, u32[]{:S(2)}) collective-permute-start(bf16[64,2048]{1,0:T(8,128)(2,1)S(1)} %attend.5.refs_1_.rest_4_.rest_0_), channel_id=1, source_target_pairs={{0,8},{4,12},{8,0},{12,4},{1,9},{5,13},{9,1},{13,5},{2,10},{6,14},... | collective-permute-start | bytes 786440 | tf_op jit(solution)/shard_map/ppermute | solution.py:378
  75.7 17.2 %collective-permute-start.17 = (bf16[160,1792]{1,0:T(8,128)(2,1)S(1)}, bf16[160,1792]{1,0:T(8,128)(2,1)S(1)}, u32[]{:S(2)}, u32[]{:S(2)}) collective-permute-start(bf16[160,1792]{1,0:T(8,128)(2,1)S(1)} %get-tuple-element.42.refs_0_), channel_id=1, source_target_pairs={{0,1},{3,2},{4,5},{7,6},{8,9},{11,10},{12,13},{15,14},{16,17},{19,... | collective-permute-start | bytes 1720328 | tf_op jit(solution)/shard_map/ppermute | solution.py:555
  80.0 9.1 %collective-permute-start.19 = (bf16[64,2048]{1,0:T(8,128)(2,1)S(1)}, bf16[64,2048]{1,0:T(8,128)(2,1)S(1)}, u32[]{:S(2)}, u32[]{:S(2)}) collective-permute-start(bf16[64,2048]{1,0:T(8,128)(2,1)S(1)} %attend.5.refs_1_.rest_4_.rest_0_), channel_id=1, source_target_pairs={{0,4},{4,0},{8,12},{12,8},{1,5},{5,1},{9,13},{13,9},{2,6},{6,2},{1... | collective-permute-start | bytes 786440 | tf_op jit(solution)/shard_map/ppermute | solution.py:403
  80.3 8.8 %collective-permute-start.20 = (bf16[64,2048]{1,0:T(8,128)(2,1)S(1)}, bf16[64,2048]{1,0:T(8,128)(2,1)S(1)}, u32[]{:S(2)}, u32[]{:S(2)}) collective-permute-start(bf16[64,2048]{1,0:T(8,128)(2,1)S(1)} %stack.7), channel_id=1, source_target_pairs={{0,4},{4,0},{8,12},{12,8},{1,5},{5,1},{9,13},{13,9},{2,6},{6,2},{1... | collective-permute-start | bytes 786440 | tf_op jit(solution)/shard_map/ppermute | solution.py:403
  80.9 8.2 %collective-permute-start.14 = (bf16[48,1792]{1,0:T(8,128)(2,1)S(1)}, bf16[48,1792]{1,0:T(8,128)(2,1)S(1)}, u32[]{:S(2)}, u32[]{:S(2)}) collective-permute-start(bf16[48,1792]{1,0:T(8,128)(2,1)S(1)} %add.15.refs_2_), channel_id=1, source_target_pairs={{1,0},{2,3},{5,4},{6,7},{9,8},{10,11},{13,12},{14,15},{17,16},{18,... | collective-permute-start | bytes 516104 | tf_op jit(solution)/shard_map/ppermute | solution.py:561
  82.2 11.6 %collective-permute-start.16 = (bf16[128,1792]{1,0:T(8,128)(2,1)S(1)}, bf16[128,1792]{1,0:T(8,128)(2,1)S(1)}, u32[]{:S(2)}, u32[]{:S(2)}) collective-permute-start(bf16[128,1792]{1,0:T(8,128)(2,1)S(1)} %add.16.refs_4_.refs_1_), channel_id=1, source_target_pairs={{1,2},{2,1},{5,6},{6,5},{9,10},{10,9},{13,14},{14,13},{17,18},{18,... | collective-permute-start | bytes 1376264 | tf_op jit(solution)/shard_map/ppermute | solution.py:558
  91.5 12.0 %collective-permute-start.22 = (bf16[128,1792]{1,0:T(8,128)(2,1)S(1)}, bf16[128,1792]{1,0:T(8,128)(2,1)S(1)}, u32[]{:S(2)}, u32[]{:S(2)}) collective-permute-start(bf16[128,1792]{1,0:T(8,128)(2,1)S(1)} %get-tuple-element.45.refs_0_), channel_id=1, source_target_pairs={{0,1},{3,2},{4,5},{7,6},{8,9},{11,10},{12,13},{15,14},{16,17},{19,... | collective-permute-start | bytes 1376264 | tf_op jit(solution)/shard_map/ppermute | solution.py:555
  93.1 12.5 %collective-permute-start.24 = (bf16[160,1792]{1,0:T(8,128)(2,1)S(1)}, bf16[160,1792]{1,0:T(8,128)(2,1)S(1)}, u32[]{:S(2)}, u32[]{:S(2)}) collective-permute-start(bf16[160,1792]{1,0:T(8,128)(2,1)S(1)} %add.18.refs_2_), channel_id=1, source_target_pairs={{1,2},{2,1},{5,6},{6,5},{9,10},{10,9},{13,14},{14,13},{17,18},{18,... | collective-permute-start | bytes 1720328 | tf_op jit(solution)/shard_map/ppermute | solution.py:558
  93.9 11.6 %collective-permute-start.21 = (bf16[64,1792]{1,0:T(8,128)(2,1)S(1)}, bf16[64,1792]{1,0:T(8,128)(2,1)S(1)}, u32[]{:S(2)}, u32[]{:S(2)}) collective-permute-start(bf16[64,1792]{1,0:T(8,128)(2,1)S(1)} %add.19.refs_2_), channel_id=1, source_target_pairs={{1,0},{2,3},{5,4},{6,7},{9,8},{10,11},{13,12},{14,15},{17,16},{18,... | collective-permute-start | bytes 688136 | tf_op jit(solution)/shard_map/ppermute | solution.py:561
  95.2 18.2 %collective-permute-start.23 = (bf16[144,1792]{1,0:T(8,128)(2,1)S(1)}, bf16[144,1792]{1,0:T(8,128)(2,1)S(1)}, u32[]{:S(2)}, u32[]{:S(2)}) collective-permute-start(bf16[144,1792]{1,0:T(8,128)(2,1)S(1)} %get-tuple-element.46.refs_0_), channel_id=1, source_target_pairs={{0,1},{3,2},{4,5},{7,6},{8,9},{11,10},{12,13},{15,14},{16,17},{19,... | collective-permute-start | bytes 1548296 | tf_op jit(solution)/shard_map/ppermute | solution.py:555
  103.5 4.2 %collective-permute-start.26 = (bf16[64,1792]{1,0:T(8,128)(2,1)S(1)}, bf16[64,1792]{1,0:T(8,128)(2,1)S(1)}, u32[]{:S(2)}, u32[]{:S(2)}) collective-permute-start(bf16[64,1792]{1,0:T(8,128)(2,1)S(1)} %add.20.refs_4_), channel_id=1, source_target_pairs={{1,2},{2,1},{5,6},{6,5},{9,10},{10,9},{13,14},{14,13},{17,18},{18,... | collective-permute-start | bytes 688136 | tf_op jit(solution)/shard_map/ppermute | solution.py:558
  105.8 13.5 %collective-permute-start.25 = (bf16[80,1792]{1,0:T(8,128)(2,1)S(1)}, bf16[80,1792]{1,0:T(8,128)(2,1)S(1)}, u32[]{:S(2)}, u32[]{:S(2)}) collective-permute-start(bf16[80,1792]{1,0:T(8,128)(2,1)S(1)} %add.23.refs_2_), channel_id=1, source_target_pairs={{1,0},{2,3},{5,4},{6,7},{9,8},{10,11},{13,12},{14,15},{17,16},{18,... | collective-permute-start | bytes 860168 | tf_op jit(solution)/shard_map/ppermute | solution.py:561
  107.1 12.3 %collective-permute-start.27 = (bf16[64,1792]{1,0:T(8,128)(2,1)S(1)}, bf16[64,1792]{1,0:T(8,128)(2,1)S(1)}, u32[]{:S(2)}, u32[]{:S(2)}) collective-permute-start(bf16[64,1792]{1,0:T(8,128)(2,1)S(1)} %add.22.refs_2_), channel_id=1, source_target_pairs={{1,2},{2,1},{5,6},{6,5},{9,10},{10,9},{13,14},{14,13},{17,18},{18,... | collective-permute-start | bytes 688136 | tf_op jit(solution)/shard_map/ppermute | solution.py:558
  107.8 15.5 %collective-permute-start.28 = (bf16[64,1792]{1,0:T(8,128)(2,1)S(1)}, bf16[64,1792]{1,0:T(8,128)(2,1)S(1)}, u32[]{:S(2)}, u32[]{:S(2)}) collective-permute-start(bf16[64,1792]{1,0:T(8,128)(2,1)S(1)} %add.24.refs_4_), channel_id=1, source_target_pairs={{1,0},{2,3},{5,4},{6,7},{9,8},{10,11},{13,12},{14,15},{17,16},{18,... | collective-permute-start | bytes 688136 | tf_op jit(solution)/shard_map/ppermute | solution.py:561

commit v6 on v5

--- a/solution.py
+++ b/solution.py
@@ -11,7 +11,7 @@
 HIDDEN = -1e30
 LANES = 128
 MIB = 1024 * 1024
-WEIGHT_PIECES = 16
+PIECES = 4
 
 SMEM = pl.BlockSpec(memory_space=pltpu.SMEM)
 VMEM = pl.BlockSpec(memory_space=pltpu.VMEM)
@@ -33,7 +33,7 @@
 
 def chunk_sizes(tok_group):
     if tok_group == 256:
-        return (48, 64, 80, 64)
+        return (48, 80, 64, 64)
     return (tok_group,)
 
 
@@ -101,7 +101,13 @@
         out[:, h * dv:(h + 1) * dv] = dot(att[h * t:(h + 1) * t, :], wv[h]).astype(jnp.bfloat16)
 
 
-def first_kernel(fresh, exp_scale, table, offset, q_nope, q_rope_hbm, wk_hbm, wv_hbm, cache_latent,
+def pieces(source, target, sems, first):
+    size = source.shape[0] // PIECES
+    return [pltpu.make_async_copy(source.at[pl.ds(i * size, size)], target.at[pl.ds(i * size, size)],
+                                  sems.at[first + i]) for i in range(PIECES)]
+
+
+def first_kernel(fresh, exp_scale, me, z, table, offset, q_nope, q_rope_hbm, wk_hbm, wv_hbm, cache_latent,
                  cache_rope, new_latent, new_rope_t, out, keys, wk, wv, q_rope, q, att, sems, wsems):
     heads = q_nope.shape[0]
     t = out.shape[0]
@@ -111,76 +117,71 @@
     prior = blocks * block_len
     tok_group = new_latent.shape[0]
 
-    rope_copy = pltpu.make_async_copy(
-        q_rope_hbm.at[pl.ds(0, t)], q_rope.at[pl.ds(0, t)], wsems.at[0])
-    rope_copy.start()
-    wk_copies = [pltpu.make_async_copy(wk_hbm.at[h], wk.at[h], wsems.at[1 + h]) for h in range(heads)]
+    rope_copy = pltpu.make_async_copy(q_rope_hbm, q_rope, wsems.at[0])
+    wk_copies = pieces(wk_hbm, wk, wsems, 1)
+    wv_copies = pieces(wv_hbm, wv, wsems, 1 + PIECES)
     for c in wk_copies:
         c.start()
+    rope_copy.start()
     copies = []
     for i in range(blocks):
-        b = table[0, i]
-        rows = pl.ds(i * block_len, block_len)
         copies.append(pltpu.make_async_copy(
-            cache_latent.at[b], keys.at[rows, pl.ds(0, latent)], sems.at[2 * i]))
-        copies.append(pltpu.make_async_copy(
-            cache_rope.at[b], keys.at[rows, pl.ds(latent, LANES)], sems.at[2 * i + 1]))
+            cache_latent.at[table[0, i]],
+            keys.at[pl.ds(i * block_len, block_len), pl.ds(0, latent)], sems.at[i]))
     copies.append(pltpu.make_async_copy(
-        new_latent, keys.at[pl.ds(prior, tok_group), pl.ds(0, latent)], sems.at[2 * blocks]))
-    for c in copies:
+        new_latent, keys.at[pl.ds(prior, tok_group), pl.ds(0, latent)], sems.at[blocks]))
+    for c in copies + wv_copies:
         c.start()
-    wv_copies = [
-        pltpu.make_async_copy(wv_hbm.at[h], wv.at[h], wsems.at[1 + heads + h]) for h in range(heads)]
-    for c in wv_copies:
-        c.start()
-    if t < tok_group:
-        others = pltpu.make_async_copy(
-            q_rope_hbm.at[pl.ds(t, tok_group - t)], q_rope.at[pl.ds(t, tok_group - t)],
-            sems.at[2 * blocks + 1])
-        others.start()
 
     keys[prior:, latent:] = rope_rows(new_rope_t[...])
+    lane = lax.broadcasted_iota(jnp.int32, (block_len, LANES), 1)
+    pos = lax.broadcasted_iota(jnp.int32, (block_len, LANES), 0)
+    for i in range(blocks):
+        hide = jnp.where((lane == rope_dim) & (pos >= offset[0] - i * block_len), HIDDEN, 0.0)
+        rope = cache_rope[table[0, i]].astype(jnp.float32) + hide
+        keys[i * block_len:(i + 1) * block_len, latent:] = rope.astype(jnp.bfloat16)
+
     rope_copy.wait()
-    build_queries(q, q_nope, q_rope, 0, wk, lambda h: wk_copies[h].wait())
-
+
+    def ready(h):
+        if h * PIECES % heads == 0:
+            wk_copies[h * PIECES // heads].wait()
+
+    build_queries(q, q_nope, q_rope, 0, wk, ready)
     for c in copies:
         c.wait()
-    lane = lax.broadcasted_iota(jnp.int32, (prior, LANES), 1)
-    pos = lax.broadcasted_iota(jnp.int32, (prior, LANES), 0)
-    hide = jnp.where((lane == rope_dim) & (pos >= offset[0]), HIDDEN, 0.0)
-    keys[:prior, latent:] = (keys[:prior, latent:].astype(jnp.float32) + hide).astype(jnp.bfloat16)
     prefill(q, keys, att, heads, t, 0, prior, fresh, exp_scale)
     for c in wv_copies:
         c.wait()
     head_outputs(out, att, wv, t)
-    if t < tok_group:
-        others.wait()
-
-
-def second_kernel(first, fresh, prior, exp_scale, n_after, me, ids, q_nope, q_rope, wk, wv, keys, w_hbm,
-                  cache_latent, cache_rope, *rest):
-    rest = rest[n_after:]
-    groups = ids.shape[2]
-    out, w, packed = rest[0], rest[1], rest[2:2 + groups]
-    q, att, sems = rest[2 + groups:]
+
+
+def pack_kernel(me, ids, cache_latent, cache_rope, *rest):
+    outs, sems = rest[:-1], rest[-1]
+    groups = len(outs)
+    block_len, latent = cache_latent.shape[1:]
+    copies = []
+    for s, out in enumerate(outs):
+        to = lax.rem(me[0] + s, groups)
+        for k in range(ids.shape[1]):
+            rows = pl.ds(k * block_len, block_len)
+            copies.append(pltpu.make_async_copy(
+                cache_latent.at[ids[0, k, to]], out.at[rows, pl.ds(0, latent)], sems.at[len(copies)]))
+    for c in copies:
+        c.start()
+    for s, out in enumerate(outs):
+        to = lax.rem(me[0] + s, groups)
+        for k in range(ids.shape[1]):
+            out[k * block_len:(k + 1) * block_len, latent:] = cache_rope[ids[0, k, to]]
+    for c in copies:
+        c.wait()
+
+
+def second_kernel(first, fresh, prior, exp_scale, n_after, q_nope, q_rope, wk, wv, keys, w_hbm, *rest):
+    out, w, q, att, sems = rest[n_after:]
     heads = q_nope.shape[0]
     t = out.shape[0]
-    block_len, latent = cache_latent.shape[1:]
-    capacity = ids.shape[1]
-    copies = []
-    for s in range(groups):
-        to = lax.rem(me[0] + s, groups)
-        for k in range(capacity):
-            b = ids[0, k, to]
-            rows = pl.ds(k * block_len, block_len)
-            copies.append(pltpu.make_async_copy(
-                cache_latent.at[b], packed[s].at[rows, pl.ds(0, latent)], sems.at[len(copies)]))
-            copies.append(pltpu.make_async_copy(
-                cache_rope.at[b], packed[s].at[rows, pl.ds(latent, LANES)], sems.at[len(copies)]))
-    depth = w.shape[0] // WEIGHT_PIECES
-    for i in range(WEIGHT_PIECES):
-        rows = pl.ds(i * depth, depth)
-        copies.append(pltpu.make_async_copy(w_hbm.at[rows], w.at[rows], sems.at[len(copies)]))
+    copies = pieces(w_hbm, w, sems, 0)
     for c in copies:
         c.start()
     build_queries(q, q_nope, q_rope, first, wk)
@@ -200,26 +201,27 @@
 
 
 def last_kernel(first, fresh, prior, prefill_len, exp_scale, n_after, me, q_nope, q_rope, wk, wv, keys,
-                cache_latent, cache_rope, decode_table, decode_length, *rest):
+                flat_latent, cache_rope, decode_table, decode_length, *rest):
     received = rest[:-5 - n_after]
     out, q, att, dkeys, sems = rest[-5:]
     groups = len(received)
     heads = q_nope.shape[0]
     t = out.shape[0]
-    pool, block_len, latent = cache_latent.shape
+    pool, block_len, _ = cache_rope.shape
+    latent = flat_latent.shape[1]
     got = received[0].shape[0]
     ext = pool * block_len + groups * got
     tail = dkeys.shape[0] - ext
     start = keys.shape[0] - tail
     copies = []
-    for i in range(pool):
-        rows = pl.ds(i * block_len, block_len)
+    for i in range(PIECES):
+        rows = pl.ds(i * pool * block_len // PIECES, pool * block_len // PIECES)
         copies.append(pltpu.make_async_copy(
-            cache_latent.at[i], dkeys.at[rows, pl.ds(0, latent)], sems.at[2 * i]))
-        copies.append(pltpu.make_async_copy(
-            cache_rope.at[i], dkeys.at[rows, pl.ds(latent, LANES)], sems.at[2 * i + 1]))
+            flat_latent.at[rows], dkeys.at[rows, pl.ds(0, latent)], sems.at[i]))
     for c in copies:
         c.start()
+    for i in range(pool):
+        dkeys[i * block_len:(i + 1) * block_len, latent:] = cache_rope[i]
     for s in range(groups):
         source = lax.rem(me[0] + groups - s, groups)
         at = pl.multiple_of(pool * block_len + source * got, block_len)
@@ -272,6 +274,7 @@
 
 COST = pl.CostEstimate(flops=1000, bytes_accessed=1000, transcendentals=0)
 LONG = pl.CostEstimate(flops=40_000_000_000, bytes_accessed=1000, transcendentals=0)
+SHORT = pl.CostEstimate(flops=6_000_000_000, bytes_accessed=1000, transcendentals=0)
 
 
 def in_hbm(x):
@@ -474,17 +477,17 @@
                        jax.ShapeDtypeStruct(absorb_key.shape, bf16),
                        jax.ShapeDtypeStruct(absorb_value.shape, bf16),
                        jax.ShapeDtypeStruct(query_rope.shape, bf16)],
-            in_specs=[SMEM, SMEM, VMEM, HBM, HBM, HBM, HBM, ANY, HBM, VMEM],
+            in_specs=[SMEM] * 4 + [VMEM, HBM, HBM, HBM, HBM, VMEM, HBM, VMEM],
             out_specs=[VMEM] * 5,
             scratch_shapes=[
                 *scratch(t),
-                pltpu.SemaphoreType.DMA((2 * blocks + 2,)),
-                pltpu.SemaphoreType.DMA((2 * heads + 1,)),
+                pltpu.SemaphoreType.DMA((blocks + 1,)),
+                pltpu.SemaphoreType.DMA((2 * PIECES + 1,)),
             ],
             name="attend_first",
             compiler_params=params(20),
             cost_estimate=LONG,
-        )(prefill_table, prefill_offset, q_nope, in_hbm(query_rope), in_hbm(absorb_key),
+        )(me[None], z[None], prefill_table, prefill_offset, q_nope, in_hbm(query_rope), in_hbm(absorb_key),
           in_hbm(absorb_value), in_hbm(cache_latent), padded_rope,
           in_hbm(new_latent), new_rope.T)
 
@@ -499,19 +502,17 @@
         static = (starts[n], fresh_of(n), prior)
         if n == 1:
             kernel = functools.partial(second_kernel, *static, exp_scale, len(after))
-            args = [me[None], send_blocks.transpose(0, 2, 1)] + args + [
-                in_hbm(output_weight), in_hbm(cache_latent), padded_rope]
-            specs = [SMEM, SMEM] + specs + [HBM, HBM, ANY]
+            args.append(in_hbm(output_weight))
+            specs = specs + [HBM]
             outs.append(jax.ShapeDtypeStruct(output_weight.shape, bf16))
-            outs += [jax.ShapeDtypeStruct((capacity * block_len, width), bf16)] * groups
-            scratches.append(pltpu.SemaphoreType.DMA((2 * groups * capacity + WEIGHT_PIECES,)))
+            scratches.append(pltpu.SemaphoreType.DMA((PIECES,)))
         elif n == len(sizes) - 1:
             kernel = functools.partial(last_kernel, *static, prefill_len, exp_scale, len(after))
             args = [me[None]] + args + [
-                in_hbm(cache_latent), padded_rope, decode_table.T, decode_length, *brought]
-            specs = [SMEM] + specs + [HBM, ANY, SMEM, SMEM] + [VMEM] * len(brought)
+                in_hbm(cache_latent.reshape(pool * block_len, latent)), padded_rope, decode_table.T, decode_length, *brought]
+            specs = [SMEM] + specs + [HBM, VMEM, SMEM, SMEM] + [VMEM] * len(brought)
             span = pool * block_len + groups * capacity * block_len + min(LANES, tok_group)
-            scratches += [pltpu.VMEM((span, width), bf16), pltpu.SemaphoreType.DMA((2 * pool,))]
+            scratches += [pltpu.VMEM((span, width), bf16), pltpu.SemaphoreType.DMA((PIECES,))]
             limit = 26
         else:
             kernel = functools.partial(later_kernel, *static, exp_scale, len(after))
@@ -523,24 +524,34 @@
             scratch_shapes=scratches,
             name="attend",
             compiler_params=params(limit),
-            cost_estimate=LONG,
+            cost_estimate=SHORT if n == len(sizes) - 1 else LONG,
         )(*args, *after)
 
-    def migrate(packed):
+    def migrate():
+        packed = pl.pallas_call(
+            pack_kernel,
+            out_shape=[jax.ShapeDtypeStruct((capacity * block_len, width), bf16)] * groups,
+            in_specs=[SMEM, SMEM, HBM, VMEM],
+            out_specs=[VMEM] * groups,
+            scratch_shapes=[pltpu.SemaphoreType.DMA((groups * capacity,))],
+            name="pack",
+            compiler_params=params(8),
+            cost_estimate=COST,
+        )(me[None], send_blocks.transpose(0, 2, 1), in_hbm(cache_latent), padded_rope)
         return [packed[0]] + [
             lax.ppermute(packed[s], "dp", [(i, (i + s) % groups) for i in range(groups)])
             for s in range(1, groups)]
 
+    brought = migrate()
     x0, *held = first_chunk()
     if not on_line:
         outs = []
-        w = brought = None
+        w = None
         for n, t in enumerate(sizes):
             if n == 0:
                 x = x0
             elif n == 1:
-                x, w, *packed = attend(n, held, ())
-                brought = migrate(packed)
+                x, w = attend(n, held, ())
             else:
                 x, = attend(n, held, (), brought)
             mine = shift_groups(x)
@@ -565,10 +576,9 @@
         return [x, came, swap_cores(x), swap_cores(stack([came], after))]
 
     t0, t1, t2, t3 = sizes
-    x1, w, *packed = attend(1, held, (x0,))
+    x1, w = attend(1, held, (x0, *brought))
     own0, rest0 = project(where, gather(x0, (x1,)), w, (3,), (), (x1,))
     in0 = inward(rest0)
-    brought = migrate(packed)
     x2, = attend(2, held, (own0,))
     own1, rest1 = project(where, gather(x1, (x2,)), w, (3,), (), (x2,))
     in1 = inward(rest1)
@@ -581,11 +591,12 @@
     on1 = across(to_across1)
     to_out0 = add(t0, [(rest0, 2 * t0), (on0, 0)], (own2,))
     out0 = outward(to_out0)
-    done0 = add(t0, [(own0, 0), (in0, 2 * t0), (on0, t0), (out0, 0)], (to_across1,))
     own3, rest3, near = project(
-        where, gather(x3, (to_across1, to_out0)), w, (2, 1), (near2,), (done0,))
+        where, gather(x3, (to_across1, to_out0)), w, (2, 1), (near2,),
+        (to_across1, to_out0))
+    done0 = add(t0, [(own0, 0), (in0, 2 * t0), (on0, t0), (out0, 0)], (own3,))
     in3 = inward(rest3)
-    to_across2 = add(2 * t2, [(rest2, 0), (in2, 0)], (own3,))
+    to_across2 = add(2 * t2, [(rest2, 0), (in2, 0)], (done0,))
     on2 = across(to_across2)
     near_in = inward(near)
     to_out1 = add(t1, [(rest1, 2 * t1), (on1, 0)], (to_across2,))

time: 125 us -> 113 us (0.904)
  local copies, waits for them, and re-layouts: 19.9 us -> 2.67 us
  waiting for transfers between devices: 22.3 us -> 28 us
  starting transfers between devices: 40.4 us -> 37.7 us
  Pallas kernels: 40.6 us -> 43 us
    unnamed x57 -> x13, local copies, waits for them, and re-layouts: 19.2 us -> 0.97 us
    ppermute x5, starting transfers between devices: 22.1 us -> 18.9 us  [inward(): return lax.ppermute(x, 'tp', INWARD)]
    ppermute x4, waiting for transfers between devices: 17 us -> 19.7 us  [outward(): return lax.ppermute(x, 'tp', OUTWARD)]
    ppermute x3, starting transfers between devices: 2.62 us -> 4.46 us  [migrate(): lax.ppermute(packed[s], 'dp', [(i, (i + s) % groups) for i in range(group...]
    pallas_call x0 -> x1, Pallas kernels: none -> 1.69 us  [migrate(): pl.pallas_call(pack_kernel, out_shape=[jax.ShapeDtypeStruct((capacity * b...]
    ppermute x4, waiting for transfers between devices: 0.01 us -> 1.49 us  [shift_groups(): lax.ppermute(x, 'dp', [(i, (i + s) % groups) for i in range(groups)])]
  transfers between devices with their start and end apart: 29 -> 29, of which waited for: 6 -> 9; matrix products, arithmetic and copies ran while one was open for 0% -> 0% of each run, Pallas kernels for 25% -> 36%
where the time goes in v6:
time: 113 us; the launch traced here: 112 us
  Pallas kernels  43 us (38%)
  starting transfers between devices  37.7 us (33%)
  waiting for transfers between devices  28 us (25%)
  local copies, waits for them, and re-layouts  2.67 us (2%)
    pallas_call x3, Pallas kernels, attend(): pl.pallas_call(kernel, out_shape=outs, in_specs=specs + [ANY] * len(after...  22.7 us
    ppermute x4, waiting for transfers between devices, outward(): return lax.ppermute(x, 'tp', OUTWARD)  19.7 us
    ppermute x5, starting transfers between devices, inward(): return lax.ppermute(x, 'tp', INWARD)  18.9 us
    pallas_call x4, Pallas kernels, project(): pl.pallas_call(functools.partial(project_kernel, len(parts), tails, place...  9.07 us
    pallas_call x1, Pallas kernels, first_chunk(): pl.pallas_call(functools.partial(first_kernel, fresh_of(0), exp_scale), o...  7.37 us
    ppermute x4, starting transfers between devices, outward(): return lax.ppermute(x, 'tp', OUTWARD)  5.17 us
    ppermute x5, waiting for transfers between devices, inward(): return lax.ppermute(x, 'tp', INWARD)  4.8 us
    ppermute x3, starting transfers between devices, migrate(): lax.ppermute(packed[s], 'dp', [(i, (i + s) % groups) for i in range(group...  4.46 us
  transfers between devices with their start and end apart: 29, of which 9 were waited for; matrix products, arithmetic and copies ran while one was open for 0% of the time, Pallas kernels for 36%

profile of v6, /device:TPU:0, one launch (start us, length us, event | category | flops | bytes accessed | tf_op | source)
XLA Modules:
  0.0 112.4 jit_solution(9318514669023323427)
XLA Ops:
  0.0 1.6 %reshape.6 = bf16[32,64,64]{2,1,0:T(8,128)(2,1)S(1)} reshape(bf16[32,4096]{1,0:T(8,128)(2,1)} %param.19) | data formatting | bytes 524288 | tf_op jit(solution)/shard_map/reshape | solution.py:459
  1.6 0.1 pad.4.cache_rope
  1.7 0.0 copy-start
  1.7 0.7 copy-done
  2.4 1.7 %pack.1 = (bf16[128,640]{1,0:T(8,128)(2,1)S(1)}, bf16[128,640]{1,0:T(8,128)(2,1)S(1)}, bf16[128,640]{1,0:T(8,128)(2,1)S(1)}, bf16[128,640]{1,0:T(8,128)(2,1)S(1)}) custom-call(s32[1]{0:T(128)} %bitcast.me, s32[1,2,4]{2,1,0:T(2,128)S(1)} %bitcast.13, bf16[32,64,512]{2,1,0:T(8,128)(2,1)} %cache_latent.3, bf16[32,64,128]{2,1,0:T(8,128)(2,1)S(1)} %pad.4.cache_rope), custom_call_target="tpu_custom_call" | custom-call | flops 1000 | bytes 1000 | tf_op jit(solution)/shard_map/pack/pallas_call | solution.py:531
  4.1 0.5 collective-permute-start
  4.6 2.6 %collective-permute-start.1 = (bf16[128,640]{1,0:T(8,128)(2,1)S(1)}, bf16[128,640]{1,0:T(8,128)(2,1)S(1)}, u32[]{:S(2)}, u32[]{:S(2)}) collective-permute-start(bf16[128,640]{1,0:T(8,128)(2,1)S(1)} %get-tuple-element.33), channel_id=1, source_target_pairs={{0,8},{4,12},{8,0},{12,4},{1,9},{5,13},{9,1},{13,5},{2,10},{6,14},... | collective-permute-start | bytes 491528 | tf_op jit(solution)/shard_map/ppermute | solution.py:542
  7.2 1.4 %collective-permute-start.2 = (bf16[128,640]{1,0:T(8,128)(2,1)S(1)}, bf16[128,640]{1,0:T(8,128)(2,1)S(1)}, u32[]{:S(2)}, u32[]{:S(2)}) collective-permute-start(bf16[128,640]{1,0:T(8,128)(2,1)S(1)} %get-tuple-element.34), channel_id=1, source_target_pairs={{0,12},{4,0},{8,4},{12,8},{1,13},{5,1},{9,5},{13,9},{2,14},{6,2},{... | collective-permute-start | bytes 491528 | tf_op jit(solution)/shard_map/ppermute | solution.py:542
  8.6 0.3 copy.17
  9.5 7.4 %attend_first.1 = (bf16[48,2048]{1,0:T(8,128)(2,1)S(1)}, bf16[1280,640]{1,0:T(8,128)(2,1)S(1)}, bf16[16,128,512]{2,1,0:T(8,128)(2,1)S(1)}, bf16[16,512,128]{2,1,0:T(8,128)(2,1)S(1)}, bf16[256,1024]{1,0:T(8,128)(2,1)S(1)}) custom-call(s32[1]{0:T(128)} %bitcast.me, s32[1]{0:T(128)} %bitcast.1.z, s32[1,16]{1,0:T(1,128)S(1)} %copy-done.3, s32[1]{0:T(128)S(6)} %copy.18.offset, ...), custom_call_target="tpu_custom_call" | custom-call | flops 40000000000 | bytes 1000 | tf_op jit(solution)/shard_map/attend_first/pallas_call | solution.py:473
  16.9 0.4 collective-permute-start.3
  17.2 0.0 collective-permute-start.4
  17.3 0.0 collective-permute-done.rest_2_.rest_1_
  17.3 8.4 %attend.3 = (bf16[80,2048]{1,0:T(8,128)(2,1)S(1)}, bf16[2048,1792]{1,0:T(8,128)(2,1)S(1)}) custom-call(bf16[16,256,128]{2,1,0:T(8,128)(2,1)S(1)} %bitcast.10, bf16[256,1024]{1,0:T(8,128)(2,1)S(1)} %get-tuple-element.26.q_rope, bf16[16,128,512]{2,1,0:T(8,128)(2,1)S(1)} %get-tuple-element.27.wk, bf16[16,512,128]{2,1,0:T(8,128)(2,1)S(1)} %get-tuple-element.28.wv, ...), custom_call_target="tpu_custom_call" | custom-call | flops 40000000000 | bytes 1000 | tf_op jit(solution)/shard_map/attend/pallas_call | solution.py:519
  25.7 0.6 collective-permute-start.5
  26.3 1.7 %collective-permute-start.7 = (bf16[80,2048]{1,0:T(8,128)(2,1)S(1)}, bf16[80,2048]{1,0:T(8,128)(2,1)S(1)}, u32[]{:S(2)}, u32[]{:S(2)}) collective-permute-start(bf16[80,2048]{1,0:T(8,128)(2,1)S(1)} %get-tuple-element.36.refs_1_.rest_4_.rest_0_), channel_id=1, source_target_pairs={{0,8},{4,12},{8,0},{12,4},{1,9},{5,13},{9,1},{13,5},{2,10},{6,14},... | collective-permute-start | bytes 983048 | tf_op jit(solution)/shard_map/ppermute | solution.py:381
  28.0 1.8 %project.4 = (bf16[48,1792]{1,0:T(8,128)(2,1)S(1)}, bf16[144,1792]{1,0:T(8,128)(2,1)S(1)}) custom-call(s32[1]{0:T(128)} %bitcast.me, s32[1]{0:T(128)} %bitcast.1.z, bf16[2048,1792]{1,0:T(8,128)(2,1)S(1)} %get-tuple-element.35.w, bf16[48,2048]{1,0:T(8,128)(2,1)S(1)} %get-tuple-element.30.rest_0_, bf16[48,2048]{1,0:T(8,128)(2,1)S(1)} %collective-permute-done.3.refs_0_.rest_1_, ...), custom_call_target="tpu_custom_call" | custom-call | flops 1000 | bytes 1000 | tf_op jit(solution)/shard_map/project/pallas_call | solution.py:316
  29.8 3.7 %collective-permute-start.6 = (bf16[144,1792]{1,0:T(8,128)(2,1)S(1)}, bf16[144,1792]{1,0:T(8,128)(2,1)S(1)}, u32[]{:S(2)}, u32[]{:S(2)}) collective-permute-start(bf16[144,1792]{1,0:T(8,128)(2,1)S(1)} %get-tuple-element.38.refs_0_), channel_id=1, source_target_pairs={{0,1},{3,2},{4,5},{7,6},{8,9},{11,10},{12,13},{15,14},{16,17},{19,... | collective-permute-start | bytes 1548296 | tf_op jit(solution)/shard_map/ppermute | solution.py:566
  33.5 4.9 %attend.4.refs_1_.rest_4_.rest_0_ = bf16[64,2048]{1,0:T(8,128)(2,1)S(1)} custom-call(bf16[16,256,128]{2,1,0:T(8,128)(2,1)S(1)} %bitcast.11, bf16[256,1024]{1,0:T(8,128)(2,1)S(1)} %get-tuple-element.26.q_rope, bf16[16,128,512]{2,1,0:T(8,128)(2,1)S(1)} %get-tuple-element.27.wk, bf16[16,512,128]{2,1,0:T(8,128)(2,1)S(1)} %get-tuple-element.28.wv, ...), custom_call_target="tpu_custom_call" | custom-call | flops 40000000000 | bytes 1000 | tf_op jit(solution)/shard_map/attend/pallas_call | solution.py:519
  38.4 0.0 copy-start.2
  38.4 0.0 copy-start.4
  38.4 0.3 collective-permute-start.9
  38.7 1.4 %collective-permute-done.9.rest_3_ = bf16[80,2048]{1,0:T(8,128)(2,1)S(1)} collective-permute-done((bf16[80,2048]{1,0:T(8,128)(2,1)S(1)}, bf16[80,2048]{1,0:T(8,128)(2,1)S(1)}, u32[]{:S(2)}, u32[]{:S(2)}) %collective-permute-start.9) | collective-permute-done | bytes 327712 | tf_op jit(solution)/shard_map/ppermute | solution.py:406
  40.1 2.8 %project.5 = (bf16[80,1792]{1,0:T(8,128)(2,1)S(1)}, bf16[240,1792]{1,0:T(8,128)(2,1)S(1)}) custom-call(s32[1]{0:T(128)} %bitcast.me, s32[1]{0:T(128)} %bitcast.1.z, bf16[2048,1792]{1,0:T(8,128)(2,1)S(1)} %get-tuple-element.35.w, bf16[80,2048]{1,0:T(8,128)(2,1)S(1)} %get-tuple-element.36.refs_1_.rest_4_.rest_0_, ...), custom_call_target="tpu_custom_call" | custom-call | flops 1000 | bytes 1000 | tf_op jit(solution)/shard_map/project/pallas_call | solution.py:316
  42.9 1.5 %collective-permute-start.17 = (bf16[240,1792]{1,0:T(8,128)(2,1)S(1)}, bf16[240,1792]{1,0:T(8,128)(2,1)S(1)}, u32[]{:S(2)}, u32[]{:S(2)}) collective-permute-start(bf16[240,1792]{1,0:T(8,128)(2,1)S(1)} %get-tuple-element.41.refs_0_), channel_id=1, source_target_pairs={{0,1},{3,2},{4,5},{7,6},{8,9},{11,10},{12,13},{15,14},{16,17},{19,... | collective-permute-start | bytes 2580488 | tf_op jit(solution)/shard_map/ppermute | solution.py:566
  44.4 1.5 %collective-permute-start.11 = (bf16[64,2048]{1,0:T(8,128)(2,1)S(1)}, bf16[64,2048]{1,0:T(8,128)(2,1)S(1)}, u32[]{:S(2)}, u32[]{:S(2)}) collective-permute-start(bf16[64,2048]{1,0:T(8,128)(2,1)S(1)} %attend.4.refs_1_.rest_4_.rest_0_), channel_id=1, source_target_pairs={{0,8},{4,12},{8,0},{12,4},{1,9},{5,13},{9,1},{13,5},{2,10},{6,14},... | collective-permute-start | bytes 786440 | tf_op jit(solution)/shard_map/ppermute | solution.py:381
  45.9 0.1 add.14.rest_4_
  45.9 0.7 collective-permute-start.10
  46.6 9.4 %attend.5.refs_1_.rest_4_.rest_0_ = bf16[64,2048]{1,0:T(8,128)(2,1)S(1)} custom-call(s32[1]{0:T(128)} %bitcast.me, bf16[16,256,128]{2,1,0:T(8,128)(2,1)S(1)} %bitcast.12, bf16[256,1024]{1,0:T(8,128)(2,1)S(1)} %get-tuple-element.26.q_rope, bf16[16,128,512]{2,1,0:T(8,128)(2,1)S(1)} %get-tuple-element.27.wk, bf16[16,512,128]{2,1,0:T(8,128)(2,1)S(1)} %get-tuple-element.28.wv, ...), custom_call_target="tpu_custom_call" | custom-call | flops 6000000000 | bytes 1000 | tf_op jit(solution)/shard_map/attend/pallas_call | solution.py:519
  56.1 0.6 collective-permute-start.13
  56.7 0.6 collective-permute-start.15
  57.3 0.6 collective-permute-done.13.rest_3_
  57.8 2.3 %project.6 = (bf16[64,1792]{1,0:T(8,128)(2,1)S(1)}, bf16[128,1792]{1,0:T(8,128)(2,1)S(1)}, bf16[64,1792]{1,0:T(8,128)(2,1)S(1)}) custom-call(s32[1]{0:T(128)} %bitcast.me, s32[1]{0:T(128)} %bitcast.1.z, bf16[2048,1792]{1,0:T(8,128)(2,1)S(1)} %get-tuple-element.35.w, bf16[64,2048]{1,0:T(8,128)(2,1)S(1)} %attend.4.refs_1_.rest_4_.rest_0_, ...), custom_call_target="tpu_custom_call" | custom-call | flops 1000 | bytes 1000 | tf_op jit(solution)/shard_map/project/pallas_call | solution.py:316
  60.2 3.2 %collective-permute-done.17.refs_1_ = bf16[240,1792]{1,0:T(8,128)(2,1)S(1)} collective-permute-done((bf16[240,1792]{1,0:T(8,128)(2,1)S(1)}, bf16[240,1792]{1,0:T(8,128)(2,1)S(1)}, u32[]{:S(2)}, u32[]{:S(2)}) %collective-permute-start.17) | collective-permute-done | bytes 860192 | tf_op jit(solution)/shard_map/ppermute | solution.py:566
  63.3 0.1 add.16.refs_1_.rest_5_
  63.5 1.5 %collective-permute-done.15.refs_0_.rest_1_ = bf16[64,2048]{1,0:T(8,128)(2,1)S(1)} collective-permute-done((bf16[64,2048]{1,0:T(8,128)(2,1)S(1)}, bf16[64,2048]{1,0:T(8,128)(2,1)S(1)}, u32[]{:S(2)}, u32[]{:S(2)}) %collective-permute-start.15) | collective-permute-done | bytes 262176 | tf_op jit(solution)/shard_map/ppermute | solution.py:381
  65.0 0.1 collective-permute-start.18
  65.1 6.3 %collective-permute-start.20 = (bf16[128,1792]{1,0:T(8,128)(2,1)S(1)}, bf16[128,1792]{1,0:T(8,128)(2,1)S(1)}, u32[]{:S(2)}, u32[]{:S(2)}) collective-permute-start(bf16[128,1792]{1,0:T(8,128)(2,1)S(1)} %get-tuple-element.44.refs_0_), channel_id=1, source_target_pairs={{0,1},{3,2},{4,5},{7,6},{8,9},{11,10},{12,13},{15,14},{16,17},{19,... | collective-permute-start | bytes 1376264 | tf_op jit(solution)/shard_map/ppermute | solution.py:566
  71.3 0.7 collective-permute-start.19
  72.1 2.3 %project.7 = (bf16[64,1792]{1,0:T(8,128)(2,1)S(1)}, bf16[128,1792]{1,0:T(8,128)(2,1)S(1)}, bf16[128,1792]{1,0:T(8,128)(2,1)S(1)}) custom-call(s32[1]{0:T(128)} %bitcast.me, s32[1]{0:T(128)} %bitcast.1.z, bf16[2048,1792]{1,0:T(8,128)(2,1)S(1)} %get-tuple-element.35.w, bf16[64,2048]{1,0:T(8,128)(2,1)S(1)} %attend.5.refs_1_.rest_4_.rest_0_, ...), custom_call_target="tpu_custom_call" | custom-call | flops 1000 | bytes 1000 | tf_op jit(solution)/shard_map/project/pallas_call | solution.py:316
  74.3 3.0 %collective-permute-start.22 = (bf16[128,1792]{1,0:T(8,128)(2,1)S(1)}, bf16[128,1792]{1,0:T(8,128)(2,1)S(1)}, u32[]{:S(2)}, u32[]{:S(2)}) collective-permute-start(bf16[128,1792]{1,0:T(8,128)(2,1)S(1)} %get-tuple-element.45.refs_0_), channel_id=1, source_target_pairs={{0,1},{3,2},{4,5},{7,6},{8,9},{11,10},{12,13},{15,14},{16,17},{19,... | collective-permute-start | bytes 1376264 | tf_op jit(solution)/shard_map/ppermute | solution.py:566
  77.3 1.3 %collective-permute-start.14 = (bf16[48,1792]{1,0:T(8,128)(2,1)S(1)}, bf16[48,1792]{1,0:T(8,128)(2,1)S(1)}, u32[]{:S(2)}, u32[]{:S(2)}) collective-permute-start(bf16[48,1792]{1,0:T(8,128)(2,1)S(1)} %add.15.refs_2_.rest_6_), channel_id=1, source_target_pairs={{1,0},{2,3},{5,4},{6,7},{9,8},{10,11},{13,12},{14,15},{17,16},{18,... | collective-permute-start | bytes 516104 | tf_op jit(solution)/shard_map/ppermute | solution.py:572
  78.6 6.8 %collective-permute-done.14.refs_3_ = bf16[48,1792]{1,0:T(8,128)(2,1)S(1)} collective-permute-done((bf16[48,1792]{1,0:T(8,128)(2,1)S(1)}, bf16[48,1792]{1,0:T(8,128)(2,1)S(1)}, u32[]{:S(2)}, u32[]{:S(2)}) %collective-permute-start.14) | collective-permute-done | bytes 172064 | tf_op jit(solution)/shard_map/ppermute | solution.py:572
  85.4 0.1 add.17.refs_2_.refs_0_
  85.5 0.1 add.18.refs_2_
  85.6 0.7 collective-permute-start.24
  86.3 0.1 add.19.refs_2_
  86.4 1.3 %collective-permute-start.21 = (bf16[80,1792]{1,0:T(8,128)(2,1)S(1)}, bf16[80,1792]{1,0:T(8,128)(2,1)S(1)}, u32[]{:S(2)}, u32[]{:S(2)}) collective-permute-start(bf16[80,1792]{1,0:T(8,128)(2,1)S(1)} %add.19.refs_2_), channel_id=1, source_target_pairs={{1,0},{2,3},{5,4},{6,7},{9,8},{10,11},{13,12},{14,15},{17,16},{18,... | collective-permute-start | bytes 860168 | tf_op jit(solution)/shard_map/ppermute | solution.py:572
  87.7 4.6 %collective-permute-start.23 = (bf16[128,1792]{1,0:T(8,128)(2,1)S(1)}, bf16[128,1792]{1,0:T(8,128)(2,1)S(1)}, u32[]{:S(2)}, u32[]{:S(2)}) collective-permute-start(bf16[128,1792]{1,0:T(8,128)(2,1)S(1)} %get-tuple-element.46.refs_0_), channel_id=1, source_target_pairs={{0,1},{3,2},{4,5},{7,6},{8,9},{11,10},{12,13},{15,14},{16,17},{19,... | collective-permute-start | bytes 1376264 | tf_op jit(solution)/shard_map/ppermute | solution.py:566
  92.3 0.1 add.20.refs_4_
  92.4 0.7 collective-permute-start.26
  93.1 3.0 %collective-permute-done.21.refs_3_ = bf16[80,1792]{1,0:T(8,128)(2,1)S(1)} collective-permute-done((bf16[80,1792]{1,0:T(8,128)(2,1)S(1)}, bf16[80,1792]{1,0:T(8,128)(2,1)S(1)}, u32[]{:S(2)}, u32[]{:S(2)}) %collective-permute-start.21) | collective-permute-done | bytes 286752 | tf_op jit(solution)/shard_map/ppermute | solution.py:572
  96.1 0.2 add.21.refs_2_.refs_1_
  96.3 0.1 add.22.refs_2_
  96.3 0.7 collective-permute-start.27
  97.0 0.1 add.23.refs_2_
  97.1 1.3 %collective-permute-start.25 = (bf16[64,1792]{1,0:T(8,128)(2,1)S(1)}, bf16[64,1792]{1,0:T(8,128)(2,1)S(1)}, u32[]{:S(2)}, u32[]{:S(2)}) collective-permute-start(bf16[64,1792]{1,0:T(8,128)(2,1)S(1)} %add.23.refs_2_), channel_id=1, source_target_pairs={{1,0},{2,3},{5,4},{6,7},{9,8},{10,11},{13,12},{14,15},{17,16},{18,... | collective-permute-start | bytes 688136 | tf_op jit(solution)/shard_map/ppermute | solution.py:572
  98.4 0.1 add.24.refs_4_
  98.5 1.3 %collective-permute-start.28 = (bf16[64,1792]{1,0:T(8,128)(2,1)S(1)}, bf16[64,1792]{1,0:T(8,128)(2,1)S(1)}, u32[]{:S(2)}, u32[]{:S(2)}) collective-permute-start(bf16[64,1792]{1,0:T(8,128)(2,1)S(1)} %add.24.refs_4_), channel_id=1, source_target_pairs={{1,0},{2,3},{5,4},{6,7},{9,8},{10,11},{13,12},{14,15},{17,16},{18,... | collective-permute-start | bytes 688136 | tf_op jit(solution)/shard_map/ppermute | solution.py:572
  99.8 1.6 %collective-permute-done.23.refs_1_.refs_4_ = bf16[128,1792]{1,0:T(8,128)(2,1)S(1)} collective-permute-done((bf16[128,1792]{1,0:T(8,128)(2,1)S(1)}, bf16[128,1792]{1,0:T(8,128)(2,1)S(1)}, u32[]{:S(2)}, u32[]{:S(2)}) %collective-permute-start.23) | collective-permute-done | bytes 458784 | tf_op jit(solution)/shard_map/ppermute | solution.py:566
  101.4 7.0 %collective-permute-done.25.refs_3_ = bf16[64,1792]{1,0:T(8,128)(2,1)S(1)} collective-permute-done((bf16[64,1792]{1,0:T(8,128)(2,1)S(1)}, bf16[64,1792]{1,0:T(8,128)(2,1)S(1)}, u32[]{:S(2)}, u32[]{:S(2)}) %collective-permute-start.25) | collective-permute-done | bytes 229408 | tf_op jit(solution)/shard_map/ppermute | solution.py:572
  108.4 0.1 add.25.refs_2_
  108.5 2.8 %collective-permute-done.28.refs_6_ = bf16[64,1792]{1,0:T(8,128)(2,1)S(1)} collective-permute-done((bf16[64,1792]{1,0:T(8,128)(2,1)S(1)}, bf16[64,1792]{1,0:T(8,128)(2,1)S(1)}, u32[]{:S(2)}, u32[]{:S(2)}) %collective-permute-start.28) | collective-permute-done | bytes 229408 | tf_op jit(solution)/shard_map/ppermute | solution.py:572
  111.4 1.1 finish.1
  (35 shorter events, 0.2 us)
Async XLA Ops:
  0.0 8.6 %copy-start.5 = (bf16[256,16,128]{2,1,0:T(8,128)(2,1)S(1)}, bf16[256,16,128]{2,1,0:T(8,128)(2,1)}, u32[]{:S(2)}) copy-start(bf16[256,16,128]{2,1,0:T(8,128)(2,1)} %param.14) | copy-start | bytes 3145732
  1.7 0.7 copy-start
  2.4 7.1 %copy-start.1 = (bf16[256,64]{0,1:T(8,128)(2,1)S(1)}, bf16[256,64]{0,1:T(8,128)(2,1)}, u32[]{:S(2)}) copy-start(bf16[256,64]{0,1:T(8,128)(2,1)} %param.17) | copy-start | bytes 98308
  2.4 7.1 %copy-start.3 = (s32[1,16]{1,0:T(1,128)S(1)}, s32[1,16]{1,0:T(1,128)}, u32[]{:S(2)}) copy-start(s32[1,16]{1,0:T(1,128)} %table.1) | copy-start | bytes 196
  4.1 13.2 %collective-permute-start = (bf16[128,640]{1,0:T(8,128)(2,1)S(1)}, bf16[128,640]{1,0:T(8,128)(2,1)S(1)}, u32[]{:S(2)}, u32[]{:S(2)}) collective-permute-start(bf16[128,640]{1,0:T(8,128)(2,1)S(1)} %get-tuple-element.32), channel_id=1, source_target_pairs={{0,4},{4,8},{8,12},{12,0},{1,5},{5,9},{9,13},{13,1},{2,6},{6,10},{... | collective-permute-start | bytes 491528 | tf_op jit(solution)/shard_map/ppermute | solution.py:542
  4.6 12.7 %collective-permute-start.1 = (bf16[128,640]{1,0:T(8,128)(2,1)S(1)}, bf16[128,640]{1,0:T(8,128)(2,1)S(1)}, u32[]{:S(2)}, u32[]{:S(2)}) collective-permute-start(bf16[128,640]{1,0:T(8,128)(2,1)S(1)} %get-tuple-element.33), channel_id=1, source_target_pairs={{0,8},{4,12},{8,0},{12,4},{1,9},{5,13},{9,1},{13,5},{2,10},{6,14},... | collective-permute-start | bytes 491528 | tf_op jit(solution)/shard_map/ppermute | solution.py:542
  7.2 10.1 %collective-permute-start.2 = (bf16[128,640]{1,0:T(8,128)(2,1)S(1)}, bf16[128,640]{1,0:T(8,128)(2,1)S(1)}, u32[]{:S(2)}, u32[]{:S(2)}) collective-permute-start(bf16[128,640]{1,0:T(8,128)(2,1)S(1)} %get-tuple-element.34), channel_id=1, source_target_pairs={{0,12},{4,0},{8,4},{12,8},{1,13},{5,1},{9,5},{13,9},{2,14},{6,2},{... | collective-permute-start | bytes 491528 | tf_op jit(solution)/shard_map/ppermute | solution.py:542
  16.9 8.8 %collective-permute-start.3 = (bf16[48,2048]{1,0:T(8,128)(2,1)S(1)}, bf16[48,2048]{1,0:T(8,128)(2,1)S(1)}, u32[]{:S(2)}, u32[]{:S(2)}) collective-permute-start(bf16[48,2048]{1,0:T(8,128)(2,1)S(1)} %get-tuple-element.30.rest_0_), channel_id=1, source_target_pairs={{0,8},{4,12},{8,0},{12,4},{1,9},{5,13},{9,1},{13,5},{2,10},{6,14},... | collective-permute-start | bytes 589832 | tf_op jit(solution)/shard_map/ppermute | solution.py:381
  17.2 10.8 %collective-permute-start.4 = (bf16[48,2048]{1,0:T(8,128)(2,1)S(1)}, bf16[48,2048]{1,0:T(8,128)(2,1)S(1)}, u32[]{:S(2)}, u32[]{:S(2)}) collective-permute-start(bf16[48,2048]{1,0:T(8,128)(2,1)S(1)} %get-tuple-element.30.rest_0_), channel_id=1, source_target_pairs={{0,4},{4,0},{8,12},{12,8},{1,5},{5,1},{9,13},{13,9},{2,6},{6,2},{1... | collective-permute-start | bytes 589832 | tf_op jit(solution)/shard_map/ppermute | solution.py:406
  25.7 2.3 %collective-permute-start.5 = (bf16[48,2048]{1,0:T(8,128)(2,1)S(1)}, bf16[48,2048]{1,0:T(8,128)(2,1)S(1)}, u32[]{:S(2)}, u32[]{:S(2)}) collective-permute-start(bf16[48,2048]{1,0:T(8,128)(2,1)S(1)} %stack.4), channel_id=1, source_target_pairs={{0,4},{4,0},{8,12},{12,8},{1,5},{5,1},{9,13},{13,9},{2,6},{6,2},{1... | collective-permute-start | bytes 589832 | tf_op jit(solution)/shard_map/ppermute | solution.py:406
  26.3 12.1 %collective-permute-start.7 = (bf16[80,2048]{1,0:T(8,128)(2,1)S(1)}, bf16[80,2048]{1,0:T(8,128)(2,1)S(1)}, u32[]{:S(2)}, u32[]{:S(2)}) collective-permute-start(bf16[80,2048]{1,0:T(8,128)(2,1)S(1)} %get-tuple-element.36.refs_1_.rest_4_.rest_0_), channel_id=1, source_target_pairs={{0,8},{4,12},{8,0},{12,4},{1,9},{5,13},{9,1},{13,5},{2,10},{6,14},... | collective-permute-start | bytes 983048 | tf_op jit(solution)/shard_map/ppermute | solution.py:381
  28.0 10.7 %collective-permute-start.8 = (bf16[80,2048]{1,0:T(8,128)(2,1)S(1)}, bf16[80,2048]{1,0:T(8,128)(2,1)S(1)}, u32[]{:S(2)}, u32[]{:S(2)}) collective-permute-start(bf16[80,2048]{1,0:T(8,128)(2,1)S(1)} %get-tuple-element.36.refs_1_.rest_4_.rest_0_), channel_id=1, source_target_pairs={{0,4},{4,0},{8,12},{12,8},{1,5},{5,1},{9,13},{13,9},{2,6},{6,2},{1... | collective-permute-start | bytes 983048 | tf_op jit(solution)/shard_map/ppermute | solution.py:406
  29.8 16.1 %collective-permute-start.6 = (bf16[144,1792]{1,0:T(8,128)(2,1)S(1)}, bf16[144,1792]{1,0:T(8,128)(2,1)S(1)}, u32[]{:S(2)}, u32[]{:S(2)}) collective-permute-start(bf16[144,1792]{1,0:T(8,128)(2,1)S(1)} %get-tuple-element.38.refs_0_), channel_id=1, source_target_pairs={{0,1},{3,2},{4,5},{7,6},{8,9},{11,10},{12,13},{15,14},{16,17},{19,... | collective-permute-start | bytes 1548296 | tf_op jit(solution)/shard_map/ppermute | solution.py:566
  38.4 8.2 %copy-start.2 = (s32[16,4]{0,1:T(4,128)S(1)}, s32[16,4]{0,1:T(4,128)}, u32[]{:S(2)}) copy-start(s32[16,4]{0,1:T(4,128)} %param.26) | copy-start | bytes 772
  38.4 8.2 %copy-start.4 = (s32[16]{0:T(128)S(1)}, s32[16]{0:T(128)}, u32[]{:S(2)}) copy-start(s32[16]{0:T(128)} %decode_length.1) | copy-start | bytes 196
  38.4 1.7 %collective-permute-start.9 = (bf16[80,2048]{1,0:T(8,128)(2,1)S(1)}, bf16[80,2048]{1,0:T(8,128)(2,1)S(1)}, u32[]{:S(2)}, u32[]{:S(2)}) collective-permute-start(bf16[80,2048]{1,0:T(8,128)(2,1)S(1)} %stack.5), channel_id=1, source_target_pairs={{0,4},{4,0},{8,12},{12,8},{1,5},{5,1},{9,13},{13,9},{2,6},{6,2},{1... | collective-permute-start | bytes 983048 | tf_op jit(solution)/shard_map/ppermute | solution.py:406
  42.9 20.4 %collective-permute-start.17 = (bf16[240,1792]{1,0:T(8,128)(2,1)S(1)}, bf16[240,1792]{1,0:T(8,128)(2,1)S(1)}, u32[]{:S(2)}, u32[]{:S(2)}) collective-permute-start(bf16[240,1792]{1,0:T(8,128)(2,1)S(1)} %get-tuple-element.41.refs_0_), channel_id=1, source_target_pairs={{0,1},{3,2},{4,5},{7,6},{8,9},{11,10},{12,13},{15,14},{16,17},{19,... | collective-permute-start | bytes 2580488 | tf_op jit(solution)/shard_map/ppermute | solution.py:566
  44.4 11.7 %collective-permute-start.11 = (bf16[64,2048]{1,0:T(8,128)(2,1)S(1)}, bf16[64,2048]{1,0:T(8,128)(2,1)S(1)}, u32[]{:S(2)}, u32[]{:S(2)}) collective-permute-start(bf16[64,2048]{1,0:T(8,128)(2,1)S(1)} %attend.4.refs_1_.rest_4_.rest_0_), channel_id=1, source_target_pairs={{0,8},{4,12},{8,0},{12,4},{1,9},{5,13},{9,1},{13,5},{2,10},{6,14},... | collective-permute-start | bytes 786440 | tf_op jit(solution)/shard_map/ppermute | solution.py:381
  45.8 11.4 %collective-permute-start.12 = (bf16[64,2048]{1,0:T(8,128)(2,1)S(1)}, bf16[64,2048]{1,0:T(8,128)(2,1)S(1)}, u32[]{:S(2)}, u32[]{:S(2)}) collective-permute-start(bf16[64,2048]{1,0:T(8,128)(2,1)S(1)} %attend.4.refs_1_.rest_4_.rest_0_), channel_id=1, source_target_pairs={{0,4},{4,0},{8,12},{12,8},{1,5},{5,1},{9,13},{13,9},{2,6},{6,2},{1... | collective-permute-start | bytes 786440 | tf_op jit(solution)/shard_map/ppermute | solution.py:406
  45.9 14.2 %collective-permute-start.10 = (bf16[96,1792]{1,0:T(8,128)(2,1)S(1)}, bf16[96,1792]{1,0:T(8,128)(2,1)S(1)}, u32[]{:S(2)}, u32[]{:S(2)}) collective-permute-start(bf16[96,1792]{1,0:T(8,128)(2,1)S(1)} %add.14.rest_4_), channel_id=1, source_target_pairs={{1,2},{2,1},{5,6},{6,5},{9,10},{10,9},{13,14},{14,13},{17,18},{18,... | collective-permute-start | bytes 1032200 | tf_op jit(solution)/shard_map/ppermute | solution.py:569
  56.1 1.7 %collective-permute-start.13 = (bf16[64,2048]{1,0:T(8,128)(2,1)S(1)}, bf16[64,2048]{1,0:T(8,128)(2,1)S(1)}, u32[]{:S(2)}, u32[]{:S(2)}) collective-permute-start(bf16[64,2048]{1,0:T(8,128)(2,1)S(1)} %stack.6), channel_id=1, source_target_pairs={{0,4},{4,0},{8,12},{12,8},{1,5},{5,1},{9,13},{13,9},{2,6},{6,2},{1... | collective-permute-start | bytes 786440 | tf_op jit(solution)/shard_map/ppermute | solution.py:406
  56.7 8.3 %collective-permute-start.15 = (bf16[64,2048]{1,0:T(8,128)(2,1)S(1)}, bf16[64,2048]{1,0:T(8,128)(2,1)S(1)}, u32[]{:S(2)}, u32[]{:S(2)}) collective-permute-start(bf16[64,2048]{1,0:T(8,128)(2,1)S(1)} %attend.5.refs_1_.rest_4_.rest_0_), channel_id=1, source_target_pairs={{0,8},{4,12},{8,0},{12,4},{1,9},{5,13},{9,1},{13,5},{2,10},{6,14},... | collective-permute-start | bytes 786440 | tf_op jit(solution)/shard_map/ppermute | solution.py:381
  57.3 14.8 %collective-permute-start.16 = (bf16[64,2048]{1,0:T(8,128)(2,1)S(1)}, bf16[64,2048]{1,0:T(8,128)(2,1)S(1)}, u32[]{:S(2)}, u32[]{:S(2)}) collective-permute-start(bf16[64,2048]{1,0:T(8,128)(2,1)S(1)} %attend.5.refs_1_.rest_4_.rest_0_), channel_id=1, source_target_pairs={{0,4},{4,0},{8,12},{12,8},{1,5},{5,1},{9,13},{13,9},{2,6},{6,2},{1... | collective-permute-start | bytes 786440 | tf_op jit(solution)/shard_map/ppermute | solution.py:406
  65.0 7.1 %collective-permute-start.18 = (bf16[64,2048]{1,0:T(8,128)(2,1)S(1)}, bf16[64,2048]{1,0:T(8,128)(2,1)S(1)}, u32[]{:S(2)}, u32[]{:S(2)}) collective-permute-start(bf16[64,2048]{1,0:T(8,128)(2,1)S(1)} %stack.7), channel_id=1, source_target_pairs={{0,4},{4,0},{8,12},{12,8},{1,5},{5,1},{9,13},{13,9},{2,6},{6,2},{1... | collective-permute-start | bytes 786440 | tf_op jit(solution)/shard_map/ppermute | solution.py:406
  65.1 20.4 %collective-permute-start.20 = (bf16[128,1792]{1,0:T(8,128)(2,1)S(1)}, bf16[128,1792]{1,0:T(8,128)(2,1)S(1)}, u32[]{:S(2)}, u32[]{:S(2)}) collective-permute-start(bf16[128,1792]{1,0:T(8,128)(2,1)S(1)} %get-tuple-element.44.refs_0_), channel_id=1, source_target_pairs={{0,1},{3,2},{4,5},{7,6},{8,9},{11,10},{12,13},{15,14},{16,17},{19,... | collective-permute-start | bytes 1376264 | tf_op jit(solution)/shard_map/ppermute | solution.py:566
  71.3 15.0 %collective-permute-start.19 = (bf16[160,1792]{1,0:T(8,128)(2,1)S(1)}, bf16[160,1792]{1,0:T(8,128)(2,1)S(1)}, u32[]{:S(2)}, u32[]{:S(2)}) collective-permute-start(bf16[160,1792]{1,0:T(8,128)(2,1)S(1)} %add.16.refs_1_.rest_5_), channel_id=1, source_target_pairs={{1,2},{2,1},{5,6},{6,5},{9,10},{10,9},{13,14},{14,13},{17,18},{18,... | collective-permute-start | bytes 1720328 | tf_op jit(solution)/shard_map/ppermute | solution.py:569
  74.3 18.0 %collective-permute-start.22 = (bf16[128,1792]{1,0:T(8,128)(2,1)S(1)}, bf16[128,1792]{1,0:T(8,128)(2,1)S(1)}, u32[]{:S(2)}, u32[]{:S(2)}) collective-permute-start(bf16[128,1792]{1,0:T(8,128)(2,1)S(1)} %get-tuple-element.45.refs_0_), channel_id=1, source_target_pairs={{0,1},{3,2},{4,5},{7,6},{8,9},{11,10},{12,13},{15,14},{16,17},{19,... | collective-permute-start | bytes 1376264 | tf_op jit(solution)/shard_map/ppermute | solution.py:566
  77.3 8.1 %collective-permute-start.14 = (bf16[48,1792]{1,0:T(8,128)(2,1)S(1)}, bf16[48,1792]{1,0:T(8,128)(2,1)S(1)}, u32[]{:S(2)}, u32[]{:S(2)}) collective-permute-start(bf16[48,1792]{1,0:T(8,128)(2,1)S(1)} %add.15.refs_2_.rest_6_), channel_id=1, source_target_pairs={{1,0},{2,3},{5,4},{6,7},{9,8},{10,11},{13,12},{14,15},{17,16},{18,... | collective-permute-start | bytes 516104 | tf_op jit(solution)/shard_map/ppermute | solution.py:572
  85.6 11.4 %collective-permute-start.24 = (bf16[128,1792]{1,0:T(8,128)(2,1)S(1)}, bf16[128,1792]{1,0:T(8,128)(2,1)S(1)}, u32[]{:S(2)}, u32[]{:S(2)}) collective-permute-start(bf16[128,1792]{1,0:T(8,128)(2,1)S(1)} %add.18.refs_2_), channel_id=1, source_target_pairs={{1,2},{2,1},{5,6},{6,5},{9,10},{10,9},{13,14},{14,13},{17,18},{18,... | collective-permute-start | bytes 1376264 | tf_op jit(solution)/shard_map/ppermute | solution.py:569
  86.4 9.7 %collective-permute-start.21 = (bf16[80,1792]{1,0:T(8,128)(2,1)S(1)}, bf16[80,1792]{1,0:T(8,128)(2,1)S(1)}, u32[]{:S(2)}, u32[]{:S(2)}) collective-permute-start(bf16[80,1792]{1,0:T(8,128)(2,1)S(1)} %add.19.refs_2_), channel_id=1, source_target_pairs={{1,0},{2,3},{5,4},{6,7},{9,8},{10,11},{13,12},{14,15},{17,16},{18,... | collective-permute-start | bytes 860168 | tf_op jit(solution)/shard_map/ppermute | solution.py:572
  87.7 13.7 %collective-permute-start.23 = (bf16[128,1792]{1,0:T(8,128)(2,1)S(1)}, bf16[128,1792]{1,0:T(8,128)(2,1)S(1)}, u32[]{:S(2)}, u32[]{:S(2)}) collective-permute-start(bf16[128,1792]{1,0:T(8,128)(2,1)S(1)} %get-tuple-element.46.refs_0_), channel_id=1, source_target_pairs={{0,1},{3,2},{4,5},{7,6},{8,9},{11,10},{12,13},{15,14},{16,17},{19,... | collective-permute-start | bytes 1376264 | tf_op jit(solution)/shard_map/ppermute | solution.py:566
  92.4 6.0 %collective-permute-start.26 = (bf16[64,1792]{1,0:T(8,128)(2,1)S(1)}, bf16[64,1792]{1,0:T(8,128)(2,1)S(1)}, u32[]{:S(2)}, u32[]{:S(2)}) collective-permute-start(bf16[64,1792]{1,0:T(8,128)(2,1)S(1)} %add.20.refs_4_), channel_id=1, source_target_pairs={{1,2},{2,1},{5,6},{6,5},{9,10},{10,9},{13,14},{14,13},{17,18},{18,... | collective-permute-start | bytes 688136 | tf_op jit(solution)/shard_map/ppermute | solution.py:569
  96.3 12.2 %collective-permute-start.27 = (bf16[64,1792]{1,0:T(8,128)(2,1)S(1)}, bf16[64,1792]{1,0:T(8,128)(2,1)S(1)}, u32[]{:S(2)}, u32[]{:S(2)}) collective-permute-start(bf16[64,1792]{1,0:T(8,128)(2,1)S(1)} %add.22.refs_2_), channel_id=1, source_target_pairs={{1,2},{2,1},{5,6},{6,5},{9,10},{10,9},{13,14},{14,13},{17,18},{18,... | collective-permute-start | bytes 688136 | tf_op jit(solution)/shard_map/ppermute | solution.py:569
  97.1 11.3 %collective-permute-start.25 = (bf16[64,1792]{1,0:T(8,128)(2,1)S(1)}, bf16[64,1792]{1,0:T(8,128)(2,1)S(1)}, u32[]{:S(2)}, u32[]{:S(2)}) collective-permute-start(bf16[64,1792]{1,0:T(8,128)(2,1)S(1)} %add.23.refs_2_), channel_id=1, source_target_pairs={{1,0},{2,3},{5,4},{6,7},{9,8},{10,11},{13,12},{14,15},{17,16},{18,... | collective-permute-start | bytes 688136 | tf_op jit(solution)/shard_map/ppermute | solution.py:572
  98.5 12.9 %collective-permute-start.28 = (bf16[64,1792]{1,0:T(8,128)(2,1)S(1)}, bf16[64,1792]{1,0:T(8,128)(2,1)S(1)}, u32[]{:S(2)}, u32[]{:S(2)}) collective-permute-start(bf16[64,1792]{1,0:T(8,128)(2,1)S(1)} %add.24.refs_4_), channel_id=1, source_target_pairs={{1,0},{2,3},{5,4},{6,7},{9,8},{10,11},{13,12},{14,15},{17,16},{18,... | collective-permute-start | bytes 688136 | tf_op jit(solution)/shard_map/ppermute | solution.py:572

commit v7 on v6

--- a/solution.py
+++ b/solution.py
@@ -33,7 +33,7 @@
 
 def chunk_sizes(tok_group):
     if tok_group == 256:
-        return (48, 80, 64, 64)
+        return (48, 64, 80, 64)
     return (tok_group,)
 
 
@@ -117,12 +117,13 @@
     prior = blocks * block_len
     tok_group = new_latent.shape[0]
 
-    rope_copy = pltpu.make_async_copy(q_rope_hbm, q_rope, wsems.at[0])
-    wk_copies = pieces(wk_hbm, wk, wsems, 1)
-    wv_copies = pieces(wv_hbm, wv, wsems, 1 + PIECES)
-    for c in wk_copies:
+    rope_copies = [pltpu.make_async_copy(
+        q_rope_hbm.at[pl.ds(at, size)], q_rope.at[pl.ds(at, size)], wsems.at[n])
+        for n, (at, size) in enumerate(((0, t), (t, tok_group - t))) if size]
+    wk_copies = pieces(wk_hbm, wk, wsems, 2)
+    later = pieces(wv_hbm, wv, wsems, 2 + PIECES) + rope_copies[1:]
+    for c in wk_copies + rope_copies[:1]:
         c.start()
-    rope_copy.start()
     copies = []
     for i in range(blocks):
         copies.append(pltpu.make_async_copy(
@@ -130,7 +131,7 @@
             keys.at[pl.ds(i * block_len, block_len), pl.ds(0, latent)], sems.at[i]))
     copies.append(pltpu.make_async_copy(
         new_latent, keys.at[pl.ds(prior, tok_group), pl.ds(0, latent)], sems.at[blocks]))
-    for c in copies + wv_copies:
+    for c in copies:
         c.start()
 
     keys[prior:, latent:] = rope_rows(new_rope_t[...])
@@ -141,7 +142,7 @@
         rope = cache_rope[table[0, i]].astype(jnp.float32) + hide
         keys[i * block_len:(i + 1) * block_len, latent:] = rope.astype(jnp.bfloat16)
 
-    rope_copy.wait()
+    rope_copies[0].wait()
 
     def ready(h):
         if h * PIECES % heads == 0:
@@ -150,43 +151,32 @@
     build_queries(q, q_nope, q_rope, 0, wk, ready)
     for c in copies:
         c.wait()
+    for c in later:
+        c.start()
     prefill(q, keys, att, heads, t, 0, prior, fresh, exp_scale)
-    for c in wv_copies:
+    for c in later:
         c.wait()
     head_outputs(out, att, wv, t)
 
 
-def pack_kernel(me, ids, cache_latent, cache_rope, *rest):
-    outs, sems = rest[:-1], rest[-1]
-    groups = len(outs)
+def pack_kernel(n_after, plan, me, ids, cache_latent, cache_rope, *rest):
+    outs, sems = rest[n_after:-1], rest[-1]
     block_len, latent = cache_latent.shape[1:]
     copies = []
-    for s, out in enumerate(outs):
-        to = lax.rem(me[0] + s, groups)
-        for k in range(ids.shape[1]):
-            rows = pl.ds(k * block_len, block_len)
-            copies.append(pltpu.make_async_copy(
-                cache_latent.at[ids[0, k, to]], out.at[rows, pl.ds(0, latent)], sems.at[len(copies)]))
-    for c in copies:
-        c.start()
-    for s, out in enumerate(outs):
-        to = lax.rem(me[0] + s, groups)
-        for k in range(ids.shape[1]):
-            out[k * block_len:(k + 1) * block_len, latent:] = cache_rope[ids[0, k, to]]
-    for c in copies:
-        c.wait()
-
-
-def second_kernel(first, fresh, prior, exp_scale, n_after, q_nope, q_rope, wk, wv, keys, w_hbm, *rest):
-    out, w, q, att, sems = rest[n_after:]
-    heads = q_nope.shape[0]
-    t = out.shape[0]
-    copies = pieces(w_hbm, w, sems, 0)
-    for c in copies:
-        c.start()
-    build_queries(q, q_nope, q_rope, first, wk)
-    prefill(q, keys, att, heads, t, first, prior, fresh, exp_scale)
-    head_outputs(out, att, wv, t)
+    places = []
+    for out, targets in zip(outs, plan):
+        row = 0
+        for target in targets:
+            to = target(me[0])
+            for k in range(ids.shape[1]):
+                places.append((out, row, ids[0, k, to]))
+                row += block_len
+    for n, (out, row, b) in enumerate(places):
+        copies.append(pltpu.make_async_copy(
+            cache_latent.at[b], out.at[pl.ds(row, block_len), pl.ds(0, latent)], sems.at[n]))
+        copies[-1].start()
+    for out, row, b in places:
+        out[row:row + block_len, latent:] = cache_rope[b]
     for c in copies:
         c.wait()
 
@@ -200,16 +190,15 @@
     head_outputs(out, att, wv, t)
 
 
-def last_kernel(first, fresh, prior, prefill_len, exp_scale, n_after, me, q_nope, q_rope, wk, wv, keys,
+def last_kernel(first, fresh, prior, prefill_len, exp_scale, n_after, spots, got, me, q_nope, q_rope, wk, wv, keys,
                 flat_latent, cache_rope, decode_table, decode_length, *rest):
     received = rest[:-5 - n_after]
     out, q, att, dkeys, sems = rest[-5:]
-    groups = len(received)
+    groups = len(spots)
     heads = q_nope.shape[0]
     t = out.shape[0]
     pool, block_len, _ = cache_rope.shape
     latent = flat_latent.shape[1]
-    got = received[0].shape[0]
     ext = pool * block_len + groups * got
     tail = dkeys.shape[0] - ext
     start = keys.shape[0] - tail
@@ -222,10 +211,9 @@
         c.start()
     for i in range(pool):
         dkeys[i * block_len:(i + 1) * block_len, latent:] = cache_rope[i]
-    for s in range(groups):
-        source = lax.rem(me[0] + groups - s, groups)
-        at = pl.multiple_of(pool * block_len + source * got, block_len)
-        dkeys[pl.ds(at, got), :] = received[s][...]
+    for n, row, source in spots:
+        at = pl.multiple_of(pool * block_len + source(me[0]) * got, block_len)
+        dkeys[pl.ds(at, got), :] = received[n][row:row + got, :]
     dkeys[ext:, :] = keys[start:, :]
 
     build_queries(q, q_nope, q_rope, first, wk)
@@ -325,26 +313,34 @@
     )(me[None], z[None], w, *parts, *earlier, *after)
 
 
-def add_kernel(spans, n_after, *refs):
+def add_kernel(sums, *refs):
     out = refs[-1]
-    n = out.shape[0]
-    total = None
-    for ref, at in zip(refs, spans):
-        x = ref[at:at + n, :].astype(jnp.float32)
-        total = x if total is None else total + x
-    out[...] = total.astype(jnp.bfloat16)
-
-
-def add(rows, terms, after=()):
+    row = i = 0
+    for rows, spans in sums:
+        total = None
+        for at in spans:
+            x = refs[i][at:at + rows, :].astype(jnp.float32)
+            total = x if total is None else total + x
+            i += 1
+        out[row:row + rows, :] = total.astype(jnp.bfloat16)
+        row += rows
+
+
+def add_all(sums, after=()):
+    terms = [x for _, parts in sums for x, _ in parts]
     return pl.pallas_call(
-        functools.partial(add_kernel, [at for _, at in terms], len(after)),
-        out_shape=jax.ShapeDtypeStruct((rows, terms[0][0].shape[1]), jnp.bfloat16),
+        functools.partial(add_kernel, [(rows, [at for _, at in parts]) for rows, parts in sums]),
+        out_shape=jax.ShapeDtypeStruct((sum(rows for rows, _ in sums), terms[0].shape[1]), jnp.bfloat16),
         in_specs=[VMEM] * len(terms) + [ANY] * len(after),
         out_specs=VMEM,
         name="add",
         compiler_params=params(8),
         cost_estimate=COST,
-    )(*[x for x, _ in terms], *after)
+    )(*terms, *after)
+
+
+def add(rows, terms, after=()):
+    return add_all([(rows, terms)], after)
 
 
 def finish_kernel(n_ready, spans, *refs):
@@ -353,7 +349,7 @@
     for ref in refs[:n_ready]:
         out[row:row + ref.shape[0], :] = ref[...]
         row += ref.shape[0]
-    add_kernel(spans, 0, *refs[n_ready:-1], out.at[row:, :])
+    add_kernel([(out.shape[0] - row, spans)], *refs[n_ready:-1], out.at[row:, :])
 
 
 def finish(ready, terms):
@@ -382,24 +378,26 @@
                   for s in range(step, groups, step)]
 
 
-def stack_kernel(count, *refs):
+def stack_kernel(firsts, *refs):
     out, at = refs[-1], 0
-    for ref in refs[:count]:
-        out[at:at + ref.shape[0], :] = ref[...]
-        at += ref.shape[0]
+    for ref, first in zip(refs, firsts):
+        n = ref.shape[0] - first
+        out[at:at + n, :] = ref[first:, :]
+        at += n
 
 
 def stack(parts, after=()):
-    rows = sum(p.shape[0] for p in parts)
+    parts = [p if isinstance(p, tuple) else (p, 0) for p in parts]
+    rows = sum(p.shape[0] - first for p, first in parts)
     return pl.pallas_call(
-        functools.partial(stack_kernel, len(parts)),
-        out_shape=jax.ShapeDtypeStruct((rows, parts[0].shape[1]), parts[0].dtype),
+        functools.partial(stack_kernel, [first for _, first in parts]),
+        out_shape=jax.ShapeDtypeStruct((rows, parts[0][0].shape[1]), jnp.bfloat16),
         in_specs=[VMEM] * len(parts) + [ANY] * len(after),
         out_specs=VMEM,
         name="stack",
         compiler_params=params(4),
         cost_estimate=COST,
-    )(*parts, *after)
+    )(*[p for p, _ in parts], *after)
 
 
 def swap_cores(x):
@@ -482,7 +480,7 @@
             scratch_shapes=[
                 *scratch(t),
                 pltpu.SemaphoreType.DMA((blocks + 1,)),
-                pltpu.SemaphoreType.DMA((2 * PIECES + 1,)),
+                pltpu.SemaphoreType.DMA((2 * PIECES + 2,)),
             ],
             name="attend_first",
             compiler_params=params(20),
@@ -496,18 +494,13 @@
         t = sizes[n]
         args = [q_nope, q_rope, wk, wv, keys]
         specs = [VMEM] * 5
-        outs = [jax.ShapeDtypeStruct((t, heads * dv), bf16)]
         scratches = scratch(t)
         limit = 20
         static = (starts[n], fresh_of(n), prior)
-        if n == 1:
-            kernel = functools.partial(second_kernel, *static, exp_scale, len(after))
-            args.append(in_hbm(output_weight))
-            specs = specs + [HBM]
-            outs.append(jax.ShapeDtypeStruct(output_weight.shape, bf16))
-            scratches.append(pltpu.SemaphoreType.DMA((PIECES,)))
-        elif n == len(sizes) - 1:
-            kernel = functools.partial(last_kernel, *static, prefill_len, exp_scale, len(after))
+        if n == len(sizes) - 1:
+            brought, spots = brought
+            kernel = functools.partial(
+                last_kernel, *static, prefill_len, exp_scale, len(after), spots, capacity * block_len)
             args = [me[None]] + args + [
                 in_hbm(cache_latent.reshape(pool * block_len, latent)), padded_rope, decode_table.T, decode_length, *brought]
             specs = [SMEM] + specs + [HBM, VMEM, SMEM, SMEM] + [VMEM] * len(brought)
@@ -518,46 +511,45 @@
             kernel = functools.partial(later_kernel, *static, exp_scale, len(after))
         return pl.pallas_call(
             kernel,
-            out_shape=outs,
+            out_shape=jax.ShapeDtypeStruct((t, heads * dv), bf16),
             in_specs=specs + [ANY] * len(after),
-            out_specs=[VMEM] * len(outs),
+            out_specs=VMEM,
             scratch_shapes=scratches,
             name="attend",
             compiler_params=params(limit),
             cost_estimate=SHORT if n == len(sizes) - 1 else LONG,
         )(*args, *after)
 
-    def migrate():
-        packed = pl.pallas_call(
-            pack_kernel,
-            out_shape=[jax.ShapeDtypeStruct((capacity * block_len, width), bf16)] * groups,
-            in_specs=[SMEM, SMEM, HBM, VMEM],
-            out_specs=[VMEM] * groups,
+    def pack(plan, after):
+        return pl.pallas_call(
+            functools.partial(pack_kernel, len(after), plan),
+            out_shape=[jax.ShapeDtypeStruct((len(p) * capacity * block_len, width), bf16) for p in plan],
+            in_specs=[SMEM, SMEM, HBM, VMEM] + [ANY] * len(after),
+            out_specs=[VMEM] * len(plan),
             scratch_shapes=[pltpu.SemaphoreType.DMA((groups * capacity,))],
             name="pack",
             compiler_params=params(8),
             cost_estimate=COST,
-        )(me[None], send_blocks.transpose(0, 2, 1), in_hbm(cache_latent), padded_rope)
+        )(me[None], send_blocks.transpose(0, 2, 1), in_hbm(cache_latent), padded_rope, *after)
+
+    def migrate():
+        packed = pack([(lambda g, s=s: lax.rem(g + s, groups),) for s in range(groups)], ())
         return [packed[0]] + [
             lax.ppermute(packed[s], "dp", [(i, (i + s) % groups) for i in range(groups)])
-            for s in range(1, groups)]
-
-    brought = migrate()
+            for s in range(1, groups)
+        ], [(s, 0, lambda g, s=s: lax.rem(g + groups - s, groups)) for s in range(groups)]
+
+    w = output_weight
     x0, *held = first_chunk()
     if not on_line:
         outs = []
-        w = None
+        brought = migrate()
         for n, t in enumerate(sizes):
-            if n == 0:
-                x = x0
-            elif n == 1:
-                x, w = attend(n, held, ())
-            else:
-                x, = attend(n, held, (), brought)
+            x = attend(n, held, (), brought) if n else x0
             mine = shift_groups(x)
             if groups % 2 == 0:
                 mine += [swap_cores(y) for y in mine]
-            own, others = project(where, mine, output_weight, (groups - 1,))
+            own, others = project(where, mine, w, (groups - 1,))
             partials = jnp.concatenate([own, others], axis=0).reshape(groups, t, columns)
             outs.append(lax.psum_scatter(partials, "tp", scatter_dimension=0, tiled=False))
         return jnp.concatenate(outs, axis=0)
@@ -576,42 +568,46 @@
         return [x, came, swap_cores(x), swap_cores(stack([came], after))]
 
     t0, t1, t2, t3 = sizes
-    x1, w = attend(1, held, (x0, *brought))
+    apart = [lambda g, k=k: g ^ k for k in range(4)]
+    own_blocks, core_blocks, far_blocks = pack([(apart[0],), (apart[1],), (apart[2], apart[3])], ())
+    x_blocks = lax.ppermute(far_blocks, "dp", [(i, i ^ 2) for i in range(groups)])
+    x1 = attend(1, held, (x0,))
+    half = capacity * block_len
+    on_blocks = swap_cores(stack([core_blocks, (x_blocks, half)], (x0,)))
+    brought = ((own_blocks, x_blocks, on_blocks), [(0, 0, apart[0]), (1, 0, apart[2]), (2, 0, apart[1]), (2, half, apart[3])])
     own0, rest0 = project(where, gather(x0, (x1,)), w, (3,), (), (x1,))
     in0 = inward(rest0)
-    x2, = attend(2, held, (own0,))
+    x2 = attend(2, held, (own0, on_blocks))
     own1, rest1 = project(where, gather(x1, (x2,)), w, (3,), (), (x2,))
     in1 = inward(rest1)
     to_across0 = add(2 * t0, [(rest0, 0), (in0, 0)], (own1,))
     on0 = across(to_across0)
-    x3, = attend(3, held, (to_across0,), brought)
+    x3 = attend(3, held, (to_across0,), brought)
     own2, rest2, near2 = project(where, gather(x2, (x3,)), w, (2, 1), (), (x3,))
     in2 = inward(rest2)
-    to_across1 = add(2 * t1, [(rest1, 0), (in1, 0)], (own2,))
+    to_across1 = add(2 * t1, [(rest1, 0), (in1, 0)], (own2, on0))
     on1 = across(to_across1)
-    to_out0 = add(t0, [(rest0, 2 * t0), (on0, 0)], (own2,))
-    out0 = outward(to_out0)
     own3, rest3, near = project(
-        where, gather(x3, (to_across1, to_out0)), w, (2, 1), (near2,),
-        (to_across1, to_out0))
-    done0 = add(t0, [(own0, 0), (in0, 2 * t0), (on0, t0), (out0, 0)], (own3,))
+        where, gather(x3, (own2,)), w, (2, 1), (near2,), (to_across1,))
     in3 = inward(rest3)
-    to_across2 = add(2 * t2, [(rest2, 0), (in2, 0)], (done0,))
+    to_across2 = add(2 * t2, [(rest2, 0), (in2, 0)], (own3,))
     on2 = across(to_across2)
     near_in = inward(near)
-    to_out1 = add(t1, [(rest1, 2 * t1), (on1, 0)], (to_across2,))
-    out1 = outward(to_out1)
-    to_far = add(t3, [(rest3, 0), (in3, 0)], (to_out1,))
+    to_out01 = add_all([(t0, [(rest0, 2 * t0), (on0, 0)]), (t1, [(rest1, 2 * t1), (on1, 0)])],
+                       (to_across2,))
+    out01 = outward(to_out01)
+    to_far = add(t3, [(rest3, 0), (in3, 0)], (to_out01,))
     far_on = across(to_far)
-    done1 = add(t1, [(own1, 0), (in1, 2 * t1), (on1, t1), (out1, 0)], (to_far,))
-    to_mid = add(t3, [(rest3, t3), (in3, t3)], (done1,))
+    to_mid = add(t3, [(rest3, t3), (in3, t3)], (to_far,))
     mid_on = across(to_mid)
-    to_out2 = add(t2, [(near2, 0), (on2, 0)], (to_mid,))
+    done01 = add_all([(t0, [(own0, 0), (in0, 2 * t0), (on0, t0), (out01, 0)]),
+                      (t1, [(own1, 0), (in1, 2 * t1), (on1, t1), (out01, t0)])], (to_mid,))
+    to_out2 = add(t2, [(near2, 0), (on2, 0)], (done01,))
     out2 = outward(to_out2)
     to_out3 = add(t3, [(near, t2), (far_on, 0)], (to_out2,))
     out3 = outward(to_out3)
     done2 = add(t2, [(own2, 0), (near_in, 0), (on2, t2), (out2, 0)], (to_out3,))
-    return finish([done0, done1, done2], [(own3, 0), (near_in, t2), (mid_on, 0), (out3, 0)])
+    return finish([done01, done2], [(own3, 0), (near_in, t2), (mid_on, 0), (out3, 0)])
 
 
 def solution(mesh):

time: 113 us -> 106 us (0.938)
  waiting for transfers between devices: 28 us -> 21.4 us
  Pallas kernels: 43 us -> 40.3 us
  starting transfers between devices: 37.7 us -> 40.4 us
    ppermute x5, starting transfers between devices: 18.9 us -> 24.8 us  [inward(): return lax.ppermute(x, 'tp', INWARD)]
    ppermute x4 -> x3, waiting for transfers between devices: 19.7 us -> 14.1 us  [outward(): return lax.ppermute(x, 'tp', OUTWARD)]
    pallas_call x20 -> x19, Pallas kernels: 25.5 us -> 22.9 us  [the longest x3 20.1 us: attend(): pl.pallas_call(kernel, out_shape=jax.ShapeDtypeStruct((t, heads * dv), bf...]
    ppermute x3 -> x1, starting transfers between devices: 4.46 us -> 3 us  [body(): lax.ppermute(far_blocks, 'dp', [(i, i ^ 2) for i in range(groups)])]
    ppermute x4 -> x3, starting transfers between devices: 5.17 us -> 3.88 us  [outward(): return lax.ppermute(x, 'tp', OUTWARD)]
  transfers between devices with their start and end apart: 29 -> 27, of which waited for: 9 -> 11; matrix products, arithmetic and copies ran while one was open for 0% -> 0% of each run, Pallas kernels for 36% -> 35%
where the time goes in v7:
time: 106 us
  starting transfers between devices  40.4 us (38%)
  Pallas kernels  40.3 us (38%)
  waiting for transfers between devices  21.4 us (20%)
  local copies, waits for them, and re-layouts  2.68 us (3%)
  between operations  1.1 us (1%)
    ppermute x5, starting transfers between devices, inward(): return lax.ppermute(x, 'tp', INWARD)  24.8 us
    pallas_call x3, Pallas kernels, attend(): pl.pallas_call(kernel, out_shape=jax.ShapeDtypeStruct((t, heads * dv), bf...  20.1 us
    ppermute x3, waiting for transfers between devices, outward(): return lax.ppermute(x, 'tp', OUTWARD)  14.1 us
    pallas_call x4, Pallas kernels, project(): pl.pallas_call(functools.partial(project_kernel, len(parts), tails, place...  9.08 us
    pallas_call x1, Pallas kernels, first_chunk(): pl.pallas_call(functools.partial(first_kernel, fresh_of(0), exp_scale), o...  7.22 us
    ppermute x5, waiting for transfers between devices, inward(): return lax.ppermute(x, 'tp', INWARD)  5.42 us
    ppermute x3, starting transfers between devices, outward(): return lax.ppermute(x, 'tp', OUTWARD)  3.88 us
    ppermute x4, starting transfers between devices, shift_groups(): lax.ppermute(x, 'dp', [(i, (i + s) % groups) for i in range(groups)])  3.42 us
  transfers between devices with their start and end apart: 27, of which 11 were waited for; matrix products, arithmetic and copies ran while one was open for 0% of the time, Pallas kernels for 35%

profile of v7, /device:TPU:0, one launch (start us, length us, event | category | flops | bytes accessed | tf_op | source)
XLA Modules:
  0.0 105.8 jit_solution(6803597486337360601)
XLA Ops:
  0.0 1.6 %reshape.6 = bf16[32,64,64]{2,1,0:T(8,128)(2,1)S(1)} reshape(bf16[32,4096]{1,0:T(8,128)(2,1)} %param.19) | data formatting | bytes 524288 | tf_op jit(solution)/shard_map/reshape | solution.py:457
  1.6 0.1 pad.4.cache_rope
  1.7 0.0 copy-start
  1.7 0.7 copy-done
  2.4 1.7 %pack.1 = (bf16[128,640]{1,0:T(8,128)(2,1)S(1)}, bf16[128,640]{1,0:T(8,128)(2,1)S(1)}, bf16[256,640]{1,0:T(8,128)(2,1)S(1)}) custom-call(s32[1]{0:T(128)} %bitcast.me, s32[1,2,4]{2,1,0:T(2,128)S(1)} %bitcast.15, bf16[32,64,512]{2,1,0:T(8,128)(2,1)} %cache_latent.3, bf16[32,64,128]{2,1,0:T(8,128)(2,1)S(1)} %pad.4.cache_rope), custom_call_target="tpu_custom_call" | custom-call | flops 1000 | bytes 1000 | tf_op jit(solution)/shard_map/pack/pallas_call | solution.py:524
  4.1 3.0 %collective-permute-start.6 = (bf16[256,640]{1,0:T(8,128)(2,1)S(1)}, bf16[256,640]{1,0:T(8,128)(2,1)S(1)}, u32[]{:S(2)}, u32[]{:S(2)}) collective-permute-start(bf16[256,640]{1,0:T(8,128)(2,1)S(1)} %get-tuple-element.31), channel_id=1, source_target_pairs={{0,8},{4,12},{8,0},{12,4},{1,9},{5,13},{9,1},{13,5},{2,10},{6,14},... | collective-permute-start | bytes 983048 | tf_op jit(solution)/shard_map/ppermute | solution.py:573
  7.1 0.3 copy.17
  8.0 7.2 %attend_first.1 = (bf16[48,2048]{1,0:T(8,128)(2,1)S(1)}, bf16[1280,640]{1,0:T(8,128)(2,1)S(1)}, bf16[16,128,512]{2,1,0:T(8,128)(2,1)S(1)}, bf16[16,512,128]{2,1,0:T(8,128)(2,1)S(1)}, bf16[256,1024]{1,0:T(8,128)(2,1)S(1)}) custom-call(s32[1]{0:T(128)} %bitcast.me, s32[1]{0:T(128)} %bitcast.1.z, s32[1,16]{1,0:T(1,128)S(1)} %copy-done.3, s32[1]{0:T(128)S(6)} %copy.18.offset, ...), custom_call_target="tpu_custom_call" | custom-call | flops 40000000000 | bytes 1000 | tf_op jit(solution)/shard_map/attend_first/pallas_call | solution.py:471
  15.3 0.1 collective-permute-start
  15.4 0.1 collective-permute-start.1
  15.5 0.5 collective-permute-start.7
  16.0 4.7 %attend.3.refs_1_.rest_4_.rest_0_ = bf16[64,2048]{1,0:T(8,128)(2,1)S(1)} custom-call(bf16[16,256,128]{2,1,0:T(8,128)(2,1)S(1)} %bitcast.12, bf16[256,1024]{1,0:T(8,128)(2,1)S(1)} %get-tuple-element.24.q_rope, bf16[16,128,512]{2,1,0:T(8,128)(2,1)S(1)} %get-tuple-element.25.wk, bf16[16,512,128]{2,1,0:T(8,128)(2,1)S(1)} %get-tuple-element.26.wv, ...), custom_call_target="tpu_custom_call" | custom-call | flops 40000000000 | bytes 1000 | tf_op jit(solution)/shard_map/attend/pallas_call | solution.py:512
  20.8 0.9 collective-permute-done.refs_0_.rest_1_
  21.7 0.1 collective-permute-start.2
  21.8 1.1 %collective-permute-start.4 = (bf16[64,2048]{1,0:T(8,128)(2,1)S(1)}, bf16[64,2048]{1,0:T(8,128)(2,1)S(1)}, u32[]{:S(2)}, u32[]{:S(2)}) collective-permute-start(bf16[64,2048]{1,0:T(8,128)(2,1)S(1)} %attend.3.refs_1_.rest_4_.rest_0_), channel_id=1, source_target_pairs={{0,8},{4,12},{8,0},{12,4},{1,9},{5,13},{9,1},{13,5},{2,10},{6,14},... | collective-permute-start | bytes 786440 | tf_op jit(solution)/shard_map/ppermute | solution.py:377
  22.9 0.2 collective-permute-start.5
  23.1 0.2 collective-permute-done.2.rest_3_
  23.2 1.7 %project.4 = (bf16[48,1792]{1,0:T(8,128)(2,1)S(1)}, bf16[144,1792]{1,0:T(8,128)(2,1)S(1)}) custom-call(s32[1]{0:T(128)} %bitcast.me, s32[1]{0:T(128)} %bitcast.1.z, bf16[2048,1792]{1,0:T(8,128)(2,1)S(1)} %bitcast.10, bf16[48,2048]{1,0:T(8,128)(2,1)S(1)} %get-tuple-element.23.rest_0_.refs_2_, bf16[48,2048]{1,0:T(8,128)(2,1)S(1)} %collective-permute-done.refs_0_.rest_1_, ...), custom_call_target="tpu_custom_call" | custom-call | flops 1000 | bytes 1000 | tf_op jit(solution)/shard_map/project/pallas_call | solution.py:304
  25.0 3.7 %collective-permute-start.3 = (bf16[144,1792]{1,0:T(8,128)(2,1)S(1)}, bf16[144,1792]{1,0:T(8,128)(2,1)S(1)}, u32[]{:S(2)}, u32[]{:S(2)}) collective-permute-start(bf16[144,1792]{1,0:T(8,128)(2,1)S(1)} %get-tuple-element.29.refs_0_), channel_id=1, source_target_pairs={{0,1},{3,2},{4,5},{7,6},{8,9},{11,10},{12,13},{15,14},{16,17},{19,... | collective-permute-start | bytes 1548296 | tf_op jit(solution)/shard_map/ppermute | solution.py:558
  28.7 5.9 %attend.4.refs_1_.rest_4_.rest_0_ = bf16[80,2048]{1,0:T(8,128)(2,1)S(1)} custom-call(bf16[16,256,128]{2,1,0:T(8,128)(2,1)S(1)} %bitcast.13, bf16[256,1024]{1,0:T(8,128)(2,1)S(1)} %get-tuple-element.24.q_rope, bf16[16,128,512]{2,1,0:T(8,128)(2,1)S(1)} %get-tuple-element.25.wk, bf16[16,512,128]{2,1,0:T(8,128)(2,1)S(1)} %get-tuple-element.26.wv, ...), custom_call_target="tpu_custom_call" | custom-call | flops 40000000000 | bytes 1000 | tf_op jit(solution)/shard_map/attend/pallas_call | solution.py:512
  34.6 0.0 copy-start.2
  34.6 0.1 collective-permute-start.8
  34.7 1.1 %collective-permute-start.11 = (bf16[80,2048]{1,0:T(8,128)(2,1)S(1)}, bf16[80,2048]{1,0:T(8,128)(2,1)S(1)}, u32[]{:S(2)}, u32[]{:S(2)}) collective-permute-start(bf16[80,2048]{1,0:T(8,128)(2,1)S(1)} %attend.4.refs_1_.rest_4_.rest_0_), channel_id=1, source_target_pairs={{0,8},{4,12},{8,0},{12,4},{1,9},{5,13},{9,1},{13,5},{2,10},{6,14},... | collective-permute-start | bytes 983048 | tf_op jit(solution)/shard_map/ppermute | solution.py:377
  35.8 0.2 collective-permute-start.12
  36.0 0.2 collective-permute-done.8.rest_3_
  36.2 2.3 %project.5 = (bf16[64,1792]{1,0:T(8,128)(2,1)S(1)}, bf16[192,1792]{1,0:T(8,128)(2,1)S(1)}) custom-call(s32[1]{0:T(128)} %bitcast.me, s32[1]{0:T(128)} %bitcast.1.z, bf16[2048,1792]{1,0:T(8,128)(2,1)S(1)} %bitcast.10, bf16[64,2048]{1,0:T(8,128)(2,1)S(1)} %attend.3.refs_1_.rest_4_.rest_0_, bf16[64,2048]{1,0:T(8,128)(2,1)S(1)} %collective-permute-done.4.refs_0_.rest_1_, ...), custom_call_target="tpu_custom_call" | custom-call | flops 1000 | bytes 1000 | tf_op jit(solution)/shard_map/project/pallas_call | solution.py:304
  38.5 1.6 %collective-permute-start.10 = (bf16[192,1792]{1,0:T(8,128)(2,1)S(1)}, bf16[192,1792]{1,0:T(8,128)(2,1)S(1)}, u32[]{:S(2)}, u32[]{:S(2)}) collective-permute-start(bf16[192,1792]{1,0:T(8,128)(2,1)S(1)} %get-tuple-element.33.refs_0_.refs_2_), channel_id=1, source_target_pairs={{0,1},{3,2},{4,5},{7,6},{8,9},{11,10},{12,13},{15,14},{16,17},{19,... | collective-permute-start | bytes 2064392 | tf_op jit(solution)/shard_map/ppermute | solution.py:558
  40.1 0.1 add.12.rest_3_
  40.2 9.5 %attend.5.refs_1_.rest_4_.rest_0_ = bf16[64,2048]{1,0:T(8,128)(2,1)S(1)} custom-call(s32[1]{0:T(128)} %bitcast.me, bf16[16,256,128]{2,1,0:T(8,128)(2,1)S(1)} %bitcast.14, bf16[256,1024]{1,0:T(8,128)(2,1)S(1)} %get-tuple-element.24.q_rope, bf16[16,128,512]{2,1,0:T(8,128)(2,1)S(1)} %get-tuple-element.25.wk, bf16[16,512,128]{2,1,0:T(8,128)(2,1)S(1)} %get-tuple-element.26.wv, ...), custom_call_target="tpu_custom_call" | custom-call | flops 6000000000 | bytes 1000 | tf_op jit(solution)/shard_map/attend/pallas_call | solution.py:512
  49.7 0.2 collective-permute-start.13
  49.9 0.7 collective-permute-start.9
  50.6 1.1 %collective-permute-start.16 = (bf16[64,2048]{1,0:T(8,128)(2,1)S(1)}, bf16[64,2048]{1,0:T(8,128)(2,1)S(1)}, u32[]{:S(2)}, u32[]{:S(2)}) collective-permute-start(bf16[64,2048]{1,0:T(8,128)(2,1)S(1)} %attend.5.refs_1_.rest_4_.rest_0_), channel_id=1, source_target_pairs={{0,8},{4,12},{8,0},{12,4},{1,9},{5,13},{9,1},{13,5},{2,10},{6,14},... | collective-permute-start | bytes 786440 | tf_op jit(solution)/shard_map/ppermute | solution.py:377
  51.7 2.8 %project.6 = (bf16[80,1792]{1,0:T(8,128)(2,1)S(1)}, bf16[160,1792]{1,0:T(8,128)(2,1)S(1)}, bf16[80,1792]{1,0:T(8,128)(2,1)S(1)}) custom-call(s32[1]{0:T(128)} %bitcast.me, s32[1]{0:T(128)} %bitcast.1.z, bf16[2048,1792]{1,0:T(8,128)(2,1)S(1)} %bitcast.10, bf16[80,2048]{1,0:T(8,128)(2,1)S(1)} %attend.4.refs_1_.rest_4_.rest_0_, ...), custom_call_target="tpu_custom_call" | custom-call | flops 1000 | bytes 1000 | tf_op jit(solution)/shard_map/project/pallas_call | solution.py:304
  54.5 6.8 %collective-permute-start.15 = (bf16[160,1792]{1,0:T(8,128)(2,1)S(1)}, bf16[160,1792]{1,0:T(8,128)(2,1)S(1)}, u32[]{:S(2)}, u32[]{:S(2)}) collective-permute-start(bf16[160,1792]{1,0:T(8,128)(2,1)S(1)} %get-tuple-element.36.refs_0_), channel_id=1, source_target_pairs={{0,1},{3,2},{4,5},{7,6},{8,9},{11,10},{12,13},{15,14},{16,17},{19,... | collective-permute-start | bytes 1720328 | tf_op jit(solution)/shard_map/ppermute | solution.py:558
  61.3 0.1 collective-permute-start.17
  61.4 0.5 collective-permute-start.18
  62.0 0.1 add.13.rest_5_
  62.1 0.7 collective-permute-start.14
  62.8 0.1 collective-permute-done.17.rest_2_
  62.9 0.4 collective-permute-done.18.rest_3_
  63.3 2.3 %project.7 = (bf16[64,1792]{1,0:T(8,128)(2,1)S(1)}, bf16[128,1792]{1,0:T(8,128)(2,1)S(1)}, bf16[144,1792]{1,0:T(8,128)(2,1)S(1)}) custom-call(s32[1]{0:T(128)} %bitcast.me, s32[1]{0:T(128)} %bitcast.1.z, bf16[2048,1792]{1,0:T(8,128)(2,1)S(1)} %bitcast.10, bf16[64,2048]{1,0:T(8,128)(2,1)S(1)} %attend.5.refs_1_.rest_4_.rest_0_, ...), custom_call_target="tpu_custom_call" | custom-call | flops 1000 | bytes 1000 | tf_op jit(solution)/shard_map/project/pallas_call | solution.py:304
  65.6 6.6 %collective-permute-start.20 = (bf16[128,1792]{1,0:T(8,128)(2,1)S(1)}, bf16[128,1792]{1,0:T(8,128)(2,1)S(1)}, u32[]{:S(2)}, u32[]{:S(2)}) collective-permute-start(bf16[128,1792]{1,0:T(8,128)(2,1)S(1)} %get-tuple-element.39.refs_0_), channel_id=1, source_target_pairs={{0,1},{3,2},{4,5},{7,6},{8,9},{11,10},{12,13},{15,14},{16,17},{19,... | collective-permute-start | bytes 1376264 | tf_op jit(solution)/shard_map/ppermute | solution.py:558
  72.2 2.4 %collective-permute-done.15.refs_1_ = bf16[160,1792]{1,0:T(8,128)(2,1)S(1)} collective-permute-done((bf16[160,1792]{1,0:T(8,128)(2,1)S(1)}, bf16[160,1792]{1,0:T(8,128)(2,1)S(1)}, u32[]{:S(2)}, u32[]{:S(2)}) %collective-permute-start.15) | collective-permute-done | bytes 573472 | tf_op jit(solution)/shard_map/ppermute | solution.py:558
  74.6 0.1 add.14.refs_4_
  74.8 0.7 collective-permute-start.22
  75.5 0.1 add.15.refs_2_
  75.6 1.3 %collective-permute-start.19 = (bf16[112,1792]{1,0:T(8,128)(2,1)S(1)}, bf16[112,1792]{1,0:T(8,128)(2,1)S(1)}, u32[]{:S(2)}, u32[]{:S(2)}) collective-permute-start(bf16[112,1792]{1,0:T(8,128)(2,1)S(1)} %add.15.refs_2_), channel_id=1, source_target_pairs={{1,0},{2,3},{5,4},{6,7},{9,8},{10,11},{13,12},{14,15},{17,16},{18,... | collective-permute-start | bytes 1204232 | tf_op jit(solution)/shard_map/ppermute | solution.py:564
  76.9 6.1 %collective-permute-start.21 = (bf16[144,1792]{1,0:T(8,128)(2,1)S(1)}, bf16[144,1792]{1,0:T(8,128)(2,1)S(1)}, u32[]{:S(2)}, u32[]{:S(2)}) collective-permute-start(bf16[144,1792]{1,0:T(8,128)(2,1)S(1)} %get-tuple-element.40.refs_0_), channel_id=1, source_target_pairs={{0,1},{3,2},{4,5},{7,6},{8,9},{11,10},{12,13},{15,14},{16,17},{19,... | collective-permute-start | bytes 1548296 | tf_op jit(solution)/shard_map/ppermute | solution.py:558
  83.0 1.5 %collective-permute-done.20.refs_1_ = bf16[128,1792]{1,0:T(8,128)(2,1)S(1)} collective-permute-done((bf16[128,1792]{1,0:T(8,128)(2,1)S(1)}, bf16[128,1792]{1,0:T(8,128)(2,1)S(1)}, u32[]{:S(2)}, u32[]{:S(2)}) %collective-permute-start.20) | collective-permute-done | bytes 458784 | tf_op jit(solution)/shard_map/ppermute | solution.py:558
  84.5 0.1 add.16.refs_2_
  84.5 0.7 collective-permute-start.24
  85.2 0.1 add.17.refs_8_
  85.3 4.0 %collective-permute-done.19.refs_3_.refs_7_ = bf16[112,1792]{1,0:T(8,128)(2,1)S(1)} collective-permute-done((bf16[112,1792]{1,0:T(8,128)(2,1)S(1)}, bf16[112,1792]{1,0:T(8,128)(2,1)S(1)}, u32[]{:S(2)}, u32[]{:S(2)}) %collective-permute-start.19) | collective-permute-done | bytes 401440 | tf_op jit(solution)/shard_map/ppermute | solution.py:564
  89.2 0.2 add.18.refs_2_.refs_0_
  89.5 0.1 add.19.refs_2_
  89.6 1.3 %collective-permute-start.23 = (bf16[80,1792]{1,0:T(8,128)(2,1)S(1)}, bf16[80,1792]{1,0:T(8,128)(2,1)S(1)}, u32[]{:S(2)}, u32[]{:S(2)}) collective-permute-start(bf16[80,1792]{1,0:T(8,128)(2,1)S(1)} %add.19.refs_2_), channel_id=1, source_target_pairs={{1,0},{2,3},{5,4},{6,7},{9,8},{10,11},{13,12},{14,15},{17,16},{18,... | collective-permute-start | bytes 860168 | tf_op jit(solution)/shard_map/ppermute | solution.py:564
  90.9 0.7 collective-permute-start.25
  91.5 0.1 add.20.refs_4_
  91.6 1.3 %collective-permute-start.26 = (bf16[64,1792]{1,0:T(8,128)(2,1)S(1)}, bf16[64,1792]{1,0:T(8,128)(2,1)S(1)}, u32[]{:S(2)}, u32[]{:S(2)}) collective-permute-start(bf16[64,1792]{1,0:T(8,128)(2,1)S(1)} %add.20.refs_4_), channel_id=1, source_target_pairs={{1,0},{2,3},{5,4},{6,7},{9,8},{10,11},{13,12},{14,15},{17,16},{18,... | collective-permute-start | bytes 688136 | tf_op jit(solution)/shard_map/ppermute | solution.py:564
  92.9 1.6 %collective-permute-done.21.refs_1_.refs_3_ = bf16[144,1792]{1,0:T(8,128)(2,1)S(1)} collective-permute-done((bf16[144,1792]{1,0:T(8,128)(2,1)S(1)}, bf16[144,1792]{1,0:T(8,128)(2,1)S(1)}, u32[]{:S(2)}, u32[]{:S(2)}) %collective-permute-start.21) | collective-permute-done | bytes 516128 | tf_op jit(solution)/shard_map/ppermute | solution.py:558
  94.5 7.8 %collective-permute-done.23.refs_3_ = bf16[80,1792]{1,0:T(8,128)(2,1)S(1)} collective-permute-done((bf16[80,1792]{1,0:T(8,128)(2,1)S(1)}, bf16[80,1792]{1,0:T(8,128)(2,1)S(1)}, u32[]{:S(2)}, u32[]{:S(2)}) %collective-permute-start.23) | collective-permute-done | bytes 286752 | tf_op jit(solution)/shard_map/ppermute | solution.py:564
  102.3 0.1 add.21.refs_1_
  102.5 2.3 %collective-permute-done.26.refs_5_ = bf16[64,1792]{1,0:T(8,128)(2,1)S(1)} collective-permute-done((bf16[64,1792]{1,0:T(8,128)(2,1)S(1)}, bf16[64,1792]{1,0:T(8,128)(2,1)S(1)}, u32[]{:S(2)}, u32[]{:S(2)}) %collective-permute-start.26) | collective-permute-done | bytes 229408 | tf_op jit(solution)/shard_map/ppermute | solution.py:564
  104.7 1.1 %finish.1 = bf16[256,1792]{1,0:T(8,128)(2,1)} custom-call(bf16[112,1792]{1,0:T(8,128)(2,1)S(1)} %add.18.refs_2_.refs_0_, bf16[80,1792]{1,0:T(8,128)(2,1)S(1)} %add.21.refs_1_, bf16[64,1792]{1,0:T(8,128)(2,1)S(1)} %get-tuple-element.38.refs_2_, bf16[144,1792]{1,0:T(8,128)(2,1)S(1)} %collective-permute-done.21.refs_1_.refs_3_, ...), custom_call_target="tpu_custom_call" | custom-call | flops 1000 | bytes 1000 | tf_op jit(solution)/shard_map/finish/pallas_call | solution.py:357
  (35 shorter events, 0.2 us)
Async XLA Ops:
  0.0 7.1 %copy-start.5 = (bf16[256,16,128]{2,1,0:T(8,128)(2,1)S(1)}, bf16[256,16,128]{2,1,0:T(8,128)(2,1)}, u32[]{:S(2)}) copy-start(bf16[256,16,128]{2,1,0:T(8,128)(2,1)} %param.14) | copy-start | bytes 3145732
  1.7 0.7 copy-start
  2.4 5.6 %copy-start.1 = (bf16[256,64]{0,1:T(8,128)(2,1)S(1)}, bf16[256,64]{0,1:T(8,128)(2,1)}, u32[]{:S(2)}) copy-start(bf16[256,64]{0,1:T(8,128)(2,1)} %param.17) | copy-start | bytes 98308
  2.4 5.6 %copy-start.3 = (s32[1,16]{1,0:T(1,128)S(1)}, s32[1,16]{1,0:T(1,128)}, u32[]{:S(2)}) copy-start(s32[1,16]{1,0:T(1,128)} %table.1) | copy-start | bytes 196
  4.1 11.3 %collective-permute-start.6 = (bf16[256,640]{1,0:T(8,128)(2,1)S(1)}, bf16[256,640]{1,0:T(8,128)(2,1)S(1)}, u32[]{:S(2)}, u32[]{:S(2)}) collective-permute-start(bf16[256,640]{1,0:T(8,128)(2,1)S(1)} %get-tuple-element.31), channel_id=1, source_target_pairs={{0,8},{4,12},{8,0},{12,4},{1,9},{5,13},{9,1},{13,5},{2,10},{6,14},... | collective-permute-start | bytes 983048 | tf_op jit(solution)/shard_map/ppermute | solution.py:573
  15.3 6.4 %collective-permute-start = (bf16[48,2048]{1,0:T(8,128)(2,1)S(1)}, bf16[48,2048]{1,0:T(8,128)(2,1)S(1)}, u32[]{:S(2)}, u32[]{:S(2)}) collective-permute-start(bf16[48,2048]{1,0:T(8,128)(2,1)S(1)} %get-tuple-element.23.rest_0_.refs_2_), channel_id=1, source_target_pairs={{0,8},{4,12},{8,0},{12,4},{1,9},{5,13},{9,1},{13,5},{2,10},{6,14},... | collective-permute-start | bytes 589832 | tf_op jit(solution)/shard_map/ppermute | solution.py:377
  15.4 7.7 %collective-permute-start.1 = (bf16[48,2048]{1,0:T(8,128)(2,1)S(1)}, bf16[48,2048]{1,0:T(8,128)(2,1)S(1)}, u32[]{:S(2)}, u32[]{:S(2)}) collective-permute-start(bf16[48,2048]{1,0:T(8,128)(2,1)S(1)} %get-tuple-element.23.rest_0_.refs_2_), channel_id=1, source_target_pairs={{0,4},{4,0},{8,12},{12,8},{1,5},{5,1},{9,13},{13,9},{2,6},{6,2},{1... | collective-permute-start | bytes 589832 | tf_op jit(solution)/shard_map/ppermute | solution.py:404
  15.5 13.2 %collective-permute-start.7 = (bf16[256,640]{1,0:T(8,128)(2,1)S(1)}, bf16[256,640]{1,0:T(8,128)(2,1)S(1)}, u32[]{:S(2)}, u32[]{:S(2)}) collective-permute-start(bf16[256,640]{1,0:T(8,128)(2,1)S(1)} %stack.6), channel_id=1, source_target_pairs={{0,4},{4,0},{8,12},{12,8},{1,5},{5,1},{9,13},{13,9},{2,6},{6,2},{1... | collective-permute-start | bytes 983048 | tf_op jit(solution)/shard_map/ppermute | solution.py:404
  16.0 7.2 %slice-start = ((s8[7340032]{0:T(1024)(128)(4,1)}), s8[4194304]{0:T(1024)(128)(4,1)S(1)}, s32[]{:S(2)}) async-start(s8[7340032]{0:T(1024)(128)(4,1)} %bitcast.9), calls=%async_computation | async-start | bytes 8388608
  16.0 7.2 %slice-start.1 = ((s8[7340032]{0:T(1024)(128)(4,1)}), s8[3145728]{0:T(1024)(128)(4,1)S(1)}, s32[]{:S(2)}) async-start(s8[7340032]{0:T(1024)(128)(4,1)} %bitcast.9), calls=%async_computation.1 | async-start | bytes 6291456
  21.7 1.5 %collective-permute-start.2 = (bf16[48,2048]{1,0:T(8,128)(2,1)S(1)}, bf16[48,2048]{1,0:T(8,128)(2,1)S(1)}, u32[]{:S(2)}, u32[]{:S(2)}) collective-permute-start(bf16[48,2048]{1,0:T(8,128)(2,1)S(1)} %stack.5), channel_id=1, source_target_pairs={{0,4},{4,0},{8,12},{12,8},{1,5},{5,1},{9,13},{13,9},{2,6},{6,2},{1... | collective-permute-start | bytes 589832 | tf_op jit(solution)/shard_map/ppermute | solution.py:404
  21.8 12.8 %collective-permute-start.4 = (bf16[64,2048]{1,0:T(8,128)(2,1)S(1)}, bf16[64,2048]{1,0:T(8,128)(2,1)S(1)}, u32[]{:S(2)}, u32[]{:S(2)}) collective-permute-start(bf16[64,2048]{1,0:T(8,128)(2,1)S(1)} %attend.3.refs_1_.rest_4_.rest_0_), channel_id=1, source_target_pairs={{0,8},{4,12},{8,0},{12,4},{1,9},{5,13},{9,1},{13,5},{2,10},{6,14},... | collective-permute-start | bytes 786440 | tf_op jit(solution)/shard_map/ppermute | solution.py:377
  22.9 13.1 %collective-permute-start.5 = (bf16[64,2048]{1,0:T(8,128)(2,1)S(1)}, bf16[64,2048]{1,0:T(8,128)(2,1)S(1)}, u32[]{:S(2)}, u32[]{:S(2)}) collective-permute-start(bf16[64,2048]{1,0:T(8,128)(2,1)S(1)} %attend.3.refs_1_.rest_4_.rest_0_), channel_id=1, source_target_pairs={{0,4},{4,0},{8,12},{12,8},{1,5},{5,1},{9,13},{13,9},{2,6},{6,2},{1... | collective-permute-start | bytes 786440 | tf_op jit(solution)/shard_map/ppermute | solution.py:404
  25.0 15.1 %collective-permute-start.3 = (bf16[144,1792]{1,0:T(8,128)(2,1)S(1)}, bf16[144,1792]{1,0:T(8,128)(2,1)S(1)}, u32[]{:S(2)}, u32[]{:S(2)}) collective-permute-start(bf16[144,1792]{1,0:T(8,128)(2,1)S(1)} %get-tuple-element.29.refs_0_), channel_id=1, source_target_pairs={{0,1},{3,2},{4,5},{7,6},{8,9},{11,10},{12,13},{15,14},{16,17},{19,... | collective-permute-start | bytes 1548296 | tf_op jit(solution)/shard_map/ppermute | solution.py:558
  34.6 5.6 %copy-start.2 = (s32[16,4]{0,1:T(4,128)S(1)}, s32[16,4]{0,1:T(4,128)}, u32[]{:S(2)}) copy-start(s32[16,4]{0,1:T(4,128)} %param.26) | copy-start | bytes 772
  34.6 5.6 %copy-start.4 = (s32[16]{0:T(128)S(1)}, s32[16]{0:T(128)}, u32[]{:S(2)}) copy-start(s32[16]{0:T(128)} %decode_length.1) | copy-start | bytes 196
  34.6 1.6 %collective-permute-start.8 = (bf16[64,2048]{1,0:T(8,128)(2,1)S(1)}, bf16[64,2048]{1,0:T(8,128)(2,1)S(1)}, u32[]{:S(2)}, u32[]{:S(2)}) collective-permute-start(bf16[64,2048]{1,0:T(8,128)(2,1)S(1)} %stack.7), channel_id=1, source_target_pairs={{0,4},{4,0},{8,12},{12,8},{1,5},{5,1},{9,13},{13,9},{2,6},{6,2},{1... | collective-permute-start | bytes 786440 | tf_op jit(solution)/shard_map/ppermute | solution.py:404
  34.7 14.9 %collective-permute-start.11 = (bf16[80,2048]{1,0:T(8,128)(2,1)S(1)}, bf16[80,2048]{1,0:T(8,128)(2,1)S(1)}, u32[]{:S(2)}, u32[]{:S(2)}) collective-permute-start(bf16[80,2048]{1,0:T(8,128)(2,1)S(1)} %attend.4.refs_1_.rest_4_.rest_0_), channel_id=1, source_target_pairs={{0,8},{4,12},{8,0},{12,4},{1,9},{5,13},{9,1},{13,5},{2,10},{6,14},... | collective-permute-start | bytes 983048 | tf_op jit(solution)/shard_map/ppermute | solution.py:377
  35.8 15.9 %collective-permute-start.12 = (bf16[80,2048]{1,0:T(8,128)(2,1)S(1)}, bf16[80,2048]{1,0:T(8,128)(2,1)S(1)}, u32[]{:S(2)}, u32[]{:S(2)}) collective-permute-start(bf16[80,2048]{1,0:T(8,128)(2,1)S(1)} %attend.4.refs_1_.rest_4_.rest_0_), channel_id=1, source_target_pairs={{0,4},{4,0},{8,12},{12,8},{1,5},{5,1},{9,13},{13,9},{2,6},{6,2},{1... | collective-permute-start | bytes 983048 | tf_op jit(solution)/shard_map/ppermute | solution.py:404
  38.5 23.5 %collective-permute-start.10 = (bf16[192,1792]{1,0:T(8,128)(2,1)S(1)}, bf16[192,1792]{1,0:T(8,128)(2,1)S(1)}, u32[]{:S(2)}, u32[]{:S(2)}) collective-permute-start(bf16[192,1792]{1,0:T(8,128)(2,1)S(1)} %get-tuple-element.33.refs_0_.refs_2_), channel_id=1, source_target_pairs={{0,1},{3,2},{4,5},{7,6},{8,9},{11,10},{12,13},{15,14},{16,17},{19,... | collective-permute-start | bytes 2064392 | tf_op jit(solution)/shard_map/ppermute | solution.py:558
  49.7 2.0 %collective-permute-start.13 = (bf16[80,2048]{1,0:T(8,128)(2,1)S(1)}, bf16[80,2048]{1,0:T(8,128)(2,1)S(1)}, u32[]{:S(2)}, u32[]{:S(2)}) collective-permute-start(bf16[80,2048]{1,0:T(8,128)(2,1)S(1)} %stack.8), channel_id=1, source_target_pairs={{0,4},{4,0},{8,12},{12,8},{1,5},{5,1},{9,13},{13,9},{2,6},{6,2},{1... | collective-permute-start | bytes 983048 | tf_op jit(solution)/shard_map/ppermute | solution.py:404
  49.9 12.1 %collective-permute-start.9 = (bf16[96,1792]{1,0:T(8,128)(2,1)S(1)}, bf16[96,1792]{1,0:T(8,128)(2,1)S(1)}, u32[]{:S(2)}, u32[]{:S(2)}) collective-permute-start(bf16[96,1792]{1,0:T(8,128)(2,1)S(1)} %add.12.rest_3_), channel_id=1, source_target_pairs={{1,2},{2,1},{5,6},{6,5},{9,10},{10,9},{13,14},{14,13},{17,18},{18,... | collective-permute-start | bytes 1032200 | tf_op jit(solution)/shard_map/ppermute | solution.py:561
  50.6 10.8 %collective-permute-start.16 = (bf16[64,2048]{1,0:T(8,128)(2,1)S(1)}, bf16[64,2048]{1,0:T(8,128)(2,1)S(1)}, u32[]{:S(2)}, u32[]{:S(2)}) collective-permute-start(bf16[64,2048]{1,0:T(8,128)(2,1)S(1)} %attend.5.refs_1_.rest_4_.rest_0_), channel_id=1, source_target_pairs={{0,8},{4,12},{8,0},{12,4},{1,9},{5,13},{9,1},{13,5},{2,10},{6,14},... | collective-permute-start | bytes 786440 | tf_op jit(solution)/shard_map/ppermute | solution.py:377
  54.5 20.1 %collective-permute-start.15 = (bf16[160,1792]{1,0:T(8,128)(2,1)S(1)}, bf16[160,1792]{1,0:T(8,128)(2,1)S(1)}, u32[]{:S(2)}, u32[]{:S(2)}) collective-permute-start(bf16[160,1792]{1,0:T(8,128)(2,1)S(1)} %get-tuple-element.36.refs_0_), channel_id=1, source_target_pairs={{0,1},{3,2},{4,5},{7,6},{8,9},{11,10},{12,13},{15,14},{16,17},{19,... | collective-permute-start | bytes 1720328 | tf_op jit(solution)/shard_map/ppermute | solution.py:558
  61.3 1.6 %collective-permute-start.17 = (bf16[64,2048]{1,0:T(8,128)(2,1)S(1)}, bf16[64,2048]{1,0:T(8,128)(2,1)S(1)}, u32[]{:S(2)}, u32[]{:S(2)}) collective-permute-start(bf16[64,2048]{1,0:T(8,128)(2,1)S(1)} %attend.5.refs_1_.rest_4_.rest_0_), channel_id=1, source_target_pairs={{0,4},{4,0},{8,12},{12,8},{1,5},{5,1},{9,13},{13,9},{2,6},{6,2},{1... | collective-permute-start | bytes 786440 | tf_op jit(solution)/shard_map/ppermute | solution.py:404
  61.4 1.9 %collective-permute-start.18 = (bf16[64,2048]{1,0:T(8,128)(2,1)S(1)}, bf16[64,2048]{1,0:T(8,128)(2,1)S(1)}, u32[]{:S(2)}, u32[]{:S(2)}) collective-permute-start(bf16[64,2048]{1,0:T(8,128)(2,1)S(1)} %stack.9), channel_id=1, source_target_pairs={{0,4},{4,0},{8,12},{12,8},{1,5},{5,1},{9,13},{13,9},{2,6},{6,2},{1... | collective-permute-start | bytes 786440 | tf_op jit(solution)/shard_map/ppermute | solution.py:404
  62.1 13.4 %collective-permute-start.14 = (bf16[128,1792]{1,0:T(8,128)(2,1)S(1)}, bf16[128,1792]{1,0:T(8,128)(2,1)S(1)}, u32[]{:S(2)}, u32[]{:S(2)}) collective-permute-start(bf16[128,1792]{1,0:T(8,128)(2,1)S(1)} %add.13.rest_5_), channel_id=1, source_target_pairs={{1,2},{2,1},{5,6},{6,5},{9,10},{10,9},{13,14},{14,13},{17,18},{18,... | collective-permute-start | bytes 1376264 | tf_op jit(solution)/shard_map/ppermute | solution.py:561
  65.6 18.9 %collective-permute-start.20 = (bf16[128,1792]{1,0:T(8,128)(2,1)S(1)}, bf16[128,1792]{1,0:T(8,128)(2,1)S(1)}, u32[]{:S(2)}, u32[]{:S(2)}) collective-permute-start(bf16[128,1792]{1,0:T(8,128)(2,1)S(1)} %get-tuple-element.39.refs_0_), channel_id=1, source_target_pairs={{0,1},{3,2},{4,5},{7,6},{8,9},{11,10},{12,13},{15,14},{16,17},{19,... | collective-permute-start | bytes 1376264 | tf_op jit(solution)/shard_map/ppermute | solution.py:558
  74.8 14.7 %collective-permute-start.22 = (bf16[160,1792]{1,0:T(8,128)(2,1)S(1)}, bf16[160,1792]{1,0:T(8,128)(2,1)S(1)}, u32[]{:S(2)}, u32[]{:S(2)}) collective-permute-start(bf16[160,1792]{1,0:T(8,128)(2,1)S(1)} %add.14.refs_4_), channel_id=1, source_target_pairs={{1,2},{2,1},{5,6},{6,5},{9,10},{10,9},{13,14},{14,13},{17,18},{18,... | collective-permute-start | bytes 1720328 | tf_op jit(solution)/shard_map/ppermute | solution.py:561
  75.6 13.7 %collective-permute-start.19 = (bf16[112,1792]{1,0:T(8,128)(2,1)S(1)}, bf16[112,1792]{1,0:T(8,128)(2,1)S(1)}, u32[]{:S(2)}, u32[]{:S(2)}) collective-permute-start(bf16[112,1792]{1,0:T(8,128)(2,1)S(1)} %add.15.refs_2_), channel_id=1, source_target_pairs={{1,0},{2,3},{5,4},{6,7},{9,8},{10,11},{13,12},{14,15},{17,16},{18,... | collective-permute-start | bytes 1204232 | tf_op jit(solution)/shard_map/ppermute | solution.py:564
  76.9 17.6 %collective-permute-start.21 = (bf16[144,1792]{1,0:T(8,128)(2,1)S(1)}, bf16[144,1792]{1,0:T(8,128)(2,1)S(1)}, u32[]{:S(2)}, u32[]{:S(2)}) collective-permute-start(bf16[144,1792]{1,0:T(8,128)(2,1)S(1)} %get-tuple-element.40.refs_0_), channel_id=1, source_target_pairs={{0,1},{3,2},{4,5},{7,6},{8,9},{11,10},{12,13},{15,14},{16,17},{19,... | collective-permute-start | bytes 1548296 | tf_op jit(solution)/shard_map/ppermute | solution.py:558
  84.5 7.0 %collective-permute-start.24 = (bf16[64,1792]{1,0:T(8,128)(2,1)S(1)}, bf16[64,1792]{1,0:T(8,128)(2,1)S(1)}, u32[]{:S(2)}, u32[]{:S(2)}) collective-permute-start(bf16[64,1792]{1,0:T(8,128)(2,1)S(1)} %add.16.refs_2_), channel_id=1, source_target_pairs={{1,2},{2,1},{5,6},{6,5},{9,10},{10,9},{13,14},{14,13},{17,18},{18,... | collective-permute-start | bytes 688136 | tf_op jit(solution)/shard_map/ppermute | solution.py:561
  89.6 12.7 %collective-permute-start.23 = (bf16[80,1792]{1,0:T(8,128)(2,1)S(1)}, bf16[80,1792]{1,0:T(8,128)(2,1)S(1)}, u32[]{:S(2)}, u32[]{:S(2)}) collective-permute-start(bf16[80,1792]{1,0:T(8,128)(2,1)S(1)} %add.19.refs_2_), channel_id=1, source_target_pairs={{1,0},{2,3},{5,4},{6,7},{9,8},{10,11},{13,12},{14,15},{17,16},{18,... | collective-permute-start | bytes 860168 | tf_op jit(solution)/shard_map/ppermute | solution.py:564
  90.9 11.6 %collective-permute-start.25 = (bf16[64,1792]{1,0:T(8,128)(2,1)S(1)}, bf16[64,1792]{1,0:T(8,128)(2,1)S(1)}, u32[]{:S(2)}, u32[]{:S(2)}) collective-permute-start(bf16[64,1792]{1,0:T(8,128)(2,1)S(1)} %add.17.refs_8_), channel_id=1, source_target_pairs={{1,2},{2,1},{5,6},{6,5},{9,10},{10,9},{13,14},{14,13},{17,18},{18,... | collective-permute-start | bytes 688136 | tf_op jit(solution)/shard_map/ppermute | solution.py:561
  91.6 13.1 %collective-permute-start.26 = (bf16[64,1792]{1,0:T(8,128)(2,1)S(1)}, bf16[64,1792]{1,0:T(8,128)(2,1)S(1)}, u32[]{:S(2)}, u32[]{:S(2)}) collective-permute-start(bf16[64,1792]{1,0:T(8,128)(2,1)S(1)} %add.20.refs_4_), channel_id=1, source_target_pairs={{1,0},{2,3},{5,4},{6,7},{9,8},{10,11},{13,12},{14,15},{17,16},{18,... | collective-permute-start | bytes 688136 | tf_op jit(solution)/shard_map/ppermute | solution.py:564

commit v8 on v7

--- a/solution.py
+++ b/solution.py
@@ -33,7 +33,7 @@
 
 def chunk_sizes(tok_group):
     if tok_group == 256:
-        return (48, 64, 80, 64)
+        return (48, 80, 80, 48)
     return (tok_group,)
 
 
@@ -273,9 +273,8 @@
     parts, rest, x = rest[:n_parts], rest[n_parts:], rest[-1]
     own, outs = rest[-2 - len(tails)], rest[-1 - len(tails):-1]
     t = own.shape[0]
-    lead = outs[-1].shape[0] - tails[-1] * t
-    if lead:
-        outs[-1][:lead, :] = rest[0][...]
+    if outs[0].shape[0] > tails[0] * t:
+        outs[0][tails[0] * t:, :] = rest[0][...]
     for i, part in enumerate(parts):
         place = 0
         for g, row in enumerate(places):
@@ -289,8 +288,7 @@
         own[:, at:at + step] = y[:t]
         row = t
         for i, n in enumerate(tails):
-            skip = lead if i == len(tails) - 1 else 0
-            outs[i][skip:skip + n * t, at:at + step] = y[row:row + n * t]
+            outs[i][:n * t, at:at + step] = y[row:row + n * t]
             row += n * t
 
 
@@ -299,7 +297,7 @@
     rows = sum(p.shape[0] for p in parts)
     t = rows // (1 + sum(tails))
     sizes = [t] + [n * t for n in tails]
-    sizes[-1] += sum(e.shape[0] for e in earlier)
+    sizes[1] += sum(e.shape[0] for e in earlier)
     places, me, z = where
     return pl.pallas_call(
         functools.partial(project_kernel, len(parts), tails, places),
@@ -569,15 +567,17 @@
 
     t0, t1, t2, t3 = sizes
     apart = [lambda g, k=k: g ^ k for k in range(4)]
-    own_blocks, core_blocks, far_blocks = pack([(apart[0],), (apart[1],), (apart[2], apart[3])], ())
-    x_blocks = lax.ppermute(far_blocks, "dp", [(i, i ^ 2) for i in range(groups)])
-    x1 = attend(1, held, (x0,))
+    own_blocks, core_blocks, far_blocks = pack(
+        [(apart[0],), (apart[1],), (apart[2], apart[3])], (x0,))
+    x1 = attend(1, held, (own_blocks,))
     half = capacity * block_len
-    on_blocks = swap_cores(stack([core_blocks, (x_blocks, half)], (x0,)))
-    brought = ((own_blocks, x_blocks, on_blocks), [(0, 0, apart[0]), (1, 0, apart[2]), (2, 0, apart[1]), (2, half, apart[3])])
+    x_blocks = lax.ppermute(stack([far_blocks], (x1,)), "dp", [(i, i ^ 2) for i in range(groups)])
     own0, rest0 = project(where, gather(x0, (x1,)), w, (3,), (), (x1,))
     in0 = inward(rest0)
-    x2 = attend(2, held, (own0, on_blocks))
+    x2 = attend(2, held, (own0,))
+    on_blocks = swap_cores(stack([core_blocks, (x_blocks, half)], (x2,)))
+    brought = ((own_blocks, x_blocks, on_blocks), [
+        (0, 0, apart[0]), (1, 0, apart[2]), (2, 0, apart[1]), (2, half, apart[3])])
     own1, rest1 = project(where, gather(x1, (x2,)), w, (3,), (), (x2,))
     in1 = inward(rest1)
     to_across0 = add(2 * t0, [(rest0, 0), (in0, 0)], (own1,))
@@ -587,27 +587,27 @@
     in2 = inward(rest2)
     to_across1 = add(2 * t1, [(rest1, 0), (in1, 0)], (own2, on0))
     on1 = across(to_across1)
-    own3, rest3, near = project(
+    own3, rest3, near3 = project(
         where, gather(x3, (own2,)), w, (2, 1), (near2,), (to_across1,))
     in3 = inward(rest3)
     to_across2 = add(2 * t2, [(rest2, 0), (in2, 0)], (own3,))
     on2 = across(to_across2)
-    near_in = inward(near)
     to_out01 = add_all([(t0, [(rest0, 2 * t0), (on0, 0)]), (t1, [(rest1, 2 * t1), (on1, 0)])],
                        (to_across2,))
     out01 = outward(to_out01)
     to_far = add(t3, [(rest3, 0), (in3, 0)], (to_out01,))
     far_on = across(to_far)
+    near_in = inward(stack([near3], (to_far,)))
     to_mid = add(t3, [(rest3, t3), (in3, t3)], (to_far,))
     mid_on = across(to_mid)
     done01 = add_all([(t0, [(own0, 0), (in0, 2 * t0), (on0, t0), (out01, 0)]),
                       (t1, [(own1, 0), (in1, 2 * t1), (on1, t1), (out01, t0)])], (to_mid,))
     to_out2 = add(t2, [(near2, 0), (on2, 0)], (done01,))
     out2 = outward(to_out2)
-    to_out3 = add(t3, [(near, t2), (far_on, 0)], (to_out2,))
+    to_out3 = add(t3, [(near3, 0), (far_on, 0)], (to_out2, near_in))
     out3 = outward(to_out3)
-    done2 = add(t2, [(own2, 0), (near_in, 0), (on2, t2), (out2, 0)], (to_out3,))
-    return finish([done01, done2], [(own3, 0), (near_in, t2), (mid_on, 0), (out3, 0)])
+    done2 = add(t2, [(own2, 0), (in3, 2 * t3), (on2, t2), (out2, 0)], (to_out3,))
+    return finish([done01, done2], [(own3, 0), (near_in, 0), (mid_on, 0), (out3, 0)])
 
 
 def solution(mesh):

time: 106 us -> 111 us (1.047)
  waiting for transfers between devices: 21.4 us -> 31.1 us
  starting transfers between devices: 40.4 us -> 35.8 us
    ppermute x5, waiting for transfers between devices: 5.42 us -> 13.2 us  [inward(): return lax.ppermute(x, 'tp', INWARD)]
    ppermute x5, starting transfers between devices: 24.8 us -> 20.3 us  [inward(): return lax.ppermute(x, 'tp', INWARD)]
    ppermute x3, waiting for transfers between devices: 14.1 us -> 9.82 us  [outward(): return lax.ppermute(x, 'tp', OUTWARD)]
    ppermute x1, waiting for transfers between devices: 0.01 us -> 3.1 us  [body(): lax.ppermute(stack([far_blocks], (x1,)), 'dp', [(i, i ^ 2) for i in range...]
    ppermute x4, waiting for transfers between devices: 0.94 us -> 2.65 us  [shift_groups(): lax.ppermute(x, 'dp', [(i, (i + s) % groups) for i in range(groups)])]
    ppermute x4, starting transfers between devices: 3.42 us -> 5 us  [shift_groups(): lax.ppermute(x, 'dp', [(i, (i + s) % groups) for i in range(groups)])]
    ppermute x9, waiting for transfers between devices: 0.9 us -> 2.31 us  [swap_cores(): lax.ppermute(x, 'dp', [(i, i ^ 1) for i in range(lax.axis_size('dp'))])]
  transfers between devices with their start and end apart: 27 -> 27, of which waited for: 11 -> 10; matrix products, arithmetic and copies ran while one was open for 0% -> 0% of each run, Pallas kernels for 35% -> 29%
where the time goes in v8:
time: 111 us; the launch traced here: 110 us
  Pallas kernels  40 us (36%)
  starting transfers between devices  35.8 us (32%)
  waiting for transfers between devices  31.1 us (28%)
  local copies, waits for them, and re-layouts  2.25 us (2%)
  between operations  1.16 us (1%)
    ppermute x5, starting transfers between devices, inward(): return lax.ppermute(x, 'tp', INWARD)  20.3 us
    pallas_call x3, Pallas kernels, attend(): pl.pallas_call(kernel, out_shape=jax.ShapeDtypeStruct((t, heads * dv), bf...  19.7 us
    ppermute x5, waiting for transfers between devices, inward(): return lax.ppermute(x, 'tp', INWARD)  13.2 us
    ppermute x3, waiting for transfers between devices, outward(): return lax.ppermute(x, 'tp', OUTWARD)  9.82 us
    pallas_call x4, Pallas kernels, project(): pl.pallas_call(functools.partial(project_kernel, len(parts), tails, place...  9.09 us
    pallas_call x1, Pallas kernels, first_chunk(): pl.pallas_call(functools.partial(first_kernel, fresh_of(0), exp_scale), o...  7.23 us
    ppermute x4, starting transfers between devices, shift_groups(): lax.ppermute(x, 'dp', [(i, (i + s) % groups) for i in range(groups)])  5 us
    ppermute x3, starting transfers between devices, outward(): return lax.ppermute(x, 'tp', OUTWARD)  3.88 us
  transfers between devices with their start and end apart: 27, of which 10 were waited for; matrix products, arithmetic and copies ran while one was open for 0% of the time, Pallas kernels for 29%

profile of v8, /device:TPU:0, one launch (start us, length us, event | category | flops | bytes accessed | tf_op | source)
XLA Modules:
  0.0 110.3 jit_solution(9045496498081019352)
XLA Ops:
  0.0 1.5 %copy.17 = bf16[256,16,128]{2,0,1:T(8,128)(2,1)S(1)} copy(bf16[256,16,128]{2,1,0:T(8,128)(2,1)} %param.14) | data formatting | bytes 2097152 | tf_op args[0]
  1.6 0.5 reshape.6
  2.8 0.1 pad.4.cache_rope
  2.9 0.0 copy-start
  2.9 7.2 %attend_first.1 = (bf16[48,2048]{1,0:T(8,128)(2,1)S(1)}, bf16[1280,640]{1,0:T(8,128)(2,1)S(1)}, bf16[16,128,512]{2,1,0:T(8,128)(2,1)S(1)}, bf16[16,512,128]{2,1,0:T(8,128)(2,1)S(1)}, bf16[256,1024]{1,0:T(8,128)(2,1)S(1)}) custom-call(s32[1]{0:T(128)} %bitcast.me, s32[1]{0:T(128)} %bitcast.1.z, s32[1,16]{1,0:T(1,128)S(1)} %copy-done.3, s32[1]{0:T(128)S(6)} %copy.18.offset, ...), custom_call_target="tpu_custom_call" | custom-call | flops 40000000000 | bytes 1000 | tf_op jit(solution)/shard_map/attend_first/pallas_call | solution.py:469
  10.2 3.0 %collective-permute-start = (bf16[48,2048]{1,0:T(8,128)(2,1)S(1)}, bf16[48,2048]{1,0:T(8,128)(2,1)S(1)}, u32[]{:S(2)}, u32[]{:S(2)}) collective-permute-start(bf16[48,2048]{1,0:T(8,128)(2,1)S(1)} %get-tuple-element.23.rest_0_), channel_id=1, source_target_pairs={{0,8},{4,12},{8,0},{12,4},{1,9},{5,13},{9,1},{13,5},{2,10},{6,14},... | collective-permute-start | bytes 589832 | tf_op jit(solution)/shard_map/ppermute | solution.py:375
  13.2 0.0 collective-permute-start.1
  13.2 1.7 %pack.1 = (bf16[128,640]{1,0:T(8,128)(2,1)S(1)}, bf16[128,640]{1,0:T(8,128)(2,1)S(1)}, bf16[256,640]{1,0:T(8,128)(2,1)S(1)}) custom-call(s32[1]{0:T(128)} %bitcast.me, s32[1,2,4]{2,1,0:T(2,128)S(1)} %bitcast.15, bf16[32,64,512]{2,1,0:T(8,128)(2,1)} %cache_latent.3, bf16[32,64,128]{2,1,0:T(8,128)(2,1)S(1)} %pad.4.cache_rope, ...), custom_call_target="tpu_custom_call" | custom-call | flops 1000 | bytes 1000 | tf_op jit(solution)/shard_map/pack/pallas_call | solution.py:522
  14.9 0.0 slice-start
  14.9 0.0 slice-start.1
  14.9 5.8 %attend.3.refs_1_.rest_4_.rest_0_ = bf16[80,2048]{1,0:T(8,128)(2,1)S(1)} custom-call(bf16[16,256,128]{2,1,0:T(8,128)(2,1)S(1)} %bitcast.12, bf16[256,1024]{1,0:T(8,128)(2,1)S(1)} %get-tuple-element.24.q_rope, bf16[16,128,512]{2,1,0:T(8,128)(2,1)S(1)} %get-tuple-element.25.wk, bf16[16,512,128]{2,1,0:T(8,128)(2,1)S(1)} %get-tuple-element.26.wv, ...), custom_call_target="tpu_custom_call" | custom-call | flops 40000000000 | bytes 1000 | tf_op jit(solution)/shard_map/attend/pallas_call | solution.py:510
  20.7 0.0 collective-permute-done.refs_0_.rest_1_
  20.7 0.6 collective-permute-start.2
  21.3 0.1 collective-permute-start.4
  21.4 0.1 collective-permute-start.5
  21.5 1.9 %collective-permute-start.11 = (bf16[256,640]{1,0:T(8,128)(2,1)S(1)}, bf16[256,640]{1,0:T(8,128)(2,1)S(1)}, u32[]{:S(2)}, u32[]{:S(2)}) collective-permute-start(bf16[256,640]{1,0:T(8,128)(2,1)S(1)} %stack.9), channel_id=1, source_target_pairs={{0,8},{4,12},{8,0},{12,4},{1,9},{5,13},{9,1},{13,5},{2,10},{6,14},... | collective-permute-start | bytes 983048 | tf_op jit(solution)/shard_map/ppermute | solution.py:574
  23.4 0.0 collective-permute-done.2.rest_3_
  23.5 1.8 %project.4 = (bf16[48,1792]{1,0:T(8,128)(2,1)S(1)}, bf16[144,1792]{1,0:T(8,128)(2,1)S(1)}) custom-call(s32[1]{0:T(128)} %bitcast.me, s32[1]{0:T(128)} %bitcast.1.z, bf16[2048,1792]{1,0:T(8,128)(2,1)S(1)} %bitcast.10, bf16[48,2048]{1,0:T(8,128)(2,1)S(1)} %get-tuple-element.23.rest_0_, bf16[48,2048]{1,0:T(8,128)(2,1)S(1)} %collective-permute-done.refs_0_.rest_1_, ...), custom_call_target="tpu_custom_call" | custom-call | flops 1000 | bytes 1000 | tf_op jit(solution)/shard_map/project/pallas_call | solution.py:302
  25.2 3.7 %collective-permute-start.3 = (bf16[144,1792]{1,0:T(8,128)(2,1)S(1)}, bf16[144,1792]{1,0:T(8,128)(2,1)S(1)}, u32[]{:S(2)}, u32[]{:S(2)}) collective-permute-start(bf16[144,1792]{1,0:T(8,128)(2,1)S(1)} %get-tuple-element.30.refs_0_), channel_id=1, source_target_pairs={{0,1},{3,2},{4,5},{7,6},{8,9},{11,10},{12,13},{15,14},{16,17},{19,... | collective-permute-start | bytes 1548296 | tf_op jit(solution)/shard_map/ppermute | solution.py:556
  28.9 5.9 %attend.4.refs_1_.rest_4_.refs_2_.rest_0_ = bf16[80,2048]{1,0:T(8,128)(2,1)S(1)} custom-call(bf16[16,256,128]{2,1,0:T(8,128)(2,1)S(1)} %bitcast.13, bf16[256,1024]{1,0:T(8,128)(2,1)S(1)} %get-tuple-element.24.q_rope, bf16[16,128,512]{2,1,0:T(8,128)(2,1)S(1)} %get-tuple-element.25.wk, bf16[16,512,128]{2,1,0:T(8,128)(2,1)S(1)} %get-tuple-element.26.wv, ...), custom_call_target="tpu_custom_call" | custom-call | flops 40000000000 | bytes 1000 | tf_op jit(solution)/shard_map/attend/pallas_call | solution.py:510
  34.8 0.1 collective-permute-start.6
  34.9 3.1 %collective-permute-done.11.refs_1_.rest_1_ = bf16[256,640]{1,0:T(8,128)(2,1)S(1)} collective-permute-done((bf16[256,640]{1,0:T(8,128)(2,1)S(1)}, bf16[256,640]{1,0:T(8,128)(2,1)S(1)}, u32[]{:S(2)}, u32[]{:S(2)}) %collective-permute-start.11) | collective-permute-done | bytes 327712 | tf_op jit(solution)/shard_map/ppermute | solution.py:574
  38.0 0.0 copy-start.2
  38.1 0.0 copy-start.4
  38.1 0.1 collective-permute-start.12
  38.1 0.4 collective-permute-start.9
  38.5 0.2 collective-permute-start.10
  38.7 2.8 %project.5 = (bf16[80,1792]{1,0:T(8,128)(2,1)S(1)}, bf16[240,1792]{1,0:T(8,128)(2,1)S(1)}) custom-call(s32[1]{0:T(128)} %bitcast.me, s32[1]{0:T(128)} %bitcast.1.z, bf16[2048,1792]{1,0:T(8,128)(2,1)S(1)} %bitcast.10, bf16[80,2048]{1,0:T(8,128)(2,1)S(1)} %attend.3.refs_1_.rest_4_.rest_0_, bf16[80,2048]{1,0:T(8,128)(2,1)S(1)} %collective-permute-done.4.refs_0_.rest_1_, ...), custom_call_target="tpu_custom_call" | custom-call | flops 1000 | bytes 1000 | tf_op jit(solution)/shard_map/project/pallas_call | solution.py:302
  41.5 4.0 %collective-permute-start.8 = (bf16[240,1792]{1,0:T(8,128)(2,1)S(1)}, bf16[240,1792]{1,0:T(8,128)(2,1)S(1)}, u32[]{:S(2)}, u32[]{:S(2)}) collective-permute-start(bf16[240,1792]{1,0:T(8,128)(2,1)S(1)} %get-tuple-element.32.refs_0_.refs_2_), channel_id=1, source_target_pairs={{0,1},{3,2},{4,5},{7,6},{8,9},{11,10},{12,13},{15,14},{16,17},{19,... | collective-permute-start | bytes 2580488 | tf_op jit(solution)/shard_map/ppermute | solution.py:556
  45.5 0.1 add.12.rest_3_
  45.6 8.1 %attend.5.refs_1_.rest_4_.rest_0_ = bf16[48,2048]{1,0:T(8,128)(2,1)S(1)} custom-call(s32[1]{0:T(128)} %bitcast.me, bf16[16,256,128]{2,1,0:T(8,128)(2,1)S(1)} %bitcast.14, bf16[256,1024]{1,0:T(8,128)(2,1)S(1)} %get-tuple-element.24.q_rope, bf16[16,128,512]{2,1,0:T(8,128)(2,1)S(1)} %get-tuple-element.25.wk, bf16[16,512,128]{2,1,0:T(8,128)(2,1)S(1)} %get-tuple-element.26.wv, ...), custom_call_target="tpu_custom_call" | custom-call | flops 6000000000 | bytes 1000 | tf_op jit(solution)/shard_map/attend/pallas_call | solution.py:510
  53.7 0.1 collective-permute-start.13
  53.9 0.7 collective-permute-start.7
  54.6 0.9 collective-permute-done.13.rest_3_
  55.4 2.8 %project.6 = (bf16[80,1792]{1,0:T(8,128)(2,1)S(1)}, bf16[160,1792]{1,0:T(8,128)(2,1)S(1)}, bf16[80,1792]{1,0:T(8,128)(2,1)S(1)}) custom-call(s32[1]{0:T(128)} %bitcast.me, s32[1]{0:T(128)} %bitcast.1.z, bf16[2048,1792]{1,0:T(8,128)(2,1)S(1)} %bitcast.10, bf16[80,2048]{1,0:T(8,128)(2,1)S(1)} %attend.4.refs_1_.rest_4_.refs_2_.rest_0_, ...), custom_call_target="tpu_custom_call" | custom-call | flops 1000 | bytes 1000 | tf_op jit(solution)/shard_map/project/pallas_call | solution.py:302
  58.2 3.5 %collective-permute-start.15 = (bf16[160,1792]{1,0:T(8,128)(2,1)S(1)}, bf16[160,1792]{1,0:T(8,128)(2,1)S(1)}, u32[]{:S(2)}, u32[]{:S(2)}) collective-permute-start(bf16[160,1792]{1,0:T(8,128)(2,1)S(1)} %get-tuple-element.36.refs_0_), channel_id=1, source_target_pairs={{0,1},{3,2},{4,5},{7,6},{8,9},{11,10},{12,13},{15,14},{16,17},{19,... | collective-permute-start | bytes 1720328 | tf_op jit(solution)/shard_map/ppermute | solution.py:556
  61.7 1.6 %collective-permute-start.16 = (bf16[48,2048]{1,0:T(8,128)(2,1)S(1)}, bf16[48,2048]{1,0:T(8,128)(2,1)S(1)}, u32[]{:S(2)}, u32[]{:S(2)}) collective-permute-start(bf16[48,2048]{1,0:T(8,128)(2,1)S(1)} %attend.5.refs_1_.rest_4_.rest_0_), channel_id=1, source_target_pairs={{0,8},{4,12},{8,0},{12,4},{1,9},{5,13},{9,1},{13,5},{2,10},{6,14},... | collective-permute-start | bytes 589832 | tf_op jit(solution)/shard_map/ppermute | solution.py:375
  63.3 1.4 %collective-permute-done.8.refs_1_.refs_5_ = bf16[240,1792]{1,0:T(8,128)(2,1)S(1)} collective-permute-done((bf16[240,1792]{1,0:T(8,128)(2,1)S(1)}, bf16[240,1792]{1,0:T(8,128)(2,1)S(1)}, u32[]{:S(2)}, u32[]{:S(2)}) %collective-permute-start.8) | collective-permute-done | bytes 860192 | tf_op jit(solution)/shard_map/ppermute | solution.py:556
  64.6 0.1 add.13.rest_5_
  64.8 0.7 collective-permute-start.14
  65.5 0.1 collective-permute-start.17
  65.6 2.6 %collective-permute-done.16.refs_0_.rest_1_ = bf16[48,2048]{1,0:T(8,128)(2,1)S(1)} collective-permute-done((bf16[48,2048]{1,0:T(8,128)(2,1)S(1)}, bf16[48,2048]{1,0:T(8,128)(2,1)S(1)}, u32[]{:S(2)}, u32[]{:S(2)}) %collective-permute-start.16) | collective-permute-done | bytes 196640 | tf_op jit(solution)/shard_map/ppermute | solution.py:375
  68.2 0.1 collective-permute-start.18
  68.3 1.4 %collective-permute-done.18.rest_3_ = bf16[48,2048]{1,0:T(8,128)(2,1)S(1)} collective-permute-done((bf16[48,2048]{1,0:T(8,128)(2,1)S(1)}, bf16[48,2048]{1,0:T(8,128)(2,1)S(1)}, u32[]{:S(2)}, u32[]{:S(2)}) %collective-permute-start.18) | collective-permute-done | bytes 196640 | tf_op jit(solution)/shard_map/ppermute | solution.py:402
  69.7 1.7 %project.7 = (bf16[48,1792]{1,0:T(8,128)(2,1)S(1)}, bf16[176,1792]{1,0:T(8,128)(2,1)S(1)}, bf16[48,1792]{1,0:T(8,128)(2,1)S(1)}) custom-call(s32[1]{0:T(128)} %bitcast.me, s32[1]{0:T(128)} %bitcast.1.z, bf16[2048,1792]{1,0:T(8,128)(2,1)S(1)} %bitcast.10, bf16[48,2048]{1,0:T(8,128)(2,1)S(1)} %attend.5.refs_1_.rest_4_.rest_0_, ...), custom_call_target="tpu_custom_call" | custom-call | flops 1000 | bytes 1000 | tf_op jit(solution)/shard_map/project/pallas_call | solution.py:302
  71.5 4.8 %collective-permute-start.20 = (bf16[176,1792]{1,0:T(8,128)(2,1)S(1)}, bf16[176,1792]{1,0:T(8,128)(2,1)S(1)}, u32[]{:S(2)}, u32[]{:S(2)}) collective-permute-start(bf16[176,1792]{1,0:T(8,128)(2,1)S(1)} %get-tuple-element.39.refs_0_), channel_id=1, source_target_pairs={{0,1},{3,2},{4,5},{7,6},{8,9},{11,10},{12,13},{15,14},{16,17},{19,... | collective-permute-start | bytes 1892360 | tf_op jit(solution)/shard_map/ppermute | solution.py:556
  76.3 0.1 collective-permute-done.15.refs_1_
  76.4 0.1 add.14.refs_4_
  76.5 0.7 collective-permute-start.21
  77.2 0.1 add.15.refs_2_
  77.3 1.3 %collective-permute-start.19 = (bf16[128,1792]{1,0:T(8,128)(2,1)S(1)}, bf16[128,1792]{1,0:T(8,128)(2,1)S(1)}, u32[]{:S(2)}, u32[]{:S(2)}) collective-permute-start(bf16[128,1792]{1,0:T(8,128)(2,1)S(1)} %add.15.refs_2_), channel_id=1, source_target_pairs={{1,0},{2,3},{5,4},{6,7},{9,8},{10,11},{13,12},{14,15},{17,16},{18,... | collective-permute-start | bytes 1376264 | tf_op jit(solution)/shard_map/ppermute | solution.py:562
  78.6 11.5 %collective-permute-done.20.refs_1_ = bf16[176,1792]{1,0:T(8,128)(2,1)S(1)} collective-permute-done((bf16[176,1792]{1,0:T(8,128)(2,1)S(1)}, bf16[176,1792]{1,0:T(8,128)(2,1)S(1)}, u32[]{:S(2)}, u32[]{:S(2)}) %collective-permute-start.20) | collective-permute-done | bytes 630816 | tf_op jit(solution)/shard_map/ppermute | solution.py:556
  90.2 4.4 %collective-permute-start.24 = (bf16[48,1792]{1,0:T(8,128)(2,1)S(1)}, bf16[48,1792]{1,0:T(8,128)(2,1)S(1)}, u32[]{:S(2)}, u32[]{:S(2)}) collective-permute-start(bf16[48,1792]{1,0:T(8,128)(2,1)S(1)} %stack.13), channel_id=1, source_target_pairs={{0,1},{3,2},{4,5},{7,6},{8,9},{11,10},{12,13},{15,14},{16,17},{19,... | collective-permute-start | bytes 516104 | tf_op jit(solution)/shard_map/ppermute | solution.py:556
  94.6 0.7 collective-permute-start.23
  95.4 0.2 add.18.refs_2_.refs_0_
  95.6 0.1 add.19.refs_2_
  95.7 1.3 %collective-permute-start.22 = (bf16[80,1792]{1,0:T(8,128)(2,1)S(1)}, bf16[80,1792]{1,0:T(8,128)(2,1)S(1)}, u32[]{:S(2)}, u32[]{:S(2)}) collective-permute-start(bf16[80,1792]{1,0:T(8,128)(2,1)S(1)} %add.19.refs_2_), channel_id=1, source_target_pairs={{1,0},{2,3},{5,4},{6,7},{9,8},{10,11},{13,12},{14,15},{17,16},{18,... | collective-permute-start | bytes 860168 | tf_op jit(solution)/shard_map/ppermute | solution.py:562
  97.0 0.7 collective-permute-start.25
  97.7 0.2 collective-permute-done.24.refs_3_
  97.9 1.3 %collective-permute-start.26 = (bf16[48,1792]{1,0:T(8,128)(2,1)S(1)}, bf16[48,1792]{1,0:T(8,128)(2,1)S(1)}, u32[]{:S(2)}, u32[]{:S(2)}) collective-permute-start(bf16[48,1792]{1,0:T(8,128)(2,1)S(1)} %add.20.refs_4_), channel_id=1, source_target_pairs={{1,0},{2,3},{5,4},{6,7},{9,8},{10,11},{13,12},{14,15},{17,16},{18,... | collective-permute-start | bytes 516104 | tf_op jit(solution)/shard_map/ppermute | solution.py:562
  99.2 8.0 %collective-permute-done.22.refs_3_ = bf16[80,1792]{1,0:T(8,128)(2,1)S(1)} collective-permute-done((bf16[80,1792]{1,0:T(8,128)(2,1)S(1)}, bf16[80,1792]{1,0:T(8,128)(2,1)S(1)}, u32[]{:S(2)}, u32[]{:S(2)}) %collective-permute-start.22) | collective-permute-done | bytes 286752 | tf_op jit(solution)/shard_map/ppermute | solution.py:562
  107.2 0.1 add.21.refs_1_
  107.4 1.8 %collective-permute-done.26.refs_5_ = bf16[48,1792]{1,0:T(8,128)(2,1)S(1)} collective-permute-done((bf16[48,1792]{1,0:T(8,128)(2,1)S(1)}, bf16[48,1792]{1,0:T(8,128)(2,1)S(1)}, u32[]{:S(2)}, u32[]{:S(2)}) %collective-permute-start.26) | collective-permute-done | bytes 172064 | tf_op jit(solution)/shard_map/ppermute | solution.py:562
  109.2 1.1 finish.1
  (37 shorter events, 0.3 us)
Async XLA Ops:
  0.0 1.5 %copy-start.5 = (bf16[32,4096]{1,0:T(8,128)(2,1)S(1)}, bf16[32,4096]{1,0:T(8,128)(2,1)}, u32[]{:S(2)}) copy-start(bf16[32,4096]{1,0:T(8,128)(2,1)} %param.19) | copy-start | bytes 786436
  0.0 2.9 %copy-start.1 = (bf16[256,64]{0,1:T(8,128)(2,1)S(1)}, bf16[256,64]{0,1:T(8,128)(2,1)}, u32[]{:S(2)}) copy-start(bf16[256,64]{0,1:T(8,128)(2,1)} %param.17) | copy-start | bytes 98308
  0.0 2.9 %copy-start.3 = (s32[1,16]{1,0:T(1,128)S(1)}, s32[1,16]{1,0:T(1,128)}, u32[]{:S(2)}) copy-start(s32[1,16]{1,0:T(1,128)} %table.1) | copy-start | bytes 196
  2.9 10.3 %copy-start = (s32[1,4,2]{1,2,0:T(2,128)S(1)}, s32[1,4,2]{1,2,0:T(2,128)}, u32[]{:S(2)}) copy-start(s32[1,4,2]{1,2,0:T(2,128)} %param.23) | copy-start | bytes 100
  10.2 10.5 %collective-permute-start = (bf16[48,2048]{1,0:T(8,128)(2,1)S(1)}, bf16[48,2048]{1,0:T(8,128)(2,1)S(1)}, u32[]{:S(2)}, u32[]{:S(2)}) collective-permute-start(bf16[48,2048]{1,0:T(8,128)(2,1)S(1)} %get-tuple-element.23.rest_0_), channel_id=1, source_target_pairs={{0,8},{4,12},{8,0},{12,4},{1,9},{5,13},{9,1},{13,5},{2,10},{6,14},... | collective-permute-start | bytes 589832 | tf_op jit(solution)/shard_map/ppermute | solution.py:375
  13.2 10.2 %collective-permute-start.1 = (bf16[48,2048]{1,0:T(8,128)(2,1)S(1)}, bf16[48,2048]{1,0:T(8,128)(2,1)S(1)}, u32[]{:S(2)}, u32[]{:S(2)}) collective-permute-start(bf16[48,2048]{1,0:T(8,128)(2,1)S(1)} %get-tuple-element.23.rest_0_), channel_id=1, source_target_pairs={{0,4},{4,0},{8,12},{12,8},{1,5},{5,1},{9,13},{13,9},{2,6},{6,2},{1... | collective-permute-start | bytes 589832 | tf_op jit(solution)/shard_map/ppermute | solution.py:402
  14.9 8.6 %slice-start = ((s8[7340032]{0:T(1024)(128)(4,1)}), s8[4194304]{0:T(1024)(128)(4,1)S(1)}, s32[]{:S(2)}) async-start(s8[7340032]{0:T(1024)(128)(4,1)} %bitcast.9), calls=%async_computation | async-start | bytes 8388608
  14.9 8.5 %slice-start.1 = ((s8[7340032]{0:T(1024)(128)(4,1)}), s8[3145728]{0:T(1024)(128)(4,1)S(1)}, s32[]{:S(2)}) async-start(s8[7340032]{0:T(1024)(128)(4,1)} %bitcast.9), calls=%async_computation.1 | async-start | bytes 6291456
  20.7 2.7 %collective-permute-start.2 = (bf16[48,2048]{1,0:T(8,128)(2,1)S(1)}, bf16[48,2048]{1,0:T(8,128)(2,1)S(1)}, u32[]{:S(2)}, u32[]{:S(2)}) collective-permute-start(bf16[48,2048]{1,0:T(8,128)(2,1)S(1)} %stack.7), channel_id=1, source_target_pairs={{0,4},{4,0},{8,12},{12,8},{1,5},{5,1},{9,13},{13,9},{2,6},{6,2},{1... | collective-permute-start | bytes 589832 | tf_op jit(solution)/shard_map/ppermute | solution.py:402
  21.3 13.5 %collective-permute-start.4 = (bf16[80,2048]{1,0:T(8,128)(2,1)S(1)}, bf16[80,2048]{1,0:T(8,128)(2,1)S(1)}, u32[]{:S(2)}, u32[]{:S(2)}) collective-permute-start(bf16[80,2048]{1,0:T(8,128)(2,1)S(1)} %attend.3.refs_1_.rest_4_.rest_0_), channel_id=1, source_target_pairs={{0,8},{4,12},{8,0},{12,4},{1,9},{5,13},{9,1},{13,5},{2,10},{6,14},... | collective-permute-start | bytes 983048 | tf_op jit(solution)/shard_map/ppermute | solution.py:375
  21.4 17.1 %collective-permute-start.5 = (bf16[80,2048]{1,0:T(8,128)(2,1)S(1)}, bf16[80,2048]{1,0:T(8,128)(2,1)S(1)}, u32[]{:S(2)}, u32[]{:S(2)}) collective-permute-start(bf16[80,2048]{1,0:T(8,128)(2,1)S(1)} %attend.3.refs_1_.rest_4_.rest_0_), channel_id=1, source_target_pairs={{0,4},{4,0},{8,12},{12,8},{1,5},{5,1},{9,13},{13,9},{2,6},{6,2},{1... | collective-permute-start | bytes 983048 | tf_op jit(solution)/shard_map/ppermute | solution.py:402
  21.5 16.5 %collective-permute-start.11 = (bf16[256,640]{1,0:T(8,128)(2,1)S(1)}, bf16[256,640]{1,0:T(8,128)(2,1)S(1)}, u32[]{:S(2)}, u32[]{:S(2)}) collective-permute-start(bf16[256,640]{1,0:T(8,128)(2,1)S(1)} %stack.9), channel_id=1, source_target_pairs={{0,8},{4,12},{8,0},{12,4},{1,9},{5,13},{9,1},{13,5},{2,10},{6,14},... | collective-permute-start | bytes 983048 | tf_op jit(solution)/shard_map/ppermute | solution.py:574
  25.2 20.3 %collective-permute-start.3 = (bf16[144,1792]{1,0:T(8,128)(2,1)S(1)}, bf16[144,1792]{1,0:T(8,128)(2,1)S(1)}, u32[]{:S(2)}, u32[]{:S(2)}) collective-permute-start(bf16[144,1792]{1,0:T(8,128)(2,1)S(1)} %get-tuple-element.30.refs_0_), channel_id=1, source_target_pairs={{0,1},{3,2},{4,5},{7,6},{8,9},{11,10},{12,13},{15,14},{16,17},{19,... | collective-permute-start | bytes 1548296 | tf_op jit(solution)/shard_map/ppermute | solution.py:556
  34.8 3.8 %collective-permute-start.6 = (bf16[80,2048]{1,0:T(8,128)(2,1)S(1)}, bf16[80,2048]{1,0:T(8,128)(2,1)S(1)}, u32[]{:S(2)}, u32[]{:S(2)}) collective-permute-start(bf16[80,2048]{1,0:T(8,128)(2,1)S(1)} %stack.8), channel_id=1, source_target_pairs={{0,4},{4,0},{8,12},{12,8},{1,5},{5,1},{9,13},{13,9},{2,6},{6,2},{1... | collective-permute-start | bytes 983048 | tf_op jit(solution)/shard_map/ppermute | solution.py:402
  38.0 7.5 %copy-start.2 = (s32[16,4]{0,1:T(4,128)S(1)}, s32[16,4]{0,1:T(4,128)}, u32[]{:S(2)}) copy-start(s32[16,4]{0,1:T(4,128)} %param.26) | copy-start | bytes 772
  38.1 7.5 %copy-start.4 = (s32[16]{0:T(128)S(1)}, s32[16]{0:T(128)}, u32[]{:S(2)}) copy-start(s32[16]{0:T(128)} %decode_length.1) | copy-start | bytes 196
  38.1 7.5 %collective-permute-start.12 = (bf16[256,640]{1,0:T(8,128)(2,1)S(1)}, bf16[256,640]{1,0:T(8,128)(2,1)S(1)}, u32[]{:S(2)}, u32[]{:S(2)}) collective-permute-start(bf16[256,640]{1,0:T(8,128)(2,1)S(1)} %stack.10), channel_id=1, source_target_pairs={{0,4},{4,0},{8,12},{12,8},{1,5},{5,1},{9,13},{13,9},{2,6},{6,2},{1... | collective-permute-start | bytes 983048 | tf_op jit(solution)/shard_map/ppermute | solution.py:402
  38.1 15.5 %collective-permute-start.9 = (bf16[80,2048]{1,0:T(8,128)(2,1)S(1)}, bf16[80,2048]{1,0:T(8,128)(2,1)S(1)}, u32[]{:S(2)}, u32[]{:S(2)}) collective-permute-start(bf16[80,2048]{1,0:T(8,128)(2,1)S(1)} %attend.4.refs_1_.rest_4_.refs_2_.rest_0_), channel_id=1, source_target_pairs={{0,8},{4,12},{8,0},{12,4},{1,9},{5,13},{9,1},{13,5},{2,10},{6,14},... | collective-permute-start | bytes 983048 | tf_op jit(solution)/shard_map/ppermute | solution.py:375
  38.5 16.0 %collective-permute-start.10 = (bf16[80,2048]{1,0:T(8,128)(2,1)S(1)}, bf16[80,2048]{1,0:T(8,128)(2,1)S(1)}, u32[]{:S(2)}, u32[]{:S(2)}) collective-permute-start(bf16[80,2048]{1,0:T(8,128)(2,1)S(1)} %attend.4.refs_1_.rest_4_.refs_2_.rest_0_), channel_id=1, source_target_pairs={{0,4},{4,0},{8,12},{12,8},{1,5},{5,1},{9,13},{13,9},{2,6},{6,2},{1... | collective-permute-start | bytes 983048 | tf_op jit(solution)/shard_map/ppermute | solution.py:402
  41.5 23.2 %collective-permute-start.8 = (bf16[240,1792]{1,0:T(8,128)(2,1)S(1)}, bf16[240,1792]{1,0:T(8,128)(2,1)S(1)}, u32[]{:S(2)}, u32[]{:S(2)}) collective-permute-start(bf16[240,1792]{1,0:T(8,128)(2,1)S(1)} %get-tuple-element.32.refs_0_.refs_2_), channel_id=1, source_target_pairs={{0,1},{3,2},{4,5},{7,6},{8,9},{11,10},{12,13},{15,14},{16,17},{19,... | collective-permute-start | bytes 2580488 | tf_op jit(solution)/shard_map/ppermute | solution.py:556
  53.7 1.7 %collective-permute-start.13 = (bf16[80,2048]{1,0:T(8,128)(2,1)S(1)}, bf16[80,2048]{1,0:T(8,128)(2,1)S(1)}, u32[]{:S(2)}, u32[]{:S(2)}) collective-permute-start(bf16[80,2048]{1,0:T(8,128)(2,1)S(1)} %stack.11), channel_id=1, source_target_pairs={{0,4},{4,0},{8,12},{12,8},{1,5},{5,1},{9,13},{13,9},{2,6},{6,2},{1... | collective-permute-start | bytes 983048 | tf_op jit(solution)/shard_map/ppermute | solution.py:402
  53.9 9.4 %collective-permute-start.7 = (bf16[96,1792]{1,0:T(8,128)(2,1)S(1)}, bf16[96,1792]{1,0:T(8,128)(2,1)S(1)}, u32[]{:S(2)}, u32[]{:S(2)}) collective-permute-start(bf16[96,1792]{1,0:T(8,128)(2,1)S(1)} %add.12.rest_3_), channel_id=1, source_target_pairs={{1,2},{2,1},{5,6},{6,5},{9,10},{10,9},{13,14},{14,13},{17,18},{18,... | collective-permute-start | bytes 1032200 | tf_op jit(solution)/shard_map/ppermute | solution.py:559
  58.2 18.1 %collective-permute-start.15 = (bf16[160,1792]{1,0:T(8,128)(2,1)S(1)}, bf16[160,1792]{1,0:T(8,128)(2,1)S(1)}, u32[]{:S(2)}, u32[]{:S(2)}) collective-permute-start(bf16[160,1792]{1,0:T(8,128)(2,1)S(1)} %get-tuple-element.36.refs_0_), channel_id=1, source_target_pairs={{0,1},{3,2},{4,5},{7,6},{8,9},{11,10},{12,13},{15,14},{16,17},{19,... | collective-permute-start | bytes 1720328 | tf_op jit(solution)/shard_map/ppermute | solution.py:556
  61.7 6.5 %collective-permute-start.16 = (bf16[48,2048]{1,0:T(8,128)(2,1)S(1)}, bf16[48,2048]{1,0:T(8,128)(2,1)S(1)}, u32[]{:S(2)}, u32[]{:S(2)}) collective-permute-start(bf16[48,2048]{1,0:T(8,128)(2,1)S(1)} %attend.5.refs_1_.rest_4_.rest_0_), channel_id=1, source_target_pairs={{0,8},{4,12},{8,0},{12,4},{1,9},{5,13},{9,1},{13,5},{2,10},{6,14},... | collective-permute-start | bytes 589832 | tf_op jit(solution)/shard_map/ppermute | solution.py:375
  64.8 12.4 %collective-permute-start.14 = (bf16[160,1792]{1,0:T(8,128)(2,1)S(1)}, bf16[160,1792]{1,0:T(8,128)(2,1)S(1)}, u32[]{:S(2)}, u32[]{:S(2)}) collective-permute-start(bf16[160,1792]{1,0:T(8,128)(2,1)S(1)} %add.13.rest_5_), channel_id=1, source_target_pairs={{1,2},{2,1},{5,6},{6,5},{9,10},{10,9},{13,14},{14,13},{17,18},{18,... | collective-permute-start | bytes 1720328 | tf_op jit(solution)/shard_map/ppermute | solution.py:559
  65.5 2.8 %collective-permute-start.17 = (bf16[48,2048]{1,0:T(8,128)(2,1)S(1)}, bf16[48,2048]{1,0:T(8,128)(2,1)S(1)}, u32[]{:S(2)}, u32[]{:S(2)}) collective-permute-start(bf16[48,2048]{1,0:T(8,128)(2,1)S(1)} %attend.5.refs_1_.rest_4_.rest_0_), channel_id=1, source_target_pairs={{0,4},{4,0},{8,12},{12,8},{1,5},{5,1},{9,13},{13,9},{2,6},{6,2},{1... | collective-permute-start | bytes 589832 | tf_op jit(solution)/shard_map/ppermute | solution.py:402
  68.2 1.5 %collective-permute-start.18 = (bf16[48,2048]{1,0:T(8,128)(2,1)S(1)}, bf16[48,2048]{1,0:T(8,128)(2,1)S(1)}, u32[]{:S(2)}, u32[]{:S(2)}) collective-permute-start(bf16[48,2048]{1,0:T(8,128)(2,1)S(1)} %stack.12), channel_id=1, source_target_pairs={{0,4},{4,0},{8,12},{12,8},{1,5},{5,1},{9,13},{13,9},{2,6},{6,2},{1... | collective-permute-start | bytes 589832 | tf_op jit(solution)/shard_map/ppermute | solution.py:402
  71.5 18.7 %collective-permute-start.20 = (bf16[176,1792]{1,0:T(8,128)(2,1)S(1)}, bf16[176,1792]{1,0:T(8,128)(2,1)S(1)}, u32[]{:S(2)}, u32[]{:S(2)}) collective-permute-start(bf16[176,1792]{1,0:T(8,128)(2,1)S(1)} %get-tuple-element.39.refs_0_), channel_id=1, source_target_pairs={{0,1},{3,2},{4,5},{7,6},{8,9},{11,10},{12,13},{15,14},{16,17},{19,... | collective-permute-start | bytes 1892360 | tf_op jit(solution)/shard_map/ppermute | solution.py:556
  76.5 19.1 %collective-permute-start.21 = (bf16[160,1792]{1,0:T(8,128)(2,1)S(1)}, bf16[160,1792]{1,0:T(8,128)(2,1)S(1)}, u32[]{:S(2)}, u32[]{:S(2)}) collective-permute-start(bf16[160,1792]{1,0:T(8,128)(2,1)S(1)} %add.14.refs_4_), channel_id=1, source_target_pairs={{1,2},{2,1},{5,6},{6,5},{9,10},{10,9},{13,14},{14,13},{17,18},{18,... | collective-permute-start | bytes 1720328 | tf_op jit(solution)/shard_map/ppermute | solution.py:559
  77.3 18.0 %collective-permute-start.19 = (bf16[128,1792]{1,0:T(8,128)(2,1)S(1)}, bf16[128,1792]{1,0:T(8,128)(2,1)S(1)}, u32[]{:S(2)}, u32[]{:S(2)}) collective-permute-start(bf16[128,1792]{1,0:T(8,128)(2,1)S(1)} %add.15.refs_2_), channel_id=1, source_target_pairs={{1,0},{2,3},{5,4},{6,7},{9,8},{10,11},{13,12},{14,15},{17,16},{18,... | collective-permute-start | bytes 1376264 | tf_op jit(solution)/shard_map/ppermute | solution.py:562
  90.2 7.7 %collective-permute-start.24 = (bf16[48,1792]{1,0:T(8,128)(2,1)S(1)}, bf16[48,1792]{1,0:T(8,128)(2,1)S(1)}, u32[]{:S(2)}, u32[]{:S(2)}) collective-permute-start(bf16[48,1792]{1,0:T(8,128)(2,1)S(1)} %stack.13), channel_id=1, source_target_pairs={{0,1},{3,2},{4,5},{7,6},{8,9},{11,10},{12,13},{15,14},{16,17},{19,... | collective-permute-start | bytes 516104 | tf_op jit(solution)/shard_map/ppermute | solution.py:556
  94.6 3.3 %collective-permute-start.23 = (bf16[48,1792]{1,0:T(8,128)(2,1)S(1)}, bf16[48,1792]{1,0:T(8,128)(2,1)S(1)}, u32[]{:S(2)}, u32[]{:S(2)}) collective-permute-start(bf16[48,1792]{1,0:T(8,128)(2,1)S(1)} %add.16.refs_2_.refs_1_), channel_id=1, source_target_pairs={{1,2},{2,1},{5,6},{6,5},{9,10},{10,9},{13,14},{14,13},{17,18},{18,... | collective-permute-start | bytes 516104 | tf_op jit(solution)/shard_map/ppermute | solution.py:559
  95.7 11.6 %collective-permute-start.22 = (bf16[80,1792]{1,0:T(8,128)(2,1)S(1)}, bf16[80,1792]{1,0:T(8,128)(2,1)S(1)}, u32[]{:S(2)}, u32[]{:S(2)}) collective-permute-start(bf16[80,1792]{1,0:T(8,128)(2,1)S(1)} %add.19.refs_2_), channel_id=1, source_target_pairs={{1,0},{2,3},{5,4},{6,7},{9,8},{10,11},{13,12},{14,15},{17,16},{18,... | collective-permute-start | bytes 860168 | tf_op jit(solution)/shard_map/ppermute | solution.py:562
  97.0 10.4 %collective-permute-start.25 = (bf16[48,1792]{1,0:T(8,128)(2,1)S(1)}, bf16[48,1792]{1,0:T(8,128)(2,1)S(1)}, u32[]{:S(2)}, u32[]{:S(2)}) collective-permute-start(bf16[48,1792]{1,0:T(8,128)(2,1)S(1)} %add.17.refs_8_), channel_id=1, source_target_pairs={{1,2},{2,1},{5,6},{6,5},{9,10},{10,9},{13,14},{14,13},{17,18},{18,... | collective-permute-start | bytes 516104 | tf_op jit(solution)/shard_map/ppermute | solution.py:559
  97.9 11.3 %collective-permute-start.26 = (bf16[48,1792]{1,0:T(8,128)(2,1)S(1)}, bf16[48,1792]{1,0:T(8,128)(2,1)S(1)}, u32[]{:S(2)}, u32[]{:S(2)}) collective-permute-start(bf16[48,1792]{1,0:T(8,128)(2,1)S(1)} %add.20.refs_4_), channel_id=1, source_target_pairs={{1,0},{2,3},{5,4},{6,7},{9,8},{10,11},{13,12},{14,15},{17,16},{18,... | collective-permute-start | bytes 516104 | tf_op jit(solution)/shard_map/ppermute | solution.py:562

commit v9 on v7

--- a/solution.py
+++ b/solution.py
@@ -132,7 +132,7 @@
     copies.append(pltpu.make_async_copy(
         new_latent, keys.at[pl.ds(prior, tok_group), pl.ds(0, latent)], sems.at[blocks]))
     for c in copies:
-        c.start()
+        c.start(priority=1)
 
     keys[prior:, latent:] = rope_rows(new_rope_t[...])
     lane = lax.broadcasted_iota(jnp.int32, (block_len, LANES), 1)
@@ -581,16 +581,16 @@
     own1, rest1 = project(where, gather(x1, (x2,)), w, (3,), (), (x2,))
     in1 = inward(rest1)
     to_across0 = add(2 * t0, [(rest0, 0), (in0, 0)], (own1,))
-    on0 = across(to_across0)
     x3 = attend(3, held, (to_across0,), brought)
     own2, rest2, near2 = project(where, gather(x2, (x3,)), w, (2, 1), (), (x3,))
     in2 = inward(rest2)
-    to_across1 = add(2 * t1, [(rest1, 0), (in1, 0)], (own2, on0))
+    on0 = across(stack([to_across0], (own2,)))
+    to_across1 = add(2 * t1, [(rest1, 0), (in1, 0)], (own2,))
     on1 = across(to_across1)
     own3, rest3, near = project(
         where, gather(x3, (own2,)), w, (2, 1), (near2,), (to_across1,))
     in3 = inward(rest3)
-    to_across2 = add(2 * t2, [(rest2, 0), (in2, 0)], (own3,))
+    to_across2 = add(2 * t2, [(rest2, 0), (in2, 0)], (own3, on0))
     on2 = across(to_across2)
     near_in = inward(near)
     to_out01 = add_all([(t0, [(rest0, 2 * t0), (on0, 0)]), (t1, [(rest1, 2 * t1), (on1, 0)])],

time: 106 us -> 106 us (level)
    ppermute x5, waiting for transfers between devices: 5.42 us -> 2.98 us  [inward(): return lax.ppermute(x, 'tp', INWARD)]
    ppermute x3, waiting for transfers between devices: 14.1 us -> 16 us  [outward(): return lax.ppermute(x, 'tp', OUTWARD)]
  transfers between devices with their start and end apart: 27 -> 27, of which waited for: 11 -> 10; matrix products, arithmetic and copies ran while one was open for 0% -> 0% of each run, Pallas kernels for 35% -> 35%
where the time goes in v9:
time: 106 us; the launch traced here: 105 us
  starting transfers between devices  40.2 us (38%)
  Pallas kernels  39.9 us (38%)
  waiting for transfers between devices  21.2 us (20%)
  local copies, waits for them, and re-layouts  2.68 us (3%)
  between operations  1.13 us (1%)
    ppermute x5, starting transfers between devices, inward(): return lax.ppermute(x, 'tp', INWARD)  24.6 us
    pallas_call x3, Pallas kernels, attend(): pl.pallas_call(kernel, out_shape=jax.ShapeDtypeStruct((t, heads * dv), bf...  20.1 us
    ppermute x3, waiting for transfers between devices, outward(): return lax.ppermute(x, 'tp', OUTWARD)  16 us
    pallas_call x4, Pallas kernels, project(): pl.pallas_call(functools.partial(project_kernel, len(parts), tails, place...  9.09 us
    pallas_call x1, Pallas kernels, first_chunk(): pl.pallas_call(functools.partial(first_kernel, fresh_of(0), exp_scale), o...  6.86 us
    ppermute x3, starting transfers between devices, outward(): return lax.ppermute(x, 'tp', OUTWARD)  3.88 us
    ppermute x5, starting transfers between devices, across(): return lax.ppermute(x, 'tp', ACROSS)  3.42 us
    ppermute x4, starting transfers between devices, shift_groups(): lax.ppermute(x, 'dp', [(i, (i + s) % groups) for i in range(groups)])  3.36 us
  transfers between devices with their start and end apart: 27, of which 10 were waited for; matrix products, arithmetic and copies ran while one was open for 0% of the time, Pallas kernels for 35%

profile of v9, /device:TPU:0, one launch (start us, length us, event | category | flops | bytes accessed | tf_op | source)
XLA Modules:
  0.0 105.1 jit_solution(5322867566458152791)
XLA Ops:
  0.0 1.6 %reshape.6 = bf16[32,64,64]{2,1,0:T(8,128)(2,1)S(1)} reshape(bf16[32,4096]{1,0:T(8,128)(2,1)} %param.19) | data formatting | bytes 524288 | tf_op jit(solution)/shard_map/reshape | solution.py:457
  1.6 0.1 pad.4.cache_rope
  1.7 0.0 copy-start
  1.7 0.7 copy-done
  2.4 1.7 %pack.1 = (bf16[128,640]{1,0:T(8,128)(2,1)S(1)}, bf16[128,640]{1,0:T(8,128)(2,1)S(1)}, bf16[256,640]{1,0:T(8,128)(2,1)S(1)}) custom-call(s32[1]{0:T(128)} %bitcast.me, s32[1,2,4]{2,1,0:T(2,128)S(1)} %bitcast.15, bf16[32,64,512]{2,1,0:T(8,128)(2,1)} %cache_latent.3, bf16[32,64,128]{2,1,0:T(8,128)(2,1)S(1)} %pad.4.cache_rope), custom_call_target="tpu_custom_call" | custom-call | flops 1000 | bytes 1000 | tf_op jit(solution)/shard_map/pack/pallas_call | solution.py:524
  4.1 3.0 %collective-permute-start.6 = (bf16[256,640]{1,0:T(8,128)(2,1)S(1)}, bf16[256,640]{1,0:T(8,128)(2,1)S(1)}, u32[]{:S(2)}, u32[]{:S(2)}) collective-permute-start(bf16[256,640]{1,0:T(8,128)(2,1)S(1)} %get-tuple-element.31), channel_id=1, source_target_pairs={{0,8},{4,12},{8,0},{12,4},{1,9},{5,13},{9,1},{13,5},{2,10},{6,14},... | collective-permute-start | bytes 983048 | tf_op jit(solution)/shard_map/ppermute | solution.py:573
  7.1 0.3 copy.17
  8.0 6.9 %attend_first.1 = (bf16[48,2048]{1,0:T(8,128)(2,1)S(1)}, bf16[1280,640]{1,0:T(8,128)(2,1)S(1)}, bf16[16,128,512]{2,1,0:T(8,128)(2,1)S(1)}, bf16[16,512,128]{2,1,0:T(8,128)(2,1)S(1)}, bf16[256,1024]{1,0:T(8,128)(2,1)S(1)}) custom-call(s32[1]{0:T(128)} %bitcast.me, s32[1]{0:T(128)} %bitcast.1.z, s32[1,16]{1,0:T(1,128)S(1)} %copy-done.3, s32[1]{0:T(128)S(6)} %copy.18.offset, ...), custom_call_target="tpu_custom_call" | custom-call | flops 40000000000 | bytes 1000 | tf_op jit(solution)/shard_map/attend_first/pallas_call | solution.py:471
  14.9 0.1 collective-permute-start
  15.0 0.1 collective-permute-start.1
  15.1 0.5 collective-permute-start.7
  15.7 4.7 %attend.3.refs_1_.rest_4_.rest_0_ = bf16[64,2048]{1,0:T(8,128)(2,1)S(1)} custom-call(bf16[16,256,128]{2,1,0:T(8,128)(2,1)S(1)} %bitcast.12, bf16[256,1024]{1,0:T(8,128)(2,1)S(1)} %get-tuple-element.24.q_rope, bf16[16,128,512]{2,1,0:T(8,128)(2,1)S(1)} %get-tuple-element.25.wk, bf16[16,512,128]{2,1,0:T(8,128)(2,1)S(1)} %get-tuple-element.26.wv, ...), custom_call_target="tpu_custom_call" | custom-call | flops 40000000000 | bytes 1000 | tf_op jit(solution)/shard_map/attend/pallas_call | solution.py:512
  20.4 0.9 collective-permute-done.refs_0_.rest_1_
  21.4 0.1 collective-permute-start.2
  21.4 1.1 %collective-permute-start.4 = (bf16[64,2048]{1,0:T(8,128)(2,1)S(1)}, bf16[64,2048]{1,0:T(8,128)(2,1)S(1)}, u32[]{:S(2)}, u32[]{:S(2)}) collective-permute-start(bf16[64,2048]{1,0:T(8,128)(2,1)S(1)} %attend.3.refs_1_.rest_4_.rest_0_), channel_id=1, source_target_pairs={{0,8},{4,12},{8,0},{12,4},{1,9},{5,13},{9,1},{13,5},{2,10},{6,14},... | collective-permute-start | bytes 786440 | tf_op jit(solution)/shard_map/ppermute | solution.py:377
  22.5 0.2 collective-permute-start.5
  22.7 0.1 collective-permute-done.2.rest_3_
  22.9 1.7 %project.4 = (bf16[48,1792]{1,0:T(8,128)(2,1)S(1)}, bf16[144,1792]{1,0:T(8,128)(2,1)S(1)}) custom-call(s32[1]{0:T(128)} %bitcast.me, s32[1]{0:T(128)} %bitcast.1.z, bf16[2048,1792]{1,0:T(8,128)(2,1)S(1)} %bitcast.10, bf16[48,2048]{1,0:T(8,128)(2,1)S(1)} %get-tuple-element.23.rest_0_.refs_2_, bf16[48,2048]{1,0:T(8,128)(2,1)S(1)} %collective-permute-done.refs_0_.rest_1_, ...), custom_call_target="tpu_custom_call" | custom-call | flops 1000 | bytes 1000 | tf_op jit(solution)/shard_map/project/pallas_call | solution.py:304
  24.6 3.7 %collective-permute-start.3 = (bf16[144,1792]{1,0:T(8,128)(2,1)S(1)}, bf16[144,1792]{1,0:T(8,128)(2,1)S(1)}, u32[]{:S(2)}, u32[]{:S(2)}) collective-permute-start(bf16[144,1792]{1,0:T(8,128)(2,1)S(1)} %get-tuple-element.29.refs_0_), channel_id=1, source_target_pairs={{0,1},{3,2},{4,5},{7,6},{8,9},{11,10},{12,13},{15,14},{16,17},{19,... | collective-permute-start | bytes 1548296 | tf_op jit(solution)/shard_map/ppermute | solution.py:558
  28.3 5.9 %attend.4.refs_1_.rest_4_.rest_0_ = bf16[80,2048]{1,0:T(8,128)(2,1)S(1)} custom-call(bf16[16,256,128]{2,1,0:T(8,128)(2,1)S(1)} %bitcast.13, bf16[256,1024]{1,0:T(8,128)(2,1)S(1)} %get-tuple-element.24.q_rope, bf16[16,128,512]{2,1,0:T(8,128)(2,1)S(1)} %get-tuple-element.25.wk, bf16[16,512,128]{2,1,0:T(8,128)(2,1)S(1)} %get-tuple-element.26.wv, ...), custom_call_target="tpu_custom_call" | custom-call | flops 40000000000 | bytes 1000 | tf_op jit(solution)/shard_map/attend/pallas_call | solution.py:512
  34.2 0.0 copy-start.2
  34.2 0.0 copy-start.4
  34.3 0.1 collective-permute-start.8
  34.3 1.1 %collective-permute-start.9 = (bf16[80,2048]{1,0:T(8,128)(2,1)S(1)}, bf16[80,2048]{1,0:T(8,128)(2,1)S(1)}, u32[]{:S(2)}, u32[]{:S(2)}) collective-permute-start(bf16[80,2048]{1,0:T(8,128)(2,1)S(1)} %attend.4.refs_1_.rest_4_.rest_0_), channel_id=1, source_target_pairs={{0,8},{4,12},{8,0},{12,4},{1,9},{5,13},{9,1},{13,5},{2,10},{6,14},... | collective-permute-start | bytes 983048 | tf_op jit(solution)/shard_map/ppermute | solution.py:377
  35.4 0.2 collective-permute-start.10
  35.6 0.2 collective-permute-done.8.rest_3_
  35.9 2.3 %project.5 = (bf16[64,1792]{1,0:T(8,128)(2,1)S(1)}, bf16[192,1792]{1,0:T(8,128)(2,1)S(1)}) custom-call(s32[1]{0:T(128)} %bitcast.me, s32[1]{0:T(128)} %bitcast.1.z, bf16[2048,1792]{1,0:T(8,128)(2,1)S(1)} %bitcast.10, bf16[64,2048]{1,0:T(8,128)(2,1)S(1)} %attend.3.refs_1_.rest_4_.rest_0_, bf16[64,2048]{1,0:T(8,128)(2,1)S(1)} %collective-permute-done.4.refs_0_.rest_1_, ...), custom_call_target="tpu_custom_call" | custom-call | flops 1000 | bytes 1000 | tf_op jit(solution)/shard_map/project/pallas_call | solution.py:304
  38.1 1.6 %collective-permute-start.13 = (bf16[192,1792]{1,0:T(8,128)(2,1)S(1)}, bf16[192,1792]{1,0:T(8,128)(2,1)S(1)}, u32[]{:S(2)}, u32[]{:S(2)}) collective-permute-start(bf16[192,1792]{1,0:T(8,128)(2,1)S(1)} %get-tuple-element.35.refs_0_.refs_2_), channel_id=1, source_target_pairs={{0,1},{3,2},{4,5},{7,6},{8,9},{11,10},{12,13},{15,14},{16,17},{19,... | collective-permute-start | bytes 2064392 | tf_op jit(solution)/shard_map/ppermute | solution.py:558
  39.7 0.1 add.12.rest_3_.refs_0_
  39.8 9.5 %attend.5.refs_1_.rest_4_.rest_0_ = bf16[64,2048]{1,0:T(8,128)(2,1)S(1)} custom-call(s32[1]{0:T(128)} %bitcast.me, bf16[16,256,128]{2,1,0:T(8,128)(2,1)S(1)} %bitcast.14, bf16[256,1024]{1,0:T(8,128)(2,1)S(1)} %get-tuple-element.24.q_rope, bf16[16,128,512]{2,1,0:T(8,128)(2,1)S(1)} %get-tuple-element.25.wk, bf16[16,512,128]{2,1,0:T(8,128)(2,1)S(1)} %get-tuple-element.26.wv, ...), custom_call_target="tpu_custom_call" | custom-call | flops 6000000000 | bytes 1000 | tf_op jit(solution)/shard_map/attend/pallas_call | solution.py:512
  49.3 0.2 collective-permute-start.11
  49.5 1.0 collective-permute-start.16
  50.6 0.4 collective-permute-done.11.rest_3_
  51.0 2.8 %project.6 = (bf16[80,1792]{1,0:T(8,128)(2,1)S(1)}, bf16[160,1792]{1,0:T(8,128)(2,1)S(1)}, bf16[80,1792]{1,0:T(8,128)(2,1)S(1)}) custom-call(s32[1]{0:T(128)} %bitcast.me, s32[1]{0:T(128)} %bitcast.1.z, bf16[2048,1792]{1,0:T(8,128)(2,1)S(1)} %bitcast.10, bf16[80,2048]{1,0:T(8,128)(2,1)S(1)} %attend.4.refs_1_.rest_4_.rest_0_, ...), custom_call_target="tpu_custom_call" | custom-call | flops 1000 | bytes 1000 | tf_op jit(solution)/shard_map/project/pallas_call | solution.py:304
  53.8 4.2 %collective-permute-start.15 = (bf16[160,1792]{1,0:T(8,128)(2,1)S(1)}, bf16[160,1792]{1,0:T(8,128)(2,1)S(1)}, u32[]{:S(2)}, u32[]{:S(2)}) collective-permute-start(bf16[160,1792]{1,0:T(8,128)(2,1)S(1)} %get-tuple-element.36.refs_0_), channel_id=1, source_target_pairs={{0,1},{3,2},{4,5},{7,6},{8,9},{11,10},{12,13},{15,14},{16,17},{19,... | collective-permute-start | bytes 1720328 | tf_op jit(solution)/shard_map/ppermute | solution.py:558
  58.1 0.7 collective-permute-start.12
  58.8 0.1 collective-permute-start.17
  58.9 0.5 collective-permute-start.18
  59.4 0.1 add.13.rest_5_
  59.5 0.7 collective-permute-start.14
  60.2 0.1 collective-permute-done.17.rest_2_
  60.4 0.4 collective-permute-done.18.rest_3_
  60.7 2.3 %project.7 = (bf16[64,1792]{1,0:T(8,128)(2,1)S(1)}, bf16[128,1792]{1,0:T(8,128)(2,1)S(1)}, bf16[144,1792]{1,0:T(8,128)(2,1)S(1)}) custom-call(s32[1]{0:T(128)} %bitcast.me, s32[1]{0:T(128)} %bitcast.1.z, bf16[2048,1792]{1,0:T(8,128)(2,1)S(1)} %bitcast.10, bf16[64,2048]{1,0:T(8,128)(2,1)S(1)} %attend.5.refs_1_.rest_4_.rest_0_, ...), custom_call_target="tpu_custom_call" | custom-call | flops 1000 | bytes 1000 | tf_op jit(solution)/shard_map/project/pallas_call | solution.py:304
  63.0 5.3 %collective-permute-start.20 = (bf16[128,1792]{1,0:T(8,128)(2,1)S(1)}, bf16[128,1792]{1,0:T(8,128)(2,1)S(1)}, u32[]{:S(2)}, u32[]{:S(2)}) collective-permute-start(bf16[128,1792]{1,0:T(8,128)(2,1)S(1)} %get-tuple-element.39.refs_0_), channel_id=1, source_target_pairs={{0,1},{3,2},{4,5},{7,6},{8,9},{11,10},{12,13},{15,14},{16,17},{19,... | collective-permute-start | bytes 1376264 | tf_op jit(solution)/shard_map/ppermute | solution.py:558
  68.4 3.0 %collective-permute-done.15.refs_1_ = bf16[160,1792]{1,0:T(8,128)(2,1)S(1)} collective-permute-done((bf16[160,1792]{1,0:T(8,128)(2,1)S(1)}, bf16[160,1792]{1,0:T(8,128)(2,1)S(1)}, u32[]{:S(2)}, u32[]{:S(2)}) %collective-permute-start.15) | collective-permute-done | bytes 573472 | tf_op jit(solution)/shard_map/ppermute | solution.py:558
  71.3 0.1 add.14.refs_4_
  71.5 0.7 collective-permute-start.22
  72.2 0.1 add.15.refs_2_
  72.3 1.3 %collective-permute-start.19 = (bf16[112,1792]{1,0:T(8,128)(2,1)S(1)}, bf16[112,1792]{1,0:T(8,128)(2,1)S(1)}, u32[]{:S(2)}, u32[]{:S(2)}) collective-permute-start(bf16[112,1792]{1,0:T(8,128)(2,1)S(1)} %add.15.refs_2_), channel_id=1, source_target_pairs={{1,0},{2,3},{5,4},{6,7},{9,8},{10,11},{13,12},{14,15},{17,16},{18,... | collective-permute-start | bytes 1204232 | tf_op jit(solution)/shard_map/ppermute | solution.py:564
  73.6 9.8 %collective-permute-start.21 = (bf16[144,1792]{1,0:T(8,128)(2,1)S(1)}, bf16[144,1792]{1,0:T(8,128)(2,1)S(1)}, u32[]{:S(2)}, u32[]{:S(2)}) collective-permute-start(bf16[144,1792]{1,0:T(8,128)(2,1)S(1)} %get-tuple-element.40.refs_0_), channel_id=1, source_target_pairs={{0,1},{3,2},{4,5},{7,6},{8,9},{11,10},{12,13},{15,14},{16,17},{19,... | collective-permute-start | bytes 1548296 | tf_op jit(solution)/shard_map/ppermute | solution.py:558
  83.4 0.1 add.16.refs_2_
  83.5 0.7 collective-permute-start.24
  84.2 0.1 add.17.refs_8_
  84.2 5.1 %collective-permute-done.19.refs_3_.refs_7_ = bf16[112,1792]{1,0:T(8,128)(2,1)S(1)} collective-permute-done((bf16[112,1792]{1,0:T(8,128)(2,1)S(1)}, bf16[112,1792]{1,0:T(8,128)(2,1)S(1)}, u32[]{:S(2)}, u32[]{:S(2)}) %collective-permute-start.19) | collective-permute-done | bytes 401440 | tf_op jit(solution)/shard_map/ppermute | solution.py:564
  89.4 0.2 add.18.refs_2_.refs_0_
  89.6 0.1 add.19.refs_2_
  89.7 1.3 %collective-permute-start.23 = (bf16[80,1792]{1,0:T(8,128)(2,1)S(1)}, bf16[80,1792]{1,0:T(8,128)(2,1)S(1)}, u32[]{:S(2)}, u32[]{:S(2)}) collective-permute-start(bf16[80,1792]{1,0:T(8,128)(2,1)S(1)} %add.19.refs_2_), channel_id=1, source_target_pairs={{1,0},{2,3},{5,4},{6,7},{9,8},{10,11},{13,12},{14,15},{17,16},{18,... | collective-permute-start | bytes 860168 | tf_op jit(solution)/shard_map/ppermute | solution.py:564
  91.0 0.7 collective-permute-start.25
  91.7 0.1 add.20.refs_4_
  91.7 1.3 %collective-permute-start.26 = (bf16[64,1792]{1,0:T(8,128)(2,1)S(1)}, bf16[64,1792]{1,0:T(8,128)(2,1)S(1)}, u32[]{:S(2)}, u32[]{:S(2)}) collective-permute-start(bf16[64,1792]{1,0:T(8,128)(2,1)S(1)} %add.20.refs_4_), channel_id=1, source_target_pairs={{1,0},{2,3},{5,4},{6,7},{9,8},{10,11},{13,12},{14,15},{17,16},{18,... | collective-permute-start | bytes 688136 | tf_op jit(solution)/shard_map/ppermute | solution.py:564
  93.0 7.3 %collective-permute-done.23.refs_3_ = bf16[80,1792]{1,0:T(8,128)(2,1)S(1)} collective-permute-done((bf16[80,1792]{1,0:T(8,128)(2,1)S(1)}, bf16[80,1792]{1,0:T(8,128)(2,1)S(1)}, u32[]{:S(2)}, u32[]{:S(2)}) %collective-permute-start.23) | collective-permute-done | bytes 286752 | tf_op jit(solution)/shard_map/ppermute | solution.py:564
  100.3 0.1 add.21.refs_1_
  100.5 3.6 %collective-permute-done.26.refs_5_ = bf16[64,1792]{1,0:T(8,128)(2,1)S(1)} collective-permute-done((bf16[64,1792]{1,0:T(8,128)(2,1)S(1)}, bf16[64,1792]{1,0:T(8,128)(2,1)S(1)}, u32[]{:S(2)}, u32[]{:S(2)}) %collective-permute-start.26) | collective-permute-done | bytes 229408 | tf_op jit(solution)/shard_map/ppermute | solution.py:564
  104.1 1.1 %finish.1 = bf16[256,1792]{1,0:T(8,128)(2,1)} custom-call(bf16[112,1792]{1,0:T(8,128)(2,1)S(1)} %add.18.refs_2_.refs_0_, bf16[80,1792]{1,0:T(8,128)(2,1)S(1)} %add.21.refs_1_, bf16[64,1792]{1,0:T(8,128)(2,1)S(1)} %get-tuple-element.38.refs_2_, bf16[144,1792]{1,0:T(8,128)(2,1)S(1)} %collective-permute-done.21.refs_1_.refs_3_, ...), custom_call_target="tpu_custom_call" | custom-call | flops 1000 | bytes 1000 | tf_op jit(solution)/shard_map/finish/pallas_call | solution.py:357
  (36 shorter events, 0.2 us)
Async XLA Ops:
  0.0 7.1 %copy-start.5 = (bf16[256,16,128]{2,1,0:T(8,128)(2,1)S(1)}, bf16[256,16,128]{2,1,0:T(8,128)(2,1)}, u32[]{:S(2)}) copy-start(bf16[256,16,128]{2,1,0:T(8,128)(2,1)} %param.14) | copy-start | bytes 3145732
  1.7 0.7 copy-start
  2.4 5.6 %copy-start.1 = (bf16[256,64]{0,1:T(8,128)(2,1)S(1)}, bf16[256,64]{0,1:T(8,128)(2,1)}, u32[]{:S(2)}) copy-start(bf16[256,64]{0,1:T(8,128)(2,1)} %param.17) | copy-start | bytes 98308
  2.4 5.6 %copy-start.3 = (s32[1,16]{1,0:T(1,128)S(1)}, s32[1,16]{1,0:T(1,128)}, u32[]{:S(2)}) copy-start(s32[1,16]{1,0:T(1,128)} %table.1) | copy-start | bytes 196
  4.1 11.0 %collective-permute-start.6 = (bf16[256,640]{1,0:T(8,128)(2,1)S(1)}, bf16[256,640]{1,0:T(8,128)(2,1)S(1)}, u32[]{:S(2)}, u32[]{:S(2)}) collective-permute-start(bf16[256,640]{1,0:T(8,128)(2,1)S(1)} %get-tuple-element.31), channel_id=1, source_target_pairs={{0,8},{4,12},{8,0},{12,4},{1,9},{5,13},{9,1},{13,5},{2,10},{6,14},... | collective-permute-start | bytes 983048 | tf_op jit(solution)/shard_map/ppermute | solution.py:573
  14.9 6.4 %collective-permute-start = (bf16[48,2048]{1,0:T(8,128)(2,1)S(1)}, bf16[48,2048]{1,0:T(8,128)(2,1)S(1)}, u32[]{:S(2)}, u32[]{:S(2)}) collective-permute-start(bf16[48,2048]{1,0:T(8,128)(2,1)S(1)} %get-tuple-element.23.rest_0_.refs_2_), channel_id=1, source_target_pairs={{0,8},{4,12},{8,0},{12,4},{1,9},{5,13},{9,1},{13,5},{2,10},{6,14},... | collective-permute-start | bytes 589832 | tf_op jit(solution)/shard_map/ppermute | solution.py:377
  15.0 7.7 %collective-permute-start.1 = (bf16[48,2048]{1,0:T(8,128)(2,1)S(1)}, bf16[48,2048]{1,0:T(8,128)(2,1)S(1)}, u32[]{:S(2)}, u32[]{:S(2)}) collective-permute-start(bf16[48,2048]{1,0:T(8,128)(2,1)S(1)} %get-tuple-element.23.rest_0_.refs_2_), channel_id=1, source_target_pairs={{0,4},{4,0},{8,12},{12,8},{1,5},{5,1},{9,13},{13,9},{2,6},{6,2},{1... | collective-permute-start | bytes 589832 | tf_op jit(solution)/shard_map/ppermute | solution.py:404
  15.1 13.2 %collective-permute-start.7 = (bf16[256,640]{1,0:T(8,128)(2,1)S(1)}, bf16[256,640]{1,0:T(8,128)(2,1)S(1)}, u32[]{:S(2)}, u32[]{:S(2)}) collective-permute-start(bf16[256,640]{1,0:T(8,128)(2,1)S(1)} %stack.7), channel_id=1, source_target_pairs={{0,4},{4,0},{8,12},{12,8},{1,5},{5,1},{9,13},{13,9},{2,6},{6,2},{1... | collective-permute-start | bytes 983048 | tf_op jit(solution)/shard_map/ppermute | solution.py:404
  15.7 7.2 %slice-start = ((s8[7340032]{0:T(1024)(128)(4,1)}), s8[4194304]{0:T(1024)(128)(4,1)S(1)}, s32[]{:S(2)}) async-start(s8[7340032]{0:T(1024)(128)(4,1)} %bitcast.9), calls=%async_computation | async-start | bytes 8388608
  15.7 7.2 %slice-start.1 = ((s8[7340032]{0:T(1024)(128)(4,1)}), s8[3145728]{0:T(1024)(128)(4,1)S(1)}, s32[]{:S(2)}) async-start(s8[7340032]{0:T(1024)(128)(4,1)} %bitcast.9), calls=%async_computation.1 | async-start | bytes 6291456
  21.4 1.5 %collective-permute-start.2 = (bf16[48,2048]{1,0:T(8,128)(2,1)S(1)}, bf16[48,2048]{1,0:T(8,128)(2,1)S(1)}, u32[]{:S(2)}, u32[]{:S(2)}) collective-permute-start(bf16[48,2048]{1,0:T(8,128)(2,1)S(1)} %stack.6), channel_id=1, source_target_pairs={{0,4},{4,0},{8,12},{12,8},{1,5},{5,1},{9,13},{13,9},{2,6},{6,2},{1... | collective-permute-start | bytes 589832 | tf_op jit(solution)/shard_map/ppermute | solution.py:404
  21.4 12.8 %collective-permute-start.4 = (bf16[64,2048]{1,0:T(8,128)(2,1)S(1)}, bf16[64,2048]{1,0:T(8,128)(2,1)S(1)}, u32[]{:S(2)}, u32[]{:S(2)}) collective-permute-start(bf16[64,2048]{1,0:T(8,128)(2,1)S(1)} %attend.3.refs_1_.rest_4_.rest_0_), channel_id=1, source_target_pairs={{0,8},{4,12},{8,0},{12,4},{1,9},{5,13},{9,1},{13,5},{2,10},{6,14},... | collective-permute-start | bytes 786440 | tf_op jit(solution)/shard_map/ppermute | solution.py:377
  22.5 13.1 %collective-permute-start.5 = (bf16[64,2048]{1,0:T(8,128)(2,1)S(1)}, bf16[64,2048]{1,0:T(8,128)(2,1)S(1)}, u32[]{:S(2)}, u32[]{:S(2)}) collective-permute-start(bf16[64,2048]{1,0:T(8,128)(2,1)S(1)} %attend.3.refs_1_.rest_4_.rest_0_), channel_id=1, source_target_pairs={{0,4},{4,0},{8,12},{12,8},{1,5},{5,1},{9,13},{13,9},{2,6},{6,2},{1... | collective-permute-start | bytes 786440 | tf_op jit(solution)/shard_map/ppermute | solution.py:404
  24.6 15.1 %collective-permute-start.3 = (bf16[144,1792]{1,0:T(8,128)(2,1)S(1)}, bf16[144,1792]{1,0:T(8,128)(2,1)S(1)}, u32[]{:S(2)}, u32[]{:S(2)}) collective-permute-start(bf16[144,1792]{1,0:T(8,128)(2,1)S(1)} %get-tuple-element.29.refs_0_), channel_id=1, source_target_pairs={{0,1},{3,2},{4,5},{7,6},{8,9},{11,10},{12,13},{15,14},{16,17},{19,... | collective-permute-start | bytes 1548296 | tf_op jit(solution)/shard_map/ppermute | solution.py:558
  34.2 5.6 %copy-start.2 = (s32[16,4]{0,1:T(4,128)S(1)}, s32[16,4]{0,1:T(4,128)}, u32[]{:S(2)}) copy-start(s32[16,4]{0,1:T(4,128)} %param.26) | copy-start | bytes 772
  34.2 5.6 %copy-start.4 = (s32[16]{0:T(128)S(1)}, s32[16]{0:T(128)}, u32[]{:S(2)}) copy-start(s32[16]{0:T(128)} %decode_length.1) | copy-start | bytes 196
  34.3 1.6 %collective-permute-start.8 = (bf16[64,2048]{1,0:T(8,128)(2,1)S(1)}, bf16[64,2048]{1,0:T(8,128)(2,1)S(1)}, u32[]{:S(2)}, u32[]{:S(2)}) collective-permute-start(bf16[64,2048]{1,0:T(8,128)(2,1)S(1)} %stack.8), channel_id=1, source_target_pairs={{0,4},{4,0},{8,12},{12,8},{1,5},{5,1},{9,13},{13,9},{2,6},{6,2},{1... | collective-permute-start | bytes 786440 | tf_op jit(solution)/shard_map/ppermute | solution.py:404
  34.3 14.9 %collective-permute-start.9 = (bf16[80,2048]{1,0:T(8,128)(2,1)S(1)}, bf16[80,2048]{1,0:T(8,128)(2,1)S(1)}, u32[]{:S(2)}, u32[]{:S(2)}) collective-permute-start(bf16[80,2048]{1,0:T(8,128)(2,1)S(1)} %attend.4.refs_1_.rest_4_.rest_0_), channel_id=1, source_target_pairs={{0,8},{4,12},{8,0},{12,4},{1,9},{5,13},{9,1},{13,5},{2,10},{6,14},... | collective-permute-start | bytes 983048 | tf_op jit(solution)/shard_map/ppermute | solution.py:377
  35.4 15.1 %collective-permute-start.10 = (bf16[80,2048]{1,0:T(8,128)(2,1)S(1)}, bf16[80,2048]{1,0:T(8,128)(2,1)S(1)}, u32[]{:S(2)}, u32[]{:S(2)}) collective-permute-start(bf16[80,2048]{1,0:T(8,128)(2,1)S(1)} %attend.4.refs_1_.rest_4_.rest_0_), channel_id=1, source_target_pairs={{0,4},{4,0},{8,12},{12,8},{1,5},{5,1},{9,13},{13,9},{2,6},{6,2},{1... | collective-permute-start | bytes 983048 | tf_op jit(solution)/shard_map/ppermute | solution.py:404
  38.1 21.3 %collective-permute-start.13 = (bf16[192,1792]{1,0:T(8,128)(2,1)S(1)}, bf16[192,1792]{1,0:T(8,128)(2,1)S(1)}, u32[]{:S(2)}, u32[]{:S(2)}) collective-permute-start(bf16[192,1792]{1,0:T(8,128)(2,1)S(1)} %get-tuple-element.35.refs_0_.refs_2_), channel_id=1, source_target_pairs={{0,1},{3,2},{4,5},{7,6},{8,9},{11,10},{12,13},{15,14},{16,17},{19,... | collective-permute-start | bytes 2064392 | tf_op jit(solution)/shard_map/ppermute | solution.py:558
  49.3 1.7 %collective-permute-start.11 = (bf16[80,2048]{1,0:T(8,128)(2,1)S(1)}, bf16[80,2048]{1,0:T(8,128)(2,1)S(1)}, u32[]{:S(2)}, u32[]{:S(2)}) collective-permute-start(bf16[80,2048]{1,0:T(8,128)(2,1)S(1)} %stack.9), channel_id=1, source_target_pairs={{0,4},{4,0},{8,12},{12,8},{1,5},{5,1},{9,13},{13,9},{2,6},{6,2},{1... | collective-permute-start | bytes 983048 | tf_op jit(solution)/shard_map/ppermute | solution.py:404
  49.5 9.3 %collective-permute-start.16 = (bf16[64,2048]{1,0:T(8,128)(2,1)S(1)}, bf16[64,2048]{1,0:T(8,128)(2,1)S(1)}, u32[]{:S(2)}, u32[]{:S(2)}) collective-permute-start(bf16[64,2048]{1,0:T(8,128)(2,1)S(1)} %attend.5.refs_1_.rest_4_.rest_0_), channel_id=1, source_target_pairs={{0,8},{4,12},{8,0},{12,4},{1,9},{5,13},{9,1},{13,5},{2,10},{6,14},... | collective-permute-start | bytes 786440 | tf_op jit(solution)/shard_map/ppermute | solution.py:377
  53.8 17.5 %collective-permute-start.15 = (bf16[160,1792]{1,0:T(8,128)(2,1)S(1)}, bf16[160,1792]{1,0:T(8,128)(2,1)S(1)}, u32[]{:S(2)}, u32[]{:S(2)}) collective-permute-start(bf16[160,1792]{1,0:T(8,128)(2,1)S(1)} %get-tuple-element.36.refs_0_), channel_id=1, source_target_pairs={{0,1},{3,2},{4,5},{7,6},{8,9},{11,10},{12,13},{15,14},{16,17},{19,... | collective-permute-start | bytes 1720328 | tf_op jit(solution)/shard_map/ppermute | solution.py:558
  58.1 10.3 %collective-permute-start.12 = (bf16[96,1792]{1,0:T(8,128)(2,1)S(1)}, bf16[96,1792]{1,0:T(8,128)(2,1)S(1)}, u32[]{:S(2)}, u32[]{:S(2)}) collective-permute-start(bf16[96,1792]{1,0:T(8,128)(2,1)S(1)} %stack.10), channel_id=1, source_target_pairs={{1,2},{2,1},{5,6},{6,5},{9,10},{10,9},{13,14},{14,13},{17,18},{18,... | collective-permute-start | bytes 1032200 | tf_op jit(solution)/shard_map/ppermute | solution.py:561
  58.8 1.6 %collective-permute-start.17 = (bf16[64,2048]{1,0:T(8,128)(2,1)S(1)}, bf16[64,2048]{1,0:T(8,128)(2,1)S(1)}, u32[]{:S(2)}, u32[]{:S(2)}) collective-permute-start(bf16[64,2048]{1,0:T(8,128)(2,1)S(1)} %attend.5.refs_1_.rest_4_.rest_0_), channel_id=1, source_target_pairs={{0,4},{4,0},{8,12},{12,8},{1,5},{5,1},{9,13},{13,9},{2,6},{6,2},{1... | collective-permute-start | bytes 786440 | tf_op jit(solution)/shard_map/ppermute | solution.py:404
  58.9 1.9 %collective-permute-start.18 = (bf16[64,2048]{1,0:T(8,128)(2,1)S(1)}, bf16[64,2048]{1,0:T(8,128)(2,1)S(1)}, u32[]{:S(2)}, u32[]{:S(2)}) collective-permute-start(bf16[64,2048]{1,0:T(8,128)(2,1)S(1)} %stack.11), channel_id=1, source_target_pairs={{0,4},{4,0},{8,12},{12,8},{1,5},{5,1},{9,13},{13,9},{2,6},{6,2},{1... | collective-permute-start | bytes 786440 | tf_op jit(solution)/shard_map/ppermute | solution.py:404
  59.5 12.6 %collective-permute-start.14 = (bf16[128,1792]{1,0:T(8,128)(2,1)S(1)}, bf16[128,1792]{1,0:T(8,128)(2,1)S(1)}, u32[]{:S(2)}, u32[]{:S(2)}) collective-permute-start(bf16[128,1792]{1,0:T(8,128)(2,1)S(1)} %add.13.rest_5_), channel_id=1, source_target_pairs={{1,2},{2,1},{5,6},{6,5},{9,10},{10,9},{13,14},{14,13},{17,18},{18,... | collective-permute-start | bytes 1376264 | tf_op jit(solution)/shard_map/ppermute | solution.py:561
  63.0 20.4 %collective-permute-start.20 = (bf16[128,1792]{1,0:T(8,128)(2,1)S(1)}, bf16[128,1792]{1,0:T(8,128)(2,1)S(1)}, u32[]{:S(2)}, u32[]{:S(2)}) collective-permute-start(bf16[128,1792]{1,0:T(8,128)(2,1)S(1)} %get-tuple-element.39.refs_0_), channel_id=1, source_target_pairs={{0,1},{3,2},{4,5},{7,6},{8,9},{11,10},{12,13},{15,14},{16,17},{19,... | collective-permute-start | bytes 1376264 | tf_op jit(solution)/shard_map/ppermute | solution.py:558
  71.5 18.1 %collective-permute-start.22 = (bf16[160,1792]{1,0:T(8,128)(2,1)S(1)}, bf16[160,1792]{1,0:T(8,128)(2,1)S(1)}, u32[]{:S(2)}, u32[]{:S(2)}) collective-permute-start(bf16[160,1792]{1,0:T(8,128)(2,1)S(1)} %add.14.refs_4_), channel_id=1, source_target_pairs={{1,2},{2,1},{5,6},{6,5},{9,10},{10,9},{13,14},{14,13},{17,18},{18,... | collective-permute-start | bytes 1720328 | tf_op jit(solution)/shard_map/ppermute | solution.py:561
  72.3 17.1 %collective-permute-start.19 = (bf16[112,1792]{1,0:T(8,128)(2,1)S(1)}, bf16[112,1792]{1,0:T(8,128)(2,1)S(1)}, u32[]{:S(2)}, u32[]{:S(2)}) collective-permute-start(bf16[112,1792]{1,0:T(8,128)(2,1)S(1)} %add.15.refs_2_), channel_id=1, source_target_pairs={{1,0},{2,3},{5,4},{6,7},{9,8},{10,11},{13,12},{14,15},{17,16},{18,... | collective-permute-start | bytes 1204232 | tf_op jit(solution)/shard_map/ppermute | solution.py:564
  73.6 19.4 %collective-permute-start.21 = (bf16[144,1792]{1,0:T(8,128)(2,1)S(1)}, bf16[144,1792]{1,0:T(8,128)(2,1)S(1)}, u32[]{:S(2)}, u32[]{:S(2)}) collective-permute-start(bf16[144,1792]{1,0:T(8,128)(2,1)S(1)} %get-tuple-element.40.refs_0_), channel_id=1, source_target_pairs={{0,1},{3,2},{4,5},{7,6},{8,9},{11,10},{12,13},{15,14},{16,17},{19,... | collective-permute-start | bytes 1548296 | tf_op jit(solution)/shard_map/ppermute | solution.py:558
  83.5 8.2 %collective-permute-start.24 = (bf16[64,1792]{1,0:T(8,128)(2,1)S(1)}, bf16[64,1792]{1,0:T(8,128)(2,1)S(1)}, u32[]{:S(2)}, u32[]{:S(2)}) collective-permute-start(bf16[64,1792]{1,0:T(8,128)(2,1)S(1)} %add.16.refs_2_), channel_id=1, source_target_pairs={{1,2},{2,1},{5,6},{6,5},{9,10},{10,9},{13,14},{14,13},{17,18},{18,... | collective-permute-start | bytes 688136 | tf_op jit(solution)/shard_map/ppermute | solution.py:561
  89.7 10.7 %collective-permute-start.23 = (bf16[80,1792]{1,0:T(8,128)(2,1)S(1)}, bf16[80,1792]{1,0:T(8,128)(2,1)S(1)}, u32[]{:S(2)}, u32[]{:S(2)}) collective-permute-start(bf16[80,1792]{1,0:T(8,128)(2,1)S(1)} %add.19.refs_2_), channel_id=1, source_target_pairs={{1,0},{2,3},{5,4},{6,7},{9,8},{10,11},{13,12},{14,15},{17,16},{18,... | collective-permute-start | bytes 860168 | tf_op jit(solution)/shard_map/ppermute | solution.py:564
  91.0 9.5 %collective-permute-start.25 = (bf16[64,1792]{1,0:T(8,128)(2,1)S(1)}, bf16[64,1792]{1,0:T(8,128)(2,1)S(1)}, u32[]{:S(2)}, u32[]{:S(2)}) collective-permute-start(bf16[64,1792]{1,0:T(8,128)(2,1)S(1)} %add.17.refs_8_), channel_id=1, source_target_pairs={{1,2},{2,1},{5,6},{6,5},{9,10},{10,9},{13,14},{14,13},{17,18},{18,... | collective-permute-start | bytes 688136 | tf_op jit(solution)/shard_map/ppermute | solution.py:561
  91.7 12.3 %collective-permute-start.26 = (bf16[64,1792]{1,0:T(8,128)(2,1)S(1)}, bf16[64,1792]{1,0:T(8,128)(2,1)S(1)}, u32[]{:S(2)}, u32[]{:S(2)}) collective-permute-start(bf16[64,1792]{1,0:T(8,128)(2,1)S(1)} %add.20.refs_4_), channel_id=1, source_target_pairs={{1,0},{2,3},{5,4},{6,7},{9,8},{10,11},{13,12},{14,15},{17,16},{18,... | collective-permute-start | bytes 688136 | tf_op jit(solution)/shard_map/ppermute | solution.py:564

commit v10 on v7

--- a/solution.py
+++ b/solution.py
@@ -33,7 +33,7 @@
 
 def chunk_sizes(tok_group):
     if tok_group == 256:
-        return (48, 64, 80, 64)
+        return (64, 80, 64, 48)
     return (tok_group,)
 
 
@@ -132,7 +132,7 @@
     copies.append(pltpu.make_async_copy(
         new_latent, keys.at[pl.ds(prior, tok_group), pl.ds(0, latent)], sems.at[blocks]))
     for c in copies:
-        c.start()
+        c.start(priority=1)
 
     keys[prior:, latent:] = rope_rows(new_rope_t[...])
     lane = lax.broadcasted_iota(jnp.int32, (block_len, LANES), 1)
@@ -583,16 +583,15 @@
     to_across0 = add(2 * t0, [(rest0, 0), (in0, 0)], (own1,))
     on0 = across(to_across0)
     x3 = attend(3, held, (to_across0,), brought)
-    own2, rest2, near2 = project(where, gather(x2, (x3,)), w, (2, 1), (), (x3,))
+    own2, rest2 = project(where, gather(x2, (x3,)), w, (3,), (), (x3,))
     in2 = inward(rest2)
     to_across1 = add(2 * t1, [(rest1, 0), (in1, 0)], (own2, on0))
     on1 = across(to_across1)
-    own3, rest3, near = project(
-        where, gather(x3, (own2,)), w, (2, 1), (near2,), (to_across1,))
+    own3, rest3 = project(
+        where, gather(x3, (own2,)), w, (3,), (), (to_across1,))
     in3 = inward(rest3)
     to_across2 = add(2 * t2, [(rest2, 0), (in2, 0)], (own3,))
     on2 = across(to_across2)
-    near_in = inward(near)
     to_out01 = add_all([(t0, [(rest0, 2 * t0), (on0, 0)]), (t1, [(rest1, 2 * t1), (on1, 0)])],
                        (to_across2,))
     out01 = outward(to_out01)
@@ -602,12 +601,12 @@
     mid_on = across(to_mid)
     done01 = add_all([(t0, [(own0, 0), (in0, 2 * t0), (on0, t0), (out01, 0)]),
                       (t1, [(own1, 0), (in1, 2 * t1), (on1, t1), (out01, t0)])], (to_mid,))
-    to_out2 = add(t2, [(near2, 0), (on2, 0)], (done01,))
+    to_out2 = add(t2, [(rest2, 2 * t2), (on2, 0)], (done01,))
     out2 = outward(to_out2)
-    to_out3 = add(t3, [(near, t2), (far_on, 0)], (to_out2,))
+    to_out3 = add(t3, [(rest3, 2 * t3), (far_on, 0)], (to_out2,))
     out3 = outward(to_out3)
-    done2 = add(t2, [(own2, 0), (near_in, 0), (on2, t2), (out2, 0)], (to_out3,))
-    return finish([done01, done2], [(own3, 0), (near_in, t2), (mid_on, 0), (out3, 0)])
+    done2 = add(t2, [(own2, 0), (in2, 2 * t2), (on2, t2), (out2, 0)], (to_out3,))
+    return finish([done01, done2], [(own3, 0), (in3, 2 * t3), (mid_on, 0), (out3, 0)])
 
 
 def solution(mesh):

time: 106 us -> 112 us (1.057)
  waiting for transfers between devices: 21.4 us -> 37.1 us
  starting transfers between devices: 40.4 us -> 30.1 us
    ppermute x5 -> x4, starting transfers between devices: 24.8 us -> 15.8 us  [inward(): return lax.ppermute(x, 'tp', INWARD)]
    ppermute x5 -> x4, waiting for transfers between devices: 5.42 us -> 14.1 us  [inward(): return lax.ppermute(x, 'tp', INWARD)]
    ppermute x4, waiting for transfers between devices: 0.94 us -> 7.16 us  [shift_groups(): lax.ppermute(x, 'dp', [(i, (i + s) % groups) for i in range(groups)])]
    ppermute x9, waiting for transfers between devices: 0.9 us -> 4.11 us  [swap_cores(): lax.ppermute(x, 'dp', [(i, i ^ 1) for i in range(lax.axis_size('dp'))])]
    ppermute x3, waiting for transfers between devices: 14.1 us -> 11.8 us  [outward(): return lax.ppermute(x, 'tp', OUTWARD)]
    pallas_call x3, Pallas kernels: 20.1 us -> 18.8 us  [attend(): pl.pallas_call(kernel, out_shape=jax.ShapeDtypeStruct((t, heads * dv), bf...]
  transfers between devices with their start and end apart: 27 -> 26, of which waited for: 11 -> 12; matrix products, arithmetic and copies ran while one was open for 0% -> 0% of each run, Pallas kernels for 35% -> 34%
where the time goes in v10:
time: 112 us; the launch traced here: 111 us
  Pallas kernels  40.1 us (36%)
  waiting for transfers between devices  37.1 us (33%)
  starting transfers between devices  30.1 us (27%)
  local copies, waits for them, and re-layouts  2.68 us (2%)
    pallas_call x3, Pallas kernels, attend(): pl.pallas_call(kernel, out_shape=jax.ShapeDtypeStruct((t, heads * dv), bf...  18.8 us
    ppermute x4, starting transfers between devices, inward(): return lax.ppermute(x, 'tp', INWARD)  15.8 us
    ppermute x4, waiting for transfers between devices, inward(): return lax.ppermute(x, 'tp', INWARD)  14.1 us
    ppermute x3, waiting for transfers between devices, outward(): return lax.ppermute(x, 'tp', OUTWARD)  11.8 us
    pallas_call x4, Pallas kernels, project(): pl.pallas_call(functools.partial(project_kernel, len(parts), tails, place...  9.26 us
    pallas_call x1, Pallas kernels, first_chunk(): pl.pallas_call(functools.partial(first_kernel, fresh_of(0), exp_scale), o...  8.16 us
    ppermute x4, waiting for transfers between devices, shift_groups(): lax.ppermute(x, 'dp', [(i, (i + s) % groups) for i in range(groups)])  7.16 us
    ppermute x9, waiting for transfers between devices, swap_cores(): lax.ppermute(x, 'dp', [(i, i ^ 1) for i in range(lax.axis_size('dp'))])  4.11 us
  transfers between devices with their start and end apart: 26, of which 12 were waited for; matrix products, arithmetic and copies ran while one was open for 0% of the time, Pallas kernels for 34%

profile of v10, /device:TPU:0, one launch (start us, length us, event | category | flops | bytes accessed | tf_op | source)
XLA Modules:
  0.0 111.1 jit_solution(11166063644029516846)
XLA Ops:
  0.0 1.6 %reshape.6 = bf16[32,64,64]{2,1,0:T(8,128)(2,1)S(1)} reshape(bf16[32,4096]{1,0:T(8,128)(2,1)} %param.19) | data formatting | bytes 524288 | tf_op jit(solution)/shard_map/reshape | solution.py:457
  1.6 0.1 pad.4.cache_rope
  1.7 0.0 copy-start
  1.7 0.7 copy-done
  2.4 1.7 %pack.1 = (bf16[128,640]{1,0:T(8,128)(2,1)S(1)}, bf16[128,640]{1,0:T(8,128)(2,1)S(1)}, bf16[256,640]{1,0:T(8,128)(2,1)S(1)}) custom-call(s32[1]{0:T(128)} %bitcast.me, s32[1,2,4]{2,1,0:T(2,128)S(1)} %bitcast.15, bf16[32,64,512]{2,1,0:T(8,128)(2,1)} %cache_latent.3, bf16[32,64,128]{2,1,0:T(8,128)(2,1)S(1)} %pad.4.cache_rope), custom_call_target="tpu_custom_call" | custom-call | flops 1000 | bytes 1000 | tf_op jit(solution)/shard_map/pack/pallas_call | solution.py:524
  4.1 3.0 %collective-permute-start.6 = (bf16[256,640]{1,0:T(8,128)(2,1)S(1)}, bf16[256,640]{1,0:T(8,128)(2,1)S(1)}, u32[]{:S(2)}, u32[]{:S(2)}) collective-permute-start(bf16[256,640]{1,0:T(8,128)(2,1)S(1)} %get-tuple-element.29), channel_id=1, source_target_pairs={{0,8},{4,12},{8,0},{12,4},{1,9},{5,13},{9,1},{13,5},{2,10},{6,14},... | collective-permute-start | bytes 983048 | tf_op jit(solution)/shard_map/ppermute | solution.py:573
  7.1 0.3 copy.17
  8.0 8.2 %attend_first.1 = (bf16[64,2048]{1,0:T(8,128)(2,1)S(1)}, bf16[1280,640]{1,0:T(8,128)(2,1)S(1)}, bf16[16,128,512]{2,1,0:T(8,128)(2,1)S(1)}, bf16[16,512,128]{2,1,0:T(8,128)(2,1)S(1)}, bf16[256,1024]{1,0:T(8,128)(2,1)S(1)}) custom-call(s32[1]{0:T(128)} %bitcast.me, s32[1]{0:T(128)} %bitcast.1.z, s32[1,16]{1,0:T(1,128)S(1)} %copy-done.3, s32[1]{0:T(128)S(6)} %copy.18.offset, ...), custom_call_target="tpu_custom_call" | custom-call | flops 40000000000 | bytes 1000 | tf_op jit(solution)/shard_map/attend_first/pallas_call | solution.py:471
  16.2 0.1 collective-permute-start
  16.3 0.1 collective-permute-start.1
  16.4 0.0 collective-permute-done.6.refs_1_.rest_1_
  16.4 0.5 collective-permute-start.7
  17.0 5.8 %attend.3.refs_1_.rest_4_.rest_0_ = bf16[80,2048]{1,0:T(8,128)(2,1)S(1)} custom-call(bf16[16,256,128]{2,1,0:T(8,128)(2,1)S(1)} %bitcast.12, bf16[256,1024]{1,0:T(8,128)(2,1)S(1)} %get-tuple-element.22.q_rope, bf16[16,128,512]{2,1,0:T(8,128)(2,1)S(1)} %get-tuple-element.23.wk, bf16[16,512,128]{2,1,0:T(8,128)(2,1)S(1)} %get-tuple-element.24.wv, ...), custom_call_target="tpu_custom_call" | custom-call | flops 40000000000 | bytes 1000 | tf_op jit(solution)/shard_map/attend/pallas_call | solution.py:512
  22.8 1.2 %collective-permute-done.refs_0_.rest_1_ = bf16[64,2048]{1,0:T(8,128)(2,1)S(1)} collective-permute-done((bf16[64,2048]{1,0:T(8,128)(2,1)S(1)}, bf16[64,2048]{1,0:T(8,128)(2,1)S(1)}, u32[]{:S(2)}, u32[]{:S(2)}) %collective-permute-start) | collective-permute-done | bytes 262176 | tf_op jit(solution)/shard_map/ppermute | solution.py:377
  24.1 0.1 collective-permute-start.2
  24.1 0.8 collective-permute-start.4
  24.9 0.2 collective-permute-start.5
  25.1 0.0 collective-permute-done.1.rest_2_
  25.1 0.6 collective-permute-done.2.rest_3_
  25.7 2.5 %project.4 = (bf16[64,1792]{1,0:T(8,128)(2,1)S(1)}, bf16[192,1792]{1,0:T(8,128)(2,1)S(1)}) custom-call(s32[1]{0:T(128)} %bitcast.me, s32[1]{0:T(128)} %bitcast.1.z, bf16[2048,1792]{1,0:T(8,128)(2,1)S(1)} %bitcast.10, bf16[64,2048]{1,0:T(8,128)(2,1)S(1)} %get-tuple-element.21.rest_0_.refs_2_, bf16[64,2048]{1,0:T(8,128)(2,1)S(1)} %collective-permute-done.refs_0_.rest_1_, ...), custom_call_target="tpu_custom_call" | custom-call | flops 1000 | bytes 1000 | tf_op jit(solution)/shard_map/project/pallas_call | solution.py:304
  28.1 3.5 %collective-permute-start.3 = (bf16[192,1792]{1,0:T(8,128)(2,1)S(1)}, bf16[192,1792]{1,0:T(8,128)(2,1)S(1)}, u32[]{:S(2)}, u32[]{:S(2)}) collective-permute-start(bf16[192,1792]{1,0:T(8,128)(2,1)S(1)} %get-tuple-element.27.refs_0_), channel_id=1, source_target_pairs={{0,1},{3,2},{4,5},{7,6},{8,9},{11,10},{12,13},{15,14},{16,17},{19,... | collective-permute-start | bytes 2064392 | tf_op jit(solution)/shard_map/ppermute | solution.py:558
  31.7 4.9 %attend.4.refs_1_.rest_4_.rest_0_ = bf16[64,2048]{1,0:T(8,128)(2,1)S(1)} custom-call(bf16[16,256,128]{2,1,0:T(8,128)(2,1)S(1)} %bitcast.13, bf16[256,1024]{1,0:T(8,128)(2,1)S(1)} %get-tuple-element.22.q_rope, bf16[16,128,512]{2,1,0:T(8,128)(2,1)S(1)} %get-tuple-element.23.wk, bf16[16,512,128]{2,1,0:T(8,128)(2,1)S(1)} %get-tuple-element.24.wv, ...), custom_call_target="tpu_custom_call" | custom-call | flops 40000000000 | bytes 1000 | tf_op jit(solution)/shard_map/attend/pallas_call | solution.py:512
  36.6 0.1 collective-permute-start.8
  36.7 0.8 collective-permute-start.11
  37.5 0.2 collective-permute-start.12
  37.7 0.0 collective-permute-done.5.rest_2_
  37.7 0.6 collective-permute-done.8.rest_3_
  38.3 2.8 %project.5 = (bf16[80,1792]{1,0:T(8,128)(2,1)S(1)}, bf16[240,1792]{1,0:T(8,128)(2,1)S(1)}) custom-call(s32[1]{0:T(128)} %bitcast.me, s32[1]{0:T(128)} %bitcast.1.z, bf16[2048,1792]{1,0:T(8,128)(2,1)S(1)} %bitcast.10, bf16[80,2048]{1,0:T(8,128)(2,1)S(1)} %attend.3.refs_1_.rest_4_.rest_0_, bf16[80,2048]{1,0:T(8,128)(2,1)S(1)} %collective-permute-done.4.refs_0_.rest_1_, ...), custom_call_target="tpu_custom_call" | custom-call | flops 1000 | bytes 1000 | tf_op jit(solution)/shard_map/project/pallas_call | solution.py:304
  41.1 0.0 copy-start.2
  41.1 0.0 copy-start.4
  41.1 1.3 %collective-permute-start.10 = (bf16[240,1792]{1,0:T(8,128)(2,1)S(1)}, bf16[240,1792]{1,0:T(8,128)(2,1)S(1)}, u32[]{:S(2)}, u32[]{:S(2)}) collective-permute-start(bf16[240,1792]{1,0:T(8,128)(2,1)S(1)} %get-tuple-element.31.refs_0_.refs_2_), channel_id=1, source_target_pairs={{0,1},{3,2},{4,5},{7,6},{8,9},{11,10},{12,13},{15,14},{16,17},{19,... | collective-permute-start | bytes 2580488 | tf_op jit(solution)/shard_map/ppermute | solution.py:558
  42.5 4.9 %collective-permute-done.3.refs_1_ = bf16[192,1792]{1,0:T(8,128)(2,1)S(1)} collective-permute-done((bf16[192,1792]{1,0:T(8,128)(2,1)S(1)}, bf16[192,1792]{1,0:T(8,128)(2,1)S(1)}, u32[]{:S(2)}, u32[]{:S(2)}) %collective-permute-start.3) | collective-permute-done | bytes 688160 | tf_op jit(solution)/shard_map/ppermute | solution.py:558
  47.4 0.1 add.12.rest_3_
  47.5 0.9 collective-permute-start.9
  48.4 8.1 %attend.5.refs_1_.rest_4_.rest_0_ = bf16[48,2048]{1,0:T(8,128)(2,1)S(1)} custom-call(s32[1]{0:T(128)} %bitcast.me, bf16[16,256,128]{2,1,0:T(8,128)(2,1)S(1)} %bitcast.14, bf16[256,1024]{1,0:T(8,128)(2,1)S(1)} %get-tuple-element.22.q_rope, bf16[16,128,512]{2,1,0:T(8,128)(2,1)S(1)} %get-tuple-element.23.wk, bf16[16,512,128]{2,1,0:T(8,128)(2,1)S(1)} %get-tuple-element.24.wv, ...), custom_call_target="tpu_custom_call" | custom-call | flops 6000000000 | bytes 1000 | tf_op jit(solution)/shard_map/attend/pallas_call | solution.py:512
  56.5 0.1 collective-permute-start.13
  56.6 1.5 %collective-permute-done.13.rest_3_ = bf16[64,2048]{1,0:T(8,128)(2,1)S(1)} collective-permute-done((bf16[64,2048]{1,0:T(8,128)(2,1)S(1)}, bf16[64,2048]{1,0:T(8,128)(2,1)S(1)}, u32[]{:S(2)}, u32[]{:S(2)}) %collective-permute-start.13) | collective-permute-done | bytes 262176 | tf_op jit(solution)/shard_map/ppermute | solution.py:404
  58.2 2.3 %project.6 = (bf16[64,1792]{1,0:T(8,128)(2,1)S(1)}, bf16[192,1792]{1,0:T(8,128)(2,1)S(1)}) custom-call(s32[1]{0:T(128)} %bitcast.me, s32[1]{0:T(128)} %bitcast.1.z, bf16[2048,1792]{1,0:T(8,128)(2,1)S(1)} %bitcast.10, bf16[64,2048]{1,0:T(8,128)(2,1)S(1)} %attend.4.refs_1_.rest_4_.rest_0_, bf16[64,2048]{1,0:T(8,128)(2,1)S(1)} %collective-permute-done.11.refs_0_.rest_1_, ...), custom_call_target="tpu_custom_call" | custom-call | flops 1000 | bytes 1000 | tf_op jit(solution)/shard_map/project/pallas_call | solution.py:304
  60.4 7.2 %collective-permute-start.15 = (bf16[192,1792]{1,0:T(8,128)(2,1)S(1)}, bf16[192,1792]{1,0:T(8,128)(2,1)S(1)}, u32[]{:S(2)}, u32[]{:S(2)}) collective-permute-start(bf16[192,1792]{1,0:T(8,128)(2,1)S(1)} %get-tuple-element.34.refs_0_), channel_id=1, source_target_pairs={{0,1},{3,2},{4,5},{7,6},{8,9},{11,10},{12,13},{15,14},{16,17},{19,... | collective-permute-start | bytes 2064392 | tf_op jit(solution)/shard_map/ppermute | solution.py:558
  67.7 0.1 add.13.rest_4_
  67.8 0.7 collective-permute-start.14
  68.5 0.8 collective-permute-start.16
  69.3 5.9 %collective-permute-done.16.refs_0_.rest_1_ = bf16[48,2048]{1,0:T(8,128)(2,1)S(1)} collective-permute-done((bf16[48,2048]{1,0:T(8,128)(2,1)S(1)}, bf16[48,2048]{1,0:T(8,128)(2,1)S(1)}, u32[]{:S(2)}, u32[]{:S(2)}) %collective-permute-start.16) | collective-permute-done | bytes 196640 | tf_op jit(solution)/shard_map/ppermute | solution.py:377
  75.3 0.1 collective-permute-start.18
  75.4 1.4 %collective-permute-done.18.rest_3_ = bf16[48,2048]{1,0:T(8,128)(2,1)S(1)} collective-permute-done((bf16[48,2048]{1,0:T(8,128)(2,1)S(1)}, bf16[48,2048]{1,0:T(8,128)(2,1)S(1)}, u32[]{:S(2)}, u32[]{:S(2)}) %collective-permute-start.18) | collective-permute-done | bytes 196640 | tf_op jit(solution)/shard_map/ppermute | solution.py:404
  76.8 1.7 %project.7 = (bf16[48,1792]{1,0:T(8,128)(2,1)S(1)}, bf16[144,1792]{1,0:T(8,128)(2,1)S(1)}) custom-call(s32[1]{0:T(128)} %bitcast.me, s32[1]{0:T(128)} %bitcast.1.z, bf16[2048,1792]{1,0:T(8,128)(2,1)S(1)} %bitcast.10, bf16[48,2048]{1,0:T(8,128)(2,1)S(1)} %attend.5.refs_1_.rest_4_.rest_0_, bf16[48,2048]{1,0:T(8,128)(2,1)S(1)} %collective-permute-done.16.refs_0_.rest_1_, ...), custom_call_target="tpu_custom_call" | custom-call | flops 1000 | bytes 1000 | tf_op jit(solution)/shard_map/project/pallas_call | solution.py:304
  78.5 3.7 %collective-permute-start.20 = (bf16[144,1792]{1,0:T(8,128)(2,1)S(1)}, bf16[144,1792]{1,0:T(8,128)(2,1)S(1)}, u32[]{:S(2)}, u32[]{:S(2)}) collective-permute-start(bf16[144,1792]{1,0:T(8,128)(2,1)S(1)} %get-tuple-element.36.refs_0_), channel_id=1, source_target_pairs={{0,1},{3,2},{4,5},{7,6},{8,9},{11,10},{12,13},{15,14},{16,17},{19,... | collective-permute-start | bytes 1548296 | tf_op jit(solution)/shard_map/ppermute | solution.py:558
  82.3 0.3 collective-permute-done.15.refs_1_
  82.6 0.1 add.14.refs_4_
  82.7 0.1 add.15.refs_2_
  82.8 1.3 %collective-permute-start.19 = (bf16[144,1792]{1,0:T(8,128)(2,1)S(1)}, bf16[144,1792]{1,0:T(8,128)(2,1)S(1)}, u32[]{:S(2)}, u32[]{:S(2)}) collective-permute-start(bf16[144,1792]{1,0:T(8,128)(2,1)S(1)} %add.15.refs_2_), channel_id=1, source_target_pairs={{1,0},{2,3},{5,4},{6,7},{9,8},{10,11},{13,12},{14,15},{17,16},{18,... | collective-permute-start | bytes 1548296 | tf_op jit(solution)/shard_map/ppermute | solution.py:564
  84.1 0.7 collective-permute-start.21
  84.8 8.8 %collective-permute-done.20.refs_1_.refs_3_ = bf16[144,1792]{1,0:T(8,128)(2,1)S(1)} collective-permute-done((bf16[144,1792]{1,0:T(8,128)(2,1)S(1)}, bf16[144,1792]{1,0:T(8,128)(2,1)S(1)}, u32[]{:S(2)}, u32[]{:S(2)}) %collective-permute-start.20) | collective-permute-done | bytes 516128 | tf_op jit(solution)/shard_map/ppermute | solution.py:558
  93.7 0.7 collective-permute-start.23
  94.4 3.5 %collective-permute-done.19.refs_3_.refs_7_ = bf16[144,1792]{1,0:T(8,128)(2,1)S(1)} collective-permute-done((bf16[144,1792]{1,0:T(8,128)(2,1)S(1)}, bf16[144,1792]{1,0:T(8,128)(2,1)S(1)}, u32[]{:S(2)}, u32[]{:S(2)}) %collective-permute-start.19) | collective-permute-done | bytes 516128 | tf_op jit(solution)/shard_map/ppermute | solution.py:564
  97.9 0.3 add.18.refs_2_.refs_0_
  98.2 0.1 add.19.refs_2_
  98.3 1.3 %collective-permute-start.22 = (bf16[64,1792]{1,0:T(8,128)(2,1)S(1)}, bf16[64,1792]{1,0:T(8,128)(2,1)S(1)}, u32[]{:S(2)}, u32[]{:S(2)}) collective-permute-start(bf16[64,1792]{1,0:T(8,128)(2,1)S(1)} %add.19.refs_2_), channel_id=1, source_target_pairs={{1,0},{2,3},{5,4},{6,7},{9,8},{10,11},{13,12},{14,15},{17,16},{18,... | collective-permute-start | bytes 688136 | tf_op jit(solution)/shard_map/ppermute | solution.py:564
  99.6 0.7 collective-permute-start.24
  100.3 1.3 %collective-permute-start.25 = (bf16[48,1792]{1,0:T(8,128)(2,1)S(1)}, bf16[48,1792]{1,0:T(8,128)(2,1)S(1)}, u32[]{:S(2)}, u32[]{:S(2)}) collective-permute-start(bf16[48,1792]{1,0:T(8,128)(2,1)S(1)} %add.20.refs_4_), channel_id=1, source_target_pairs={{1,0},{2,3},{5,4},{6,7},{9,8},{10,11},{13,12},{14,15},{17,16},{18,... | collective-permute-start | bytes 516104 | tf_op jit(solution)/shard_map/ppermute | solution.py:564
  101.6 5.4 %collective-permute-done.22.refs_3_ = bf16[64,1792]{1,0:T(8,128)(2,1)S(1)} collective-permute-done((bf16[64,1792]{1,0:T(8,128)(2,1)S(1)}, bf16[64,1792]{1,0:T(8,128)(2,1)S(1)}, u32[]{:S(2)}, u32[]{:S(2)}) %collective-permute-start.22) | collective-permute-done | bytes 229408 | tf_op jit(solution)/shard_map/ppermute | solution.py:564
  107.0 0.1 add.21.refs_1_
  107.1 2.9 %collective-permute-done.25.refs_5_ = bf16[48,1792]{1,0:T(8,128)(2,1)S(1)} collective-permute-done((bf16[48,1792]{1,0:T(8,128)(2,1)S(1)}, bf16[48,1792]{1,0:T(8,128)(2,1)S(1)}, u32[]{:S(2)}, u32[]{:S(2)}) %collective-permute-start.25) | collective-permute-done | bytes 172064 | tf_op jit(solution)/shard_map/ppermute | solution.py:564
  110.0 1.1 finish.1
  (33 shorter events, 0.3 us)
Async XLA Ops:
  0.0 7.1 %copy-start.5 = (bf16[256,16,128]{2,1,0:T(8,128)(2,1)S(1)}, bf16[256,16,128]{2,1,0:T(8,128)(2,1)}, u32[]{:S(2)}) copy-start(bf16[256,16,128]{2,1,0:T(8,128)(2,1)} %param.14) | copy-start | bytes 3145732
  1.7 0.7 copy-start
  2.4 5.6 %copy-start.1 = (bf16[256,64]{0,1:T(8,128)(2,1)S(1)}, bf16[256,64]{0,1:T(8,128)(2,1)}, u32[]{:S(2)}) copy-start(bf16[256,64]{0,1:T(8,128)(2,1)} %param.17) | copy-start | bytes 98308
  2.4 5.6 %copy-start.3 = (s32[1,16]{1,0:T(1,128)S(1)}, s32[1,16]{1,0:T(1,128)}, u32[]{:S(2)}) copy-start(s32[1,16]{1,0:T(1,128)} %table.1) | copy-start | bytes 196
  4.1 12.3 %collective-permute-start.6 = (bf16[256,640]{1,0:T(8,128)(2,1)S(1)}, bf16[256,640]{1,0:T(8,128)(2,1)S(1)}, u32[]{:S(2)}, u32[]{:S(2)}) collective-permute-start(bf16[256,640]{1,0:T(8,128)(2,1)S(1)} %get-tuple-element.29), channel_id=1, source_target_pairs={{0,8},{4,12},{8,0},{12,4},{1,9},{5,13},{9,1},{13,5},{2,10},{6,14},... | collective-permute-start | bytes 983048 | tf_op jit(solution)/shard_map/ppermute | solution.py:573
  16.2 7.8 %collective-permute-start = (bf16[64,2048]{1,0:T(8,128)(2,1)S(1)}, bf16[64,2048]{1,0:T(8,128)(2,1)S(1)}, u32[]{:S(2)}, u32[]{:S(2)}) collective-permute-start(bf16[64,2048]{1,0:T(8,128)(2,1)S(1)} %get-tuple-element.21.rest_0_.refs_2_), channel_id=1, source_target_pairs={{0,8},{4,12},{8,0},{12,4},{1,9},{5,13},{9,1},{13,5},{2,10},{6,14},... | collective-permute-start | bytes 786440 | tf_op jit(solution)/shard_map/ppermute | solution.py:377
  16.3 8.8 %collective-permute-start.1 = (bf16[64,2048]{1,0:T(8,128)(2,1)S(1)}, bf16[64,2048]{1,0:T(8,128)(2,1)S(1)}, u32[]{:S(2)}, u32[]{:S(2)}) collective-permute-start(bf16[64,2048]{1,0:T(8,128)(2,1)S(1)} %get-tuple-element.21.rest_0_.refs_2_), channel_id=1, source_target_pairs={{0,4},{4,0},{8,12},{12,8},{1,5},{5,1},{9,13},{13,9},{2,6},{6,2},{1... | collective-permute-start | bytes 786440 | tf_op jit(solution)/shard_map/ppermute | solution.py:404
  16.4 15.2 %collective-permute-start.7 = (bf16[256,640]{1,0:T(8,128)(2,1)S(1)}, bf16[256,640]{1,0:T(8,128)(2,1)S(1)}, u32[]{:S(2)}, u32[]{:S(2)}) collective-permute-start(bf16[256,640]{1,0:T(8,128)(2,1)S(1)} %stack.6), channel_id=1, source_target_pairs={{0,4},{4,0},{8,12},{12,8},{1,5},{5,1},{9,13},{13,9},{2,6},{6,2},{1... | collective-permute-start | bytes 983048 | tf_op jit(solution)/shard_map/ppermute | solution.py:404
  17.0 8.7 %slice-start = ((s8[7340032]{0:T(1024)(128)(4,1)}), s8[4194304]{0:T(1024)(128)(4,1)S(1)}, s32[]{:S(2)}) async-start(s8[7340032]{0:T(1024)(128)(4,1)} %bitcast.9), calls=%async_computation | async-start | bytes 8388608
  17.0 8.7 %slice-start.1 = ((s8[7340032]{0:T(1024)(128)(4,1)}), s8[3145728]{0:T(1024)(128)(4,1)S(1)}, s32[]{:S(2)}) async-start(s8[7340032]{0:T(1024)(128)(4,1)} %bitcast.9), calls=%async_computation.1 | async-start | bytes 6291456
  24.1 1.6 %collective-permute-start.2 = (bf16[64,2048]{1,0:T(8,128)(2,1)S(1)}, bf16[64,2048]{1,0:T(8,128)(2,1)S(1)}, u32[]{:S(2)}, u32[]{:S(2)}) collective-permute-start(bf16[64,2048]{1,0:T(8,128)(2,1)S(1)} %stack.5), channel_id=1, source_target_pairs={{0,4},{4,0},{8,12},{12,8},{1,5},{5,1},{9,13},{13,9},{2,6},{6,2},{1... | collective-permute-start | bytes 786440 | tf_op jit(solution)/shard_map/ppermute | solution.py:404
  24.1 12.4 %collective-permute-start.4 = (bf16[80,2048]{1,0:T(8,128)(2,1)S(1)}, bf16[80,2048]{1,0:T(8,128)(2,1)S(1)}, u32[]{:S(2)}, u32[]{:S(2)}) collective-permute-start(bf16[80,2048]{1,0:T(8,128)(2,1)S(1)} %attend.3.refs_1_.rest_4_.rest_0_), channel_id=1, source_target_pairs={{0,8},{4,12},{8,0},{12,4},{1,9},{5,13},{9,1},{13,5},{2,10},{6,14},... | collective-permute-start | bytes 983048 | tf_op jit(solution)/shard_map/ppermute | solution.py:377
  24.9 12.7 %collective-permute-start.5 = (bf16[80,2048]{1,0:T(8,128)(2,1)S(1)}, bf16[80,2048]{1,0:T(8,128)(2,1)S(1)}, u32[]{:S(2)}, u32[]{:S(2)}) collective-permute-start(bf16[80,2048]{1,0:T(8,128)(2,1)S(1)} %attend.3.refs_1_.rest_4_.rest_0_), channel_id=1, source_target_pairs={{0,4},{4,0},{8,12},{12,8},{1,5},{5,1},{9,13},{13,9},{2,6},{6,2},{1... | collective-permute-start | bytes 983048 | tf_op jit(solution)/shard_map/ppermute | solution.py:404
  28.1 19.3 %collective-permute-start.3 = (bf16[192,1792]{1,0:T(8,128)(2,1)S(1)}, bf16[192,1792]{1,0:T(8,128)(2,1)S(1)}, u32[]{:S(2)}, u32[]{:S(2)}) collective-permute-start(bf16[192,1792]{1,0:T(8,128)(2,1)S(1)} %get-tuple-element.27.refs_0_), channel_id=1, source_target_pairs={{0,1},{3,2},{4,5},{7,6},{8,9},{11,10},{12,13},{15,14},{16,17},{19,... | collective-permute-start | bytes 2064392 | tf_op jit(solution)/shard_map/ppermute | solution.py:558
  36.6 1.7 %collective-permute-start.8 = (bf16[80,2048]{1,0:T(8,128)(2,1)S(1)}, bf16[80,2048]{1,0:T(8,128)(2,1)S(1)}, u32[]{:S(2)}, u32[]{:S(2)}) collective-permute-start(bf16[80,2048]{1,0:T(8,128)(2,1)S(1)} %stack.7), channel_id=1, source_target_pairs={{0,4},{4,0},{8,12},{12,8},{1,5},{5,1},{9,13},{13,9},{2,6},{6,2},{1... | collective-permute-start | bytes 983048 | tf_op jit(solution)/shard_map/ppermute | solution.py:404
  36.7 19.8 %collective-permute-start.11 = (bf16[64,2048]{1,0:T(8,128)(2,1)S(1)}, bf16[64,2048]{1,0:T(8,128)(2,1)S(1)}, u32[]{:S(2)}, u32[]{:S(2)}) collective-permute-start(bf16[64,2048]{1,0:T(8,128)(2,1)S(1)} %attend.4.refs_1_.rest_4_.rest_0_), channel_id=1, source_target_pairs={{0,8},{4,12},{8,0},{12,4},{1,9},{5,13},{9,1},{13,5},{2,10},{6,14},... | collective-permute-start | bytes 786440 | tf_op jit(solution)/shard_map/ppermute | solution.py:377
  37.5 19.1 %collective-permute-start.12 = (bf16[64,2048]{1,0:T(8,128)(2,1)S(1)}, bf16[64,2048]{1,0:T(8,128)(2,1)S(1)}, u32[]{:S(2)}, u32[]{:S(2)}) collective-permute-start(bf16[64,2048]{1,0:T(8,128)(2,1)S(1)} %attend.4.refs_1_.rest_4_.rest_0_), channel_id=1, source_target_pairs={{0,4},{4,0},{8,12},{12,8},{1,5},{5,1},{9,13},{13,9},{2,6},{6,2},{1... | collective-permute-start | bytes 786440 | tf_op jit(solution)/shard_map/ppermute | solution.py:404
  41.1 7.3 %copy-start.2 = (s32[16,4]{0,1:T(4,128)S(1)}, s32[16,4]{0,1:T(4,128)}, u32[]{:S(2)}) copy-start(s32[16,4]{0,1:T(4,128)} %param.26) | copy-start | bytes 772
  41.1 7.3 %copy-start.4 = (s32[16]{0:T(128)S(1)}, s32[16]{0:T(128)}, u32[]{:S(2)}) copy-start(s32[16]{0:T(128)} %decode_length.1) | copy-start | bytes 196
  41.1 26.6 %collective-permute-start.10 = (bf16[240,1792]{1,0:T(8,128)(2,1)S(1)}, bf16[240,1792]{1,0:T(8,128)(2,1)S(1)}, u32[]{:S(2)}, u32[]{:S(2)}) collective-permute-start(bf16[240,1792]{1,0:T(8,128)(2,1)S(1)} %get-tuple-element.31.refs_0_.refs_2_), channel_id=1, source_target_pairs={{0,1},{3,2},{4,5},{7,6},{8,9},{11,10},{12,13},{15,14},{16,17},{19,... | collective-permute-start | bytes 2580488 | tf_op jit(solution)/shard_map/ppermute | solution.py:558
  47.5 20.2 %collective-permute-start.9 = (bf16[128,1792]{1,0:T(8,128)(2,1)S(1)}, bf16[128,1792]{1,0:T(8,128)(2,1)S(1)}, u32[]{:S(2)}, u32[]{:S(2)}) collective-permute-start(bf16[128,1792]{1,0:T(8,128)(2,1)S(1)} %add.12.rest_3_), channel_id=1, source_target_pairs={{1,2},{2,1},{5,6},{6,5},{9,10},{10,9},{13,14},{14,13},{17,18},{18,... | collective-permute-start | bytes 1376264 | tf_op jit(solution)/shard_map/ppermute | solution.py:561
  56.5 1.6 %collective-permute-start.13 = (bf16[64,2048]{1,0:T(8,128)(2,1)S(1)}, bf16[64,2048]{1,0:T(8,128)(2,1)S(1)}, u32[]{:S(2)}, u32[]{:S(2)}) collective-permute-start(bf16[64,2048]{1,0:T(8,128)(2,1)S(1)} %stack.8), channel_id=1, source_target_pairs={{0,4},{4,0},{8,12},{12,8},{1,5},{5,1},{9,13},{13,9},{2,6},{6,2},{1... | collective-permute-start | bytes 786440 | tf_op jit(solution)/shard_map/ppermute | solution.py:404
  60.4 22.2 %collective-permute-start.15 = (bf16[192,1792]{1,0:T(8,128)(2,1)S(1)}, bf16[192,1792]{1,0:T(8,128)(2,1)S(1)}, u32[]{:S(2)}, u32[]{:S(2)}) collective-permute-start(bf16[192,1792]{1,0:T(8,128)(2,1)S(1)} %get-tuple-element.34.refs_0_), channel_id=1, source_target_pairs={{0,1},{3,2},{4,5},{7,6},{8,9},{11,10},{12,13},{15,14},{16,17},{19,... | collective-permute-start | bytes 2064392 | tf_op jit(solution)/shard_map/ppermute | solution.py:558
  67.8 14.9 %collective-permute-start.14 = (bf16[160,1792]{1,0:T(8,128)(2,1)S(1)}, bf16[160,1792]{1,0:T(8,128)(2,1)S(1)}, u32[]{:S(2)}, u32[]{:S(2)}) collective-permute-start(bf16[160,1792]{1,0:T(8,128)(2,1)S(1)} %add.13.rest_4_), channel_id=1, source_target_pairs={{1,2},{2,1},{5,6},{6,5},{9,10},{10,9},{13,14},{14,13},{17,18},{18,... | collective-permute-start | bytes 1720328 | tf_op jit(solution)/shard_map/ppermute | solution.py:561
  68.5 6.7 %collective-permute-start.16 = (bf16[48,2048]{1,0:T(8,128)(2,1)S(1)}, bf16[48,2048]{1,0:T(8,128)(2,1)S(1)}, u32[]{:S(2)}, u32[]{:S(2)}) collective-permute-start(bf16[48,2048]{1,0:T(8,128)(2,1)S(1)} %attend.5.refs_1_.rest_4_.rest_0_), channel_id=1, source_target_pairs={{0,8},{4,12},{8,0},{12,4},{1,9},{5,13},{9,1},{13,5},{2,10},{6,14},... | collective-permute-start | bytes 589832 | tf_op jit(solution)/shard_map/ppermute | solution.py:377
  69.3 6.0 %collective-permute-start.17 = (bf16[48,2048]{1,0:T(8,128)(2,1)S(1)}, bf16[48,2048]{1,0:T(8,128)(2,1)S(1)}, u32[]{:S(2)}, u32[]{:S(2)}) collective-permute-start(bf16[48,2048]{1,0:T(8,128)(2,1)S(1)} %attend.5.refs_1_.rest_4_.rest_0_), channel_id=1, source_target_pairs={{0,4},{4,0},{8,12},{12,8},{1,5},{5,1},{9,13},{13,9},{2,6},{6,2},{1... | collective-permute-start | bytes 589832 | tf_op jit(solution)/shard_map/ppermute | solution.py:404
  75.3 1.5 %collective-permute-start.18 = (bf16[48,2048]{1,0:T(8,128)(2,1)S(1)}, bf16[48,2048]{1,0:T(8,128)(2,1)S(1)}, u32[]{:S(2)}, u32[]{:S(2)}) collective-permute-start(bf16[48,2048]{1,0:T(8,128)(2,1)S(1)} %stack.9), channel_id=1, source_target_pairs={{0,4},{4,0},{8,12},{12,8},{1,5},{5,1},{9,13},{13,9},{2,6},{6,2},{1... | collective-permute-start | bytes 589832 | tf_op jit(solution)/shard_map/ppermute | solution.py:404
  78.5 15.1 %collective-permute-start.20 = (bf16[144,1792]{1,0:T(8,128)(2,1)S(1)}, bf16[144,1792]{1,0:T(8,128)(2,1)S(1)}, u32[]{:S(2)}, u32[]{:S(2)}) collective-permute-start(bf16[144,1792]{1,0:T(8,128)(2,1)S(1)} %get-tuple-element.36.refs_0_), channel_id=1, source_target_pairs={{0,1},{3,2},{4,5},{7,6},{8,9},{11,10},{12,13},{15,14},{16,17},{19,... | collective-permute-start | bytes 1548296 | tf_op jit(solution)/shard_map/ppermute | solution.py:558
  82.8 15.1 %collective-permute-start.19 = (bf16[144,1792]{1,0:T(8,128)(2,1)S(1)}, bf16[144,1792]{1,0:T(8,128)(2,1)S(1)}, u32[]{:S(2)}, u32[]{:S(2)}) collective-permute-start(bf16[144,1792]{1,0:T(8,128)(2,1)S(1)} %add.15.refs_2_), channel_id=1, source_target_pairs={{1,0},{2,3},{5,4},{6,7},{9,8},{10,11},{13,12},{14,15},{17,16},{18,... | collective-permute-start | bytes 1548296 | tf_op jit(solution)/shard_map/ppermute | solution.py:564
  84.1 14.1 %collective-permute-start.21 = (bf16[128,1792]{1,0:T(8,128)(2,1)S(1)}, bf16[128,1792]{1,0:T(8,128)(2,1)S(1)}, u32[]{:S(2)}, u32[]{:S(2)}) collective-permute-start(bf16[128,1792]{1,0:T(8,128)(2,1)S(1)} %add.14.refs_4_), channel_id=1, source_target_pairs={{1,2},{2,1},{5,6},{6,5},{9,10},{10,9},{13,14},{14,13},{17,18},{18,... | collective-permute-start | bytes 1376264 | tf_op jit(solution)/shard_map/ppermute | solution.py:561
  93.7 6.6 %collective-permute-start.23 = (bf16[48,1792]{1,0:T(8,128)(2,1)S(1)}, bf16[48,1792]{1,0:T(8,128)(2,1)S(1)}, u32[]{:S(2)}, u32[]{:S(2)}) collective-permute-start(bf16[48,1792]{1,0:T(8,128)(2,1)S(1)} %add.16.refs_2_), channel_id=1, source_target_pairs={{1,2},{2,1},{5,6},{6,5},{9,10},{10,9},{13,14},{14,13},{17,18},{18,... | collective-permute-start | bytes 516104 | tf_op jit(solution)/shard_map/ppermute | solution.py:561
  98.3 8.7 %collective-permute-start.22 = (bf16[64,1792]{1,0:T(8,128)(2,1)S(1)}, bf16[64,1792]{1,0:T(8,128)(2,1)S(1)}, u32[]{:S(2)}, u32[]{:S(2)}) collective-permute-start(bf16[64,1792]{1,0:T(8,128)(2,1)S(1)} %add.19.refs_2_), channel_id=1, source_target_pairs={{1,0},{2,3},{5,4},{6,7},{9,8},{10,11},{13,12},{14,15},{17,16},{18,... | collective-permute-start | bytes 688136 | tf_op jit(solution)/shard_map/ppermute | solution.py:564
  99.6 7.5 %collective-permute-start.24 = (bf16[48,1792]{1,0:T(8,128)(2,1)S(1)}, bf16[48,1792]{1,0:T(8,128)(2,1)S(1)}, u32[]{:S(2)}, u32[]{:S(2)}) collective-permute-start(bf16[48,1792]{1,0:T(8,128)(2,1)S(1)} %add.17.refs_8_), channel_id=1, source_target_pairs={{1,2},{2,1},{5,6},{6,5},{9,10},{10,9},{13,14},{14,13},{17,18},{18,... | collective-permute-start | bytes 516104 | tf_op jit(solution)/shard_map/ppermute | solution.py:561
  100.3 9.7 %collective-permute-start.25 = (bf16[48,1792]{1,0:T(8,128)(2,1)S(1)}, bf16[48,1792]{1,0:T(8,128)(2,1)S(1)}, u32[]{:S(2)}, u32[]{:S(2)}) collective-permute-start(bf16[48,1792]{1,0:T(8,128)(2,1)S(1)} %add.20.refs_4_), channel_id=1, source_target_pairs={{1,0},{2,3},{5,4},{6,7},{9,8},{10,11},{13,12},{14,15},{17,16},{18,... | collective-permute-start | bytes 516104 | tf_op jit(solution)/shard_map/ppermute | solution.py:564

commit v11 on v9

--- a/solution.py
+++ b/solution.py
@@ -590,24 +590,24 @@
     own3, rest3, near = project(
         where, gather(x3, (own2,)), w, (2, 1), (near2,), (to_across1,))
     in3 = inward(rest3)
-    to_across2 = add(2 * t2, [(rest2, 0), (in2, 0)], (own3, on0))
-    on2 = across(to_across2)
+    to_far2 = add(t2, [(rest2, 0), (in2, 0)], (own3, on0))
+    far2_on = across(to_far2)
     near_in = inward(near)
     to_out01 = add_all([(t0, [(rest0, 2 * t0), (on0, 0)]), (t1, [(rest1, 2 * t1), (on1, 0)])],
-                       (to_across2,))
+                       (to_far2,))
     out01 = outward(to_out01)
-    to_far = add(t3, [(rest3, 0), (in3, 0)], (to_out01,))
-    far_on = across(to_far)
-    to_mid = add(t3, [(rest3, t3), (in3, t3)], (to_far,))
-    mid_on = across(to_mid)
+    to_out2 = add(t2, [(near2, 0), (far2_on, 0)], (to_out01,))
+    out2 = outward(to_out2)
+    to_far3 = add(t3, [(rest3, 0), (in3, 0)], (to_out2,))
+    far3_on = across(to_far3)
+    to_mids = add_all([(t2, [(rest2, t2), (in2, t2)]), (t3, [(rest3, t3), (in3, t3)])], (to_far3,))
+    mids_on = across(to_mids)
     done01 = add_all([(t0, [(own0, 0), (in0, 2 * t0), (on0, t0), (out01, 0)]),
-                      (t1, [(own1, 0), (in1, 2 * t1), (on1, t1), (out01, t0)])], (to_mid,))
-    to_out2 = add(t2, [(near2, 0), (on2, 0)], (done01,))
-    out2 = outward(to_out2)
-    to_out3 = add(t3, [(near, t2), (far_on, 0)], (to_out2,))
+                      (t1, [(own1, 0), (in1, 2 * t1), (on1, t1), (out01, t0)])], (to_mids,))
+    to_out3 = add(t3, [(near, t2), (far3_on, 0)], (done01,))
     out3 = outward(to_out3)
-    done2 = add(t2, [(own2, 0), (near_in, 0), (on2, t2), (out2, 0)], (to_out3,))
-    return finish([done01, done2], [(own3, 0), (near_in, t2), (mid_on, 0), (out3, 0)])
+    done2 = add(t2, [(own2, 0), (near_in, 0), (mids_on, 0), (out2, 0)], (to_out3,))
+    return finish([done01, done2], [(own3, 0), (near_in, t2), (mids_on, t2), (out3, 0)])
 
 
 def solution(mesh):

time: 106 us -> 117 us (1.10)
  starting transfers between devices: 40.2 us -> 46.7 us
  waiting for transfers between devices: 21.2 us -> 25.8 us
    ppermute x5, starting transfers between devices: 24.6 us -> 31.1 us  [inward(): return lax.ppermute(x, 'tp', INWARD)]
    ppermute x3, waiting for transfers between devices: 16 us -> 22 us  [outward(): return lax.ppermute(x, 'tp', OUTWARD)]
  transfers between devices with their start and end apart: 27 -> 27, of which waited for: 10 -> 8; matrix products, arithmetic and copies ran while one was open for 0% -> 0% of each run, Pallas kernels for 35% -> 32%
where the time goes in v11:
time: 117 us; the launch traced here: 116 us
  starting transfers between devices  46.7 us (40%)
  Pallas kernels  39.9 us (34%)
  waiting for transfers between devices  25.8 us (22%)
  local copies, waits for them, and re-layouts  2.68 us (2%)
    ppermute x5, starting transfers between devices, inward(): return lax.ppermute(x, 'tp', INWARD)  31.1 us
    ppermute x3, waiting for transfers between devices, outward(): return lax.ppermute(x, 'tp', OUTWARD)  22 us
    pallas_call x3, Pallas kernels, attend(): pl.pallas_call(kernel, out_shape=jax.ShapeDtypeStruct((t, heads * dv), bf...  20.1 us
    pallas_call x4, Pallas kernels, project(): pl.pallas_call(functools.partial(project_kernel, len(parts), tails, place...  9.09 us
    pallas_call x1, Pallas kernels, first_chunk(): pl.pallas_call(functools.partial(first_kernel, fresh_of(0), exp_scale), o...  6.86 us
    ppermute x3, starting transfers between devices, outward(): return lax.ppermute(x, 'tp', OUTWARD)  3.88 us
    ppermute x5, starting transfers between devices, across(): return lax.ppermute(x, 'tp', ACROSS)  3.42 us
    ppermute x4, starting transfers between devices, shift_groups(): lax.ppermute(x, 'dp', [(i, (i + s) % groups) for i in range(groups)])  3.36 us
  transfers between devices with their start and end apart: 27, of which 8 were waited for; matrix products, arithmetic and copies ran while one was open for 0% of the time, Pallas kernels for 32%

profile of v11, /device:TPU:0, one launch (start us, length us, event | category | flops | bytes accessed | tf_op | source)
XLA Modules:
  0.0 116.3 jit_solution(15078078834551397281)
XLA Ops:
  0.0 1.6 %reshape.6 = bf16[32,64,64]{2,1,0:T(8,128)(2,1)S(1)} reshape(bf16[32,4096]{1,0:T(8,128)(2,1)} %param.19) | data formatting | bytes 524288 | tf_op jit(solution)/shard_map/reshape | solution.py:457
  1.6 0.1 pad.4.cache_rope
  1.7 0.0 copy-start
  1.7 0.7 copy-done
  2.4 1.7 %pack.1 = (bf16[128,640]{1,0:T(8,128)(2,1)S(1)}, bf16[128,640]{1,0:T(8,128)(2,1)S(1)}, bf16[256,640]{1,0:T(8,128)(2,1)S(1)}) custom-call(s32[1]{0:T(128)} %bitcast.me, s32[1,2,4]{2,1,0:T(2,128)S(1)} %bitcast.15, bf16[32,64,512]{2,1,0:T(8,128)(2,1)} %cache_latent.3, bf16[32,64,128]{2,1,0:T(8,128)(2,1)S(1)} %pad.4.cache_rope), custom_call_target="tpu_custom_call" | custom-call | flops 1000 | bytes 1000 | tf_op jit(solution)/shard_map/pack/pallas_call | solution.py:524
  4.1 3.0 %collective-permute-start.6 = (bf16[256,640]{1,0:T(8,128)(2,1)S(1)}, bf16[256,640]{1,0:T(8,128)(2,1)S(1)}, u32[]{:S(2)}, u32[]{:S(2)}) collective-permute-start(bf16[256,640]{1,0:T(8,128)(2,1)S(1)} %get-tuple-element.31), channel_id=1, source_target_pairs={{0,8},{4,12},{8,0},{12,4},{1,9},{5,13},{9,1},{13,5},{2,10},{6,14},... | collective-permute-start | bytes 983048 | tf_op jit(solution)/shard_map/ppermute | solution.py:573
  7.1 0.3 copy.17
  8.0 6.9 %attend_first.1 = (bf16[48,2048]{1,0:T(8,128)(2,1)S(1)}, bf16[1280,640]{1,0:T(8,128)(2,1)S(1)}, bf16[16,128,512]{2,1,0:T(8,128)(2,1)S(1)}, bf16[16,512,128]{2,1,0:T(8,128)(2,1)S(1)}, bf16[256,1024]{1,0:T(8,128)(2,1)S(1)}) custom-call(s32[1]{0:T(128)} %bitcast.me, s32[1]{0:T(128)} %bitcast.1.z, s32[1,16]{1,0:T(1,128)S(1)} %copy-done.3, s32[1]{0:T(128)S(6)} %copy.18.offset, ...), custom_call_target="tpu_custom_call" | custom-call | flops 40000000000 | bytes 1000 | tf_op jit(solution)/shard_map/attend_first/pallas_call | solution.py:471
  14.9 0.1 collective-permute-start
  15.0 0.1 collective-permute-start.1
  15.1 0.5 collective-permute-start.7
  15.7 4.7 %attend.3.refs_1_.rest_4_.rest_0_ = bf16[64,2048]{1,0:T(8,128)(2,1)S(1)} custom-call(bf16[16,256,128]{2,1,0:T(8,128)(2,1)S(1)} %bitcast.12, bf16[256,1024]{1,0:T(8,128)(2,1)S(1)} %get-tuple-element.24.q_rope, bf16[16,128,512]{2,1,0:T(8,128)(2,1)S(1)} %get-tuple-element.25.wk, bf16[16,512,128]{2,1,0:T(8,128)(2,1)S(1)} %get-tuple-element.26.wv, ...), custom_call_target="tpu_custom_call" | custom-call | flops 40000000000 | bytes 1000 | tf_op jit(solution)/shard_map/attend/pallas_call | solution.py:512
  20.4 0.9 collective-permute-done.refs_0_.rest_1_
  21.4 0.1 collective-permute-start.2
  21.4 1.1 collective-permute-start.4
  22.5 0.2 collective-permute-start.5
  22.7 0.1 collective-permute-done.2.rest_3_
  22.9 1.7 %project.4 = (bf16[48,1792]{1,0:T(8,128)(2,1)S(1)}, bf16[144,1792]{1,0:T(8,128)(2,1)S(1)}) custom-call(s32[1]{0:T(128)} %bitcast.me, s32[1]{0:T(128)} %bitcast.1.z, bf16[2048,1792]{1,0:T(8,128)(2,1)S(1)} %bitcast.10, bf16[48,2048]{1,0:T(8,128)(2,1)S(1)} %get-tuple-element.23.rest_0_.refs_2_, bf16[48,2048]{1,0:T(8,128)(2,1)S(1)} %collective-permute-done.refs_0_.rest_1_, ...), custom_call_target="tpu_custom_call" | custom-call | flops 1000 | bytes 1000 | tf_op jit(solution)/shard_map/project/pallas_call | solution.py:304
  24.6 3.7 %collective-permute-start.3 = (bf16[144,1792]{1,0:T(8,128)(2,1)S(1)}, bf16[144,1792]{1,0:T(8,128)(2,1)S(1)}, u32[]{:S(2)}, u32[]{:S(2)}) collective-permute-start(bf16[144,1792]{1,0:T(8,128)(2,1)S(1)} %get-tuple-element.29.refs_0_), channel_id=1, source_target_pairs={{0,1},{3,2},{4,5},{7,6},{8,9},{11,10},{12,13},{15,14},{16,17},{19,... | collective-permute-start | bytes 1548296 | tf_op jit(solution)/shard_map/ppermute | solution.py:558
  28.3 0.0 collective-permute-done.7.rest_1_.rest_2_
  28.3 5.9 %attend.4.refs_1_.rest_4_.rest_0_ = bf16[80,2048]{1,0:T(8,128)(2,1)S(1)} custom-call(bf16[16,256,128]{2,1,0:T(8,128)(2,1)S(1)} %bitcast.13, bf16[256,1024]{1,0:T(8,128)(2,1)S(1)} %get-tuple-element.24.q_rope, bf16[16,128,512]{2,1,0:T(8,128)(2,1)S(1)} %get-tuple-element.25.wk, bf16[16,512,128]{2,1,0:T(8,128)(2,1)S(1)} %get-tuple-element.26.wv, ...), custom_call_target="tpu_custom_call" | custom-call | flops 40000000000 | bytes 1000 | tf_op jit(solution)/shard_map/attend/pallas_call | solution.py:512
  34.2 0.0 collective-permute-done.4.refs_0_.rest_1_
  34.2 0.0 copy-start.2
  34.2 0.0 copy-start.4
  34.3 0.1 collective-permute-start.8
  34.3 1.1 collective-permute-start.9
  35.4 0.2 collective-permute-start.10
  35.6 0.2 collective-permute-done.8.rest_3_
  35.9 2.3 %project.5 = (bf16[64,1792]{1,0:T(8,128)(2,1)S(1)}, bf16[192,1792]{1,0:T(8,128)(2,1)S(1)}) custom-call(s32[1]{0:T(128)} %bitcast.me, s32[1]{0:T(128)} %bitcast.1.z, bf16[2048,1792]{1,0:T(8,128)(2,1)S(1)} %bitcast.10, bf16[64,2048]{1,0:T(8,128)(2,1)S(1)} %attend.3.refs_1_.rest_4_.rest_0_, bf16[64,2048]{1,0:T(8,128)(2,1)S(1)} %collective-permute-done.4.refs_0_.rest_1_, ...), custom_call_target="tpu_custom_call" | custom-call | flops 1000 | bytes 1000 | tf_op jit(solution)/shard_map/project/pallas_call | solution.py:304
  38.1 1.6 %collective-permute-start.13 = (bf16[192,1792]{1,0:T(8,128)(2,1)S(1)}, bf16[192,1792]{1,0:T(8,128)(2,1)S(1)}, u32[]{:S(2)}, u32[]{:S(2)}) collective-permute-start(bf16[192,1792]{1,0:T(8,128)(2,1)S(1)} %get-tuple-element.35.refs_0_.refs_2_), channel_id=1, source_target_pairs={{0,1},{3,2},{4,5},{7,6},{8,9},{11,10},{12,13},{15,14},{16,17},{19,... | collective-permute-start | bytes 2064392 | tf_op jit(solution)/shard_map/ppermute | solution.py:558
  39.7 0.1 add.12.rest_3_.refs_0_
  39.8 9.5 %attend.5.refs_1_.rest_4_.rest_0_ = bf16[64,2048]{1,0:T(8,128)(2,1)S(1)} custom-call(s32[1]{0:T(128)} %bitcast.me, bf16[16,256,128]{2,1,0:T(8,128)(2,1)S(1)} %bitcast.14, bf16[256,1024]{1,0:T(8,128)(2,1)S(1)} %get-tuple-element.24.q_rope, bf16[16,128,512]{2,1,0:T(8,128)(2,1)S(1)} %get-tuple-element.25.wk, bf16[16,512,128]{2,1,0:T(8,128)(2,1)S(1)} %get-tuple-element.26.wv, ...), custom_call_target="tpu_custom_call" | custom-call | flops 6000000000 | bytes 1000 | tf_op jit(solution)/shard_map/attend/pallas_call | solution.py:512
  49.3 0.2 collective-permute-start.11
  49.5 1.0 collective-permute-start.16
  50.6 0.4 collective-permute-done.11.rest_3_
  51.0 2.8 %project.6 = (bf16[80,1792]{1,0:T(8,128)(2,1)S(1)}, bf16[160,1792]{1,0:T(8,128)(2,1)S(1)}, bf16[80,1792]{1,0:T(8,128)(2,1)S(1)}) custom-call(s32[1]{0:T(128)} %bitcast.me, s32[1]{0:T(128)} %bitcast.1.z, bf16[2048,1792]{1,0:T(8,128)(2,1)S(1)} %bitcast.10, bf16[80,2048]{1,0:T(8,128)(2,1)S(1)} %attend.4.refs_1_.rest_4_.rest_0_, ...), custom_call_target="tpu_custom_call" | custom-call | flops 1000 | bytes 1000 | tf_op jit(solution)/shard_map/project/pallas_call | solution.py:304
  53.8 4.2 %collective-permute-start.15 = (bf16[160,1792]{1,0:T(8,128)(2,1)S(1)}, bf16[160,1792]{1,0:T(8,128)(2,1)S(1)}, u32[]{:S(2)}, u32[]{:S(2)}) collective-permute-start(bf16[160,1792]{1,0:T(8,128)(2,1)S(1)} %get-tuple-element.36.refs_0_), channel_id=1, source_target_pairs={{0,1},{3,2},{4,5},{7,6},{8,9},{11,10},{12,13},{15,14},{16,17},{19,... | collective-permute-start | bytes 1720328 | tf_op jit(solution)/shard_map/ppermute | solution.py:558
  58.0 0.1 collective-permute-start.17
  58.1 0.5 collective-permute-start.18
  58.7 0.7 collective-permute-start.12
  59.4 0.1 add.13.rest_5_
  59.5 0.7 collective-permute-start.14
  60.3 2.3 %project.7 = (bf16[64,1792]{1,0:T(8,128)(2,1)S(1)}, bf16[128,1792]{1,0:T(8,128)(2,1)S(1)}, bf16[144,1792]{1,0:T(8,128)(2,1)S(1)}) custom-call(s32[1]{0:T(128)} %bitcast.me, s32[1]{0:T(128)} %bitcast.1.z, bf16[2048,1792]{1,0:T(8,128)(2,1)S(1)} %bitcast.10, bf16[64,2048]{1,0:T(8,128)(2,1)S(1)} %attend.5.refs_1_.rest_4_.rest_0_, ...), custom_call_target="tpu_custom_call" | custom-call | flops 1000 | bytes 1000 | tf_op jit(solution)/shard_map/project/pallas_call | solution.py:304
  62.6 8.2 %collective-permute-start.20 = (bf16[128,1792]{1,0:T(8,128)(2,1)S(1)}, bf16[128,1792]{1,0:T(8,128)(2,1)S(1)}, u32[]{:S(2)}, u32[]{:S(2)}) collective-permute-start(bf16[128,1792]{1,0:T(8,128)(2,1)S(1)} %get-tuple-element.39.refs_0_.refs_2_), channel_id=1, source_target_pairs={{0,1},{3,2},{4,5},{7,6},{8,9},{11,10},{12,13},{15,14},{16,17},{19,... | collective-permute-start | bytes 1376264 | tf_op jit(solution)/shard_map/ppermute | solution.py:558
  70.8 0.1 add.14.refs_4_
  70.8 0.7 collective-permute-start.21
  71.5 0.1 add.15.refs_2_
  71.6 1.3 %collective-permute-start.19 = (bf16[112,1792]{1,0:T(8,128)(2,1)S(1)}, bf16[112,1792]{1,0:T(8,128)(2,1)S(1)}, u32[]{:S(2)}, u32[]{:S(2)}) collective-permute-start(bf16[112,1792]{1,0:T(8,128)(2,1)S(1)} %add.15.refs_2_), channel_id=1, source_target_pairs={{1,0},{2,3},{5,4},{6,7},{9,8},{10,11},{13,12},{14,15},{17,16},{18,... | collective-permute-start | bytes 1204232 | tf_op jit(solution)/shard_map/ppermute | solution.py:564
  72.9 13.5 %collective-permute-start.22 = (bf16[144,1792]{1,0:T(8,128)(2,1)S(1)}, bf16[144,1792]{1,0:T(8,128)(2,1)S(1)}, u32[]{:S(2)}, u32[]{:S(2)}) collective-permute-start(bf16[144,1792]{1,0:T(8,128)(2,1)S(1)} %get-tuple-element.40.refs_0_), channel_id=1, source_target_pairs={{0,1},{3,2},{4,5},{7,6},{8,9},{11,10},{12,13},{15,14},{16,17},{19,... | collective-permute-start | bytes 1548296 | tf_op jit(solution)/shard_map/ppermute | solution.py:558
  86.5 0.1 add.16.refs_2_
  86.6 0.1 add.17.refs_4_
  86.6 0.1 add.18.refs_8_
  86.8 0.7 collective-permute-start.23
  87.5 0.7 collective-permute-start.25
  88.1 1.3 %collective-permute-start.24 = (bf16[80,1792]{1,0:T(8,128)(2,1)S(1)}, bf16[80,1792]{1,0:T(8,128)(2,1)S(1)}, u32[]{:S(2)}, u32[]{:S(2)}) collective-permute-start(bf16[80,1792]{1,0:T(8,128)(2,1)S(1)} %add.16.refs_2_), channel_id=1, source_target_pairs={{1,0},{2,3},{5,4},{6,7},{9,8},{10,11},{13,12},{14,15},{17,16},{18,... | collective-permute-start | bytes 860168 | tf_op jit(solution)/shard_map/ppermute | solution.py:564
  89.4 3.8 %collective-permute-done.19.refs_3_.refs_7_ = bf16[112,1792]{1,0:T(8,128)(2,1)S(1)} collective-permute-done((bf16[112,1792]{1,0:T(8,128)(2,1)S(1)}, bf16[112,1792]{1,0:T(8,128)(2,1)S(1)}, u32[]{:S(2)}, u32[]{:S(2)}) %collective-permute-start.19) | collective-permute-done | bytes 401440 | tf_op jit(solution)/shard_map/ppermute | solution.py:564
  93.2 0.2 add.19.refs_2_.refs_0_
  93.5 0.1 add.20.refs_4_
  93.5 1.3 %collective-permute-start.26 = (bf16[64,1792]{1,0:T(8,128)(2,1)S(1)}, bf16[64,1792]{1,0:T(8,128)(2,1)S(1)}, u32[]{:S(2)}, u32[]{:S(2)}) collective-permute-start(bf16[64,1792]{1,0:T(8,128)(2,1)S(1)} %add.20.refs_4_), channel_id=1, source_target_pairs={{1,0},{2,3},{5,4},{6,7},{9,8},{10,11},{13,12},{14,15},{17,16},{18,... | collective-permute-start | bytes 688136 | tf_op jit(solution)/shard_map/ppermute | solution.py:564
  94.8 2.1 %collective-permute-done.22.refs_1_.refs_3_ = bf16[144,1792]{1,0:T(8,128)(2,1)S(1)} collective-permute-done((bf16[144,1792]{1,0:T(8,128)(2,1)S(1)}, bf16[144,1792]{1,0:T(8,128)(2,1)S(1)}, u32[]{:S(2)}, u32[]{:S(2)}) %collective-permute-start.22) | collective-permute-done | bytes 516128 | tf_op jit(solution)/shard_map/ppermute | solution.py:558
  96.9 5.5 %collective-permute-done.24.refs_3_ = bf16[80,1792]{1,0:T(8,128)(2,1)S(1)} collective-permute-done((bf16[80,1792]{1,0:T(8,128)(2,1)S(1)}, bf16[80,1792]{1,0:T(8,128)(2,1)S(1)}, u32[]{:S(2)}, u32[]{:S(2)}) %collective-permute-start.24) | collective-permute-done | bytes 286752 | tf_op jit(solution)/shard_map/ppermute | solution.py:564
  102.4 0.1 add.21.refs_1_
  102.5 12.7 %collective-permute-done.26.refs_5_ = bf16[64,1792]{1,0:T(8,128)(2,1)S(1)} collective-permute-done((bf16[64,1792]{1,0:T(8,128)(2,1)S(1)}, bf16[64,1792]{1,0:T(8,128)(2,1)S(1)}, u32[]{:S(2)}, u32[]{:S(2)}) %collective-permute-start.26) | collective-permute-done | bytes 229408 | tf_op jit(solution)/shard_map/ppermute | solution.py:564
  115.2 1.1 finish.1
  (36 shorter events, 0.2 us)
Async XLA Ops:
  0.0 7.1 %copy-start.5 = (bf16[256,16,128]{2,1,0:T(8,128)(2,1)S(1)}, bf16[256,16,128]{2,1,0:T(8,128)(2,1)}, u32[]{:S(2)}) copy-start(bf16[256,16,128]{2,1,0:T(8,128)(2,1)} %param.14) | copy-start | bytes 3145732
  1.7 0.7 copy-start
  2.4 5.6 %copy-start.1 = (bf16[256,64]{0,1:T(8,128)(2,1)S(1)}, bf16[256,64]{0,1:T(8,128)(2,1)}, u32[]{:S(2)}) copy-start(bf16[256,64]{0,1:T(8,128)(2,1)} %param.17) | copy-start | bytes 98308
  2.4 5.6 %copy-start.3 = (s32[1,16]{1,0:T(1,128)S(1)}, s32[1,16]{1,0:T(1,128)}, u32[]{:S(2)}) copy-start(s32[1,16]{1,0:T(1,128)} %table.1) | copy-start | bytes 196
  4.1 11.0 %collective-permute-start.6 = (bf16[256,640]{1,0:T(8,128)(2,1)S(1)}, bf16[256,640]{1,0:T(8,128)(2,1)S(1)}, u32[]{:S(2)}, u32[]{:S(2)}) collective-permute-start(bf16[256,640]{1,0:T(8,128)(2,1)S(1)} %get-tuple-element.31), channel_id=1, source_target_pairs={{0,8},{4,12},{8,0},{12,4},{1,9},{5,13},{9,1},{13,5},{2,10},{6,14},... | collective-permute-start | bytes 983048 | tf_op jit(solution)/shard_map/ppermute | solution.py:573
  14.9 6.4 %collective-permute-start = (bf16[48,2048]{1,0:T(8,128)(2,1)S(1)}, bf16[48,2048]{1,0:T(8,128)(2,1)S(1)}, u32[]{:S(2)}, u32[]{:S(2)}) collective-permute-start(bf16[48,2048]{1,0:T(8,128)(2,1)S(1)} %get-tuple-element.23.rest_0_.refs_2_), channel_id=1, source_target_pairs={{0,8},{4,12},{8,0},{12,4},{1,9},{5,13},{9,1},{13,5},{2,10},{6,14},... | collective-permute-start | bytes 589832 | tf_op jit(solution)/shard_map/ppermute | solution.py:377
  15.0 7.7 %collective-permute-start.1 = (bf16[48,2048]{1,0:T(8,128)(2,1)S(1)}, bf16[48,2048]{1,0:T(8,128)(2,1)S(1)}, u32[]{:S(2)}, u32[]{:S(2)}) collective-permute-start(bf16[48,2048]{1,0:T(8,128)(2,1)S(1)} %get-tuple-element.23.rest_0_.refs_2_), channel_id=1, source_target_pairs={{0,4},{4,0},{8,12},{12,8},{1,5},{5,1},{9,13},{13,9},{2,6},{6,2},{1... | collective-permute-start | bytes 589832 | tf_op jit(solution)/shard_map/ppermute | solution.py:404
  15.1 13.2 %collective-permute-start.7 = (bf16[256,640]{1,0:T(8,128)(2,1)S(1)}, bf16[256,640]{1,0:T(8,128)(2,1)S(1)}, u32[]{:S(2)}, u32[]{:S(2)}) collective-permute-start(bf16[256,640]{1,0:T(8,128)(2,1)S(1)} %stack.7), channel_id=1, source_target_pairs={{0,4},{4,0},{8,12},{12,8},{1,5},{5,1},{9,13},{13,9},{2,6},{6,2},{1... | collective-permute-start | bytes 983048 | tf_op jit(solution)/shard_map/ppermute | solution.py:404
  15.7 7.2 %slice-start = ((s8[7340032]{0:T(1024)(128)(4,1)}), s8[4194304]{0:T(1024)(128)(4,1)S(1)}, s32[]{:S(2)}) async-start(s8[7340032]{0:T(1024)(128)(4,1)} %bitcast.9), calls=%async_computation | async-start | bytes 8388608
  15.7 7.2 %slice-start.1 = ((s8[7340032]{0:T(1024)(128)(4,1)}), s8[3145728]{0:T(1024)(128)(4,1)S(1)}, s32[]{:S(2)}) async-start(s8[7340032]{0:T(1024)(128)(4,1)} %bitcast.9), calls=%async_computation.1 | async-start | bytes 6291456
  21.4 1.5 %collective-permute-start.2 = (bf16[48,2048]{1,0:T(8,128)(2,1)S(1)}, bf16[48,2048]{1,0:T(8,128)(2,1)S(1)}, u32[]{:S(2)}, u32[]{:S(2)}) collective-permute-start(bf16[48,2048]{1,0:T(8,128)(2,1)S(1)} %stack.6), channel_id=1, source_target_pairs={{0,4},{4,0},{8,12},{12,8},{1,5},{5,1},{9,13},{13,9},{2,6},{6,2},{1... | collective-permute-start | bytes 589832 | tf_op jit(solution)/shard_map/ppermute | solution.py:404
  21.4 12.8 %collective-permute-start.4 = (bf16[64,2048]{1,0:T(8,128)(2,1)S(1)}, bf16[64,2048]{1,0:T(8,128)(2,1)S(1)}, u32[]{:S(2)}, u32[]{:S(2)}) collective-permute-start(bf16[64,2048]{1,0:T(8,128)(2,1)S(1)} %attend.3.refs_1_.rest_4_.rest_0_), channel_id=1, source_target_pairs={{0,8},{4,12},{8,0},{12,4},{1,9},{5,13},{9,1},{13,5},{2,10},{6,14},... | collective-permute-start | bytes 786440 | tf_op jit(solution)/shard_map/ppermute | solution.py:377
  22.5 13.1 %collective-permute-start.5 = (bf16[64,2048]{1,0:T(8,128)(2,1)S(1)}, bf16[64,2048]{1,0:T(8,128)(2,1)S(1)}, u32[]{:S(2)}, u32[]{:S(2)}) collective-permute-start(bf16[64,2048]{1,0:T(8,128)(2,1)S(1)} %attend.3.refs_1_.rest_4_.rest_0_), channel_id=1, source_target_pairs={{0,4},{4,0},{8,12},{12,8},{1,5},{5,1},{9,13},{13,9},{2,6},{6,2},{1... | collective-permute-start | bytes 786440 | tf_op jit(solution)/shard_map/ppermute | solution.py:404
  24.6 15.1 %collective-permute-start.3 = (bf16[144,1792]{1,0:T(8,128)(2,1)S(1)}, bf16[144,1792]{1,0:T(8,128)(2,1)S(1)}, u32[]{:S(2)}, u32[]{:S(2)}) collective-permute-start(bf16[144,1792]{1,0:T(8,128)(2,1)S(1)} %get-tuple-element.29.refs_0_), channel_id=1, source_target_pairs={{0,1},{3,2},{4,5},{7,6},{8,9},{11,10},{12,13},{15,14},{16,17},{19,... | collective-permute-start | bytes 1548296 | tf_op jit(solution)/shard_map/ppermute | solution.py:558
  34.2 5.6 %copy-start.2 = (s32[16,4]{0,1:T(4,128)S(1)}, s32[16,4]{0,1:T(4,128)}, u32[]{:S(2)}) copy-start(s32[16,4]{0,1:T(4,128)} %param.26) | copy-start | bytes 772
  34.2 5.6 %copy-start.4 = (s32[16]{0:T(128)S(1)}, s32[16]{0:T(128)}, u32[]{:S(2)}) copy-start(s32[16]{0:T(128)} %decode_length.1) | copy-start | bytes 196
  34.3 1.6 %collective-permute-start.8 = (bf16[64,2048]{1,0:T(8,128)(2,1)S(1)}, bf16[64,2048]{1,0:T(8,128)(2,1)S(1)}, u32[]{:S(2)}, u32[]{:S(2)}) collective-permute-start(bf16[64,2048]{1,0:T(8,128)(2,1)S(1)} %stack.8), channel_id=1, source_target_pairs={{0,4},{4,0},{8,12},{12,8},{1,5},{5,1},{9,13},{13,9},{2,6},{6,2},{1... | collective-permute-start | bytes 786440 | tf_op jit(solution)/shard_map/ppermute | solution.py:404
  34.3 14.9 %collective-permute-start.9 = (bf16[80,2048]{1,0:T(8,128)(2,1)S(1)}, bf16[80,2048]{1,0:T(8,128)(2,1)S(1)}, u32[]{:S(2)}, u32[]{:S(2)}) collective-permute-start(bf16[80,2048]{1,0:T(8,128)(2,1)S(1)} %attend.4.refs_1_.rest_4_.rest_0_), channel_id=1, source_target_pairs={{0,8},{4,12},{8,0},{12,4},{1,9},{5,13},{9,1},{13,5},{2,10},{6,14},... | collective-permute-start | bytes 983048 | tf_op jit(solution)/shard_map/ppermute | solution.py:377
  35.4 15.1 %collective-permute-start.10 = (bf16[80,2048]{1,0:T(8,128)(2,1)S(1)}, bf16[80,2048]{1,0:T(8,128)(2,1)S(1)}, u32[]{:S(2)}, u32[]{:S(2)}) collective-permute-start(bf16[80,2048]{1,0:T(8,128)(2,1)S(1)} %attend.4.refs_1_.rest_4_.rest_0_), channel_id=1, source_target_pairs={{0,4},{4,0},{8,12},{12,8},{1,5},{5,1},{9,13},{13,9},{2,6},{6,2},{1... | collective-permute-start | bytes 983048 | tf_op jit(solution)/shard_map/ppermute | solution.py:404
  38.1 21.3 %collective-permute-start.13 = (bf16[192,1792]{1,0:T(8,128)(2,1)S(1)}, bf16[192,1792]{1,0:T(8,128)(2,1)S(1)}, u32[]{:S(2)}, u32[]{:S(2)}) collective-permute-start(bf16[192,1792]{1,0:T(8,128)(2,1)S(1)} %get-tuple-element.35.refs_0_.refs_2_), channel_id=1, source_target_pairs={{0,1},{3,2},{4,5},{7,6},{8,9},{11,10},{12,13},{15,14},{16,17},{19,... | collective-permute-start | bytes 2064392 | tf_op jit(solution)/shard_map/ppermute | solution.py:558
  49.3 1.7 %collective-permute-start.11 = (bf16[80,2048]{1,0:T(8,128)(2,1)S(1)}, bf16[80,2048]{1,0:T(8,128)(2,1)S(1)}, u32[]{:S(2)}, u32[]{:S(2)}) collective-permute-start(bf16[80,2048]{1,0:T(8,128)(2,1)S(1)} %stack.9), channel_id=1, source_target_pairs={{0,4},{4,0},{8,12},{12,8},{1,5},{5,1},{9,13},{13,9},{2,6},{6,2},{1... | collective-permute-start | bytes 983048 | tf_op jit(solution)/shard_map/ppermute | solution.py:404
  49.5 8.6 %collective-permute-start.16 = (bf16[64,2048]{1,0:T(8,128)(2,1)S(1)}, bf16[64,2048]{1,0:T(8,128)(2,1)S(1)}, u32[]{:S(2)}, u32[]{:S(2)}) collective-permute-start(bf16[64,2048]{1,0:T(8,128)(2,1)S(1)} %attend.5.refs_1_.rest_4_.rest_0_), channel_id=1, source_target_pairs={{0,8},{4,12},{8,0},{12,4},{1,9},{5,13},{9,1},{13,5},{2,10},{6,14},... | collective-permute-start | bytes 786440 | tf_op jit(solution)/shard_map/ppermute | solution.py:377
  53.8 16.9 %collective-permute-start.15 = (bf16[160,1792]{1,0:T(8,128)(2,1)S(1)}, bf16[160,1792]{1,0:T(8,128)(2,1)S(1)}, u32[]{:S(2)}, u32[]{:S(2)}) collective-permute-start(bf16[160,1792]{1,0:T(8,128)(2,1)S(1)} %get-tuple-element.36.refs_0_), channel_id=1, source_target_pairs={{0,1},{3,2},{4,5},{7,6},{8,9},{11,10},{12,13},{15,14},{16,17},{19,... | collective-permute-start | bytes 1720328 | tf_op jit(solution)/shard_map/ppermute | solution.py:558
  58.0 2.2 %collective-permute-start.17 = (bf16[64,2048]{1,0:T(8,128)(2,1)S(1)}, bf16[64,2048]{1,0:T(8,128)(2,1)S(1)}, u32[]{:S(2)}, u32[]{:S(2)}) collective-permute-start(bf16[64,2048]{1,0:T(8,128)(2,1)S(1)} %attend.5.refs_1_.rest_4_.rest_0_), channel_id=1, source_target_pairs={{0,4},{4,0},{8,12},{12,8},{1,5},{5,1},{9,13},{13,9},{2,6},{6,2},{1... | collective-permute-start | bytes 786440 | tf_op jit(solution)/shard_map/ppermute | solution.py:404
  58.1 2.1 %collective-permute-start.18 = (bf16[64,2048]{1,0:T(8,128)(2,1)S(1)}, bf16[64,2048]{1,0:T(8,128)(2,1)S(1)}, u32[]{:S(2)}, u32[]{:S(2)}) collective-permute-start(bf16[64,2048]{1,0:T(8,128)(2,1)S(1)} %stack.11), channel_id=1, source_target_pairs={{0,4},{4,0},{8,12},{12,8},{1,5},{5,1},{9,13},{13,9},{2,6},{6,2},{1... | collective-permute-start | bytes 786440 | tf_op jit(solution)/shard_map/ppermute | solution.py:404
  58.7 12.0 %collective-permute-start.12 = (bf16[96,1792]{1,0:T(8,128)(2,1)S(1)}, bf16[96,1792]{1,0:T(8,128)(2,1)S(1)}, u32[]{:S(2)}, u32[]{:S(2)}) collective-permute-start(bf16[96,1792]{1,0:T(8,128)(2,1)S(1)} %stack.10), channel_id=1, source_target_pairs={{1,2},{2,1},{5,6},{6,5},{9,10},{10,9},{13,14},{14,13},{17,18},{18,... | collective-permute-start | bytes 1032200 | tf_op jit(solution)/shard_map/ppermute | solution.py:561
  59.5 12.0 %collective-permute-start.14 = (bf16[128,1792]{1,0:T(8,128)(2,1)S(1)}, bf16[128,1792]{1,0:T(8,128)(2,1)S(1)}, u32[]{:S(2)}, u32[]{:S(2)}) collective-permute-start(bf16[128,1792]{1,0:T(8,128)(2,1)S(1)} %add.13.rest_5_), channel_id=1, source_target_pairs={{1,2},{2,1},{5,6},{6,5},{9,10},{10,9},{13,14},{14,13},{17,18},{18,... | collective-permute-start | bytes 1376264 | tf_op jit(solution)/shard_map/ppermute | solution.py:561
  62.6 24.0 %collective-permute-start.20 = (bf16[128,1792]{1,0:T(8,128)(2,1)S(1)}, bf16[128,1792]{1,0:T(8,128)(2,1)S(1)}, u32[]{:S(2)}, u32[]{:S(2)}) collective-permute-start(bf16[128,1792]{1,0:T(8,128)(2,1)S(1)} %get-tuple-element.39.refs_0_.refs_2_), channel_id=1, source_target_pairs={{0,1},{3,2},{4,5},{7,6},{8,9},{11,10},{12,13},{15,14},{16,17},{19,... | collective-permute-start | bytes 1376264 | tf_op jit(solution)/shard_map/ppermute | solution.py:558
  70.8 15.6 %collective-permute-start.21 = (bf16[80,1792]{1,0:T(8,128)(2,1)S(1)}, bf16[80,1792]{1,0:T(8,128)(2,1)S(1)}, u32[]{:S(2)}, u32[]{:S(2)}) collective-permute-start(bf16[80,1792]{1,0:T(8,128)(2,1)S(1)} %add.14.refs_4_), channel_id=1, source_target_pairs={{1,2},{2,1},{5,6},{6,5},{9,10},{10,9},{13,14},{14,13},{17,18},{18,... | collective-permute-start | bytes 860168 | tf_op jit(solution)/shard_map/ppermute | solution.py:561
  71.6 21.6 %collective-permute-start.19 = (bf16[112,1792]{1,0:T(8,128)(2,1)S(1)}, bf16[112,1792]{1,0:T(8,128)(2,1)S(1)}, u32[]{:S(2)}, u32[]{:S(2)}) collective-permute-start(bf16[112,1792]{1,0:T(8,128)(2,1)S(1)} %add.15.refs_2_), channel_id=1, source_target_pairs={{1,0},{2,3},{5,4},{6,7},{9,8},{10,11},{13,12},{14,15},{17,16},{18,... | collective-permute-start | bytes 1204232 | tf_op jit(solution)/shard_map/ppermute | solution.py:564
  72.9 23.9 %collective-permute-start.22 = (bf16[144,1792]{1,0:T(8,128)(2,1)S(1)}, bf16[144,1792]{1,0:T(8,128)(2,1)S(1)}, u32[]{:S(2)}, u32[]{:S(2)}) collective-permute-start(bf16[144,1792]{1,0:T(8,128)(2,1)S(1)} %get-tuple-element.40.refs_0_), channel_id=1, source_target_pairs={{0,1},{3,2},{4,5},{7,6},{8,9},{11,10},{12,13},{15,14},{16,17},{19,... | collective-permute-start | bytes 1548296 | tf_op jit(solution)/shard_map/ppermute | solution.py:558
  86.8 15.6 %collective-permute-start.23 = (bf16[144,1792]{1,0:T(8,128)(2,1)S(1)}, bf16[144,1792]{1,0:T(8,128)(2,1)S(1)}, u32[]{:S(2)}, u32[]{:S(2)}) collective-permute-start(bf16[144,1792]{1,0:T(8,128)(2,1)S(1)} %add.18.refs_8_), channel_id=1, source_target_pairs={{1,2},{2,1},{5,6},{6,5},{9,10},{10,9},{13,14},{14,13},{17,18},{18,... | collective-permute-start | bytes 1548296 | tf_op jit(solution)/shard_map/ppermute | solution.py:561
  87.5 6.0 %collective-permute-start.25 = (bf16[64,1792]{1,0:T(8,128)(2,1)S(1)}, bf16[64,1792]{1,0:T(8,128)(2,1)S(1)}, u32[]{:S(2)}, u32[]{:S(2)}) collective-permute-start(bf16[64,1792]{1,0:T(8,128)(2,1)S(1)} %add.17.refs_4_), channel_id=1, source_target_pairs={{1,2},{2,1},{5,6},{6,5},{9,10},{10,9},{13,14},{14,13},{17,18},{18,... | collective-permute-start | bytes 688136 | tf_op jit(solution)/shard_map/ppermute | solution.py:561
  88.1 14.3 %collective-permute-start.24 = (bf16[80,1792]{1,0:T(8,128)(2,1)S(1)}, bf16[80,1792]{1,0:T(8,128)(2,1)S(1)}, u32[]{:S(2)}, u32[]{:S(2)}) collective-permute-start(bf16[80,1792]{1,0:T(8,128)(2,1)S(1)} %add.16.refs_2_), channel_id=1, source_target_pairs={{1,0},{2,3},{5,4},{6,7},{9,8},{10,11},{13,12},{14,15},{17,16},{18,... | collective-permute-start | bytes 860168 | tf_op jit(solution)/shard_map/ppermute | solution.py:564
  93.5 21.7 %collective-permute-start.26 = (bf16[64,1792]{1,0:T(8,128)(2,1)S(1)}, bf16[64,1792]{1,0:T(8,128)(2,1)S(1)}, u32[]{:S(2)}, u32[]{:S(2)}) collective-permute-start(bf16[64,1792]{1,0:T(8,128)(2,1)S(1)} %add.20.refs_4_), channel_id=1, source_target_pairs={{1,0},{2,3},{5,4},{6,7},{9,8},{10,11},{13,12},{14,15},{17,16},{18,... | collective-permute-start | bytes 688136 | tf_op jit(solution)/shard_map/ppermute | solution.py:564
